TPU v7x, 32 devices: a whole 2x2x4 slice. The times are simulated.
32 devices in a mesh: tm: 2 (over y), chan: 16 (over z, x, core).
Axes of the slice: x: 2, y: 2, z: 4, core: 2. Of those that a mesh axis runs over, the one named last changes fastest.
Arguments:
- signal: bfloat16 [2048, 512], P('tm', 'chan'), may hold values from -6 to 6
- mel_frames: bfloat16 [2048, 80], P('tm'), may hold values from -6 to 6
- speaker_ids: int32 [16], P('tm'), may hold values from 0 to 943
- owners: int32 [320], replicated, may hold values from 0 to 15, as said below
- master: float32 [640, 8, 1024], P('chan'), may hold values from -0.25 to 0.25
- first_moment: float32 [640, 8, 1024], P('chan'), may hold values from -96 to 96
- second_moment: float32 [640, 8, 1024], P('chan'), may hold values from 122.88 to 2048
- res_cot: bfloat16 [2048, 512], P('tm', 'chan'), may hold values from -6 to 6
- skip_cot: bfloat16 [2048, 512], P('tm', 'chan'), may hold values from -6 to 6
Outputs:
- residual: float32 [2048, 512], P('tm', 'chan')
- skipped: float32 [2048, 512], P('tm', 'chan')
- grad_input: float32 [2048, 512], P('tm', 'chan')
- new_first: float32 [640, 8, 1024], P('chan')
- new_second: float32 [640, 8, 1024], P('chan')
- new_master: float32 [640, 8, 1024], P('chan')
Inputs may be any that keep to these rules, and one draw needn't show every extreme that they name: Device d of chan owns the blocks b with owners[b] = d; no device owns more than 40 blocks, and one device owns exactly 40.
All inputs are finite; a program needn't handle non-finite values.
Results may differ from a plain program's by a relative error of at most 0.0055.
Values may be sent and summed in bfloat16 or wider, within the bound.
No kernel may reach another device: no remote copies, remote signals or barrier semaphores. Data moves between devices by JAX's collectives and lax.ppermute only.
A program may use at most 64 MiB of HBM per device.

v0:
```python
import jax
import jax.numpy as jnp
from jax import lax
from jax.sharding import PartitionSpec as P

RESID = 512
HIDDEN_SIZE = 512
MELS = 80
SPEAKERS = 944
DILATION = 8
SEG = 128
BLOCK = 8
STEP = 5
GATES = 1024
ROWS = 2560
NBLK = 320


MOMENT_DECAY = 0.5
STEP_RATE = 0.03
WEIGHT_DECAY = 0.01
EPSILON = 1e-08


def shifted_2(block, axis, distance):
    devices = range(lax.axis_size(axis))
    route = [(i - distance, i) for i in devices if i - distance in devices]
    return lax.ppermute(block, axis, route)


def place_index(owners, slots_dev):
    count = owners.shape[0]
    matches = owners[:, None] == owners[None, :]
    before = jnp.arange(count)[None, :] < jnp.arange(count)[:, None]
    ranks = jnp.sum((matches & before).astype(jnp.int32), axis=1)
    return owners * slots_dev + ranks


def local(
    signal, mel_frames, speaker_ids, owners, master, first_moment, second_moment, res_cot, skip_cot
):
    chans = lax.axis_size("chan")
    slots_dev = master.shape[0]
    tok_count = signal.shape[0]
    res_local = signal.shape[1]
    hid_local = HIDDEN_SIZE // chans
    col_count = GATES // chans
    seg_count = speaker_ids.shape[0]
    mel_start = 2 * RESID
    spk_start = mel_start + MELS
    out_start = spk_start + SPEAKERS
    places = place_index(owners, slots_dev)
    received = lax.all_to_all(
        master.astype(jnp.bfloat16), "chan", split_axis=2, concat_axis=0, tiled=True
    )
    params = received[places].reshape(ROWS, col_count)
    tap_prev = params[:RESID]
    tap_now = params[RESID:mel_start]
    mel_proj = params[mel_start:spk_start]
    speaker_table = params[spk_start:out_start]
    out_cols = params[out_start:]
    tail_prev = shifted_2(signal[-DILATION:], "tm", 1)
    inputs, tail_full = (
        lax.all_gather(signal, "chan", axis=1, tiled=True),
        lax.all_gather(tail_prev, "chan", axis=1, tiled=True),
    )
    shifted = jnp.concatenate([tail_full, inputs[:-DILATION]], 0)
    pre_act = jnp.dot(shifted, tap_prev, preferred_element_type=jnp.float32)
    pre_act = pre_act + jnp.dot(inputs, tap_now, preferred_element_type=jnp.float32)
    pre_act = pre_act + jnp.dot(mel_frames, mel_proj, preferred_element_type=jnp.float32)
    one_hot = (speaker_ids[:, None] == jnp.arange(SPEAKERS)[None, :]).astype(jnp.bfloat16)
    embedded = jnp.dot(one_hot, speaker_table, preferred_element_type=jnp.float32)
    pre_act = (pre_act.reshape(seg_count, SEG, col_count) + embedded[:, None, :]).reshape(
        tok_count, col_count
    )
    filt = jnp.tanh(pre_act[:, 0::2])
    gates = jax.nn.sigmoid(pre_act[:, 1::2])
    hidden = (filt * gates).astype(jnp.bfloat16)
    block = out_cols.reshape(lax.axis_size("chan") * res_local, hid_local, 2)
    summed = lax.psum_scatter(
        jnp.einsum("cuw,tu->cwt", block, hidden, preferred_element_type=jnp.float32),
        "chan",
        scatter_dimension=0,
        tiled=True,
    )
    resid_part = summed[:, 0, :].T
    skip_part = summed[:, 1, :].T
    cot_stack = jnp.stack([res_cot.T, skip_cot.T], axis=1)
    piece = lax.all_gather(cot_stack, "chan", axis=0, tiled=True)
    count = piece.shape[0]
    block = out_cols.reshape(count, hid_local, 2)
    grad_hid = jnp.einsum("cwt,cuw->tu", piece, block, preferred_element_type=jnp.float32)
    term = jnp.einsum("cwt,tu->cuw", piece, hidden, preferred_element_type=jnp.float32).reshape(
        count, col_count
    )
    residual = signal.astype(jnp.float32) + resid_part
    grad_filt = grad_hid * gates * (1.0 - filt * filt)
    grad_gate = grad_hid * filt * gates * (1.0 - gates)
    grad_pre = (
        jnp.stack([grad_filt, grad_gate], axis=2).reshape(tok_count, col_count).astype(jnp.bfloat16)
    )
    ahead = shifted_2(grad_pre[:DILATION], "tm", -1)
    later = jnp.concatenate([grad_pre[DILATION:], ahead], 0)
    last_dims = (((1,), (1,)), ((), ()))
    first_part = lax.dot_general(tap_now, grad_pre, last_dims, preferred_element_type=jnp.float32)
    input_part = lax.psum_scatter(
        first_part
        + lax.dot_general(tap_prev, later, last_dims, preferred_element_type=jnp.float32),
        "chan",
        scatter_dimension=0,
        tiled=True,
    )
    grad_input = res_cot.astype(jnp.float32) + input_part.T
    lead_dims = (((0,), (0,)), ((), ()))
    grad_prev = lax.dot_general(shifted, grad_pre, lead_dims, preferred_element_type=jnp.float32)
    grad_now = lax.dot_general(inputs, grad_pre, lead_dims, preferred_element_type=jnp.float32)
    grad_mel = lax.dot_general(mel_frames, grad_pre, lead_dims, preferred_element_type=jnp.float32)
    seg_sums = jnp.sum(grad_pre.astype(jnp.float32).reshape(seg_count, SEG, col_count), axis=1)
    grad_spk = lax.dot_general(
        one_hot.astype(jnp.float32),
        seg_sums,
        lead_dims,
        precision=lax.Precision.HIGHEST,
        preferred_element_type=jnp.float32,
    )
    grad_params = jnp.concatenate([grad_prev, grad_now, grad_mel, grad_spk, term], 0)
    grad_params = lax.psum(grad_params, "tm")
    outgoing = (
        jnp.zeros((chans * slots_dev, BLOCK, col_count), jnp.float32)
        .at[places]
        .set(grad_params.reshape(NBLK, BLOCK, col_count))
    )
    grad_slots = lax.all_to_all(outgoing, "chan", split_axis=0, concat_axis=2, tiled=True)
    mine = lax.axis_index("chan")
    owned = jnp.sum((owners == mine).astype(jnp.int32))
    keep = (jnp.arange(slots_dev) < owned)[:, None, None]
    first_new = MOMENT_DECAY * first_moment + (1.0 - MOMENT_DECAY) * grad_slots
    second_new = MOMENT_DECAY * second_moment + (1.0 - MOMENT_DECAY) * grad_slots * grad_slots
    first_hat = first_new / (1.0 - MOMENT_DECAY**STEP)
    second_hat = second_new / (1.0 - MOMENT_DECAY**STEP)
    stepped = master - STEP_RATE * (
        first_hat / (jnp.sqrt(second_hat) + EPSILON) + WEIGHT_DECAY * master
    )
    new_first = jnp.where(keep, first_new, first_moment)
    new_second = jnp.where(keep, second_new, second_moment)
    new_master = jnp.where(keep, stepped, master)
    return (residual, skip_part, grad_input, new_first, new_second, new_master)


def solution(mesh):
    in_specs = (
        P("tm", "chan"),
        P("tm", None),
        P("tm"),
        P(),
        P("chan", None, None),
        P("chan", None, None),
        P("chan", None, None),
        P("tm", "chan"),
        P("tm", "chan"),
    )
    out_specs = (
        P("tm", "chan"),
        P("tm", "chan"),
        P("tm", "chan"),
        P("chan", None, None),
        P("chan", None, None),
        P("chan", None, None),
    )
    return jax.shard_map(local, mesh=mesh, in_specs=in_specs, out_specs=out_specs, check_vma=False)
```

profile of v0, /device:TPU:0, one launch (start us, length us, event | category | flops | bytes accessed | tf_op | source)
XLA Modules:
  0.0 322.9 jit_solution(13504194581131500091)
XLA Ops:
  10.9 1.9 copy.102
  12.8 3.9 %reshape.82 = bf16[16,2,10240]{2,1,0:T(2,128)(2,1)} reshape(bf16[1024,8,40]{2,1,0:T(8,128)(2,1)S(1)} %bitcast.107) | data formatting | bytes 1310720
  16.7 7.5 %all-to-all-start = ((bf16[16,2,10240]{2,1,0:T(2,128)(2,1)}), bf16[16,2,10240]{2,1,0:T(2,128)(2,1)S(1)}, u32[]{:S(2)}, u32[]{:S(2)}) async-start(bf16[16,2,10240]{2,1,0:T(2,128)(2,1)} %reshape.82), calls=%async_computation | async-start | bytes 1310720 | tf_op jit(solution)/shard_map/all_to_all | solution.py:53
  25.1 3.4 %collective-permute-start = (bf16[8,32]{1,0:T(8,128)(2,1)S(1)}, bf16[8,32]{1,0:T(8,128)(2,1)S(1)}, u32[]{:S(2)}, u32[]{:S(2)}) collective-permute-start(bf16[8,32]{1,0:T(8,128)(2,1)S(1)} %copy.119), channel_id=1, source_target_pairs={{0,16},{1,17},{2,18},{3,19},{4,20},{5,21},{6,22},{7,23},{8,24},{9,... | collective-permute-start | bytes 1544 | tf_op jit(solution)/shard_map/ppermute | solution.py:28
  29.8 22.8 %all-gather = bf16[16,32,8]{1,2,0:T(8,128)(2,1)S(1)} all-gather(bf16[1,32,8]{1,2,0:T(8,128)(2,1)S(1)} %bitcast.118), channel_id=1, replica_groups=mesh['tm'=2,'chan'=16] {'chan'}, dimensions={0}, use_global_device_ids=true | all-gather | bytes 8704 | tf_op jit(solution)/shard_map/all_gather | solution.py:65
  53.0 3.3 %reshape.83 = bf16[1024,8,40]{2,1,0:T(8,128)(2,1)S(1)} reshape(bf16[16,2,10240]{2,1,0:T(2,128)(2,1)S(1)} %all-to-all-done) | data formatting | bytes 1310720
  56.3 2.9 copy.103
  59.2 2.2 gather_fusion
  61.4 1.6 copy.104
  64.5 1.9 fusion.7
  67.9 29.4 %all-gather.6.cloned.1.call-done = bf16[512,2,1024]{2,0,1:T(8,128)(2,1)} async-done(((bf16[32,2,1024]{2,0,1:T(8,128)(2,1)}), bf16[512,2,1024]{2,0,1:T(8,128)(2,1)}) %all-gather.6.cloned.1.call-update) | async-done | bytes 2097168 | tf_op jit(solution)/shard_map/all_gather | solution.py:89
  97.3 2.1 multiply_bitcast_fusion.1
  100.3 2.4 fusion.6
  102.6 1.7 convolution_bitcast_fusion.5
  105.2 1.9 reshape.59
  117.0 2.7 collective-permute-done.1
  119.7 2.7 convolution_add_fusion
  123.3 2.7 fusion.17
  126.0 32.7 %all-reduce.2.cloned.1.call-done = f32[320,8,64]{2,1,0:T(8,128)} async-done(((f32[320,8,64]{2,1,0:T(8,128)}), f32[320,8,64]{2,1,0:T(8,128)}) %all-reduce.2.cloned.1.call-update) | async-done | bytes 655376 | tf_op jit(solution)/shard_map/psum | solution.py:127
  158.9 21.1 %scatter_fusion = f32[640,8,64]{2,1,0:T(8,128)S(1)} fusion(f32[640,8,64]{2,1,0:T(8,128)S(1)} %broadcast_in_dim.31, s32[320]{0:T(512)S(1)} %get-tuple-element.12, f32[320,8,64]{2,1,0:T(8,128)} %all-reduce.2.cloned.1.call-done), kind=kCustom, calls=%fused_computation.1 | custom fusion | bytes 1967360 | tf_op jit(solution)/shard_map/scatter | solution.py:131
  180.0 2.7 reshape.84
  182.7 5.6 %all-to-all-start.1 = ((f32[16,1,20480]{2,1,0:T(1,128)}), f32[16,1,20480]{2,1,0:T(1,128)S(1)}, u32[]{:S(2)}, u32[]{:S(2)}) async-start(f32[16,1,20480]{2,1,0:T(1,128)} %reshape.84), calls=%async_computation.3 | async-start | bytes 2621440 | tf_op jit(solution)/shard_map/all_to_all | solution.py:133
  188.9 35.2 %all-to-all-done.1 = f32[16,1,20480]{2,1,0:T(1,128)S(1)} async-done(((f32[16,1,20480]{2,1,0:T(1,128)}), f32[16,1,20480]{2,1,0:T(1,128)S(1)}, u32[]{:S(2)}, u32[]{:S(2)}) %all-to-all-start.1) | async-done | bytes 1310752 | tf_op jit(solution)/shard_map/all_to_all | solution.py:133
  224.6 5.2 %reduce = f32[16,20480]{1,0:T(8,128)} reduce(f32[16,1,20480]{2,1,0:T(1,128)S(1)} %all-to-all-done.1, f32[]{:T(128)} %broadcast.50), dimensions={1}, to_apply=%all_to_all.30.reduce_sub_computation | reduce | bytes 2621444 | tf_op jit(solution)/shard_map/all_to_all | solution.py:133
  229.8 2.4 reshape.85
  232.2 3.0 copy.117
  235.2 2.3 all_to_all.33
  237.5 4.8 %subtract_select_fusion = (f32[40,8,1024]{2,1,0:T(8,128)}, f32[40,8,1024]{2,1,0:T(8,128)}, f32[40,8,1024]{2,1,0:T(8,128)}) fusion(f32[40,8,1024]{2,1,0:T(8,128)S(1)} %copy-done.2, f32[40,8,1024]{2,1,0:T(8,128)S(1)} %all_to_all.33, f32[40,8,1024]{2,1,0:T(8,128)} %param.14, f32[40,8,1024]{2,1,0:T(8,128)} %param.15, pred[40]{0:T(512)(128)(4,1)S(1)} %iota_compare_fusion.4), kind=kLoop, calls=%fused_computation.2 | loop fusion | flops 5570560 | bytes 9175080 | tf_op jit(solution)/shard_map/jit(_where)/select_n | solution.py:146
  242.4 1.6 bitcast_add_fusion
  243.9 69.3 %reduce-scatter.3.cloned.1.call-done = f32[32,2,1024]{2,0,1:T(8,128)} async-done(((f32[512,2,1024]{2,0,1:T(8,128)}), f32[32,2,1024]{2,0,1:T(8,128)}) %reduce-scatter.3.cloned.1.call-update) | async-done | bytes 262160 | tf_op jit(solution)/shard_map/reduce_scatter | solution.py:80
  313.3 1.6 fusion.10
  314.8 1.6 slice_bitcast_fusion.2
  (85 shorter events, 22.7 us)
Async XLA Ops:
  7.2 59.7 %copy-start = (bf16[1024,80]{0,1:T(8,128)(2,1)S(1)}, bf16[1024,80]{0,1:T(8,128)(2,1)}, u32[]{:S(2)}) copy-start(bf16[1024,80]{0,1:T(8,128)(2,1)} %param.10) | copy-start | bytes 491524
  7.2 57.3 %all-gather.4.cloned.1.call-start = ((), (), s32[]{:S(2)}) async-start(), calls=%async_computation.4 | async-start | bytes 1114112 | tf_op jit(solution)/shard_map/all_gather | solution.py:64
  7.9 89.4 %all-gather.6.cloned.1.call-start = ((), (), s32[]{:S(2)}) async-start(), calls=%async_computation.6 | async-start | bytes 2228224 | tf_op jit(solution)/shard_map/all_gather | solution.py:89
  16.7 11.8 %copy-start.13 = (s32[320]{0:T(512)S(1)}, s32[320]{0:T(512)}, u32[]{:S(2)}) copy-start(s32[320]{0:T(512)} %param.12) | copy-start | bytes 3844
  16.7 36.2 %all-to-all-start = ((bf16[16,2,10240]{2,1,0:T(2,128)(2,1)}), bf16[16,2,10240]{2,1,0:T(2,128)(2,1)S(1)}, u32[]{:S(2)}, u32[]{:S(2)}) async-start(bf16[16,2,10240]{2,1,0:T(2,128)(2,1)} %reshape.82), calls=%async_computation | async-start | bytes 1310720 | tf_op jit(solution)/shard_map/all_to_all | solution.py:53
  24.2 134.5 %all-reduce.2.cloned.1.call-start = ((), (), s32[]{:S(2)}) async-start(), calls=%async_computation.8 | async-start | bytes 2621440 | tf_op jit(solution)/shard_map/psum | solution.py:127
  25.1 4.7 %collective-permute-start = (bf16[8,32]{1,0:T(8,128)(2,1)S(1)}, bf16[8,32]{1,0:T(8,128)(2,1)S(1)}, u32[]{:S(2)}, u32[]{:S(2)}) collective-permute-start(bf16[8,32]{1,0:T(8,128)(2,1)S(1)} %copy.119), channel_id=1, source_target_pairs={{0,16},{1,17},{2,18},{3,19},{4,20},{5,21},{6,22},{7,23},{8,24},{9,... | collective-permute-start | bytes 1544 | tf_op jit(solution)/shard_map/ppermute | solution.py:28
  52.9 11.5 %copy-start.10 = (bf16[8,512]{0,1:T(8,128)(2,1)}, bf16[8,512]{0,1:T(8,128)(2,1)S(1)}, u32[]{:S(2)}) copy-start(bf16[8,512]{0,1:T(8,128)(2,1)S(1)} %copy.107) | copy-start | bytes 24580
  61.4 5.4 %copy-start.4 = (bf16[320,8,64]{2,1,0:T(8,128)(2,1)}, bf16[320,8,64]{2,1,0:T(8,128)(2,1)S(1)}, u32[]{:S(2)}) copy-start(bf16[320,8,64]{2,1,0:T(8,128)(2,1)S(1)} %gather_fusion) | copy-start | bytes 983044
  61.4 2.7 copy-start.14
  64.5 1.9 copy-start.3
  100.3 8.9 %copy-start.1 = (bf16[512,2,1024]{2,0,1:T(8,128)(2,1)S(1)}, bf16[512,2,1024]{2,0,1:T(8,128)(2,1)}, u32[]{:S(2)}) copy-start(bf16[512,2,1024]{2,0,1:T(8,128)(2,1)} %all-gather.6.cloned.1.call-done) | copy-start | bytes 6291460
  110.7 1.6 copy-start.6
  110.7 1.6 copy-start.11
  110.7 1.6 copy-start.12
  112.5 2.9 copy-start.5
  114.0 128.4 %reduce-scatter.5.cloned.1.call-start = ((), (), s32[]{:S(2)}) async-start(), calls=%async_computation.7 | async-start | bytes 2228224 | tf_op jit(solution)/shard_map/reduce_scatter | solution.py:106
  114.1 5.6 %collective-permute-start.1 = (bf16[8,64]{0,1:T(8,128)(2,1)S(1)}, bf16[8,64]{0,1:T(8,128)(2,1)S(1)}, u32[]{:S(2)}, u32[]{:S(2)}) collective-permute-start(bf16[8,64]{0,1:T(8,128)(2,1)S(1)} %bitcast.117), channel_id=1, source_target_pairs={{16,0},{17,1},{18,2},{19,3},{20,4},{21,5},{22,6},{23,7},{24,8},{25... | collective-permute-start | bytes 3080 | tf_op jit(solution)/shard_map/ppermute | solution.py:28
  122.4 0.8 copy-start.7
  122.4 190.8 %reduce-scatter.3.cloned.1.call-start = ((), (), s32[]{:S(2)}) async-start(), calls=%async_computation.5 | async-start | bytes 4456448 | tf_op jit(solution)/shard_map/reduce_scatter | solution.py:80
  182.7 41.4 %all-to-all-start.1 = ((f32[16,1,20480]{2,1,0:T(1,128)}), f32[16,1,20480]{2,1,0:T(1,128)S(1)}, u32[]{:S(2)}, u32[]{:S(2)}) async-start(f32[16,1,20480]{2,1,0:T(1,128)} %reshape.84), calls=%async_computation.3 | async-start | bytes 2621440 | tf_op jit(solution)/shard_map/all_to_all | solution.py:133
  235.2 2.3 copy-start.2
  237.5 4.9 %copy-start.9 = (bf16[1024,32]{0,1:T(8,128)(2,1)S(1)}, bf16[1024,32]{0,1:T(8,128)(2,1)}, u32[]{:S(2)}) copy-start(bf16[1024,32]{0,1:T(8,128)(2,1)} %param.16) | copy-start | bytes 196612
  237.5 75.8 %copy-start.8 = (bf16[1024,32]{0,1:T(8,128)(2,1)S(1)}, bf16[1024,32]{0,1:T(8,128)(2,1)}, u32[]{:S(2)}) copy-start(bf16[1024,32]{0,1:T(8,128)(2,1)} %param.9) | copy-start | bytes 196612
Sparse Core Ops, SparseCore 0:
  10.2 43.2 all-gather.3
  56.3 40.9 all-gather.5
  114.1 44.5 all-reduce.1
  162.7 75.4 reduce-scatter.4
  241.9 71.2 reduce-scatter.2
where the time goes:
time: 325 us; the launch traced here: 323 us
  waiting for transfers between devices  171 us (53%)
  local copies, waits for them, and re-layouts  58.3 us (18%)
  blocking collectives  22.8 us (7%)
  matrix products  19.5 us (6%)
  other arithmetic  19.3 us (6%)
  starting transfers between devices  18.2 us (6%)
  between operations  14.2 us (4%)
    reduce_scatter x1, waiting for transfers between devices, local(): lax.psum_scatter(jnp.einsum('cuw,tu->cwt', block, hidden, preferred_eleme...  69.3 us
    all_to_all x1, waiting for transfers between devices, local(): lax.all_to_all(outgoing, 'chan', split_axis=0, concat_axis=2, tiled=True)  35.2 us
    psum x1, waiting for transfers between devices, local(): grad_params = lax.psum(grad_params, 'tm')  32.7 us
    all_gather x1, waiting for transfers between devices, local(): piece = lax.all_gather(cot_stack, 'chan', axis=0, tiled=True)  29.4 us
    all_gather x1, blocking collectives, local(): lax.all_gather(tail_prev, 'chan', axis=1, tiled=True)  22.8 us
    scatter x1, local copies, waits for them, and re-layouts, local(): outgoing = jnp.zeros((chans * slots_dev, BLOCK, col_count), jnp.float32)....  21.1 us
    unnamed x37, local copies, waits for them, and re-layouts  13.2 us
    all_to_all x1, starting transfers between devices, local(): lax.all_to_all(master.astype(jnp.bfloat16), 'chan', split_axis=2, concat_...  7.49 us
  transfers between devices with their start and end apart: 9, of which 6 were waited for; matrix products, arithmetic and copies ran while one was open for 23% of the time, Pallas kernels for 0%

commit v1 on v0

v1 whole, which is shorter than its diff:
```python
import functools

import jax
import jax.numpy as jnp
from jax import lax
from jax.experimental import pallas as pl
from jax.experimental.pallas import tpu as pltpu
from jax.sharding import PartitionSpec as P

RESID = 512
HIDDEN_SIZE = 512
MELS = 80
SPEAKERS = 944
DILATION = 8
SEG = 128
BLOCK = 8
STEP = 5
GATES = 1024
ROWS = 2560
NBLK = 320

MOMENT_DECAY = 0.5
STEP_RATE = 0.03
WEIGHT_DECAY = 0.01
EPSILON = 1e-08

F32 = jnp.float32
BF16 = jnp.bfloat16
NN = (((1,), (0,)), ((), ()))
NT = (((1,), (1,)), ((), ()))
TN = (((0,), (0,)), ((), ()))

TAPS = 2 * RESID // BLOCK
MEL_AT = TAPS
MEL_BLOCKS = MELS // BLOCK
SEG_AT = 144
OUT_AT = 160
PACKED = 224
SPK_BLOCK = TAPS + MEL_BLOCKS
OUT_BLOCK = SPK_BLOCK + SPEAKERS // BLOCK
PIECE = 112


def dot(a, b, dims=NN):
    return lax.dot_general(a, b, dims, preferred_element_type=F32)


def iota(shape, dim):
    return lax.broadcasted_iota(jnp.int32, shape, dim)


def onehot(cond):
    return jnp.where(cond, 1.0, 0.0).astype(BF16)


def call(kernel, out, n_smem, n_in, flops=0, mbytes=1, scratch=()):
    return pl.pallas_call(
        kernel,
        out_shape=out,
        in_specs=[pl.BlockSpec(memory_space=pltpu.SMEM)] * n_smem
        + [pl.BlockSpec(memory_space=pltpu.VMEM)] * n_in,
        out_specs=jax.tree.map(lambda _: pl.BlockSpec(memory_space=pltpu.VMEM), out),
        scratch_shapes=list(scratch),
        compiler_params=pltpu.CompilerParams(vmem_limit_bytes=48 * 2**20),
        cost_estimate=pl.CostEstimate(
            flops=flops, bytes_accessed=int(mbytes * 2**20), transcendentals=0
        ),
    )


def gate_order(dim):
    natural, split = iota((256, 256), dim), iota((256, 256), 1 - dim)
    return onehot(natural == 2 * (split & 127) + (split >> 7))


def pack_weights(ids, master, out):
    half = ids[0]
    slots = master.shape[0]
    rows = 4 * slots
    here = iota((rows, 8 * slots), 0)
    there = iota((rows, 8 * slots), 1)
    row, slot = jnp.zeros_like(here), here
    for step in range(1, 4):
        past = here >= step * slots
        row = jnp.where(past, step, row)
        slot = jnp.where(past, here - step * slots, slot)
    pick = onehot(there == 8 * slot + 4 * half + row)
    flat = master[...].reshape(8 * slots, GATES).astype(BF16)
    got = dot(pick, flat)
    for z in range(4):
        for j in range(4):
            out[4 * z + j] = got[j * slots : (j + 1) * slots, 256 * z : 256 * (z + 1)].astype(BF16)


def pack_tokens(ids, sig, res, skp, halo, o0, o1, o2, o3):
    j = ids[1] & 3
    ends = []
    outs = (o0, o1, o2, o3)
    for k in range(4):
        to = j ^ k
        cut = pl.ds(pl.multiple_of(to * 256, 256), 256)
        for n, part in enumerate((sig, res, skp)):
            outs[k][32 * n : 32 * n + 32, :] = part[:, cut]
        before = sig[:, pl.ds(pl.multiple_of(jnp.maximum(to * 256 - 128, 0), 128), 128)]
        ends.append(jnp.where(to == 0, halo[...].astype(F32), before.astype(F32)))
    tails = jnp.concatenate(ends, 0).astype(BF16)
    last = onehot(iota((16, 128), 1) == iota((16, 128), 0) + 112)
    rows = dot(last, tails, NT)
    lane = iota((16, 128), 1)
    for k in range(4):
        outs[k][96:112, 0:128] = jnp.where((lane >> 5) == k, rows, 0.0).astype(BF16)
        outs[k][96:112, 128:256] = jnp.zeros((16, 128), BF16)


def place_blocks(sid, owners, pick, put, *, slots_dev):
    own_row = owners[...]
    down, across = iota((NBLK, NBLK), 0), iota((NBLK, NBLK), 1)
    row_all = jnp.broadcast_to(own_row, (NBLK, NBLK))
    own_col = jnp.sum(jnp.where(down == across, row_all, 0), axis=1, keepdims=True)
    before = (own_col == row_all) & (down < across)
    rank = jnp.sum(jnp.where(before, 1, 0), axis=0, keepdims=True)
    place = own_row * slots_dev + rank
    n = iota((PACKED, 1), 0)
    spk = jnp.zeros((PACKED, 1), jnp.int32)
    for s in range(16):
        spk = jnp.where(n == SEG_AT + s, sid[s] >> 3, spk)
    blk = jnp.where(
        n < SPK_BLOCK,
        n,
        jnp.where(n < SEG_AT, -1, jnp.where(n < OUT_AT, SPK_BLOCK + spk, n + (OUT_BLOCK - OUT_AT))),
    )
    match = jnp.broadcast_to(blk, (PACKED, NBLK)) == iota((PACKED, NBLK), 1)
    at = jnp.sum(jnp.where(match, jnp.broadcast_to(place, (PACKED, NBLK)), 0), axis=1, keepdims=True)
    at = jnp.where(blk < 0, -1, at)
    slots = pick.shape[1]
    pick[...] = onehot(jnp.broadcast_to(at, (PACKED, slots)) == iota((PACKED, slots), 1))
    same = iota((PACKED, PACKED), 0) == iota((PACKED, PACKED), 1)
    at_row = jnp.sum(jnp.where(same, jnp.broadcast_to(at, (PACKED, PACKED)), 0), axis=0, keepdims=True)
    put[...] = onehot(jnp.broadcast_to(at_row, (slots, PACKED)) == iota((slots, PACKED), 0))


def gather_blocks(pick, slots, out):
    got = dot(pick[...], slots[...]).astype(BF16)
    got = dot(got, gate_order(0)).astype(BF16)
    for n in range(8):
        out[n] = got


def scatter_blocks(put, parts, out):
    total = parts[0].astype(F32)
    for n in range(1, 8):
        total = total + parts[n].astype(F32)
    natural = dot(total.astype(BF16), gate_order(1)).astype(BF16)
    spread = dot(put[...], natural).astype(BF16)
    out[0] = spread
    out[1] = spread


def channel_of(pos, ch):
    return ((pos >> 5) ^ ch) * 32 + (pos & 31)


def layer(ids, packed, p0, p1, p2, p3, mel, grads, z0, z1, z2, z3, feat):
    half, ch = ids[0], ids[1]
    j = ch & 3
    got = (p0, p1, p2, p3)
    sq = (RESID, RESID)

    def order(dim):
        major = iota(sq, dim)
        return onehot(channel_of(iota(sq, 1 - dim), ch) == 8 * (major & 63) + (major >> 6))

    to_major = order(0)
    to_place = order(1)
    tokens = 256

    def stacked(n):
        return jnp.concatenate(
            [got[k][i, 32 * n : 32 * n + 32, :] for k in range(4) for i in range(4)], 0
        )

    sig = dot(to_major, stacked(0))
    res = dot(to_major, stacked(1)).astype(BF16)
    skp = dot(to_major, stacked(2)).astype(BF16)
    ends = []
    for k in range(4):
        end = got[k][0, 96:112, 0:128].astype(F32)
        for i in range(1, 4):
            end = end + got[k][i, 96:112, 0:128].astype(F32)
        ends.append(end)
    halo = jnp.concatenate([jnp.zeros((112, RESID), F32), jnp.concatenate(ends, 1)], 0).astype(BF16)
    halo = pltpu.roll(dot(to_major, halo, NT), DILATION, 1)
    moved = pltpu.roll(sig, DILATION, 1)
    first = iota((RESID, 128), 1) < DILATION
    shifted = jnp.concatenate([jnp.where(first, halo, moved[:, :128]), moved[:, 128:]], 1).astype(BF16)
    sig = sig.astype(BF16)
    m = iota((128, MELS), 0)
    mel_pick = onehot(((m & 15) < MEL_BLOCKS) & (iota((128, MELS), 1) == 8 * (m & 15) + (m >> 4)))
    mels = dot(mel_pick, mel[:, pl.ds(pl.multiple_of(j * tokens, tokens), tokens)]).astype(BF16)
    seg_row = iota((16, tokens), 0)
    seg_of = 8 * half + 2 * j + (iota((16, tokens), 1) >> 7)
    sub = jnp.where(iota((16, tokens), 1) < SEG, ids[2 + 2 * j] & 7, ids[3 + 2 * j] & 7)
    for r in range(8):
        feat[r, 0:64] = shifted[64 * r : 64 * r + 64]
        feat[r, 64:128] = sig[64 * r : 64 * r + 64]
        feat[r, 128:144] = mels[16 * r : 16 * r + 16]
        feat[r, 144:160] = onehot((seg_row == seg_of) & (sub == r))
    features = feat[...].reshape(8 * OUT_AT, tokens)
    conv = packed[:, 0:OUT_AT, :].reshape(8 * OUT_AT, 256)
    pre = dot(conv, features, TN)
    filt = jnp.tanh(pre[:128])
    gate = jax.nn.sigmoid(pre[128:])
    hidden = (filt * gate).astype(BF16)
    out_res = packed[:, OUT_AT:PACKED, 0:128].reshape(RESID, 128)
    out_skp = packed[:, OUT_AT:PACKED, 128:256].reshape(RESID, 128)
    res_part = dot(out_res, hidden).astype(BF16)
    skp_part = dot(out_skp, hidden).astype(BF16)
    grad_hidden = dot(out_res, res, TN) + dot(out_skp, skp, TN)
    grad_pre = jnp.concatenate(
        [
            grad_hidden * gate * (1.0 - filt * filt),
            grad_hidden * filt * gate * (1.0 - gate),
        ],
        0,
    ).astype(BF16)
    prev = packed[:, 0:64, :].reshape(RESID, 256)
    now = packed[:, 64:128, :].reshape(RESID, 256)
    later = dot(prev, grad_pre)
    kept = iota((RESID, tokens), 1) < tokens - DILATION
    in_part = dot(now, grad_pre) + jnp.where(kept, pltpu.roll(later, tokens - DILATION, 1), 0.0)
    conv_grad = dot(features, grad_pre, NT).astype(BF16)
    res_grad = dot(res, hidden, NT).astype(BF16)
    skp_grad = dot(skp, hidden, NT).astype(BF16)
    grads[:, 0:OUT_AT, :] = conv_grad.reshape(8, OUT_AT, 256)
    grads[:, OUT_AT:PACKED, 0:128] = res_grad.reshape(8, 64, 128)
    grads[:, OUT_AT:PACKED, 128:256] = skp_grad.reshape(8, 64, 128)
    res_part = dot(to_place, res_part).astype(BF16)
    skp_part = dot(to_place, skp_part).astype(BF16)
    in_part = dot(to_place, in_part.astype(BF16)).astype(BF16)
    early = dot(to_place, later[:, :128].astype(BF16)).astype(BF16)
    head = onehot(iota((16, 128), 0) == iota((16, 128), 1))
    early = dot(head, early, NT).astype(BF16)
    outs = (z0, z1, z2, z3)
    for k in range(4):
        for i in range(4):
            at = 128 * k + 32 * i
            outs[k][i, 0:32] = res_part[at : at + 32]
            outs[k][i, 32:64] = skp_part[at : at + 32]
            outs[k][i, 64:96] = in_part[at : at + 32]
            outs[k][i, 96:112, 0:128] = early[:, 128 * k : 128 * k + 128]
            outs[k][i, 96:112, 128:256] = jnp.zeros((16, 128), BF16)


def sum_units(z0, z1, z2, z3, o0, o1, o2, o3):
    for i, out in enumerate((o0, o1, o2, o3)):
        out[...] = (
            z0[i].astype(F32) + z1[i].astype(F32) + z2[i].astype(F32) + z3[i].astype(F32)
        ).astype(BF16)


def late_tail(rows, k):
    lane = onehot(iota((32, 128), 1) == 32 * k + iota((32, 128), 0))
    chans = dot(lane, rows, NT).astype(BF16)
    t = iota((16, 128), 0)
    return dot(chans, onehot((t < DILATION) & (iota((16, 128), 1) == 120 + t)))


def edge(ids, o0, o1, o2, o3, out):
    j = ids[1] & 3
    total = jnp.zeros((32, 128), F32)
    for k, piece in enumerate((o0, o1, o2, o3)):
        total = total + jnp.where(j == k, late_tail(piece[96:112, 0:128], k), 0.0)
    out[...] = total.astype(BF16)


def finish_tokens(ids, o0, o1, o2, o3, ahead, sig, res, residual, skipped, grad_in):
    j = ids[1] & 3
    pieces = (o0, o1, o2, o3)
    for k, piece in enumerate(pieces):
        cut = pl.ds(pl.multiple_of((j ^ k) * 256, 256), 256)
        residual[:, cut] = sig[:, cut].astype(F32) + piece[0:32, :].astype(F32)
        skipped[:, cut] = piece[32:64, :].astype(F32)
        grad_in[:, cut] = res[:, cut].astype(F32) + piece[64:96, :].astype(F32)
    for k, piece in enumerate(pieces):
        tail = late_tail(piece[96:112, 0:128], k)
        start = (j ^ k) * 256 - 128

        @pl.when(start >= 0)
        def _():
            cut = pl.ds(pl.multiple_of(start, 128), 128)
            grad_in[:, cut] = grad_in[:, cut] + tail

    grad_in[:, 896:1024] = grad_in[:, 896:1024] + ahead[...].astype(F32)


def update(ids, owners, grads, master, first, second, new_first, new_second, new_master):
    slots = grads.shape[1]
    owned = jnp.sum(jnp.where(owners[...] == ids[1], 1, 0))
    keep = iota((8 * slots, 1), 0) < 8 * owned
    spread = []
    for r in range(8):
        spread.append(onehot(iota((8 * slots, slots), 0) == 8 * iota((8 * slots, slots), 1) + r))
    for z in range(4):
        cut = slice(256 * z, 256 * z + 256)
        grad = dot(spread[0], grads[4 * z])
        for r in range(1, 8):
            grad = grad + dot(spread[r], grads[16 * (r // 4) + 4 * z + r % 4])
        old_m = master[:, cut]
        old_f = first[:, cut]
        old_s = second[:, cut]
        first_new = MOMENT_DECAY * old_f + (1.0 - MOMENT_DECAY) * grad
        second_new = MOMENT_DECAY * old_s + (1.0 - MOMENT_DECAY) * grad * grad
        first_hat = first_new / (1.0 - MOMENT_DECAY**STEP)
        second_hat = second_new / (1.0 - MOMENT_DECAY**STEP)
        stepped = old_m - STEP_RATE * (
            first_hat / (jnp.sqrt(second_hat) + EPSILON) + WEIGHT_DECAY * old_m
        )
        new_first[:, cut] = jnp.where(keep, first_new, old_f)
        new_second[:, cut] = jnp.where(keep, second_new, old_s)
        new_master[:, cut] = jnp.where(keep, stepped, old_m)


BOTH = ("tm", "chan")


def swap(x, k):
    n = lax.axis_size("chan")
    return lax.ppermute(x, "chan", [(i, i ^ k) for i in range(n)])


def local(
    signal, mel_frames, speaker_ids, owners, master, first_moment, second_moment, res_cot, skip_cot
):
    slots_dev = master.shape[0]
    slots = 16 * slots_dev
    half = lax.axis_index("tm")
    ids = jnp.concatenate([jnp.stack([half, lax.axis_index("chan")]).astype(jnp.int32), speaker_ids])
    sig, res, skp, mel = signal.T, res_cot.T, skip_cot.T, mel_frames.T
    own_row = owners.reshape(1, NBLK)
    share = [[16 * y + 4 * z + j for y in range(2) for j in range(4)] for z in range(4)]
    sds = jax.ShapeDtypeStruct

    halo = lax.ppermute(sig[:, -128:], "tm", [(0, 1)])
    other_ids = lax.ppermute(speaker_ids, "tm", [(0, 1), (1, 0)])
    sids = jnp.where(
        half == 0,
        jnp.concatenate([speaker_ids, other_ids]),
        jnp.concatenate([other_ids, speaker_ids]),
    )

    sent = call(pack_weights, sds((16, slots_dev, 256), BF16), 1, 1)(ids, master)
    arrived = lax.all_to_all(sent, "chan", 0, 0, tiled=True)
    piece = sds((PIECE, 256), BF16)
    o = call(pack_tokens, (piece,) * 4, 1, 4)(ids, sig, res, skp, halo)
    mine = jnp.stack([o[0], swap(o[1], 1), swap(o[2], 2), swap(o[3], 3)])
    p1, p2, p3 = (swap(mine, 4 * k) for k in (1, 2, 3))

    pick, put = call(
        functools.partial(place_blocks, slots_dev=slots_dev),
        (sds((PACKED, slots), BF16), sds((slots, PACKED), BF16)),
        1,
        1,
    )(sids, own_row)
    gathered = call(gather_blocks, sds((8, PACKED, 256), BF16), 0, 2)(
        pick, arrived.reshape(slots, 256)
    )
    packed = lax.all_to_all(gathered, BOTH, 0, 0, axis_index_groups=share)

    quad = sds((4, PIECE, 256), BF16)
    grads, z0, z1, z2, z3 = call(
        layer,
        (sds((8, PACKED, 256), BF16), quad, quad, quad, quad),
        1,
        6,
        scratch=(pltpu.VMEM((8, OUT_AT, 256), BF16),),
    )(ids, packed, mine, p1, p2, p3, mel)

    parts = lax.all_to_all(grads, BOTH, 0, 0, axis_index_groups=share)
    t1, t2, t3 = (swap(z, 4 * k) for k, z in ((1, z1), (2, z2), (3, z3)))
    o = call(sum_units, (piece,) * 4, 0, 4)(z0, t1, t2, t3)
    o = (o[0], swap(o[1], 1), swap(o[2], 2), swap(o[3], 3))
    spread = call(scatter_blocks, sds((2, slots, 256), BF16), 0, 2)(put, parts)
    returned = lax.all_to_all(spread.reshape(32, slots_dev, 256), BOTH, 0, 0)
    tail = call(edge, sds((32, 128), BF16), 1, 4)(ids, *o)
    ahead = lax.ppermute(tail, "tm", [(1, 0)])
    narrow = sds(sig.shape, F32)
    residual, skipped, grad_in = call(finish_tokens, (narrow,) * 3, 1, 7)(
        ids, *o, ahead, sig, res
    )
    flat = (8 * slots_dev, GATES)
    new = call(update, (sds(flat, F32),) * 3, 1, 5)(
        ids,
        own_row,
        returned,
        master.reshape(flat),
        first_moment.reshape(flat),
        second_moment.reshape(flat),
    )
    return (residual.T, skipped.T, grad_in.T, *(x.reshape(master.shape) for x in new))


def place_index(owners, slots_dev):
    count = owners.shape[0]
    matches = owners[:, None] == owners[None, :]
    before = jnp.arange(count)[None, :] < jnp.arange(count)[:, None]
    ranks = jnp.sum((matches & before).astype(jnp.int32), axis=1)
    return owners * slots_dev + ranks


def local_plain(
    signal, mel_frames, speaker_ids, owners, master, first_moment, second_moment, res_cot, skip_cot
):
    chans = lax.axis_size("chan")
    slots_dev = master.shape[0]
    tok_count = signal.shape[0]
    hid_local = HIDDEN_SIZE // chans
    col_count = GATES // chans
    seg_count = speaker_ids.shape[0]
    spk_start = 2 * RESID + MELS
    out_start = spk_start + SPEAKERS
    places = place_index(owners, slots_dev)
    table = places[:, None] == jnp.arange(chans * slots_dev)[None, :]
    received = lax.all_to_all(
        master.astype(BF16), "chan", split_axis=2, concat_axis=0, tiled=True
    ).reshape(chans * slots_dev, BLOCK * col_count)
    params = jnp.dot(table.astype(BF16), received, preferred_element_type=F32)
    params = params.astype(BF16).reshape(ROWS, col_count)
    tap_prev, tap_now = params[:RESID], params[RESID : 2 * RESID]
    mel_proj = params[2 * RESID : spk_start]
    speaker_table = params[spk_start:out_start]
    out_cols = params[out_start:].reshape(RESID, hid_local, 2)
    n_tm = lax.axis_size("tm")
    tail_prev = lax.ppermute(signal[-DILATION:], "tm", [(i, i + 1) for i in range(n_tm - 1)])
    inputs = lax.all_gather(signal, "chan", axis=1, tiled=True)
    tail_full = lax.all_gather(tail_prev, "chan", axis=1, tiled=True)
    shifted = jnp.concatenate([tail_full, inputs[:-DILATION]], 0)
    pre_act = jnp.dot(shifted, tap_prev, preferred_element_type=F32)
    pre_act = pre_act + jnp.dot(inputs, tap_now, preferred_element_type=F32)
    pre_act = pre_act + jnp.dot(mel_frames, mel_proj, preferred_element_type=F32)
    one_hot = (speaker_ids[:, None] == jnp.arange(SPEAKERS)[None, :]).astype(BF16)
    embedded = jnp.dot(one_hot, speaker_table, preferred_element_type=F32)
    pre_act = (pre_act.reshape(seg_count, SEG, col_count) + embedded[:, None, :]).reshape(
        tok_count, col_count
    )
    filt = jnp.tanh(pre_act[:, 0::2])
    gates = jax.nn.sigmoid(pre_act[:, 1::2])
    hidden = (filt * gates).astype(BF16)
    summed = lax.psum_scatter(
        jnp.einsum("cuw,tu->cwt", out_cols, hidden, preferred_element_type=F32),
        "chan",
        scatter_dimension=0,
        tiled=True,
    )
    cots = lax.all_gather(
        jnp.stack([res_cot.T, skip_cot.T], axis=1), "chan", axis=0, tiled=True
    )
    grad_hid = jnp.einsum("cwt,cuw->tu", cots, out_cols, preferred_element_type=F32)
    term = jnp.einsum("cwt,tu->cuw", cots, hidden, preferred_element_type=F32)
    grad_filt = grad_hid * gates * (1.0 - filt * filt)
    grad_gate = grad_hid * filt * gates * (1.0 - gates)
    grad_pre = (
        jnp.stack([grad_filt, grad_gate], axis=2).reshape(tok_count, col_count).astype(BF16)
    )
    ahead = lax.ppermute(grad_pre[:DILATION], "tm", [(i + 1, i) for i in range(n_tm - 1)])
    later = jnp.concatenate([grad_pre[DILATION:], ahead], 0)
    input_part = lax.psum_scatter(
        dot(tap_now, grad_pre, NT) + dot(tap_prev, later, NT),
        "chan",
        scatter_dimension=0,
        tiled=True,
    )
    seg_sums = jnp.sum(grad_pre.astype(F32).reshape(seg_count, SEG, col_count), axis=1)
    grad_spk = lax.dot_general(
        one_hot.astype(F32),
        seg_sums,
        TN,
        precision=lax.Precision.HIGHEST,
        preferred_element_type=F32,
    )
    grad_params = jnp.concatenate(
        [
            dot(shifted, grad_pre, TN),
            dot(inputs, grad_pre, TN),
            dot(mel_frames, grad_pre, TN),
            grad_spk,
            term.reshape(RESID, col_count),
        ],
        0,
    )
    grad_params = lax.psum(grad_params, "tm").reshape(NBLK, BLOCK * col_count)
    outgoing = lax.dot_general(
        table.astype(F32), grad_params, TN, precision=lax.Precision.HIGHEST
    ).reshape(chans * slots_dev, BLOCK, col_count)
    grad_slots = lax.all_to_all(outgoing, "chan", split_axis=0, concat_axis=2, tiled=True)
    owned = jnp.sum((owners == lax.axis_index("chan")).astype(jnp.int32))
    keep = (jnp.arange(slots_dev) < owned)[:, None, None]
    first_new = MOMENT_DECAY * first_moment + (1.0 - MOMENT_DECAY) * grad_slots
    second_new = MOMENT_DECAY * second_moment + (1.0 - MOMENT_DECAY) * grad_slots * grad_slots
    first_hat = first_new / (1.0 - MOMENT_DECAY**STEP)
    second_hat = second_new / (1.0 - MOMENT_DECAY**STEP)
    stepped = master - STEP_RATE * (
        first_hat / (jnp.sqrt(second_hat) + EPSILON) + WEIGHT_DECAY * master
    )
    return (
        signal.astype(F32) + summed[:, 0, :].T,
        summed[:, 1, :].T,
        res_cot.astype(F32) + input_part.T,
        jnp.where(keep, first_new, first_moment),
        jnp.where(keep, second_new, second_moment),
        jnp.where(keep, stepped, master),
    )


def solution(mesh):
    wide = P("tm", "chan")
    slots = P("chan", None, None)
    packed_mesh = mesh.shape["tm"] == 2 and mesh.shape["chan"] == 16
    return jax.shard_map(
        local if packed_mesh else local_plain,
        mesh=mesh,
        in_specs=(wide, P("tm", None), P("tm"), P(), slots, slots, slots, wide, wide),
        out_specs=(wide, wide, wide, slots, slots, slots),
        check_vma=False,
    )
```

time: 325 us -> 152 us (0.47)
  waiting for transfers between devices: 171 us -> 71.2 us
  local copies, waits for them, and re-layouts: 58.3 us -> 5.68 us
  matrix products: 19.5 us -> 0 us
  other arithmetic: 19.3 us -> 0.89 us
  Pallas kernels: 0 us -> 17.7 us
  starting transfers between devices: 18.2 us -> 35.5 us
  between operations: 14.2 us -> 0.79 us
  blocking collectives: 22.8 us -> 18.2 us
    reduce_scatter x2 -> x0, waiting for transfers between devices: 69.3 us -> none  [the longest x1 69.3 us: local(): lax.psum_scatter(jnp.einsum('cuw,tu->cwt', block, hidden, preferred_eleme...]
    ppermute x2 -> x15, waiting for transfers between devices: 3.07 us -> 64.8 us  [the longest x12 53.8 us: swap(): return lax.ppermute(x, 'chan', [(i, i ^ k) for i in range(n)])]
    psum x1 -> x0, waiting for transfers between devices: 32.7 us -> none  [local(): grad_params = lax.psum(grad_params, 'tm')]
    all_gather x2 -> x0, waiting for transfers between devices: 29.4 us -> none  [the longest x1 29.4 us: local(): piece = lax.all_gather(cot_stack, 'chan', axis=0, tiled=True)]
    all_to_all x2 -> x3, waiting for transfers between devices: 35.2 us -> 6.38 us  [the longest x1 6.38 us: local(): arrived = lax.all_to_all(sent, 'chan', 0, 0, tiled=True)]
    all_gather x1 -> x0, blocking collectives: 22.8 us -> none  [local(): lax.all_gather(tail_prev, 'chan', axis=1, tiled=True)]
    scatter x1 -> x0, local copies, waits for them, and re-layouts: 21.1 us -> none  [local(): outgoing = jnp.zeros((chans * slots_dev, BLOCK, col_count), jnp.float32)....]
    dot_general x13 -> x0, matrix products: 19.5 us -> none  [the longest x1 2.72 us: local(): lax.dot_general(tap_prev, later, last_dims, preferred_element_type=jnp.fl...]
  transfers between devices with their start and end apart: 9 -> 18, of which waited for: 6 -> 12; matrix products, arithmetic and copies ran while one was open for 23% -> 0% of each run, Pallas kernels for 0% -> 3%
where the time goes in v1:
time: 152 us; the launch traced here: 150 us
  waiting for transfers between devices  71.2 us (47%)
  starting transfers between devices  35.5 us (23%)
  blocking collectives  18.2 us (12%)
  Pallas kernels  17.7 us (12%)
  local copies, waits for them, and re-layouts  5.68 us (4%)
    ppermute x12, waiting for transfers between devices, swap(): return lax.ppermute(x, 'chan', [(i, i ^ k) for i in range(n)])  53.8 us
    all_to_all x1, blocking collectives, local(): parts = lax.all_to_all(grads, BOTH, 0, 0, axis_index_groups=share)  18.2 us
    ppermute x12, starting transfers between devices, swap(): return lax.ppermute(x, 'chan', [(i, i ^ k) for i in range(n)])  14.9 us
    all_to_all x1, starting transfers between devices, local(): arrived = lax.all_to_all(sent, 'chan', 0, 0, tiled=True)  7.36 us
    all_to_all x1, waiting for transfers between devices, local(): arrived = lax.all_to_all(sent, 'chan', 0, 0, tiled=True)  6.38 us
    unnamed x30, local copies, waits for them, and re-layouts  5.67 us
    pallas_call x1, Pallas kernels, local(): call(update, (sds(flat, F32),) * 3, 1, 5)  4.89 us
    ppermute x1, waiting for transfers between devices, local(): halo = lax.ppermute(sig[:, -128:], 'tm', [(0, 1)])  4.71 us
  transfers between devices with their start and end apart: 18, of which 12 were waited for; matrix products, arithmetic and copies ran while one was open for 0% of the time, Pallas kernels for 3%

profile of v1, /device:TPU:0, one launch (start us, length us, event | category | flops | bytes accessed | tf_op | source)
XLA Modules:
  0.0 149.9 jit_solution(10448914043339115198)
XLA Ops:
  1.4 1.3 copy-done
  2.8 1.6 %shard_map.137 = bf16[16,40,256]{2,1,0:T(8,128)(2,1)} custom-call(s32[10]{0:T(128)S(1)} %pad_add_fusion.ids, f32[40,8,1024]{2,1,0:T(8,128)S(1)} %copy-done), custom_call_target="tpu_custom_call" | custom-call | bytes 1048576 | tf_op jit(solution)/shard_map/pallas_call | solution.py:351
  4.4 7.4 %all-to-all-start = ((bf16[16,40,256]{2,1,0:T(8,128)(2,1)}), bf16[16,40,256]{2,1,0:T(8,128)(2,1)S(1)}, u32[]{:S(2)}, u32[]{:S(2)}) async-start(bf16[16,40,256]{2,1,0:T(8,128)(2,1)} %shard_map.137), calls=%async_computation | async-start | bytes 655360 | tf_op jit(solution)/shard_map/all_to_all | solution.py:352
  11.7 1.6 %collective-permute-start = (s32[8]{0:T(128)S(1)}, s32[8]{0:T(128)S(1)}, u32[]{:S(2)}, u32[]{:S(2)}) collective-permute-start(s32[8]{0:T(128)S(1)} %copy-done.14), channel_id=1, source_target_pairs={{0,16},{16,0},{1,17},{17,1},{2,18},{18,2},{3,19},{19,3},{4,20},{20... | collective-permute-start | bytes 104 | tf_op jit(solution)/shard_map/ppermute | solution.py:344
  13.3 2.0 %collective-permute-done = s32[8]{0:T(128)S(1)} collective-permute-done((s32[8]{0:T(128)S(1)}, s32[8]{0:T(128)S(1)}, u32[]{:S(2)}, u32[]{:S(2)}) %collective-permute-start) | collective-permute-done | bytes 64 | tf_op jit(solution)/shard_map/ppermute | solution.py:344
  16.4 6.4 %all-to-all-done = bf16[16,40,256]{2,1,0:T(8,128)(2,1)S(1)} async-done(((bf16[16,40,256]{2,1,0:T(8,128)(2,1)}), bf16[16,40,256]{2,1,0:T(8,128)(2,1)S(1)}, u32[]{:S(2)}, u32[]{:S(2)}) %all-to-all-start) | async-done | bytes 327712 | tf_op jit(solution)/shard_map/all_to_all | solution.py:352
  22.8 1.3 shard_map.138
  24.2 3.7 %all-to-all-start.1 = ((bf16[8,224,256]{2,1,0:T(8,128)(2,1)}), bf16[8,224,256]{2,1,0:T(8,128)(2,1)S(1)}, u32[]{:S(2)}, u32[]{:S(2)}) async-start(bf16[8,224,256]{2,1,0:T(8,128)(2,1)} %shard_map.138), calls=%async_computation.1 | async-start | bytes 1835008 | tf_op jit(solution)/shard_map/all_to_all | solution.py:367
  27.9 3.8 %collective-permute-start.1 = (bf16[32,128]{1,0:T(8,128)(2,1)S(1)}, bf16[32,128]{1,0:T(8,128)(2,1)S(1)}, u32[]{:S(2)}, u32[]{:S(2)}) collective-permute-start(bf16[32,128]{1,0:T(8,128)(2,1)S(1)} %slice.4), channel_id=1, source_target_pairs={{0,16},{1,17},{2,18},{3,19},{4,20},{5,21},{6,22},{7,23},{8,24},{9,... | collective-permute-start | bytes 24584 | tf_op jit(solution)/shard_map/ppermute | solution.py:343
  31.7 4.7 %collective-permute-done.1.halo = bf16[32,128]{1,0:T(8,128)(2,1)S(1)} collective-permute-done((bf16[32,128]{1,0:T(8,128)(2,1)S(1)}, bf16[32,128]{1,0:T(8,128)(2,1)S(1)}, u32[]{:S(2)}, u32[]{:S(2)}) %collective-permute-start.1) | collective-permute-done | bytes 8224 | tf_op jit(solution)/shard_map/ppermute | solution.py:343
  37.1 4.0 %collective-permute-start.3 = (bf16[112,256]{1,0:T(8,128)(2,1)S(1)}, bf16[112,256]{1,0:T(8,128)(2,1)S(1)}, u32[]{:S(2)}, u32[]{:S(2)}) collective-permute-start(bf16[112,256]{1,0:T(8,128)(2,1)S(1)} %get-tuple-element.30), channel_id=1, source_target_pairs={{0,2},{1,3},{2,0},{3,1},{4,6},{5,7},{6,4},{7,5},{8,10},{9,11},{10,... | collective-permute-start | bytes 172040 | tf_op jit(solution)/shard_map/ppermute | solution.py:328
  41.2 2.4 %collective-permute-done.3 = bf16[112,256]{1,0:T(8,128)(2,1)S(1)} collective-permute-done((bf16[112,256]{1,0:T(8,128)(2,1)S(1)}, bf16[112,256]{1,0:T(8,128)(2,1)S(1)}, u32[]{:S(2)}, u32[]{:S(2)}) %collective-permute-start.3) | collective-permute-done | bytes 57376 | tf_op jit(solution)/shard_map/ppermute | solution.py:328
  43.6 1.4 collective-permute-done.4
  45.1 1.3 collective-permute-start.7
  47.1 2.5 %collective-permute-start.5 = (bf16[4,112,256]{2,1,0:T(8,128)(2,1)S(1)}, bf16[4,112,256]{2,1,0:T(8,128)(2,1)S(1)}, u32[]{:S(2)}, u32[]{:S(2)}) collective-permute-start(bf16[4,112,256]{2,1,0:T(8,128)(2,1)S(1)} %pad_maximum_fusion.p0), channel_id=1, source_target_pairs={{0,4},{1,5},{2,6},{3,7},{4,0},{5,1},{6,2},{7,3},{8,12},{9,13},{10,... | collective-permute-start | bytes 688136 | tf_op jit(solution)/shard_map/ppermute | solution.py:328
  49.5 6.0 %collective-permute-done.7.p3 = bf16[4,112,256]{2,1,0:T(8,128)(2,1)S(1)} collective-permute-done((bf16[4,112,256]{2,1,0:T(8,128)(2,1)S(1)}, bf16[4,112,256]{2,1,0:T(8,128)(2,1)S(1)}, u32[]{:S(2)}, u32[]{:S(2)}) %collective-permute-start.7) | collective-permute-done | bytes 229408 | tf_op jit(solution)/shard_map/ppermute | solution.py:328
  55.6 11.9 %collective-permute-done.6.p2 = bf16[4,112,256]{2,1,0:T(8,128)(2,1)S(1)} collective-permute-done((bf16[4,112,256]{2,1,0:T(8,128)(2,1)S(1)}, bf16[4,112,256]{2,1,0:T(8,128)(2,1)S(1)}, u32[]{:S(2)}, u32[]{:S(2)}) %collective-permute-start.6) | collective-permute-done | bytes 229408 | tf_op jit(solution)/shard_map/ppermute | solution.py:328
  67.4 3.5 %shard_map.140 = (bf16[8,224,256]{2,1,0:T(8,128)(2,1)S(1)}, bf16[4,112,256]{2,1,0:T(8,128)(2,1)S(1)}, bf16[4,112,256]{2,1,0:T(8,128)(2,1)S(1)}, bf16[4,112,256]{2,1,0:T(8,128)(2,1)S(1)}, bf16[4,112,256]{2,1,0:T(8,128)(2,1)S(1)}) custom-call(s32[10]{0:T(128)S(1)} %pad_add_fusion.ids, bf16[8,224,256]{2,1,0:T(8,128)(2,1)S(1)} %all-to-all-done.1.packed, ...), custom_call_target="tpu_custom_call" | custom-call | bytes 1048576 | tf_op jit(solution)/shard_map/pallas_call | solution.py:370
  73.0 18.2 %all_to_all.20.parts = bf16[8,224,256]{2,1,0:T(8,128)(2,1)S(1)} all-to-all(bf16[8,224,256]{2,1,0:T(8,128)(2,1)S(1)} %get-tuple-element.44), channel_id=1, replica_groups={{0,1,2,3,16,17,18,19},{4,5,6,7,20,21,22,23},{8,9,10,11,24,25,26,27},{12..., dimensions={0} | all-to-all | bytes 1835008 | tf_op jit(solution)/shard_map/all_to_all | solution.py:378
  91.2 1.3 shard_map.144
  92.6 2.8 %all-to-all-start.3 = ((bf16[32,40,256]{2,1,0:T(8,128)(2,1)}), bf16[32,40,256]{2,1,0:T(8,128)(2,1)S(1)}, u32[]{:S(2)}, u32[]{:S(2)}) async-start(bf16[32,40,256]{2,1,0:T(8,128)(2,1)} %bitcast.14), calls=%async_computation.3 | async-start | bytes 1310720 | tf_op jit(solution)/shard_map/all_to_all | solution.py:383
  95.4 1.8 %collective-permute-start.8 = (bf16[4,112,256]{2,1,0:T(8,128)(2,1)}, bf16[4,112,256]{2,1,0:T(8,128)(2,1)S(1)}, u32[]{:S(2)}, u32[]{:S(2)}) collective-permute-start(bf16[4,112,256]{2,1,0:T(8,128)(2,1)} %copy-done.12), channel_id=1, source_target_pairs={{0,4},{1,5},{2,6},{3,7},{4,0},{5,1},{6,2},{7,3},{8,12},{9,13},{10,... | collective-permute-start | bytes 688136 | tf_op jit(solution)/shard_map/ppermute | solution.py:328
  97.2 2.4 %collective-permute-start.9 = (bf16[4,112,256]{2,1,0:T(8,128)(2,1)}, bf16[4,112,256]{2,1,0:T(8,128)(2,1)S(1)}, u32[]{:S(2)}, u32[]{:S(2)}) collective-permute-start(bf16[4,112,256]{2,1,0:T(8,128)(2,1)} %copy-done.11), channel_id=1, source_target_pairs={{0,8},{1,9},{2,10},{3,11},{4,12},{5,13},{6,14},{7,15},{8,0},{9,1},... | collective-permute-start | bytes 688136 | tf_op jit(solution)/shard_map/ppermute | solution.py:328
  99.8 16.3 %collective-permute-done.8.z1 = bf16[4,112,256]{2,1,0:T(8,128)(2,1)S(1)} collective-permute-done((bf16[4,112,256]{2,1,0:T(8,128)(2,1)}, bf16[4,112,256]{2,1,0:T(8,128)(2,1)S(1)}, u32[]{:S(2)}, u32[]{:S(2)}) %collective-permute-start.8) | collective-permute-done | bytes 229408 | tf_op jit(solution)/shard_map/ppermute | solution.py:328
  116.1 12.3 %collective-permute-done.9.z2 = bf16[4,112,256]{2,1,0:T(8,128)(2,1)S(1)} collective-permute-done((bf16[4,112,256]{2,1,0:T(8,128)(2,1)}, bf16[4,112,256]{2,1,0:T(8,128)(2,1)S(1)}, u32[]{:S(2)}, u32[]{:S(2)}) %collective-permute-start.9) | collective-permute-done | bytes 229408 | tf_op jit(solution)/shard_map/ppermute | solution.py:328
  129.5 1.5 %collective-permute-start.12 = (bf16[112,256]{1,0:T(8,128)(2,1)S(1)}, bf16[112,256]{1,0:T(8,128)(2,1)S(1)}, u32[]{:S(2)}, u32[]{:S(2)}) collective-permute-start(bf16[112,256]{1,0:T(8,128)(2,1)S(1)} %get-tuple-element.38), channel_id=1, source_target_pairs={{0,2},{1,3},{2,0},{3,1},{4,6},{5,7},{6,4},{7,5},{8,10},{9,11},{10,... | collective-permute-start | bytes 172040 | tf_op jit(solution)/shard_map/ppermute | solution.py:328
  131.4 2.5 %collective-permute-done.12.o2 = bf16[112,256]{1,0:T(8,128)(2,1)S(1)} collective-permute-done((bf16[112,256]{1,0:T(8,128)(2,1)S(1)}, bf16[112,256]{1,0:T(8,128)(2,1)S(1)}, u32[]{:S(2)}, u32[]{:S(2)}) %collective-permute-start.12) | collective-permute-done | bytes 57376 | tf_op jit(solution)/shard_map/ppermute | solution.py:328
  135.9 1.3 collective-permute-start.14
  137.2 4.2 %collective-permute-done.14.ahead = bf16[32,128]{1,0:T(8,128)(2,1)S(1)} collective-permute-done((bf16[32,128]{1,0:T(8,128)(2,1)S(1)}, bf16[32,128]{1,0:T(8,128)(2,1)S(1)}, u32[]{:S(2)}, u32[]{:S(2)}) %collective-permute-start.14) | collective-permute-done | bytes 8224 | tf_op jit(solution)/shard_map/ppermute | solution.py:385
  141.4 2.3 %shard_map.143 = (f32[32,1024]{1,0:T(8,128)}, f32[32,1024]{1,0:T(8,128)}, f32[32,1024]{1,0:T(8,128)}) custom-call(s32[10]{0:T(128)S(1)} %pad_add_fusion.ids, bf16[112,256]{1,0:T(8,128)(2,1)S(1)} %get-tuple-element.36.o0, bf16[112,256]{1,0:T(8,128)(2,1)S(1)} %collective-permute-done.11.o1, bf16[112,256]{1,0:T(8,128)(2,1)S(1)} %collective-permute-done.12.o2, ...), custom_call_target="tpu_custom_call" | custom-call | bytes 1048576 | tf_op jit(solution)/shard_map/pallas_call | solution.py:387
  143.7 1.3 copy-done.3
  145.0 4.9 %shard_map.145 = (f32[320,1024]{1,0:T(8,128)}, f32[320,1024]{1,0:T(8,128)}, f32[320,1024]{1,0:T(8,128)}) custom-call(s32[10]{0:T(128)S(1)} %pad_add_fusion.ids, s32[1,320]{1,0:T(1,128)S(1)} %reshape.39.owners, bf16[32,40,256]{2,1,0:T(8,128)(2,1)S(1)} %all-to-all-done.3.grads, f32[320,1024]{1,0:T(8,128)S(1)} %bitcast.21, f32[320,1024]{1,0:T(8,128)S(1)} %bitcast.23, ...), custom_call_target="tpu_custom_call" | custom-call | bytes 1048576 | tf_op jit(solution)/shard_map/pallas_call | solution.py:391
  (50 shorter events, 9.2 us)
Async XLA Ops:
  0.6 11.1 %copy-start.14 = (s32[8]{0:T(128)S(1)}, s32[8]{0:T(128)}, u32[]{:S(2)}) copy-start(s32[8]{0:T(128)} %param.11) | copy-start | bytes 100
  0.6 12.7 %copy-start.13 = (s32[320]{0:T(512)S(1)}, s32[320]{0:T(512)}, u32[]{:S(2)}) copy-start(s32[320]{0:T(512)} %param.12) | copy-start | bytes 3844
  1.4 1.3 copy-start
  4.4 18.5 %all-to-all-start = ((bf16[16,40,256]{2,1,0:T(8,128)(2,1)}), bf16[16,40,256]{2,1,0:T(8,128)(2,1)S(1)}, u32[]{:S(2)}, u32[]{:S(2)}) async-start(bf16[16,40,256]{2,1,0:T(8,128)(2,1)} %shard_map.137), calls=%async_computation | async-start | bytes 655360 | tf_op jit(solution)/shard_map/all_to_all | solution.py:352
  11.7 3.6 %collective-permute-start = (s32[8]{0:T(128)S(1)}, s32[8]{0:T(128)S(1)}, u32[]{:S(2)}, u32[]{:S(2)}) collective-permute-start(s32[8]{0:T(128)S(1)} %copy-done.14), channel_id=1, source_target_pairs={{0,16},{16,0},{1,17},{17,1},{2,18},{18,2},{3,19},{19,3},{4,20},{20... | collective-permute-start | bytes 104 | tf_op jit(solution)/shard_map/ppermute | solution.py:344
  22.8 5.0 %copy-start.4 = (bf16[1024,32]{0,1:T(8,128)(2,1)S(1)}, bf16[1024,32]{0,1:T(8,128)(2,1)}, u32[]{:S(2)}) copy-start(bf16[1024,32]{0,1:T(8,128)(2,1)} %param.9) | copy-start | bytes 196612
  24.1 12.3 %copy-start.5 = (bf16[1024,32]{0,1:T(8,128)(2,1)S(1)}, bf16[1024,32]{0,1:T(8,128)(2,1)}, u32[]{:S(2)}) copy-start(bf16[1024,32]{0,1:T(8,128)(2,1)} %param.16) | copy-start | bytes 196612
  24.2 12.3 %copy-start.9 = (bf16[1024,32]{0,1:T(8,128)(2,1)S(1)}, bf16[1024,32]{0,1:T(8,128)(2,1)}, u32[]{:S(2)}) copy-start(bf16[1024,32]{0,1:T(8,128)(2,1)} %param.17) | copy-start | bytes 196612
  24.2 43.3 %copy-start.8 = (bf16[1024,80]{0,1:T(8,128)(2,1)S(1)}, bf16[1024,80]{0,1:T(8,128)(2,1)}, u32[]{:S(2)}) copy-start(bf16[1024,80]{0,1:T(8,128)(2,1)} %param.10) | copy-start | bytes 491524
  24.2 43.3 %all-to-all-start.1 = ((bf16[8,224,256]{2,1,0:T(8,128)(2,1)}), bf16[8,224,256]{2,1,0:T(8,128)(2,1)S(1)}, u32[]{:S(2)}, u32[]{:S(2)}) async-start(bf16[8,224,256]{2,1,0:T(8,128)(2,1)} %shard_map.138), calls=%async_computation.1 | async-start | bytes 1835008 | tf_op jit(solution)/shard_map/all_to_all | solution.py:367
  27.9 8.5 %collective-permute-start.1 = (bf16[32,128]{1,0:T(8,128)(2,1)S(1)}, bf16[32,128]{1,0:T(8,128)(2,1)S(1)}, u32[]{:S(2)}, u32[]{:S(2)}) collective-permute-start(bf16[32,128]{1,0:T(8,128)(2,1)S(1)} %slice.4), channel_id=1, source_target_pairs={{0,16},{1,17},{2,18},{3,19},{4,20},{5,21},{6,22},{7,23},{8,24},{9,... | collective-permute-start | bytes 24584 | tf_op jit(solution)/shard_map/ppermute | solution.py:343
  37.1 4.1 %collective-permute-start.2 = (bf16[112,256]{1,0:T(8,128)(2,1)S(1)}, bf16[112,256]{1,0:T(8,128)(2,1)S(1)}, u32[]{:S(2)}, u32[]{:S(2)}) collective-permute-start(bf16[112,256]{1,0:T(8,128)(2,1)S(1)} %get-tuple-element.29), channel_id=1, source_target_pairs={{0,1},{1,0},{2,3},{3,2},{4,5},{5,4},{6,7},{7,6},{8,9},{9,8},{10,11... | collective-permute-start | bytes 172040 | tf_op jit(solution)/shard_map/ppermute | solution.py:328
  37.1 6.5 %collective-permute-start.3 = (bf16[112,256]{1,0:T(8,128)(2,1)S(1)}, bf16[112,256]{1,0:T(8,128)(2,1)S(1)}, u32[]{:S(2)}, u32[]{:S(2)}) collective-permute-start(bf16[112,256]{1,0:T(8,128)(2,1)S(1)} %get-tuple-element.30), channel_id=1, source_target_pairs={{0,2},{1,3},{2,0},{3,1},{4,6},{5,7},{6,4},{7,5},{8,10},{9,11},{10,... | collective-permute-start | bytes 172040 | tf_op jit(solution)/shard_map/ppermute | solution.py:328
  41.1 3.9 %collective-permute-start.4 = (bf16[112,256]{1,0:T(8,128)(2,1)S(1)}, bf16[112,256]{1,0:T(8,128)(2,1)S(1)}, u32[]{:S(2)}, u32[]{:S(2)}) collective-permute-start(bf16[112,256]{1,0:T(8,128)(2,1)S(1)} %get-tuple-element.31), channel_id=1, source_target_pairs={{0,3},{1,2},{2,1},{3,0},{4,7},{5,6},{6,5},{7,4},{8,11},{9,10},{10,... | collective-permute-start | bytes 172040 | tf_op jit(solution)/shard_map/ppermute | solution.py:328
  45.1 10.5 %collective-permute-start.7 = (bf16[4,112,256]{2,1,0:T(8,128)(2,1)S(1)}, bf16[4,112,256]{2,1,0:T(8,128)(2,1)S(1)}, u32[]{:S(2)}, u32[]{:S(2)}) collective-permute-start(bf16[4,112,256]{2,1,0:T(8,128)(2,1)S(1)} %pad_maximum_fusion.p0), channel_id=1, source_target_pairs={{0,12},{1,13},{2,14},{3,15},{4,8},{5,9},{6,10},{7,11},{8,4},{9,5},... | collective-permute-start | bytes 688136 | tf_op jit(solution)/shard_map/ppermute | solution.py:328
  46.4 21.1 %collective-permute-start.6 = (bf16[4,112,256]{2,1,0:T(8,128)(2,1)S(1)}, bf16[4,112,256]{2,1,0:T(8,128)(2,1)S(1)}, u32[]{:S(2)}, u32[]{:S(2)}) collective-permute-start(bf16[4,112,256]{2,1,0:T(8,128)(2,1)S(1)} %pad_maximum_fusion.p0), channel_id=1, source_target_pairs={{0,8},{1,9},{2,10},{3,11},{4,12},{5,13},{6,14},{7,15},{8,0},{9,1},... | collective-permute-start | bytes 688136 | tf_op jit(solution)/shard_map/ppermute | solution.py:328
  47.1 20.3 %collective-permute-start.5 = (bf16[4,112,256]{2,1,0:T(8,128)(2,1)S(1)}, bf16[4,112,256]{2,1,0:T(8,128)(2,1)S(1)}, u32[]{:S(2)}, u32[]{:S(2)}) collective-permute-start(bf16[4,112,256]{2,1,0:T(8,128)(2,1)S(1)} %pad_maximum_fusion.p0), channel_id=1, source_target_pairs={{0,4},{1,5},{2,6},{3,7},{4,0},{5,1},{6,2},{7,3},{8,12},{9,13},{10,... | collective-permute-start | bytes 688136 | tf_op jit(solution)/shard_map/ppermute | solution.py:328
  70.9 0.7 copy-start.10
  71.6 0.7 copy-start.11
  73.0 19.6 %copy-start.6 = (bf16[4,112,256]{2,1,0:T(8,128)(2,1)}, bf16[4,112,256]{2,1,0:T(8,128)(2,1)S(1)}, u32[]{:S(2)}) copy-start(bf16[4,112,256]{2,1,0:T(8,128)(2,1)S(1)} %get-tuple-element.32.z0) | copy-start | bytes 688132
  92.6 51.1 %copy-start.1 = (f32[40,8,1024]{2,1,0:T(8,128)S(1)}, f32[40,8,1024]{2,1,0:T(8,128)}, u32[]{:S(2)}) copy-start(f32[40,8,1024]{2,1,0:T(8,128)} %master.1) | copy-start | bytes 3932164
  92.6 51.1 %copy-start.2 = (f32[40,8,1024]{2,1,0:T(8,128)S(1)}, f32[40,8,1024]{2,1,0:T(8,128)}, u32[]{:S(2)}) copy-start(f32[40,8,1024]{2,1,0:T(8,128)} %param.14) | copy-start | bytes 3932164
  92.6 51.1 %all-to-all-start.3 = ((bf16[32,40,256]{2,1,0:T(8,128)(2,1)}), bf16[32,40,256]{2,1,0:T(8,128)(2,1)S(1)}, u32[]{:S(2)}, u32[]{:S(2)}) async-start(bf16[32,40,256]{2,1,0:T(8,128)(2,1)} %bitcast.14), calls=%async_computation.3 | async-start | bytes 1310720 | tf_op jit(solution)/shard_map/all_to_all | solution.py:383
  95.4 20.7 %collective-permute-start.8 = (bf16[4,112,256]{2,1,0:T(8,128)(2,1)}, bf16[4,112,256]{2,1,0:T(8,128)(2,1)S(1)}, u32[]{:S(2)}, u32[]{:S(2)}) collective-permute-start(bf16[4,112,256]{2,1,0:T(8,128)(2,1)} %copy-done.12), channel_id=1, source_target_pairs={{0,4},{1,5},{2,6},{3,7},{4,0},{5,1},{6,2},{7,3},{8,12},{9,13},{10,... | collective-permute-start | bytes 688136 | tf_op jit(solution)/shard_map/ppermute | solution.py:328
  97.2 31.2 %collective-permute-start.9 = (bf16[4,112,256]{2,1,0:T(8,128)(2,1)}, bf16[4,112,256]{2,1,0:T(8,128)(2,1)S(1)}, u32[]{:S(2)}, u32[]{:S(2)}) collective-permute-start(bf16[4,112,256]{2,1,0:T(8,128)(2,1)} %copy-done.11), channel_id=1, source_target_pairs={{0,8},{1,9},{2,10},{3,11},{4,12},{5,13},{6,14},{7,15},{8,0},{9,1},... | collective-permute-start | bytes 688136 | tf_op jit(solution)/shard_map/ppermute | solution.py:328
  99.6 28.8 %collective-permute-start.10 = (bf16[4,112,256]{2,1,0:T(8,128)(2,1)}, bf16[4,112,256]{2,1,0:T(8,128)(2,1)S(1)}, u32[]{:S(2)}, u32[]{:S(2)}) collective-permute-start(bf16[4,112,256]{2,1,0:T(8,128)(2,1)} %copy-done.10), channel_id=1, source_target_pairs={{0,12},{1,13},{2,14},{3,15},{4,8},{5,9},{6,10},{7,11},{8,4},{9,5},... | collective-permute-start | bytes 688136 | tf_op jit(solution)/shard_map/ppermute | solution.py:328
  128.4 0.9 copy-start.7
  129.4 1.9 %collective-permute-start.11 = (bf16[112,256]{1,0:T(8,128)(2,1)S(1)}, bf16[112,256]{1,0:T(8,128)(2,1)S(1)}, u32[]{:S(2)}, u32[]{:S(2)}) collective-permute-start(bf16[112,256]{1,0:T(8,128)(2,1)S(1)} %get-tuple-element.37), channel_id=1, source_target_pairs={{0,1},{1,0},{2,3},{3,2},{4,5},{5,4},{6,7},{7,6},{8,9},{9,8},{10,11... | collective-permute-start | bytes 172040 | tf_op jit(solution)/shard_map/ppermute | solution.py:328
  129.5 4.3 %collective-permute-start.12 = (bf16[112,256]{1,0:T(8,128)(2,1)S(1)}, bf16[112,256]{1,0:T(8,128)(2,1)S(1)}, u32[]{:S(2)}, u32[]{:S(2)}) collective-permute-start(bf16[112,256]{1,0:T(8,128)(2,1)S(1)} %get-tuple-element.38), channel_id=1, source_target_pairs={{0,2},{1,3},{2,0},{3,1},{4,6},{5,7},{6,4},{7,5},{8,10},{9,11},{10,... | collective-permute-start | bytes 172040 | tf_op jit(solution)/shard_map/ppermute | solution.py:328
  131.1 3.9 %collective-permute-start.13 = (bf16[112,256]{1,0:T(8,128)(2,1)S(1)}, bf16[112,256]{1,0:T(8,128)(2,1)S(1)}, u32[]{:S(2)}, u32[]{:S(2)}) collective-permute-start(bf16[112,256]{1,0:T(8,128)(2,1)S(1)} %get-tuple-element.39), channel_id=1, source_target_pairs={{0,3},{1,2},{2,1},{3,0},{4,7},{5,6},{6,5},{7,4},{8,11},{9,10},{10,... | collective-permute-start | bytes 172040 | tf_op jit(solution)/shard_map/ppermute | solution.py:328
  135.9 5.5 %collective-permute-start.14 = (bf16[32,128]{1,0:T(8,128)(2,1)S(1)}, bf16[32,128]{1,0:T(8,128)(2,1)S(1)}, u32[]{:S(2)}, u32[]{:S(2)}) collective-permute-start(bf16[32,128]{1,0:T(8,128)(2,1)S(1)} %shard_map.142), channel_id=1, source_target_pairs={{16,0},{17,1},{18,2},{19,3},{20,4},{21,5},{22,6},{23,7},{24,8},{25... | collective-permute-start | bytes 24584 | tf_op jit(solution)/shard_map/ppermute | solution.py:385
  143.7 1.3 copy-start.3
  (1 other events, 0.7 us)

commit v2 on v1

--- a/solution.py
+++ b/solution.py
@@ -61,7 +61,7 @@
         + [pl.BlockSpec(memory_space=pltpu.VMEM)] * n_in,
         out_specs=jax.tree.map(lambda _: pl.BlockSpec(memory_space=pltpu.VMEM), out),
         scratch_shapes=list(scratch),
-        compiler_params=pltpu.CompilerParams(vmem_limit_bytes=48 * 2**20),
+        compiler_params=pltpu.CompilerParams(vmem_limit_bytes=24 * 2**20),
         cost_estimate=pl.CostEstimate(
             flops=flops, bytes_accessed=int(mbytes * 2**20), transcendentals=0
         ),
@@ -361,6 +361,7 @@
         1,
         1,
     )(sids, own_row)
+    arrived, _ = lax.optimization_barrier((arrived, mine))
     gathered = call(gather_blocks, sds((8, PACKED, 256), BF16), 0, 2)(
         pick, arrived.reshape(slots, 256)
     )
@@ -378,6 +379,7 @@
     parts = lax.all_to_all(grads, BOTH, 0, 0, axis_index_groups=share)
     t1, t2, t3 = (swap(z, 4 * k) for k, z in ((1, z1), (2, z2), (3, z3)))
     o = call(sum_units, (piece,) * 4, 0, 4)(z0, t1, t2, t3)
+    parts, _ = lax.optimization_barrier((parts, o[0]))
     o = (o[0], swap(o[1], 1), swap(o[2], 2), swap(o[3], 3))
     spread = call(scatter_blocks, sds((2, slots, 256), BF16), 0, 2)(put, parts)
     returned = lax.all_to_all(spread.reshape(32, slots_dev, 256), BOTH, 0, 0)

time: 152 us -> 115 us (0.76)
  waiting for transfers between devices: 71.2 us -> 51.9 us
  blocking collectives: 18.2 us -> 0 us
  starting transfers between devices: 35.5 us -> 38.9 us
  local copies, waits for them, and re-layouts: 5.68 us -> 3.92 us
    all_to_all x1 -> x0, blocking collectives: 18.2 us -> none  [local(): parts = lax.all_to_all(grads, BOTH, 0, 0, axis_index_groups=share)]
    ppermute x12, waiting for transfers between devices: 53.8 us -> 46 us  [swap(): return lax.ppermute(x, 'chan', [(i, i ^ k) for i in range(n)])]
    all_to_all x1, waiting for transfers between devices: 6.38 us -> 0.01 us  [local(): arrived = lax.all_to_all(sent, 'chan', 0, 0, tiled=True)]
    all_to_all x0 -> x1, starting transfers between devices: none -> 4.2 us  [local(): parts = lax.all_to_all(grads, BOTH, 0, 0, axis_index_groups=share)]
    ppermute x1, waiting for transfers between devices: 4.71 us -> 1.23 us  [local(): halo = lax.ppermute(sig[:, -128:], 'tm', [(0, 1)])]
    ppermute x1, waiting for transfers between devices: 2.02 us -> 0.01 us  [local(): other_ids = lax.ppermute(speaker_ids, 'tm', [(0, 1), (1, 0)])]
    unnamed x30 -> x24, local copies, waits for them, and re-layouts: 5.67 us -> 3.91 us
    all_to_all x1, starting transfers between devices: 2.78 us -> 4.37 us  [local(): returned = lax.all_to_all(spread.reshape(32, slots_dev, 256), BOTH, 0, 0)]
  transfers between devices with their start and end apart: 18 -> 19, of which waited for: 12 -> 12; matrix products, arithmetic and copies ran while one was open for 0% -> 0% of each run, Pallas kernels for 3% -> 4%
where the time goes in v2:
time: 115 us; the launch traced here: 114 us
  waiting for transfers between devices  51.9 us (45%)
  starting transfers between devices  38.9 us (34%)
  Pallas kernels  18 us (16%)
  local copies, waits for them, and re-layouts  3.92 us (3%)
    ppermute x12, waiting for transfers between devices, swap(): return lax.ppermute(x, 'chan', [(i, i ^ k) for i in range(n)])  46 us
    ppermute x12, starting transfers between devices, swap(): return lax.ppermute(x, 'chan', [(i, i ^ k) for i in range(n)])  14.3 us
    all_to_all x1, starting transfers between devices, local(): arrived = lax.all_to_all(sent, 'chan', 0, 0, tiled=True)  7.36 us
    pallas_call x1, Pallas kernels, local(): call(update, (sds(flat, F32),) * 3, 1, 5)  4.89 us
    all_to_all x1, starting transfers between devices, local(): returned = lax.all_to_all(spread.reshape(32, slots_dev, 256), BOTH, 0, 0)  4.37 us
    ppermute x1, waiting for transfers between devices, local(): ahead = lax.ppermute(tail, 'tm', [(1, 0)])  4.24 us
    all_to_all x1, starting transfers between devices, local(): parts = lax.all_to_all(grads, BOTH, 0, 0, axis_index_groups=share)  4.2 us
    unnamed x24, local copies, waits for them, and re-layouts  3.91 us
  transfers between devices with their start and end apart: 19, of which 12 were waited for; matrix products, arithmetic and copies ran while one was open for 0% of the time, Pallas kernels for 4%

profile of v2, /device:TPU:0, one launch (start us, length us, event | category | flops | bytes accessed | tf_op | source)
XLA Modules:
  0.0 114.4 jit_solution(6888506110878382786)
XLA Ops:
  1.4 1.3 %copy-done = f32[40,8,1024]{2,1,0:T(8,128)S(1)} copy-done((f32[40,8,1024]{2,1,0:T(8,128)S(1)}, f32[40,8,1024]{2,1,0:T(8,128)}, u32[]{:S(2)}) %copy-start) | copy-done | bytes 1310744
  2.8 1.6 %shard_map.137 = bf16[16,40,256]{2,1,0:T(8,128)(2,1)} custom-call(s32[10]{0:T(128)S(1)} %pad_add_fusion.ids, f32[40,8,1024]{2,1,0:T(8,128)S(1)} %copy-done), custom_call_target="tpu_custom_call" | custom-call | bytes 1048576 | tf_op jit(solution)/shard_map/pallas_call | solution.py:351
  4.4 7.4 %all-to-all-start = ((bf16[16,40,256]{2,1,0:T(8,128)(2,1)}), bf16[16,40,256]{2,1,0:T(8,128)(2,1)S(1)}, u32[]{:S(2)}, u32[]{:S(2)}) async-start(bf16[16,40,256]{2,1,0:T(8,128)(2,1)} %shard_map.137), calls=%async_computation | async-start | bytes 655360 | tf_op jit(solution)/shard_map/all_to_all | solution.py:352
  11.8 3.4 %collective-permute-start.1 = (bf16[32,128]{1,0:T(8,128)(2,1)S(1)}, bf16[32,128]{1,0:T(8,128)(2,1)S(1)}, u32[]{:S(2)}, u32[]{:S(2)}) collective-permute-start(bf16[32,128]{1,0:T(8,128)(2,1)S(1)} %slice.4), channel_id=1, source_target_pairs={{0,16},{1,17},{2,18},{3,19},{4,20},{5,21},{6,22},{7,23},{8,24},{9,... | collective-permute-start | bytes 24584 | tf_op jit(solution)/shard_map/ppermute | solution.py:343
  15.3 1.2 %collective-permute-done.1.halo = bf16[32,128]{1,0:T(8,128)(2,1)S(1)} collective-permute-done((bf16[32,128]{1,0:T(8,128)(2,1)S(1)}, bf16[32,128]{1,0:T(8,128)(2,1)S(1)}, u32[]{:S(2)}, u32[]{:S(2)}) %collective-permute-start.1) | collective-permute-done | bytes 8224 | tf_op jit(solution)/shard_map/ppermute | solution.py:343
  17.2 2.0 %collective-permute-start.3 = (bf16[112,256]{1,0:T(8,128)(2,1)S(1)}, bf16[112,256]{1,0:T(8,128)(2,1)S(1)}, u32[]{:S(2)}, u32[]{:S(2)}) collective-permute-start(bf16[112,256]{1,0:T(8,128)(2,1)S(1)} %get-tuple-element.32), channel_id=1, source_target_pairs={{0,2},{1,3},{2,0},{3,1},{4,6},{5,7},{6,4},{7,5},{8,10},{9,11},{10,... | collective-permute-start | bytes 172040 | tf_op jit(solution)/shard_map/ppermute | solution.py:328
  19.4 1.0 shard_map.136
  20.4 1.4 %collective-permute-done.3 = bf16[112,256]{1,0:T(8,128)(2,1)S(1)} collective-permute-done((bf16[112,256]{1,0:T(8,128)(2,1)S(1)}, bf16[112,256]{1,0:T(8,128)(2,1)S(1)}, u32[]{:S(2)}, u32[]{:S(2)}) %collective-permute-start.3) | collective-permute-done | bytes 57376 | tf_op jit(solution)/shard_map/ppermute | solution.py:328
  21.8 1.9 %collective-permute-done.4 = bf16[112,256]{1,0:T(8,128)(2,1)S(1)} collective-permute-done((bf16[112,256]{1,0:T(8,128)(2,1)S(1)}, bf16[112,256]{1,0:T(8,128)(2,1)S(1)}, u32[]{:S(2)}, u32[]{:S(2)}) %collective-permute-start.4) | collective-permute-done | bytes 57376 | tf_op jit(solution)/shard_map/ppermute | solution.py:328
  23.8 1.3 %shard_map.139 = bf16[8,224,256]{2,1,0:T(8,128)(2,1)} custom-call(bf16[224,640]{1,0:T(8,128)(2,1)S(1)} %get-tuple-element.29.pick, bf16[640,256]{1,0:T(8,128)(2,1)S(1)} %bitcast.22), custom_call_target="tpu_custom_call" | custom-call | bytes 1048576 | tf_op jit(solution)/shard_map/pallas_call | solution.py:365
  25.1 3.8 %all-to-all-start.1 = ((bf16[8,224,256]{2,1,0:T(8,128)(2,1)}), bf16[8,224,256]{2,1,0:T(8,128)(2,1)S(1)}, u32[]{:S(2)}, u32[]{:S(2)}) async-start(bf16[8,224,256]{2,1,0:T(8,128)(2,1)} %shard_map.139), calls=%async_computation.1 | async-start | bytes 1835008 | tf_op jit(solution)/shard_map/all_to_all | solution.py:368
  29.0 1.5 %collective-permute-start.5 = (bf16[4,112,256]{2,1,0:T(8,128)(2,1)S(1)}, bf16[4,112,256]{2,1,0:T(8,128)(2,1)S(1)}, u32[]{:S(2)}, u32[]{:S(2)}) collective-permute-start(bf16[4,112,256]{2,1,0:T(8,128)(2,1)S(1)} %pad_maximum_fusion.p0), channel_id=1, source_target_pairs={{0,4},{1,5},{2,6},{3,7},{4,0},{5,1},{6,2},{7,3},{8,12},{9,13},{10,... | collective-permute-start | bytes 688136 | tf_op jit(solution)/shard_map/ppermute | solution.py:328
  30.5 2.0 %collective-permute-start.6 = (bf16[4,112,256]{2,1,0:T(8,128)(2,1)S(1)}, bf16[4,112,256]{2,1,0:T(8,128)(2,1)S(1)}, u32[]{:S(2)}, u32[]{:S(2)}) collective-permute-start(bf16[4,112,256]{2,1,0:T(8,128)(2,1)S(1)} %pad_maximum_fusion.p0), channel_id=1, source_target_pairs={{0,8},{1,9},{2,10},{3,11},{4,12},{5,13},{6,14},{7,15},{8,0},{9,1},... | collective-permute-start | bytes 688136 | tf_op jit(solution)/shard_map/ppermute | solution.py:328
  33.4 7.9 %collective-permute-done.5.p1 = bf16[4,112,256]{2,1,0:T(8,128)(2,1)S(1)} collective-permute-done((bf16[4,112,256]{2,1,0:T(8,128)(2,1)S(1)}, bf16[4,112,256]{2,1,0:T(8,128)(2,1)S(1)}, u32[]{:S(2)}, u32[]{:S(2)}) %collective-permute-start.5) | collective-permute-done | bytes 229408 | tf_op jit(solution)/shard_map/ppermute | solution.py:328
  41.3 8.5 %collective-permute-done.6.p2 = bf16[4,112,256]{2,1,0:T(8,128)(2,1)S(1)} collective-permute-done((bf16[4,112,256]{2,1,0:T(8,128)(2,1)S(1)}, bf16[4,112,256]{2,1,0:T(8,128)(2,1)S(1)}, u32[]{:S(2)}, u32[]{:S(2)}) %collective-permute-start.6) | collective-permute-done | bytes 229408 | tf_op jit(solution)/shard_map/ppermute | solution.py:328
  49.7 3.8 %shard_map.140 = (bf16[8,224,256]{2,1,0:T(8,128)(2,1)}, bf16[4,112,256]{2,1,0:T(8,128)(2,1)S(1)}, bf16[4,112,256]{2,1,0:T(8,128)(2,1)S(1)}, bf16[4,112,256]{2,1,0:T(8,128)(2,1)S(1)}, bf16[4,112,256]{2,1,0:T(8,128)(2,1)S(1)}) custom-call(s32[10]{0:T(128)S(1)} %pad_add_fusion.ids, bf16[8,224,256]{2,1,0:T(8,128)(2,1)S(1)} %all-to-all-done.1.packed, ...), custom_call_target="tpu_custom_call" | custom-call | bytes 1048576 | tf_op jit(solution)/shard_map/pallas_call | solution.py:371
  53.6 4.2 %all-to-all-start.2 = ((bf16[8,224,256]{2,1,0:T(8,128)(2,1)}), bf16[8,224,256]{2,1,0:T(8,128)(2,1)S(1)}, u32[]{:S(2)}, u32[]{:S(2)}) async-start(bf16[8,224,256]{2,1,0:T(8,128)(2,1)} %get-tuple-element.47), calls=%async_computation.2 | async-start | bytes 1835008 | tf_op jit(solution)/shard_map/all_to_all | solution.py:379
  57.8 2.0 %collective-permute-start.10 = (bf16[4,112,256]{2,1,0:T(8,128)(2,1)S(1)}, bf16[4,112,256]{2,1,0:T(8,128)(2,1)S(1)}, u32[]{:S(2)}, u32[]{:S(2)}) collective-permute-start(bf16[4,112,256]{2,1,0:T(8,128)(2,1)S(1)} %get-tuple-element.38), channel_id=1, source_target_pairs={{0,12},{1,13},{2,14},{3,15},{4,8},{5,9},{6,10},{7,11},{8,4},{9,5},... | collective-permute-start | bytes 688136 | tf_op jit(solution)/shard_map/ppermute | solution.py:328
  59.8 3.5 %collective-permute-start.8 = (bf16[4,112,256]{2,1,0:T(8,128)(2,1)S(1)}, bf16[4,112,256]{2,1,0:T(8,128)(2,1)S(1)}, u32[]{:S(2)}, u32[]{:S(2)}) collective-permute-start(bf16[4,112,256]{2,1,0:T(8,128)(2,1)S(1)} %get-tuple-element.36), channel_id=1, source_target_pairs={{0,4},{1,5},{2,6},{3,7},{4,0},{5,1},{6,2},{7,3},{8,12},{9,13},{10,... | collective-permute-start | bytes 688136 | tf_op jit(solution)/shard_map/ppermute | solution.py:328
  63.6 4.4 %collective-permute-done.10.z3 = bf16[4,112,256]{2,1,0:T(8,128)(2,1)S(1)} collective-permute-done((bf16[4,112,256]{2,1,0:T(8,128)(2,1)S(1)}, bf16[4,112,256]{2,1,0:T(8,128)(2,1)S(1)}, u32[]{:S(2)}, u32[]{:S(2)}) %collective-permute-start.10) | collective-permute-done | bytes 229408 | tf_op jit(solution)/shard_map/ppermute | solution.py:328
  68.0 4.5 %collective-permute-done.8.z1 = bf16[4,112,256]{2,1,0:T(8,128)(2,1)S(1)} collective-permute-done((bf16[4,112,256]{2,1,0:T(8,128)(2,1)S(1)}, bf16[4,112,256]{2,1,0:T(8,128)(2,1)S(1)}, u32[]{:S(2)}, u32[]{:S(2)}) %collective-permute-start.8) | collective-permute-done | bytes 229408 | tf_op jit(solution)/shard_map/ppermute | solution.py:328
  72.5 9.8 %collective-permute-done.9.z2 = bf16[4,112,256]{2,1,0:T(8,128)(2,1)S(1)} collective-permute-done((bf16[4,112,256]{2,1,0:T(8,128)(2,1)S(1)}, bf16[4,112,256]{2,1,0:T(8,128)(2,1)S(1)}, u32[]{:S(2)}, u32[]{:S(2)}) %collective-permute-start.9) | collective-permute-done | bytes 229408 | tf_op jit(solution)/shard_map/ppermute | solution.py:328
  83.7 1.3 %shard_map.144 = bf16[2,640,256]{2,1,0:T(8,128)(2,1)} custom-call(bf16[640,224]{1,0:T(8,128)(2,1)S(1)} %get-tuple-element.46.put, bf16[8,224,256]{2,1,0:T(8,128)(2,1)S(1)} %all-to-all-done.2.parts), custom_call_target="tpu_custom_call" | custom-call | bytes 1048576 | tf_op jit(solution)/shard_map/pallas_call | solution.py:384
  85.1 4.4 %all-to-all-start.3 = ((bf16[32,40,256]{2,1,0:T(8,128)(2,1)}), bf16[32,40,256]{2,1,0:T(8,128)(2,1)S(1)}, u32[]{:S(2)}, u32[]{:S(2)}) async-start(bf16[32,40,256]{2,1,0:T(8,128)(2,1)} %bitcast.14), calls=%async_computation.3 | async-start | bytes 1310720 | tf_op jit(solution)/shard_map/all_to_all | solution.py:385
  89.7 1.7 %collective-permute-start.12 = (bf16[112,256]{1,0:T(8,128)(2,1)}, bf16[112,256]{1,0:T(8,128)(2,1)S(1)}, u32[]{:S(2)}, u32[]{:S(2)}) collective-permute-start(bf16[112,256]{1,0:T(8,128)(2,1)} %copy-done.8), channel_id=1, source_target_pairs={{0,2},{1,3},{2,0},{3,1},{4,6},{5,7},{6,4},{7,5},{8,10},{9,11},{10,... | collective-permute-start | bytes 172040 | tf_op jit(solution)/shard_map/ppermute | solution.py:328
  91.4 6.9 %collective-permute-done.12.o2 = bf16[112,256]{1,0:T(8,128)(2,1)S(1)} collective-permute-done((bf16[112,256]{1,0:T(8,128)(2,1)}, bf16[112,256]{1,0:T(8,128)(2,1)S(1)}, u32[]{:S(2)}, u32[]{:S(2)}) %collective-permute-start.12) | collective-permute-done | bytes 57376 | tf_op jit(solution)/shard_map/ppermute | solution.py:328
  99.1 0.9 shard_map.142
  100.0 1.3 %collective-permute-start.14 = (bf16[32,128]{1,0:T(8,128)(2,1)S(1)}, bf16[32,128]{1,0:T(8,128)(2,1)S(1)}, u32[]{:S(2)}, u32[]{:S(2)}) collective-permute-start(bf16[32,128]{1,0:T(8,128)(2,1)S(1)} %shard_map.142), channel_id=1, source_target_pairs={{16,0},{17,1},{18,2},{19,3},{20,4},{21,5},{22,6},{23,7},{24,8},{25... | collective-permute-start | bytes 24584 | tf_op jit(solution)/shard_map/ppermute | solution.py:387
  101.3 4.2 %collective-permute-done.14.ahead = bf16[32,128]{1,0:T(8,128)(2,1)S(1)} collective-permute-done((bf16[32,128]{1,0:T(8,128)(2,1)S(1)}, bf16[32,128]{1,0:T(8,128)(2,1)S(1)}, u32[]{:S(2)}, u32[]{:S(2)}) %collective-permute-start.14) | collective-permute-done | bytes 8224 | tf_op jit(solution)/shard_map/ppermute | solution.py:387
  105.5 2.3 %shard_map.143 = (f32[32,1024]{1,0:T(8,128)}, f32[32,1024]{1,0:T(8,128)}, f32[32,1024]{1,0:T(8,128)}) custom-call(s32[10]{0:T(128)S(1)} %pad_add_fusion.ids, bf16[112,256]{1,0:T(8,128)(2,1)S(1)} %get-tuple-element.39.o0, bf16[112,256]{1,0:T(8,128)(2,1)S(1)} %collective-permute-done.11.o1, bf16[112,256]{1,0:T(8,128)(2,1)S(1)} %collective-permute-done.12.o2, ...), custom_call_target="tpu_custom_call" | custom-call | bytes 1048576 | tf_op jit(solution)/shard_map/pallas_call | solution.py:389
  108.2 1.3 %copy-done.3 = f32[40,8,1024]{2,1,0:T(8,128)S(1)} copy-done((f32[40,8,1024]{2,1,0:T(8,128)S(1)}, f32[40,8,1024]{2,1,0:T(8,128)}, u32[]{:S(2)}) %copy-start.3) | copy-done | bytes 1310744
  109.5 4.9 %shard_map.145 = (f32[320,1024]{1,0:T(8,128)}, f32[320,1024]{1,0:T(8,128)}, f32[320,1024]{1,0:T(8,128)}) custom-call(s32[10]{0:T(128)S(1)} %pad_add_fusion.ids, s32[1,320]{1,0:T(1,128)S(1)} %reshape.39.owners, bf16[32,40,256]{2,1,0:T(8,128)(2,1)S(1)} %all-to-all-done.3.grads, f32[320,1024]{1,0:T(8,128)S(1)} %bitcast.21, f32[320,1024]{1,0:T(8,128)S(1)} %bitcast.23, ...), custom_call_target="tpu_custom_call" | custom-call | bytes 1048576 | tf_op jit(solution)/shard_map/pallas_call | solution.py:393
  (45 shorter events, 5.8 us)
Async XLA Ops:
  0.6 14.6 %copy-start.11 = (s32[8]{0:T(128)S(1)}, s32[8]{0:T(128)}, u32[]{:S(2)}) copy-start(s32[8]{0:T(128)} %param.11) | copy-start | bytes 100
  0.6 14.6 %copy-start.10 = (s32[320]{0:T(512)S(1)}, s32[320]{0:T(512)}, u32[]{:S(2)}) copy-start(s32[320]{0:T(512)} %param.12) | copy-start | bytes 3844
  1.4 1.3 %copy-start = (f32[40,8,1024]{2,1,0:T(8,128)S(1)}, f32[40,8,1024]{2,1,0:T(8,128)}, u32[]{:S(2)}) copy-start(f32[40,8,1024]{2,1,0:T(8,128)} %master.1) | copy-start | bytes 3932164
  2.8 9.0 %copy-start.4 = (bf16[1024,32]{0,1:T(8,128)(2,1)S(1)}, bf16[1024,32]{0,1:T(8,128)(2,1)}, u32[]{:S(2)}) copy-start(bf16[1024,32]{0,1:T(8,128)(2,1)} %param.9) | copy-start | bytes 196612
  2.8 13.8 %copy-start.5 = (bf16[1024,32]{0,1:T(8,128)(2,1)S(1)}, bf16[1024,32]{0,1:T(8,128)(2,1)}, u32[]{:S(2)}) copy-start(bf16[1024,32]{0,1:T(8,128)(2,1)} %param.16) | copy-start | bytes 196612
  2.8 13.8 %copy-start.7 = (bf16[1024,32]{0,1:T(8,128)(2,1)S(1)}, bf16[1024,32]{0,1:T(8,128)(2,1)}, u32[]{:S(2)}) copy-start(bf16[1024,32]{0,1:T(8,128)(2,1)} %param.17) | copy-start | bytes 196612
  4.4 19.4 %all-to-all-start = ((bf16[16,40,256]{2,1,0:T(8,128)(2,1)}), bf16[16,40,256]{2,1,0:T(8,128)(2,1)S(1)}, u32[]{:S(2)}, u32[]{:S(2)}) async-start(bf16[16,40,256]{2,1,0:T(8,128)(2,1)} %shard_map.137), calls=%async_computation | async-start | bytes 655360 | tf_op jit(solution)/shard_map/all_to_all | solution.py:352
  11.8 4.8 %collective-permute-start.1 = (bf16[32,128]{1,0:T(8,128)(2,1)S(1)}, bf16[32,128]{1,0:T(8,128)(2,1)S(1)}, u32[]{:S(2)}, u32[]{:S(2)}) collective-permute-start(bf16[32,128]{1,0:T(8,128)(2,1)S(1)} %slice.4), channel_id=1, source_target_pairs={{0,16},{1,17},{2,18},{3,19},{4,20},{5,21},{6,22},{7,23},{8,24},{9,... | collective-permute-start | bytes 24584 | tf_op jit(solution)/shard_map/ppermute | solution.py:343
  15.2 4.1 %collective-permute-start = (s32[8]{0:T(128)S(1)}, s32[8]{0:T(128)S(1)}, u32[]{:S(2)}, u32[]{:S(2)}) collective-permute-start(s32[8]{0:T(128)S(1)} %copy-done.11), channel_id=1, source_target_pairs={{0,16},{16,0},{1,17},{17,1},{2,18},{18,2},{3,19},{19,3},{4,20},{20... | collective-permute-start | bytes 104 | tf_op jit(solution)/shard_map/ppermute | solution.py:344
  17.2 3.2 %collective-permute-start.2 = (bf16[112,256]{1,0:T(8,128)(2,1)S(1)}, bf16[112,256]{1,0:T(8,128)(2,1)S(1)}, u32[]{:S(2)}, u32[]{:S(2)}) collective-permute-start(bf16[112,256]{1,0:T(8,128)(2,1)S(1)} %get-tuple-element.31), channel_id=1, source_target_pairs={{0,1},{1,0},{2,3},{3,2},{4,5},{5,4},{6,7},{7,6},{8,9},{9,8},{10,11... | collective-permute-start | bytes 172040 | tf_op jit(solution)/shard_map/ppermute | solution.py:328
  17.2 4.6 %collective-permute-start.3 = (bf16[112,256]{1,0:T(8,128)(2,1)S(1)}, bf16[112,256]{1,0:T(8,128)(2,1)S(1)}, u32[]{:S(2)}, u32[]{:S(2)}) collective-permute-start(bf16[112,256]{1,0:T(8,128)(2,1)S(1)} %get-tuple-element.32), channel_id=1, source_target_pairs={{0,2},{1,3},{2,0},{3,1},{4,6},{5,7},{6,4},{7,5},{8,10},{9,11},{10,... | collective-permute-start | bytes 172040 | tf_op jit(solution)/shard_map/ppermute | solution.py:328
  19.2 4.5 %collective-permute-start.4 = (bf16[112,256]{1,0:T(8,128)(2,1)S(1)}, bf16[112,256]{1,0:T(8,128)(2,1)S(1)}, u32[]{:S(2)}, u32[]{:S(2)}) collective-permute-start(bf16[112,256]{1,0:T(8,128)(2,1)S(1)} %get-tuple-element.33), channel_id=1, source_target_pairs={{0,3},{1,2},{2,1},{3,0},{4,7},{5,6},{6,5},{7,4},{8,11},{9,10},{10,... | collective-permute-start | bytes 172040 | tf_op jit(solution)/shard_map/ppermute | solution.py:328
  23.8 25.9 %copy-start.6 = (bf16[1024,80]{0,1:T(8,128)(2,1)S(1)}, bf16[1024,80]{0,1:T(8,128)(2,1)}, u32[]{:S(2)}) copy-start(bf16[1024,80]{0,1:T(8,128)(2,1)} %param.10) | copy-start | bytes 491524
  25.1 24.6 %all-to-all-start.1 = ((bf16[8,224,256]{2,1,0:T(8,128)(2,1)}), bf16[8,224,256]{2,1,0:T(8,128)(2,1)S(1)}, u32[]{:S(2)}, u32[]{:S(2)}) async-start(bf16[8,224,256]{2,1,0:T(8,128)(2,1)} %shard_map.139), calls=%async_computation.1 | async-start | bytes 1835008 | tf_op jit(solution)/shard_map/all_to_all | solution.py:368
  29.0 12.3 %collective-permute-start.5 = (bf16[4,112,256]{2,1,0:T(8,128)(2,1)S(1)}, bf16[4,112,256]{2,1,0:T(8,128)(2,1)S(1)}, u32[]{:S(2)}, u32[]{:S(2)}) collective-permute-start(bf16[4,112,256]{2,1,0:T(8,128)(2,1)S(1)} %pad_maximum_fusion.p0), channel_id=1, source_target_pairs={{0,4},{1,5},{2,6},{3,7},{4,0},{5,1},{6,2},{7,3},{8,12},{9,13},{10,... | collective-permute-start | bytes 688136 | tf_op jit(solution)/shard_map/ppermute | solution.py:328
  30.5 19.2 %collective-permute-start.6 = (bf16[4,112,256]{2,1,0:T(8,128)(2,1)S(1)}, bf16[4,112,256]{2,1,0:T(8,128)(2,1)S(1)}, u32[]{:S(2)}, u32[]{:S(2)}) collective-permute-start(bf16[4,112,256]{2,1,0:T(8,128)(2,1)S(1)} %pad_maximum_fusion.p0), channel_id=1, source_target_pairs={{0,8},{1,9},{2,10},{3,11},{4,12},{5,13},{6,14},{7,15},{8,0},{9,1},... | collective-permute-start | bytes 688136 | tf_op jit(solution)/shard_map/ppermute | solution.py:328
  32.5 17.2 %collective-permute-start.7 = (bf16[4,112,256]{2,1,0:T(8,128)(2,1)S(1)}, bf16[4,112,256]{2,1,0:T(8,128)(2,1)S(1)}, u32[]{:S(2)}, u32[]{:S(2)}) collective-permute-start(bf16[4,112,256]{2,1,0:T(8,128)(2,1)S(1)} %pad_maximum_fusion.p0), channel_id=1, source_target_pairs={{0,12},{1,13},{2,14},{3,15},{4,8},{5,9},{6,10},{7,11},{8,4},{9,5},... | collective-permute-start | bytes 688136 | tf_op jit(solution)/shard_map/ppermute | solution.py:328
  53.6 30.1 %all-to-all-start.2 = ((bf16[8,224,256]{2,1,0:T(8,128)(2,1)}), bf16[8,224,256]{2,1,0:T(8,128)(2,1)S(1)}, u32[]{:S(2)}, u32[]{:S(2)}) async-start(bf16[8,224,256]{2,1,0:T(8,128)(2,1)} %get-tuple-element.47), calls=%async_computation.2 | async-start | bytes 1835008 | tf_op jit(solution)/shard_map/all_to_all | solution.py:379
  57.8 10.2 %collective-permute-start.10 = (bf16[4,112,256]{2,1,0:T(8,128)(2,1)S(1)}, bf16[4,112,256]{2,1,0:T(8,128)(2,1)S(1)}, u32[]{:S(2)}, u32[]{:S(2)}) collective-permute-start(bf16[4,112,256]{2,1,0:T(8,128)(2,1)S(1)} %get-tuple-element.38), channel_id=1, source_target_pairs={{0,12},{1,13},{2,14},{3,15},{4,8},{5,9},{6,10},{7,11},{8,4},{9,5},... | collective-permute-start | bytes 688136 | tf_op jit(solution)/shard_map/ppermute | solution.py:328
  59.8 12.7 %collective-permute-start.8 = (bf16[4,112,256]{2,1,0:T(8,128)(2,1)S(1)}, bf16[4,112,256]{2,1,0:T(8,128)(2,1)S(1)}, u32[]{:S(2)}, u32[]{:S(2)}) collective-permute-start(bf16[4,112,256]{2,1,0:T(8,128)(2,1)S(1)} %get-tuple-element.36), channel_id=1, source_target_pairs={{0,4},{1,5},{2,6},{3,7},{4,0},{5,1},{6,2},{7,3},{8,12},{9,13},{10,... | collective-permute-start | bytes 688136 | tf_op jit(solution)/shard_map/ppermute | solution.py:328
  63.3 19.1 %collective-permute-start.9 = (bf16[4,112,256]{2,1,0:T(8,128)(2,1)S(1)}, bf16[4,112,256]{2,1,0:T(8,128)(2,1)S(1)}, u32[]{:S(2)}, u32[]{:S(2)}) collective-permute-start(bf16[4,112,256]{2,1,0:T(8,128)(2,1)S(1)} %get-tuple-element.37), channel_id=1, source_target_pairs={{0,8},{1,9},{2,10},{3,11},{4,12},{5,13},{6,14},{7,15},{8,0},{9,1},... | collective-permute-start | bytes 688136 | tf_op jit(solution)/shard_map/ppermute | solution.py:328
  82.5 0.6 copy-start.8
  83.1 0.6 copy-start.9
  83.7 24.5 %copy-start.2 = (f32[40,8,1024]{2,1,0:T(8,128)S(1)}, f32[40,8,1024]{2,1,0:T(8,128)}, u32[]{:S(2)}) copy-start(f32[40,8,1024]{2,1,0:T(8,128)} %param.14) | copy-start | bytes 3932164
  85.0 23.1 %copy-start.1 = (f32[40,8,1024]{2,1,0:T(8,128)S(1)}, f32[40,8,1024]{2,1,0:T(8,128)}, u32[]{:S(2)}) copy-start(f32[40,8,1024]{2,1,0:T(8,128)} %master.1) | copy-start | bytes 3932164
  85.1 23.1 %all-to-all-start.3 = ((bf16[32,40,256]{2,1,0:T(8,128)(2,1)}), bf16[32,40,256]{2,1,0:T(8,128)(2,1)S(1)}, u32[]{:S(2)}, u32[]{:S(2)}) async-start(bf16[32,40,256]{2,1,0:T(8,128)(2,1)} %bitcast.14), calls=%async_computation.3 | async-start | bytes 1310720 | tf_op jit(solution)/shard_map/all_to_all | solution.py:385
  89.4 2.0 %collective-permute-start.11 = (bf16[112,256]{1,0:T(8,128)(2,1)}, bf16[112,256]{1,0:T(8,128)(2,1)S(1)}, u32[]{:S(2)}, u32[]{:S(2)}) collective-permute-start(bf16[112,256]{1,0:T(8,128)(2,1)} %copy-done.9), channel_id=1, source_target_pairs={{0,1},{1,0},{2,3},{3,2},{4,5},{5,4},{6,7},{7,6},{8,9},{9,8},{10,11... | collective-permute-start | bytes 172040 | tf_op jit(solution)/shard_map/ppermute | solution.py:328
  89.7 8.6 %collective-permute-start.12 = (bf16[112,256]{1,0:T(8,128)(2,1)}, bf16[112,256]{1,0:T(8,128)(2,1)S(1)}, u32[]{:S(2)}, u32[]{:S(2)}) collective-permute-start(bf16[112,256]{1,0:T(8,128)(2,1)} %copy-done.8), channel_id=1, source_target_pairs={{0,2},{1,3},{2,0},{3,1},{4,6},{5,7},{6,4},{7,5},{8,10},{9,11},{10,... | collective-permute-start | bytes 172040 | tf_op jit(solution)/shard_map/ppermute | solution.py:328
  91.4 7.7 %collective-permute-start.13 = (bf16[112,256]{1,0:T(8,128)(2,1)S(1)}, bf16[112,256]{1,0:T(8,128)(2,1)S(1)}, u32[]{:S(2)}, u32[]{:S(2)}) collective-permute-start(bf16[112,256]{1,0:T(8,128)(2,1)S(1)} %get-tuple-element.42), channel_id=1, source_target_pairs={{0,3},{1,2},{2,1},{3,0},{4,7},{5,6},{6,5},{7,4},{8,11},{9,10},{10,... | collective-permute-start | bytes 172040 | tf_op jit(solution)/shard_map/ppermute | solution.py:328
  100.0 5.5 %collective-permute-start.14 = (bf16[32,128]{1,0:T(8,128)(2,1)S(1)}, bf16[32,128]{1,0:T(8,128)(2,1)S(1)}, u32[]{:S(2)}, u32[]{:S(2)}) collective-permute-start(bf16[32,128]{1,0:T(8,128)(2,1)S(1)} %shard_map.142), channel_id=1, source_target_pairs={{16,0},{17,1},{18,2},{19,3},{20,4},{21,5},{22,6},{23,7},{24,8},{25... | collective-permute-start | bytes 24584 | tf_op jit(solution)/shard_map/ppermute | solution.py:387
  108.2 1.3 %copy-start.3 = (f32[40,8,1024]{2,1,0:T(8,128)S(1)}, f32[40,8,1024]{2,1,0:T(8,128)}, u32[]{:S(2)}) copy-start(f32[40,8,1024]{2,1,0:T(8,128)} %param.15) | copy-start | bytes 3932164

commit v3 on v2

--- a/solution.py
+++ b/solution.py
@@ -53,13 +53,13 @@
     return jnp.where(cond, 1.0, 0.0).astype(BF16)
 
 
-def call(kernel, out, n_smem, n_in, flops=0, mbytes=1, scratch=()):
+def call(kernel, out, n_smem, n_in, flops=0, mbytes=1, scratch=(), out_space=pltpu.VMEM):
     return pl.pallas_call(
         kernel,
         out_shape=out,
         in_specs=[pl.BlockSpec(memory_space=pltpu.SMEM)] * n_smem
         + [pl.BlockSpec(memory_space=pltpu.VMEM)] * n_in,
-        out_specs=jax.tree.map(lambda _: pl.BlockSpec(memory_space=pltpu.VMEM), out),
+        out_specs=jax.tree.map(lambda _: pl.BlockSpec(memory_space=out_space), out),
         scratch_shapes=list(scratch),
         compiler_params=pltpu.CompilerParams(vmem_limit_bytes=24 * 2**20),
         cost_estimate=pl.CostEstimate(
@@ -92,24 +92,45 @@
             out[4 * z + j] = got[j * slots : (j + 1) * slots, 256 * z : 256 * (z + 1)].astype(BF16)
 
 
-def pack_tokens(ids, sig, res, skp, halo, o0, o1, o2, o3):
-    j = ids[1] & 3
-    ends = []
+def edge_tiles(ids, sig, res, skp, mel, out):
+    cut = pl.ds(pl.multiple_of((1 - ids[0]) * 896, 128), 128)
+    for n, part in enumerate((sig, res, skp)):
+        out[32 * n : 32 * n + 32, :] = part[:, cut]
+    out[96:176, :] = mel[:, cut]
+
+
+def pack_tokens(ids, sig, res, skp, other, o0, o1, o2, o3):
+    half, j = ids[0], ids[1] & 3
     outs = (o0, o1, o2, o3)
+    parts = (sig, res, skp)
+    befores, nexts = [], ([], [], [])
     for k in range(4):
         to = j ^ k
         cut = pl.ds(pl.multiple_of(to * 256, 256), 256)
-        for n, part in enumerate((sig, res, skp)):
+        for n, part in enumerate(parts):
             outs[k][32 * n : 32 * n + 32, :] = part[:, cut]
-        before = sig[:, pl.ds(pl.multiple_of(jnp.maximum(to * 256 - 128, 0), 128), 128)]
-        ends.append(jnp.where(to == 0, halo[...].astype(F32), before.astype(F32)))
-    tails = jnp.concatenate(ends, 0).astype(BF16)
-    last = onehot(iota((16, 128), 1) == iota((16, 128), 0) + 112)
-    rows = dot(last, tails, NT)
-    lane = iota((16, 128), 1)
+        cut = pl.ds(pl.multiple_of(jnp.maximum(to * 256 - 128, 0), 128), 128)
+        edge = jnp.where(half == 1, other[0:32, :].astype(F32), 0.0)
+        befores.append(jnp.where(to == 0, edge, sig[:, cut].astype(F32)))
+        cut = pl.ds(pl.multiple_of(jnp.minimum(to * 256 + 256, 896), 128), 128)
+        for n, part in enumerate(parts):
+            edge = jnp.where(half == 0, other[32 * n : 32 * n + 32, :].astype(F32), 0.0)
+            nexts[n].append(jnp.where(to == 3, edge, part[:, cut].astype(F32)))
+    tall = [jnp.concatenate(x, 0).astype(BF16) for x in (befores, *nexts)]
+    t, lane = iota((16, 128), 0), iota((16, 128), 1)
+    top, low = t < DILATION, t >= DILATION
+    head_top = onehot(top & (lane == t))
+    head_low = onehot(low & (lane == t - DILATION))
+    last_top = onehot(top & (lane == t + 120))
+    rows = (
+        dot(last_top, tall[0], NT) + dot(head_low, tall[1], NT),
+        dot(head_top, tall[2], NT) + dot(head_low, tall[3], NT),
+    )
     for k in range(4):
-        outs[k][96:112, 0:128] = jnp.where((lane >> 5) == k, rows, 0.0).astype(BF16)
-        outs[k][96:112, 128:256] = jnp.zeros((16, 128), BF16)
+        for n in range(2):
+            outs[k][96:112, 128 * n : 128 * n + 128] = jnp.where(
+                (lane >> 5) == k, rows[n], 0.0
+            ).astype(BF16)
 
 
 def place_blocks(sid, owners, pick, put, *, slots_dev):
@@ -123,7 +144,7 @@
     n = iota((PACKED, 1), 0)
     spk = jnp.zeros((PACKED, 1), jnp.int32)
     for s in range(16):
-        spk = jnp.where(n == SEG_AT + s, sid[s] >> 3, spk)
+        spk = jnp.where(n == SEG_AT + s, sid[2 + s] >> 3, spk)
     blk = jnp.where(
         n < SPK_BLOCK,
         n,
@@ -160,11 +181,12 @@
     return ((pos >> 5) ^ ch) * 32 + (pos & 31)
 
 
-def layer(ids, packed, p0, p1, p2, p3, mel, grads, z0, z1, z2, z3, feat):
+def layer(ids, packed, p0, p1, p2, p3, mel, other, grads, z0, z1, z2, z3, feat):
     half, ch = ids[0], ids[1]
     j = ch & 3
     got = (p0, p1, p2, p3)
     sq = (RESID, RESID)
+    tokens, wide = 256, 384
 
     def order(dim):
         major = iota(sq, dim)
@@ -172,45 +194,53 @@
 
     to_major = order(0)
     to_place = order(1)
-    tokens = 256
 
     def stacked(n):
         return jnp.concatenate(
             [got[k][i, 32 * n : 32 * n + 32, :] for k in range(4) for i in range(4)], 0
         )
 
-    sig = dot(to_major, stacked(0))
-    res = dot(to_major, stacked(1)).astype(BF16)
-    skp = dot(to_major, stacked(2)).astype(BF16)
     ends = []
     for k in range(4):
-        end = got[k][0, 96:112, 0:128].astype(F32)
+        end = got[k][0, 96:112, :].astype(F32)
         for i in range(1, 4):
-            end = end + got[k][i, 96:112, 0:128].astype(F32)
+            end = end + got[k][i, 96:112, :].astype(F32)
         ends.append(end)
-    halo = jnp.concatenate([jnp.zeros((112, RESID), F32), jnp.concatenate(ends, 1)], 0).astype(BF16)
-    halo = pltpu.roll(dot(to_major, halo, NT), DILATION, 1)
-    moved = pltpu.roll(sig, DILATION, 1)
-    first = iota((RESID, 128), 1) < DILATION
-    shifted = jnp.concatenate([jnp.where(first, halo, moved[:, :128]), moved[:, 128:]], 1).astype(BF16)
+    ends = [jnp.concatenate([e[:, 128 * n : 128 * n + 128] for e in ends], 1) for n in range(2)]
+    gap = jnp.zeros((120, RESID), F32)
+    ends = jnp.concatenate(
+        [ends[0][8:16], gap[:112], ends[0][0:8], ends[1][0:8], gap, ends[1][8:16], gap], 0
+    ).astype(BF16)
+    ends = dot(to_major, ends, NT)
+    sig = jnp.concatenate([dot(to_major, stacked(0)), ends[:, 0:128]], 1)
+    res = jnp.concatenate([dot(to_major, stacked(1)), ends[:, 128:256]], 1).astype(BF16)
+    skp = jnp.concatenate([dot(to_major, stacked(2)), ends[:, 256:384]], 1).astype(BF16)
+    shifted = pltpu.roll(sig, DILATION, 1).astype(BF16)
     sig = sig.astype(BF16)
     m = iota((128, MELS), 0)
     mel_pick = onehot(((m & 15) < MEL_BLOCKS) & (iota((128, MELS), 1) == 8 * (m & 15) + (m >> 4)))
-    mels = dot(mel_pick, mel[:, pl.ds(pl.multiple_of(j * tokens, tokens), tokens)]).astype(BF16)
-    seg_row = iota((16, tokens), 0)
-    seg_of = 8 * half + 2 * j + (iota((16, tokens), 1) >> 7)
-    sub = jnp.where(iota((16, tokens), 1) < SEG, ids[2 + 2 * j] & 7, ids[3 + 2 * j] & 7)
+    cut = pl.ds(pl.multiple_of(j * tokens, tokens), tokens)
+    far = pl.ds(pl.multiple_of(jnp.minimum(j * tokens + tokens, 896), 128), 128)
+    ahead = jnp.where(j == 3, other[96:176, :].astype(F32), mel[:, far].astype(F32)).astype(BF16)
+    mels = jnp.concatenate([dot(mel_pick, mel[:, cut]), dot(mel_pick, ahead)], 1).astype(BF16)
+    seg = 8 * half + 2 * j
+    row, lane = iota((16, wide), 0), iota((16, wide), 1)
+    sub = jnp.where(
+        lane < SEG,
+        ids[2 + seg] & 7,
+        jnp.where(lane < 2 * SEG, ids[3 + seg] & 7, ids[2 + jnp.minimum(seg + 2, 15)] & 7),
+    )
     for r in range(8):
         feat[r, 0:64] = shifted[64 * r : 64 * r + 64]
         feat[r, 64:128] = sig[64 * r : 64 * r + 64]
         feat[r, 128:144] = mels[16 * r : 16 * r + 16]
-        feat[r, 144:160] = onehot((seg_row == seg_of) & (sub == r))
-    features = feat[...].reshape(8 * OUT_AT, tokens)
+        feat[r, 144:160] = onehot((row == seg + (lane >> 7)) & (sub == r))
+    features = feat[...].reshape(8 * OUT_AT, wide)
     conv = packed[:, 0:OUT_AT, :].reshape(8 * OUT_AT, 256)
     pre = dot(conv, features, TN)
     filt = jnp.tanh(pre[:128])
     gate = jax.nn.sigmoid(pre[128:])
-    hidden = (filt * gate).astype(BF16)
+    hidden = (filt[:, :tokens] * gate[:, :tokens]).astype(BF16)
     out_res = packed[:, OUT_AT:PACKED, 0:128].reshape(RESID, 128)
     out_skp = packed[:, OUT_AT:PACKED, 128:256].reshape(RESID, 128)
     res_part = dot(out_res, hidden).astype(BF16)
@@ -225,30 +255,21 @@
     ).astype(BF16)
     prev = packed[:, 0:64, :].reshape(RESID, 256)
     now = packed[:, 64:128, :].reshape(RESID, 256)
-    later = dot(prev, grad_pre)
-    kept = iota((RESID, tokens), 1) < tokens - DILATION
-    in_part = dot(now, grad_pre) + jnp.where(kept, pltpu.roll(later, tokens - DILATION, 1), 0.0)
-    conv_grad = dot(features, grad_pre, NT).astype(BF16)
-    res_grad = dot(res, hidden, NT).astype(BF16)
-    skp_grad = dot(skp, hidden, NT).astype(BF16)
+    later = pltpu.roll(dot(prev, grad_pre), wide - DILATION, 1)[:, :tokens]
+    grad_pre = grad_pre[:, :tokens]
+    in_part = (dot(now, grad_pre) + later).astype(BF16)
+    conv_grad = dot(features[:, :tokens], grad_pre, NT).astype(BF16)
+    res_grad = dot(res[:, :tokens], hidden, NT).astype(BF16)
+    skp_grad = dot(skp[:, :tokens], hidden, NT).astype(BF16)
     grads[:, 0:OUT_AT, :] = conv_grad.reshape(8, OUT_AT, 256)
     grads[:, OUT_AT:PACKED, 0:128] = res_grad.reshape(8, 64, 128)
     grads[:, OUT_AT:PACKED, 128:256] = skp_grad.reshape(8, 64, 128)
-    res_part = dot(to_place, res_part).astype(BF16)
-    skp_part = dot(to_place, skp_part).astype(BF16)
-    in_part = dot(to_place, in_part.astype(BF16)).astype(BF16)
-    early = dot(to_place, later[:, :128].astype(BF16)).astype(BF16)
-    head = onehot(iota((16, 128), 0) == iota((16, 128), 1))
-    early = dot(head, early, NT).astype(BF16)
-    outs = (z0, z1, z2, z3)
-    for k in range(4):
+    parts = [dot(to_place, part).astype(BF16) for part in (res_part, skp_part, in_part)]
+    for k, out in enumerate((z0, z1, z2, z3)):
         for i in range(4):
             at = 128 * k + 32 * i
-            outs[k][i, 0:32] = res_part[at : at + 32]
-            outs[k][i, 32:64] = skp_part[at : at + 32]
-            outs[k][i, 64:96] = in_part[at : at + 32]
-            outs[k][i, 96:112, 0:128] = early[:, 128 * k : 128 * k + 128]
-            outs[k][i, 96:112, 128:256] = jnp.zeros((16, 128), BF16)
+            for n in range(3):
+                out[i, 32 * n : 32 * n + 32] = parts[n][at : at + 32]
 
 
 def sum_units(z0, z1, z2, z3, o0, o1, o2, o3):
@@ -258,53 +279,34 @@
         ).astype(BF16)
 
 
-def late_tail(rows, k):
-    lane = onehot(iota((32, 128), 1) == 32 * k + iota((32, 128), 0))
-    chans = dot(lane, rows, NT).astype(BF16)
-    t = iota((16, 128), 0)
-    return dot(chans, onehot((t < DILATION) & (iota((16, 128), 1) == 120 + t)))
-
-
-def edge(ids, o0, o1, o2, o3, out):
+def finish_tokens(ids, o0, o1, o2, o3, sig, res, residual, skipped, grad_in):
     j = ids[1] & 3
-    total = jnp.zeros((32, 128), F32)
     for k, piece in enumerate((o0, o1, o2, o3)):
-        total = total + jnp.where(j == k, late_tail(piece[96:112, 0:128], k), 0.0)
-    out[...] = total.astype(BF16)
-
-
-def finish_tokens(ids, o0, o1, o2, o3, ahead, sig, res, residual, skipped, grad_in):
-    j = ids[1] & 3
-    pieces = (o0, o1, o2, o3)
-    for k, piece in enumerate(pieces):
         cut = pl.ds(pl.multiple_of((j ^ k) * 256, 256), 256)
         residual[:, cut] = sig[:, cut].astype(F32) + piece[0:32, :].astype(F32)
         skipped[:, cut] = piece[32:64, :].astype(F32)
         grad_in[:, cut] = res[:, cut].astype(F32) + piece[64:96, :].astype(F32)
-    for k, piece in enumerate(pieces):
-        tail = late_tail(piece[96:112, 0:128], k)
-        start = (j ^ k) * 256 - 128
-
-        @pl.when(start >= 0)
-        def _():
-            cut = pl.ds(pl.multiple_of(start, 128), 128)
-            grad_in[:, cut] = grad_in[:, cut] + tail
-
-    grad_in[:, 896:1024] = grad_in[:, 896:1024] + ahead[...].astype(F32)
-
-
-def update(ids, owners, grads, master, first, second, new_first, new_second, new_master):
+
+
+def update(ids, owners, grads, master, first, second, *refs):
+    outs, held, sems = refs[:3], refs[3:6], refs[6]
     slots = grads.shape[1]
+    rows = 8 * slots
     owned = jnp.sum(jnp.where(owners[...] == ids[1], 1, 0))
-    keep = iota((8 * slots, 1), 0) < 8 * owned
-    spread = []
+    keep = iota((rows, 1), 0) < 8 * owned
+    to, of = iota((rows, rows), 0), iota((rows, rows), 1)
+    spread = jnp.zeros((rows, rows), jnp.bool_)
     for r in range(8):
-        spread.append(onehot(iota((8 * slots, slots), 0) == 8 * iota((8 * slots, slots), 1) + r))
+        inside = (of >= r * slots) & (of < (r + 1) * slots)
+        spread = spread | (inside & (to == 8 * (of - r * slots) + r))
+    spread = onehot(spread)
+    copies = []
     for z in range(4):
         cut = slice(256 * z, 256 * z + 256)
-        grad = dot(spread[0], grads[4 * z])
-        for r in range(1, 8):
-            grad = grad + dot(spread[r], grads[16 * (r // 4) + 4 * z + r % 4])
+        grad = jnp.concatenate(
+            [grads[16 * (r // 4) + 4 * z + r % 4].astype(F32) for r in range(8)], 0
+        )
+        grad = dot(spread, grad.astype(BF16))
         old_m = master[:, cut]
         old_f = first[:, cut]
         old_s = second[:, cut]
@@ -315,9 +317,17 @@
         stepped = old_m - STEP_RATE * (
             first_hat / (jnp.sqrt(second_hat) + EPSILON) + WEIGHT_DECAY * old_m
         )
-        new_first[:, cut] = jnp.where(keep, first_new, old_f)
-        new_second[:, cut] = jnp.where(keep, second_new, old_s)
-        new_master[:, cut] = jnp.where(keep, stepped, old_m)
+        held[0][:, cut] = jnp.where(keep, first_new, old_f)
+        held[1][:, cut] = jnp.where(keep, second_new, old_s)
+        held[2][:, cut] = jnp.where(keep, stepped, old_m)
+        for n in range(3):
+            copy = pltpu.make_async_copy(
+                held[n].at[:, cut], outs[n].at[:, cut], sems.at[3 * z + n]
+            )
+            copy.start()
+            copies.append(copy)
+    for copy in copies:
+        copy.wait()
 
 
 BOTH = ("tm", "chan")
@@ -334,24 +344,28 @@
     slots_dev = master.shape[0]
     slots = 16 * slots_dev
     half = lax.axis_index("tm")
-    ids = jnp.concatenate([jnp.stack([half, lax.axis_index("chan")]).astype(jnp.int32), speaker_ids])
+    ids = jnp.stack([half, lax.axis_index("chan")]).astype(jnp.int32)
     sig, res, skp, mel = signal.T, res_cot.T, skip_cot.T, mel_frames.T
     own_row = owners.reshape(1, NBLK)
     share = [[16 * y + 4 * z + j for y in range(2) for j in range(4)] for z in range(4)]
     sds = jax.ShapeDtypeStruct
-
-    halo = lax.ppermute(sig[:, -128:], "tm", [(0, 1)])
-    other_ids = lax.ppermute(speaker_ids, "tm", [(0, 1), (1, 0)])
+    turn = [(0, 1), (1, 0)]
+
+    edges = call(edge_tiles, sds((176, 128), BF16), 1, 4)(ids, sig, res, skp, mel)
+    other = lax.ppermute(edges, "tm", turn)
+    other_ids = lax.ppermute(speaker_ids, "tm", turn)
     sids = jnp.where(
         half == 0,
         jnp.concatenate([speaker_ids, other_ids]),
         jnp.concatenate([other_ids, speaker_ids]),
     )
+    info = jnp.concatenate([ids, sids])
 
     sent = call(pack_weights, sds((16, slots_dev, 256), BF16), 1, 1)(ids, master)
+    piece = sds((PIECE, 256), BF16)
+    o = call(pack_tokens, (piece,) * 4, 1, 4)(ids, sig, res, skp, other)
+    sent, _ = lax.optimization_barrier((sent, other))
     arrived = lax.all_to_all(sent, "chan", 0, 0, tiled=True)
-    piece = sds((PIECE, 256), BF16)
-    o = call(pack_tokens, (piece,) * 4, 1, 4)(ids, sig, res, skp, halo)
     mine = jnp.stack([o[0], swap(o[1], 1), swap(o[2], 2), swap(o[3], 3)])
     p1, p2, p3 = (swap(mine, 4 * k) for k in (1, 2, 3))
 
@@ -360,37 +374,40 @@
         (sds((PACKED, slots), BF16), sds((slots, PACKED), BF16)),
         1,
         1,
-    )(sids, own_row)
+    )(info, own_row)
     arrived, _ = lax.optimization_barrier((arrived, mine))
     gathered = call(gather_blocks, sds((8, PACKED, 256), BF16), 0, 2)(
         pick, arrived.reshape(slots, 256)
     )
     packed = lax.all_to_all(gathered, BOTH, 0, 0, axis_index_groups=share)
 
-    quad = sds((4, PIECE, 256), BF16)
+    quad = sds((4, 96, 256), BF16)
     grads, z0, z1, z2, z3 = call(
         layer,
         (sds((8, PACKED, 256), BF16), quad, quad, quad, quad),
         1,
-        6,
-        scratch=(pltpu.VMEM((8, OUT_AT, 256), BF16),),
-    )(ids, packed, mine, p1, p2, p3, mel)
+        7,
+        scratch=(pltpu.VMEM((8, OUT_AT, 384), BF16),),
+    )(info, packed, mine, p1, p2, p3, mel, other)
 
     parts = lax.all_to_all(grads, BOTH, 0, 0, axis_index_groups=share)
     t1, t2, t3 = (swap(z, 4 * k) for k, z in ((1, z1), (2, z2), (3, z3)))
-    o = call(sum_units, (piece,) * 4, 0, 4)(z0, t1, t2, t3)
+    o = call(sum_units, (sds((96, 256), BF16),) * 4, 0, 4)(z0, t1, t2, t3)
     parts, _ = lax.optimization_barrier((parts, o[0]))
-    o = (o[0], swap(o[1], 1), swap(o[2], 2), swap(o[3], 3))
     spread = call(scatter_blocks, sds((2, slots, 256), BF16), 0, 2)(put, parts)
     returned = lax.all_to_all(spread.reshape(32, slots_dev, 256), BOTH, 0, 0)
-    tail = call(edge, sds((32, 128), BF16), 1, 4)(ids, *o)
-    ahead = lax.ppermute(tail, "tm", [(1, 0)])
+    o = (o[0], swap(o[1], 1), swap(o[2], 2), swap(o[3], 3))
     narrow = sds(sig.shape, F32)
-    residual, skipped, grad_in = call(finish_tokens, (narrow,) * 3, 1, 7)(
-        ids, *o, ahead, sig, res
-    )
+    residual, skipped, grad_in = call(finish_tokens, (narrow,) * 3, 1, 6)(ids, *o, sig, res)
     flat = (8 * slots_dev, GATES)
-    new = call(update, (sds(flat, F32),) * 3, 1, 5)(
+    new = call(
+        update,
+        (sds(flat, F32),) * 3,
+        1,
+        5,
+        scratch=(pltpu.VMEM(flat, F32),) * 3 + (pltpu.SemaphoreType.DMA((12,)),),
+        out_space=pl.ANY,
+    )(
         ids,
         own_row,
         returned,

time: 115 us -> 117 us (1.017)
  local copies, waits for them, and re-layouts: 3.92 us -> 10.3 us
  Pallas kernels: 18 us -> 15.6 us
  starting transfers between devices: 38.9 us -> 36.9 us
    all_to_all x1, waiting for transfers between devices: 0.34 us -> 8.52 us  [local(): returned = lax.all_to_all(spread.reshape(32, slots_dev, 256), BOTH, 0, 0)]
    unnamed x24 -> x48, local copies, waits for them, and re-layouts: 3.91 us -> 10.3 us
    ppermute x12, waiting for transfers between devices: 46 us -> 41.5 us  [swap(): return lax.ppermute(x, 'chan', [(i, i ^ k) for i in range(n)])]
    ppermute x3 -> x2, waiting for transfers between devices: 5.48 us -> 2.41 us  [the longest x1 2.41 us: local(): other_ids = lax.ppermute(speaker_ids, 'tm', turn)]
    pallas_call x6, Pallas kernels: 12.7 us -> 10.3 us  [the longest x1 3.79 us: local(): call(layer, (sds((8, PACKED, 256), BF16), quad, quad, quad, quad), 1, 7,...]
    all_to_all x1, starting transfers between devices: 7.36 us -> 5.91 us  [local(): arrived = lax.all_to_all(sent, 'chan', 0, 0, tiled=True)]
    ppermute x3 -> x2, starting transfers between devices: 4.78 us -> 4.22 us  [the longest x1 3.03 us: local(): other = lax.ppermute(edges, 'tm', turn)]
  transfers between devices with their start and end apart: 19 -> 18, of which waited for: 12 -> 12; matrix products, arithmetic and copies ran while one was open for 0% -> 0% of each run, Pallas kernels for 4% -> 4%
where the time goes in v3:
time: 117 us; the launch traced here: 116 us
  waiting for transfers between devices  52.7 us (45%)
  starting transfers between devices  36.9 us (32%)
  Pallas kernels  15.6 us (13%)
  local copies, waits for them, and re-layouts  10.3 us (9%)
    ppermute x12, waiting for transfers between devices, swap(): return lax.ppermute(x, 'chan', [(i, i ^ k) for i in range(n)])  41.5 us
    ppermute x12, starting transfers between devices, swap(): return lax.ppermute(x, 'chan', [(i, i ^ k) for i in range(n)])  14.4 us
    unnamed x48, local copies, waits for them, and re-layouts  10.3 us
    all_to_all x1, waiting for transfers between devices, local(): returned = lax.all_to_all(spread.reshape(32, slots_dev, 256), BOTH, 0, 0)  8.52 us
    all_to_all x1, starting transfers between devices, local(): arrived = lax.all_to_all(sent, 'chan', 0, 0, tiled=True)  5.91 us
    all_to_all x1, starting transfers between devices, local(): returned = lax.all_to_all(spread.reshape(32, slots_dev, 256), BOTH, 0, 0)  4.71 us
    all_to_all x1, starting transfers between devices, local(): parts = lax.all_to_all(grads, BOTH, 0, 0, axis_index_groups=share)  4.04 us
    pallas_call x1, Pallas kernels, local(): call(layer, (sds((8, PACKED, 256), BF16), quad, quad, quad, quad), 1, 7,...  3.79 us
  transfers between devices with their start and end apart: 18, of which 12 were waited for; matrix products, arithmetic and copies ran while one was open for 0% of the time, Pallas kernels for 4%

profile of v3, /device:TPU:0, one launch (start us, length us, event | category | flops | bytes accessed | tf_op | source)
XLA Modules:
  0.0 116.5 jit_solution(1339262345994311329)
XLA Ops:
  4.7 3.0 %collective-permute-start.1 = (bf16[176,128]{1,0:T(8,128)(2,1)S(1)}, bf16[176,128]{1,0:T(8,128)(2,1)S(1)}, u32[]{:S(2)}, u32[]{:S(2)}) collective-permute-start(bf16[176,128]{1,0:T(8,128)(2,1)S(1)} %shard_map.138), channel_id=1, source_target_pairs={{0,16},{16,0},{1,17},{17,1},{2,18},{18,2},{3,19},{19,3},{4,20},{20... | collective-permute-start | bytes 135176 | tf_op jit(solution)/shard_map/ppermute | solution.py:355
  7.8 1.3 %copy-done = f32[40,8,1024]{2,1,0:T(8,128)S(1)} copy-done((f32[40,8,1024]{2,1,0:T(8,128)S(1)}, f32[40,8,1024]{2,1,0:T(8,128)}, u32[]{:S(2)}) %copy-start) | copy-done | bytes 1310744
  9.1 1.6 %shard_map.137 = bf16[16,40,256]{2,1,0:T(8,128)(2,1)} custom-call(s32[2]{0:T(128)S(1)} %pad_add_fusion.ids, f32[40,8,1024]{2,1,0:T(8,128)S(1)} %copy-done), custom_call_target="tpu_custom_call" | custom-call | bytes 1048576 | tf_op jit(solution)/shard_map/pallas_call | solution.py:364
  10.7 5.9 %all-to-all-start = ((bf16[16,40,256]{2,1,0:T(8,128)(2,1)}), bf16[16,40,256]{2,1,0:T(8,128)(2,1)S(1)}, u32[]{:S(2)}, u32[]{:S(2)}) async-start(bf16[16,40,256]{2,1,0:T(8,128)(2,1)} %shard_map.137), calls=%async_computation | async-start | bytes 655360 | tf_op jit(solution)/shard_map/all_to_all | solution.py:368
  16.6 1.2 %collective-permute-start = (s32[8]{0:T(128)S(1)}, s32[8]{0:T(128)S(1)}, u32[]{:S(2)}, u32[]{:S(2)}) collective-permute-start(s32[8]{0:T(128)S(1)} %copy-done.23), channel_id=1, source_target_pairs={{0,16},{16,0},{1,17},{17,1},{2,18},{18,2},{3,19},{19,3},{4,20},{20... | collective-permute-start | bytes 104 | tf_op jit(solution)/shard_map/ppermute | solution.py:356
  17.8 2.4 %collective-permute-done = s32[8]{0:T(128)S(1)} collective-permute-done((s32[8]{0:T(128)S(1)}, s32[8]{0:T(128)S(1)}, u32[]{:S(2)}, u32[]{:S(2)}) %collective-permute-start) | collective-permute-done | bytes 64 | tf_op jit(solution)/shard_map/ppermute | solution.py:356
  21.1 2.0 %collective-permute-start.3 = (bf16[112,256]{1,0:T(8,128)(2,1)S(1)}, bf16[112,256]{1,0:T(8,128)(2,1)S(1)}, u32[]{:S(2)}, u32[]{:S(2)}) collective-permute-start(bf16[112,256]{1,0:T(8,128)(2,1)S(1)} %get-tuple-element.34), channel_id=1, source_target_pairs={{0,2},{1,3},{2,0},{3,1},{4,6},{5,7},{6,4},{7,5},{8,10},{9,11},{10,... | collective-permute-start | bytes 172040 | tf_op jit(solution)/shard_map/ppermute | solution.py:338
  23.2 1.0 shard_map.136
  25.0 1.1 collective-permute-done.3
  26.1 1.3 %collective-permute-done.4 = bf16[112,256]{1,0:T(8,128)(2,1)S(1)} collective-permute-done((bf16[112,256]{1,0:T(8,128)(2,1)S(1)}, bf16[112,256]{1,0:T(8,128)(2,1)S(1)}, u32[]{:S(2)}, u32[]{:S(2)}) %collective-permute-start.4) | collective-permute-done | bytes 57376 | tf_op jit(solution)/shard_map/ppermute | solution.py:338
  27.7 1.3 %shard_map.140 = bf16[8,224,256]{2,1,0:T(8,128)(2,1)} custom-call(bf16[224,640]{1,0:T(8,128)(2,1)S(1)} %get-tuple-element.30.pick, bf16[640,256]{1,0:T(8,128)(2,1)S(1)} %bitcast.22), custom_call_target="tpu_custom_call" | custom-call | bytes 1048576 | tf_op jit(solution)/shard_map/pallas_call | solution.py:379
  29.1 3.6 %all-to-all-start.1 = ((bf16[8,224,256]{2,1,0:T(8,128)(2,1)}), bf16[8,224,256]{2,1,0:T(8,128)(2,1)S(1)}, u32[]{:S(2)}, u32[]{:S(2)}) async-start(bf16[8,224,256]{2,1,0:T(8,128)(2,1)} %shard_map.140), calls=%async_computation.1 | async-start | bytes 1835008 | tf_op jit(solution)/shard_map/all_to_all | solution.py:382
  32.6 1.6 %collective-permute-start.5 = (bf16[4,112,256]{2,1,0:T(8,128)(2,1)S(1)}, bf16[4,112,256]{2,1,0:T(8,128)(2,1)S(1)}, u32[]{:S(2)}, u32[]{:S(2)}) collective-permute-start(bf16[4,112,256]{2,1,0:T(8,128)(2,1)S(1)} %pad_maximum_fusion.p0), channel_id=1, source_target_pairs={{0,4},{1,5},{2,6},{3,7},{4,0},{5,1},{6,2},{7,3},{8,12},{9,13},{10,... | collective-permute-start | bytes 688136 | tf_op jit(solution)/shard_map/ppermute | solution.py:338
  34.2 2.0 %collective-permute-start.6 = (bf16[4,112,256]{2,1,0:T(8,128)(2,1)S(1)}, bf16[4,112,256]{2,1,0:T(8,128)(2,1)S(1)}, u32[]{:S(2)}, u32[]{:S(2)}) collective-permute-start(bf16[4,112,256]{2,1,0:T(8,128)(2,1)S(1)} %pad_maximum_fusion.p0), channel_id=1, source_target_pairs={{0,8},{1,9},{2,10},{3,11},{4,12},{5,13},{6,14},{7,15},{8,0},{9,1},... | collective-permute-start | bytes 688136 | tf_op jit(solution)/shard_map/ppermute | solution.py:338
  37.1 7.8 %collective-permute-done.5.p1 = bf16[4,112,256]{2,1,0:T(8,128)(2,1)S(1)} collective-permute-done((bf16[4,112,256]{2,1,0:T(8,128)(2,1)S(1)}, bf16[4,112,256]{2,1,0:T(8,128)(2,1)S(1)}, u32[]{:S(2)}, u32[]{:S(2)}) %collective-permute-start.5) | collective-permute-done | bytes 229408 | tf_op jit(solution)/shard_map/ppermute | solution.py:338
  44.9 8.5 %collective-permute-done.6.p2 = bf16[4,112,256]{2,1,0:T(8,128)(2,1)S(1)} collective-permute-done((bf16[4,112,256]{2,1,0:T(8,128)(2,1)S(1)}, bf16[4,112,256]{2,1,0:T(8,128)(2,1)S(1)}, u32[]{:S(2)}, u32[]{:S(2)}) %collective-permute-start.6) | collective-permute-done | bytes 229408 | tf_op jit(solution)/shard_map/ppermute | solution.py:338
  53.4 3.8 %shard_map.141 = (bf16[8,224,256]{2,1,0:T(8,128)(2,1)}, bf16[4,96,256]{2,1,0:T(8,128)(2,1)S(1)}, bf16[4,96,256]{2,1,0:T(8,128)(2,1)S(1)}, bf16[4,96,256]{2,1,0:T(8,128)(2,1)S(1)}, bf16[4,96,256]{2,1,0:T(8,128)(2,1)S(1)}) custom-call(s32[18]{0:T(128)S(1)} %pad_add_fusion.1.sid.ids, bf16[8,224,256]{2,1,0:T(8,128)(2,1)S(1)} %all-to-all-done.1.packed, ...), custom_call_target="tpu_custom_call" | custom-call | bytes 1048576 | tf_op jit(solution)/shard_map/pallas_call | solution.py:385
  57.2 4.0 %all-to-all-start.2 = ((bf16[8,224,256]{2,1,0:T(8,128)(2,1)}), bf16[8,224,256]{2,1,0:T(8,128)(2,1)S(1)}, u32[]{:S(2)}, u32[]{:S(2)}) async-start(bf16[8,224,256]{2,1,0:T(8,128)(2,1)} %get-tuple-element.49), calls=%async_computation.2 | async-start | bytes 1835008 | tf_op jit(solution)/shard_map/all_to_all | solution.py:393
  61.3 2.3 %collective-permute-start.10 = (bf16[4,96,256]{2,1,0:T(8,128)(2,1)S(1)}, bf16[4,96,256]{2,1,0:T(8,128)(2,1)S(1)}, u32[]{:S(2)}, u32[]{:S(2)}) collective-permute-start(bf16[4,96,256]{2,1,0:T(8,128)(2,1)S(1)} %get-tuple-element.40), channel_id=1, source_target_pairs={{0,12},{1,13},{2,14},{3,15},{4,8},{5,9},{6,10},{7,11},{8,4},{9,5},... | collective-permute-start | bytes 589832 | tf_op jit(solution)/shard_map/ppermute | solution.py:338
  63.6 3.5 %collective-permute-start.8 = (bf16[4,96,256]{2,1,0:T(8,128)(2,1)S(1)}, bf16[4,96,256]{2,1,0:T(8,128)(2,1)S(1)}, u32[]{:S(2)}, u32[]{:S(2)}) collective-permute-start(bf16[4,96,256]{2,1,0:T(8,128)(2,1)S(1)} %get-tuple-element.38), channel_id=1, source_target_pairs={{0,4},{1,5},{2,6},{3,7},{4,0},{5,1},{6,2},{7,3},{8,12},{9,13},{10,... | collective-permute-start | bytes 589832 | tf_op jit(solution)/shard_map/ppermute | solution.py:338
  67.1 3.7 %collective-permute-done.10.z3 = bf16[4,96,256]{2,1,0:T(8,128)(2,1)S(1)} collective-permute-done((bf16[4,96,256]{2,1,0:T(8,128)(2,1)S(1)}, bf16[4,96,256]{2,1,0:T(8,128)(2,1)S(1)}, u32[]{:S(2)}, u32[]{:S(2)}) %collective-permute-start.10) | collective-permute-done | bytes 196640 | tf_op jit(solution)/shard_map/ppermute | solution.py:338
  70.8 3.8 %collective-permute-done.8.z1 = bf16[4,96,256]{2,1,0:T(8,128)(2,1)S(1)} collective-permute-done((bf16[4,96,256]{2,1,0:T(8,128)(2,1)S(1)}, bf16[4,96,256]{2,1,0:T(8,128)(2,1)S(1)}, u32[]{:S(2)}, u32[]{:S(2)}) %collective-permute-start.8) | collective-permute-done | bytes 196640 | tf_op jit(solution)/shard_map/ppermute | solution.py:338
  74.6 8.4 %collective-permute-done.9.z2 = bf16[4,96,256]{2,1,0:T(8,128)(2,1)S(1)} collective-permute-done((bf16[4,96,256]{2,1,0:T(8,128)(2,1)S(1)}, bf16[4,96,256]{2,1,0:T(8,128)(2,1)S(1)}, u32[]{:S(2)}, u32[]{:S(2)}) %collective-permute-start.9) | collective-permute-done | bytes 196640 | tf_op jit(solution)/shard_map/ppermute | solution.py:338
  85.6 1.0 copy-done.13
  86.6 1.4 %shard_map.144 = bf16[2,640,256]{2,1,0:T(8,128)(2,1)} custom-call(bf16[640,224]{1,0:T(8,128)(2,1)S(1)} %copy-done.13, bf16[8,224,256]{2,1,0:T(8,128)(2,1)S(1)} %all-to-all-done.2.parts), custom_call_target="tpu_custom_call" | custom-call | bytes 1048576 | tf_op jit(solution)/shard_map/pallas_call | solution.py:397
  88.0 4.7 %all-to-all-start.3 = ((bf16[32,40,256]{2,1,0:T(8,128)(2,1)}), bf16[32,40,256]{2,1,0:T(8,128)(2,1)S(1)}, u32[]{:S(2)}, u32[]{:S(2)}) async-start(bf16[32,40,256]{2,1,0:T(8,128)(2,1)} %bitcast.14), calls=%async_computation.3 | async-start | bytes 1310720 | tf_op jit(solution)/shard_map/all_to_all | solution.py:398
  93.0 1.7 %collective-permute-start.12 = (bf16[96,256]{1,0:T(8,128)(2,1)}, bf16[96,256]{1,0:T(8,128)(2,1)S(1)}, u32[]{:S(2)}, u32[]{:S(2)}) collective-permute-start(bf16[96,256]{1,0:T(8,128)(2,1)} %copy-done.20), channel_id=1, source_target_pairs={{0,2},{1,3},{2,0},{3,1},{4,6},{5,7},{6,4},{7,5},{8,10},{9,11},{10,... | collective-permute-start | bytes 147464 | tf_op jit(solution)/shard_map/ppermute | solution.py:338
  94.7 6.8 %collective-permute-done.12.o2 = bf16[96,256]{1,0:T(8,128)(2,1)S(1)} collective-permute-done((bf16[96,256]{1,0:T(8,128)(2,1)}, bf16[96,256]{1,0:T(8,128)(2,1)S(1)}, u32[]{:S(2)}, u32[]{:S(2)}) %collective-permute-start.12) | collective-permute-done | bytes 49184 | tf_op jit(solution)/shard_map/ppermute | solution.py:338
  101.6 1.3 %shard_map.143 = (f32[32,1024]{1,0:T(8,128)}, f32[32,1024]{1,0:T(8,128)}, f32[32,1024]{1,0:T(8,128)}) custom-call(s32[2]{0:T(128)S(1)} %pad_add_fusion.ids, bf16[96,256]{1,0:T(8,128)(2,1)S(1)} %copy-done.17, bf16[96,256]{1,0:T(8,128)(2,1)S(1)} %collective-permute-done.11.o1, bf16[96,256]{1,0:T(8,128)(2,1)S(1)} %collective-permute-done.12.o2, ...), custom_call_target="tpu_custom_call" | custom-call | bytes 1048576 | tf_op jit(solution)/shard_map/pallas_call | solution.py:401
  102.9 8.5 %all-to-all-done.3.grads = bf16[32,40,256]{2,1,0:T(8,128)(2,1)S(1)} async-done(((bf16[32,40,256]{2,1,0:T(8,128)(2,1)}), bf16[32,40,256]{2,1,0:T(8,128)(2,1)S(1)}, u32[]{:S(2)}, u32[]{:S(2)}) %all-to-all-start.3) | async-done | bytes 655392 | tf_op jit(solution)/shard_map/all_to_all | solution.py:398
  111.4 1.3 %copy-done.3 = f32[40,8,1024]{2,1,0:T(8,128)S(1)} copy-done((f32[40,8,1024]{2,1,0:T(8,128)S(1)}, f32[40,8,1024]{2,1,0:T(8,128)}, u32[]{:S(2)}) %copy-start.3) | copy-done | bytes 1310744
  112.7 3.8 %shard_map.145 = (f32[320,1024]{1,0:T(8,128)}, f32[320,1024]{1,0:T(8,128)}, f32[320,1024]{1,0:T(8,128)}) custom-call(s32[2]{0:T(128)S(1)} %pad_add_fusion.ids, s32[1,320]{1,0:T(1,128)S(1)} %reshape.39.owners, bf16[32,40,256]{2,1,0:T(8,128)(2,1)S(1)} %all-to-all-done.3.grads, f32[320,1024]{1,0:T(8,128)S(1)} %bitcast.21, f32[320,1024]{1,0:T(8,128)S(1)} %bitcast.23, ...), custom_call_target="tpu_custom_call" | custom-call | bytes 1048576 | tf_op jit(solution)/shard_map/pallas_call | solution.py:403
  (67 shorter events, 10.1 us)
Async XLA Ops:
  4.1 12.5 %copy-start.23 = (s32[8]{0:T(128)S(1)}, s32[8]{0:T(128)}, u32[]{:S(2)}) copy-start(s32[8]{0:T(128)} %param.11) | copy-start | bytes 100
  4.2 13.7 %copy-start.22 = (s32[320]{0:T(512)S(1)}, s32[320]{0:T(512)}, u32[]{:S(2)}) copy-start(s32[320]{0:T(512)} %param.12) | copy-start | bytes 3844
  4.2 16.2 %copy-start.7 = (bf16[1024,32]{0,1:T(8,128)(2,1)S(1)}, bf16[1024,32]{0,1:T(8,128)(2,1)}, u32[]{:S(2)}) copy-start(bf16[1024,32]{0,1:T(8,128)(2,1)} %param.9) | copy-start | bytes 196612
  4.2 16.2 %copy-start.10 = (bf16[1024,32]{0,1:T(8,128)(2,1)S(1)}, bf16[1024,32]{0,1:T(8,128)(2,1)}, u32[]{:S(2)}) copy-start(bf16[1024,32]{0,1:T(8,128)(2,1)} %param.16) | copy-start | bytes 196612
  4.2 16.2 %copy-start.15 = (bf16[1024,32]{0,1:T(8,128)(2,1)S(1)}, bf16[1024,32]{0,1:T(8,128)(2,1)}, u32[]{:S(2)}) copy-start(bf16[1024,32]{0,1:T(8,128)(2,1)} %param.17) | copy-start | bytes 196612
  4.7 6.0 %collective-permute-start.1 = (bf16[176,128]{1,0:T(8,128)(2,1)S(1)}, bf16[176,128]{1,0:T(8,128)(2,1)S(1)}, u32[]{:S(2)}, u32[]{:S(2)}) collective-permute-start(bf16[176,128]{1,0:T(8,128)(2,1)S(1)} %shard_map.138), channel_id=1, source_target_pairs={{0,16},{16,0},{1,17},{17,1},{2,18},{18,2},{3,19},{19,3},{4,20},{20... | collective-permute-start | bytes 135176 | tf_op jit(solution)/shard_map/ppermute | solution.py:355
  7.8 1.3 %copy-start = (f32[40,8,1024]{2,1,0:T(8,128)S(1)}, f32[40,8,1024]{2,1,0:T(8,128)}, u32[]{:S(2)}) copy-start(f32[40,8,1024]{2,1,0:T(8,128)} %master.1) | copy-start | bytes 3932164
  10.7 17.0 %all-to-all-start = ((bf16[16,40,256]{2,1,0:T(8,128)(2,1)}), bf16[16,40,256]{2,1,0:T(8,128)(2,1)S(1)}, u32[]{:S(2)}, u32[]{:S(2)}) async-start(bf16[16,40,256]{2,1,0:T(8,128)(2,1)} %shard_map.137), calls=%async_computation | async-start | bytes 655360 | tf_op jit(solution)/shard_map/all_to_all | solution.py:368
  16.6 3.6 %collective-permute-start = (s32[8]{0:T(128)S(1)}, s32[8]{0:T(128)S(1)}, u32[]{:S(2)}, u32[]{:S(2)}) collective-permute-start(s32[8]{0:T(128)S(1)} %copy-done.23), channel_id=1, source_target_pairs={{0,16},{16,0},{1,17},{17,1},{2,18},{18,2},{3,19},{19,3},{4,20},{20... | collective-permute-start | bytes 104 | tf_op jit(solution)/shard_map/ppermute | solution.py:356
  21.1 3.9 %collective-permute-start.2 = (bf16[112,256]{1,0:T(8,128)(2,1)S(1)}, bf16[112,256]{1,0:T(8,128)(2,1)S(1)}, u32[]{:S(2)}, u32[]{:S(2)}) collective-permute-start(bf16[112,256]{1,0:T(8,128)(2,1)S(1)} %get-tuple-element.33), channel_id=1, source_target_pairs={{0,1},{1,0},{2,3},{3,2},{4,5},{5,4},{6,7},{7,6},{8,9},{9,8},{10,11... | collective-permute-start | bytes 172040 | tf_op jit(solution)/shard_map/ppermute | solution.py:338
  21.1 5.0 %collective-permute-start.3 = (bf16[112,256]{1,0:T(8,128)(2,1)S(1)}, bf16[112,256]{1,0:T(8,128)(2,1)S(1)}, u32[]{:S(2)}, u32[]{:S(2)}) collective-permute-start(bf16[112,256]{1,0:T(8,128)(2,1)S(1)} %get-tuple-element.34), channel_id=1, source_target_pairs={{0,2},{1,3},{2,0},{3,1},{4,6},{5,7},{6,4},{7,5},{8,10},{9,11},{10,... | collective-permute-start | bytes 172040 | tf_op jit(solution)/shard_map/ppermute | solution.py:338
  23.1 4.3 %collective-permute-start.4 = (bf16[112,256]{1,0:T(8,128)(2,1)S(1)}, bf16[112,256]{1,0:T(8,128)(2,1)S(1)}, u32[]{:S(2)}, u32[]{:S(2)}) collective-permute-start(bf16[112,256]{1,0:T(8,128)(2,1)S(1)} %get-tuple-element.35), channel_id=1, source_target_pairs={{0,3},{1,2},{2,1},{3,0},{4,7},{5,6},{6,5},{7,4},{8,11},{9,10},{10,... | collective-permute-start | bytes 172040 | tf_op jit(solution)/shard_map/ppermute | solution.py:338
  27.7 25.7 %copy-start.5 = (bf16[1024,80]{0,1:T(8,128)(2,1)S(1)}, bf16[1024,80]{0,1:T(8,128)(2,1)}, u32[]{:S(2)}) copy-start(bf16[1024,80]{0,1:T(8,128)(2,1)} %param.10) | copy-start | bytes 491524
  29.1 24.4 %all-to-all-start.1 = ((bf16[8,224,256]{2,1,0:T(8,128)(2,1)}), bf16[8,224,256]{2,1,0:T(8,128)(2,1)S(1)}, u32[]{:S(2)}, u32[]{:S(2)}) async-start(bf16[8,224,256]{2,1,0:T(8,128)(2,1)} %shard_map.140), calls=%async_computation.1 | async-start | bytes 1835008 | tf_op jit(solution)/shard_map/all_to_all | solution.py:382
  32.6 12.3 %collective-permute-start.5 = (bf16[4,112,256]{2,1,0:T(8,128)(2,1)S(1)}, bf16[4,112,256]{2,1,0:T(8,128)(2,1)S(1)}, u32[]{:S(2)}, u32[]{:S(2)}) collective-permute-start(bf16[4,112,256]{2,1,0:T(8,128)(2,1)S(1)} %pad_maximum_fusion.p0), channel_id=1, source_target_pairs={{0,4},{1,5},{2,6},{3,7},{4,0},{5,1},{6,2},{7,3},{8,12},{9,13},{10,... | collective-permute-start | bytes 688136 | tf_op jit(solution)/shard_map/ppermute | solution.py:338
  34.2 19.2 %collective-permute-start.6 = (bf16[4,112,256]{2,1,0:T(8,128)(2,1)S(1)}, bf16[4,112,256]{2,1,0:T(8,128)(2,1)S(1)}, u32[]{:S(2)}, u32[]{:S(2)}) collective-permute-start(bf16[4,112,256]{2,1,0:T(8,128)(2,1)S(1)} %pad_maximum_fusion.p0), channel_id=1, source_target_pairs={{0,8},{1,9},{2,10},{3,11},{4,12},{5,13},{6,14},{7,15},{8,0},{9,1},... | collective-permute-start | bytes 688136 | tf_op jit(solution)/shard_map/ppermute | solution.py:338
  36.2 17.2 %collective-permute-start.7 = (bf16[4,112,256]{2,1,0:T(8,128)(2,1)S(1)}, bf16[4,112,256]{2,1,0:T(8,128)(2,1)S(1)}, u32[]{:S(2)}, u32[]{:S(2)}) collective-permute-start(bf16[4,112,256]{2,1,0:T(8,128)(2,1)S(1)} %pad_maximum_fusion.p0), channel_id=1, source_target_pairs={{0,12},{1,13},{2,14},{3,15},{4,8},{5,9},{6,10},{7,11},{8,4},{9,5},... | collective-permute-start | bytes 688136 | tf_op jit(solution)/shard_map/ppermute | solution.py:338
  57.2 28.4 %all-to-all-start.2 = ((bf16[8,224,256]{2,1,0:T(8,128)(2,1)}), bf16[8,224,256]{2,1,0:T(8,128)(2,1)S(1)}, u32[]{:S(2)}, u32[]{:S(2)}) async-start(bf16[8,224,256]{2,1,0:T(8,128)(2,1)} %get-tuple-element.49), calls=%async_computation.2 | async-start | bytes 1835008 | tf_op jit(solution)/shard_map/all_to_all | solution.py:393
  61.3 9.5 %collective-permute-start.10 = (bf16[4,96,256]{2,1,0:T(8,128)(2,1)S(1)}, bf16[4,96,256]{2,1,0:T(8,128)(2,1)S(1)}, u32[]{:S(2)}, u32[]{:S(2)}) collective-permute-start(bf16[4,96,256]{2,1,0:T(8,128)(2,1)S(1)} %get-tuple-element.40), channel_id=1, source_target_pairs={{0,12},{1,13},{2,14},{3,15},{4,8},{5,9},{6,10},{7,11},{8,4},{9,5},... | collective-permute-start | bytes 589832 | tf_op jit(solution)/shard_map/ppermute | solution.py:338
  63.6 11.0 %collective-permute-start.8 = (bf16[4,96,256]{2,1,0:T(8,128)(2,1)S(1)}, bf16[4,96,256]{2,1,0:T(8,128)(2,1)S(1)}, u32[]{:S(2)}, u32[]{:S(2)}) collective-permute-start(bf16[4,96,256]{2,1,0:T(8,128)(2,1)S(1)} %get-tuple-element.38), channel_id=1, source_target_pairs={{0,4},{1,5},{2,6},{3,7},{4,0},{5,1},{6,2},{7,3},{8,12},{9,13},{10,... | collective-permute-start | bytes 589832 | tf_op jit(solution)/shard_map/ppermute | solution.py:338
  67.1 15.9 %collective-permute-start.9 = (bf16[4,96,256]{2,1,0:T(8,128)(2,1)S(1)}, bf16[4,96,256]{2,1,0:T(8,128)(2,1)S(1)}, u32[]{:S(2)}, u32[]{:S(2)}) collective-permute-start(bf16[4,96,256]{2,1,0:T(8,128)(2,1)S(1)} %get-tuple-element.39), channel_id=1, source_target_pairs={{0,8},{1,9},{2,10},{3,11},{4,12},{5,13},{6,14},{7,15},{8,0},{9,1},... | collective-permute-start | bytes 589832 | tf_op jit(solution)/shard_map/ppermute | solution.py:338
  86.6 24.8 %copy-start.1 = (f32[40,8,1024]{2,1,0:T(8,128)S(1)}, f32[40,8,1024]{2,1,0:T(8,128)}, u32[]{:S(2)}) copy-start(f32[40,8,1024]{2,1,0:T(8,128)} %master.1) | copy-start | bytes 3932164
  86.6 24.8 %copy-start.2 = (f32[40,8,1024]{2,1,0:T(8,128)S(1)}, f32[40,8,1024]{2,1,0:T(8,128)}, u32[]{:S(2)}) copy-start(f32[40,8,1024]{2,1,0:T(8,128)} %param.14) | copy-start | bytes 3932164
  87.9 6.7 %copy-start.19 = (bf16[96,256]{1,0:T(8,128)(2,1)S(1)}, bf16[96,256]{1,0:T(8,128)(2,1)}, u32[]{:S(2)}) copy-start(bf16[96,256]{1,0:T(8,128)(2,1)} %copy-done.18) | copy-start | bytes 147460
  87.9 13.6 %copy-start.8 = (bf16[1024,32]{0,1:T(8,128)(2,1)S(1)}, bf16[1024,32]{0,1:T(8,128)(2,1)}, u32[]{:S(2)}) copy-start(bf16[1024,32]{0,1:T(8,128)(2,1)} %param.9) | copy-start | bytes 196612
  87.9 13.6 %copy-start.11 = (bf16[1024,32]{0,1:T(8,128)(2,1)S(1)}, bf16[1024,32]{0,1:T(8,128)(2,1)}, u32[]{:S(2)}) copy-start(bf16[1024,32]{0,1:T(8,128)(2,1)} %param.16) | copy-start | bytes 196612
  87.9 13.6 %copy-start.17 = (bf16[96,256]{1,0:T(8,128)(2,1)S(1)}, bf16[96,256]{1,0:T(8,128)(2,1)}, u32[]{:S(2)}) copy-start(bf16[96,256]{1,0:T(8,128)(2,1)} %copy-done.16) | copy-start | bytes 147460
  88.0 23.4 %all-to-all-start.3 = ((bf16[32,40,256]{2,1,0:T(8,128)(2,1)}), bf16[32,40,256]{2,1,0:T(8,128)(2,1)S(1)}, u32[]{:S(2)}, u32[]{:S(2)}) async-start(bf16[32,40,256]{2,1,0:T(8,128)(2,1)} %bitcast.14), calls=%async_computation.3 | async-start | bytes 1310720 | tf_op jit(solution)/shard_map/all_to_all | solution.py:398
  92.7 2.0 %collective-permute-start.11 = (bf16[96,256]{1,0:T(8,128)(2,1)}, bf16[96,256]{1,0:T(8,128)(2,1)S(1)}, u32[]{:S(2)}, u32[]{:S(2)}) collective-permute-start(bf16[96,256]{1,0:T(8,128)(2,1)} %copy-done.21), channel_id=1, source_target_pairs={{0,1},{1,0},{2,3},{3,2},{4,5},{5,4},{6,7},{7,6},{8,9},{9,8},{10,11... | collective-permute-start | bytes 147464 | tf_op jit(solution)/shard_map/ppermute | solution.py:338
  93.0 8.5 %collective-permute-start.12 = (bf16[96,256]{1,0:T(8,128)(2,1)}, bf16[96,256]{1,0:T(8,128)(2,1)S(1)}, u32[]{:S(2)}, u32[]{:S(2)}) collective-permute-start(bf16[96,256]{1,0:T(8,128)(2,1)} %copy-done.20), channel_id=1, source_target_pairs={{0,2},{1,3},{2,0},{3,1},{4,6},{5,7},{6,4},{7,5},{8,10},{9,11},{10,... | collective-permute-start | bytes 147464 | tf_op jit(solution)/shard_map/ppermute | solution.py:338
  94.7 6.9 %collective-permute-start.13 = (bf16[96,256]{1,0:T(8,128)(2,1)S(1)}, bf16[96,256]{1,0:T(8,128)(2,1)S(1)}, u32[]{:S(2)}, u32[]{:S(2)}) collective-permute-start(bf16[96,256]{1,0:T(8,128)(2,1)S(1)} %copy-done.19), channel_id=1, source_target_pairs={{0,3},{1,2},{2,1},{3,0},{4,7},{5,6},{6,5},{7,4},{8,11},{9,10},{10,... | collective-permute-start | bytes 147464 | tf_op jit(solution)/shard_map/ppermute | solution.py:338
  111.4 1.3 %copy-start.3 = (f32[40,8,1024]{2,1,0:T(8,128)S(1)}, f32[40,8,1024]{2,1,0:T(8,128)}, u32[]{:S(2)}) copy-start(f32[40,8,1024]{2,1,0:T(8,128)} %param.15) | copy-start | bytes 3932164
  (10 other events, 7.6 us)

commit v4 on v3

--- a/solution.py
+++ b/solution.py
@@ -53,17 +53,20 @@
     return jnp.where(cond, 1.0, 0.0).astype(BF16)
 
 
-def call(kernel, out, n_smem, n_in, flops=0, mbytes=1, scratch=(), out_space=pltpu.VMEM):
+MIB = 2**20
+VMEM, SMEM, HBM = pltpu.VMEM, pltpu.SMEM, pltpu.HBM
+
+
+def call(kernel, out, spaces, gflops=0, scratch=(), out_space=VMEM, room=40 * MIB):
     return pl.pallas_call(
         kernel,
         out_shape=out,
-        in_specs=[pl.BlockSpec(memory_space=pltpu.SMEM)] * n_smem
-        + [pl.BlockSpec(memory_space=pltpu.VMEM)] * n_in,
+        in_specs=[pl.BlockSpec(memory_space=space) for space in spaces],
         out_specs=jax.tree.map(lambda _: pl.BlockSpec(memory_space=out_space), out),
         scratch_shapes=list(scratch),
-        compiler_params=pltpu.CompilerParams(vmem_limit_bytes=24 * 2**20),
+        compiler_params=pltpu.CompilerParams(vmem_limit_bytes=64 * MIB - room),
         cost_estimate=pl.CostEstimate(
-            flops=flops, bytes_accessed=int(mbytes * 2**20), transcendentals=0
+            flops=gflops * 10**9, bytes_accessed=MIB, transcendentals=0
         ),
     )
 
@@ -73,10 +76,27 @@
     return onehot(natural == 2 * (split & 127) + (split >> 7))
 
 
-def pack_weights(ids, master, out):
-    half = ids[0]
+def begin(spk, master, sig, res, skp, mel, sent, edges, strips, sems):
+    half = lax.axis_index("tm")
     slots = master.shape[0]
     rows = 4 * slots
+    cut = pl.ds(pl.multiple_of((1 - half) * 896, 128), 128)
+    tiles = []
+    for n, part in enumerate((sig, res, skp, mel)):
+        to = edges.at[32 * n : 32 * n + part.shape[0], :]
+        tiles.append(pltpu.make_async_copy(part.at[:, cut], to, sems.at[4 + n]))
+    copies = []
+    for z in range(4):
+        part = master.at[:, :, 256 * z : 256 * z + 256]
+        copies.append(pltpu.make_async_copy(part, strips.at[z], sems.at[z]))
+    for copy in copies + tiles:
+        copy.start()
+    row, lane = iota((16, 128), 0), iota((16, 128), 1)
+    table = jnp.zeros((16, 128), jnp.int32)
+    for s in range(8):
+        code = jnp.where(row == 0, spk[s] >> 3, spk[s] & 7)
+        table = jnp.where((lane == s) & (row < 2), code, table)
+    edges[176:192, :] = table.astype(F32).astype(BF16)
     here = iota((rows, 8 * slots), 0)
     there = iota((rows, 8 * slots), 1)
     row, slot = jnp.zeros_like(here), here
@@ -85,22 +105,17 @@
         row = jnp.where(past, step, row)
         slot = jnp.where(past, here - step * slots, slot)
     pick = onehot(there == 8 * slot + 4 * half + row)
-    flat = master[...].reshape(8 * slots, GATES).astype(BF16)
-    got = dot(pick, flat)
     for z in range(4):
+        copies[z].wait()
+        got = dot(pick, strips[z].reshape(8 * slots, 256).astype(BF16))
         for j in range(4):
-            out[4 * z + j] = got[j * slots : (j + 1) * slots, 256 * z : 256 * (z + 1)].astype(BF16)
-
-
-def edge_tiles(ids, sig, res, skp, mel, out):
-    cut = pl.ds(pl.multiple_of((1 - ids[0]) * 896, 128), 128)
-    for n, part in enumerate((sig, res, skp)):
-        out[32 * n : 32 * n + 32, :] = part[:, cut]
-    out[96:176, :] = mel[:, cut]
-
-
-def pack_tokens(ids, sig, res, skp, other, o0, o1, o2, o3):
-    half, j = ids[0], ids[1] & 3
+            sent[4 * z + j] = got[j * slots : (j + 1) * slots].astype(BF16)
+    for tile in tiles:
+        tile.wait()
+
+
+def pack_tokens(sig, res, skp, other, o0, o1, o2, o3):
+    half, j = lax.axis_index("tm"), lax.axis_index("chan") & 3
     outs = (o0, o1, o2, o3)
     parts = (sig, res, skp)
     befores, nexts = [], ([], [], [])
@@ -133,7 +148,8 @@
             ).astype(BF16)
 
 
-def place_blocks(sid, owners, pick, put, *, slots_dev):
+def place_blocks(spk_ids, owners, other, at_col, at_row, *, slots_dev):
+    half = lax.axis_index("tm")
     own_row = owners[...]
     down, across = iota((NBLK, NBLK), 0), iota((NBLK, NBLK), 1)
     row_all = jnp.broadcast_to(own_row, (NBLK, NBLK))
@@ -141,10 +157,13 @@
     before = (own_col == row_all) & (down < across)
     rank = jnp.sum(jnp.where(before, 1, 0), axis=0, keepdims=True)
     place = own_row * slots_dev + rank
+    n = iota((PACKED, 128), 0)
+    far = n - SEG_AT - 8 * (1 - half) == iota((PACKED, 128), 1)
+    blocks = jnp.broadcast_to(other[176:192, :].astype(F32)[0:1], (PACKED, 128))
+    spk = jnp.sum(jnp.where(far, blocks, 0.0), axis=1, keepdims=True).astype(jnp.int32)
     n = iota((PACKED, 1), 0)
-    spk = jnp.zeros((PACKED, 1), jnp.int32)
-    for s in range(16):
-        spk = jnp.where(n == SEG_AT + s, sid[2 + s] >> 3, spk)
+    for s in range(8):
+        spk = jnp.where(n == SEG_AT + 8 * half + s, spk_ids[s] >> 3, spk)
     blk = jnp.where(
         n < SPK_BLOCK,
         n,
@@ -153,47 +172,56 @@
     match = jnp.broadcast_to(blk, (PACKED, NBLK)) == iota((PACKED, NBLK), 1)
     at = jnp.sum(jnp.where(match, jnp.broadcast_to(place, (PACKED, NBLK)), 0), axis=1, keepdims=True)
     at = jnp.where(blk < 0, -1, at)
-    slots = pick.shape[1]
-    pick[...] = onehot(jnp.broadcast_to(at, (PACKED, slots)) == iota((PACKED, slots), 1))
+    at_col[...] = jnp.broadcast_to(at, (PACKED, 128))
     same = iota((PACKED, PACKED), 0) == iota((PACKED, PACKED), 1)
-    at_row = jnp.sum(jnp.where(same, jnp.broadcast_to(at, (PACKED, PACKED)), 0), axis=0, keepdims=True)
-    put[...] = onehot(jnp.broadcast_to(at_row, (slots, PACKED)) == iota((slots, PACKED), 0))
-
-
-def gather_blocks(pick, slots, out):
-    got = dot(pick[...], slots[...]).astype(BF16)
+    row = jnp.sum(jnp.where(same, jnp.broadcast_to(at, (PACKED, PACKED)), 0), axis=0, keepdims=True)
+    at_row[...] = jnp.broadcast_to(row, (8, PACKED))
+
+
+def gather_blocks(at_col, slots, out):
+    shape = (PACKED, slots.shape[0])
+    pick = onehot(jnp.broadcast_to(at_col[:, 0:1], shape) == iota(shape, 1))
+    got = dot(pick, slots[...]).astype(BF16)
     got = dot(got, gate_order(0)).astype(BF16)
     for n in range(8):
         out[n] = got
 
 
-def scatter_blocks(put, parts, out):
+def scatter_blocks(at_row, parts, out):
     total = parts[0].astype(F32)
     for n in range(1, 8):
         total = total + parts[n].astype(F32)
     natural = dot(total.astype(BF16), gate_order(1)).astype(BF16)
-    spread = dot(put[...], natural).astype(BF16)
+    shape = (out.shape[1], PACKED)
+    put = onehot(jnp.broadcast_to(at_row[0:1, :], shape) == iota(shape, 0))
+    spread = dot(put, natural).astype(BF16)
     out[0] = spread
     out[1] = spread
 
 
+def sum_units(z0, z1, z2, z3, o0, o1, o2, o3):
+    for i, out in enumerate((o0, o1, o2, o3)):
+        out[...] = (
+            z0[i].astype(F32) + z1[i].astype(F32) + z2[i].astype(F32) + z3[i].astype(F32)
+        ).astype(BF16)
+
+
 def channel_of(pos, ch):
     return ((pos >> 5) ^ ch) * 32 + (pos & 31)
 
 
-def layer(ids, packed, p0, p1, p2, p3, mel, other, grads, z0, z1, z2, z3, feat):
-    half, ch = ids[0], ids[1]
+def to_major(ch, dim):
+    shape = (RESID, RESID)
+    major = iota(shape, dim)
+    return onehot(channel_of(iota(shape, 1 - dim), ch) == 8 * (major & 63) + (major >> 6))
+
+
+def prepare(spk, p0, p1, p2, p3, mel, other, features, res, skp):
+    half, ch = lax.axis_index("tm"), lax.axis_index("chan")
     j = ch & 3
     got = (p0, p1, p2, p3)
-    sq = (RESID, RESID)
     tokens, wide = 256, 384
-
-    def order(dim):
-        major = iota(sq, dim)
-        return onehot(channel_of(iota(sq, 1 - dim), ch) == 8 * (major & 63) + (major >> 6))
-
-    to_major = order(0)
-    to_place = order(1)
+    order = to_major(ch, 0)
 
     def stacked(n):
         return jnp.concatenate(
@@ -211,10 +239,10 @@
     ends = jnp.concatenate(
         [ends[0][8:16], gap[:112], ends[0][0:8], ends[1][0:8], gap, ends[1][8:16], gap], 0
     ).astype(BF16)
-    ends = dot(to_major, ends, NT)
-    sig = jnp.concatenate([dot(to_major, stacked(0)), ends[:, 0:128]], 1)
-    res = jnp.concatenate([dot(to_major, stacked(1)), ends[:, 128:256]], 1).astype(BF16)
-    skp = jnp.concatenate([dot(to_major, stacked(2)), ends[:, 256:384]], 1).astype(BF16)
+    ends = dot(order, ends, NT)
+    sig = jnp.concatenate([dot(order, stacked(0)), ends[:, 0:128]], 1)
+    res[...] = jnp.concatenate([dot(order, stacked(1)), ends[:, 128:256]], 1).astype(BF16)
+    skp[...] = jnp.concatenate([dot(order, stacked(2)), ends[:, 256:384]], 1).astype(BF16)
     shifted = pltpu.roll(sig, DILATION, 1).astype(BF16)
     sig = sig.astype(BF16)
     m = iota((128, MELS), 0)
@@ -225,16 +253,23 @@
     mels = jnp.concatenate([dot(mel_pick, mel[:, cut]), dot(mel_pick, ahead)], 1).astype(BF16)
     seg = 8 * half + 2 * j
     row, lane = iota((16, wide), 0), iota((16, wide), 1)
+    beyond = other[176:192, :].astype(F32)[1:2, 0:1].astype(jnp.int32)
+    beyond = jnp.where(j == 3, beyond, spk[jnp.minimum(2 * j + 2, 7)] & 7)
     sub = jnp.where(
         lane < SEG,
-        ids[2 + seg] & 7,
-        jnp.where(lane < 2 * SEG, ids[3 + seg] & 7, ids[2 + jnp.minimum(seg + 2, 15)] & 7),
+        spk[2 * j] & 7,
+        jnp.where(lane < 2 * SEG, spk[2 * j + 1] & 7, jnp.broadcast_to(beyond, (16, wide))),
     )
     for r in range(8):
-        feat[r, 0:64] = shifted[64 * r : 64 * r + 64]
-        feat[r, 64:128] = sig[64 * r : 64 * r + 64]
-        feat[r, 128:144] = mels[16 * r : 16 * r + 16]
-        feat[r, 144:160] = onehot((row == seg + (lane >> 7)) & (sub == r))
+        features[r, 0:64] = shifted[64 * r : 64 * r + 64]
+        features[r, 64:128] = sig[64 * r : 64 * r + 64]
+        features[r, 128:144] = mels[16 * r : 16 * r + 16]
+        features[r, 144:160] = onehot((row == seg + (lane >> 7)) & (sub == r))
+
+
+def layer(packed, feat, res, skp, grads, z0, z1, z2, z3):
+    tokens, wide = 256, 384
+    to_place = to_major(lax.axis_index("chan"), 1)
     features = feat[...].reshape(8 * OUT_AT, wide)
     conv = packed[:, 0:OUT_AT, :].reshape(8 * OUT_AT, 256)
     pre = dot(conv, features, TN)
@@ -245,7 +280,7 @@
     out_skp = packed[:, OUT_AT:PACKED, 128:256].reshape(RESID, 128)
     res_part = dot(out_res, hidden).astype(BF16)
     skp_part = dot(out_skp, hidden).astype(BF16)
-    grad_hidden = dot(out_res, res, TN) + dot(out_skp, skp, TN)
+    grad_hidden = dot(out_res, res[...], TN) + dot(out_skp, skp[...], TN)
     grad_pre = jnp.concatenate(
         [
             grad_hidden * gate * (1.0 - filt * filt),
@@ -272,15 +307,8 @@
                 out[i, 32 * n : 32 * n + 32] = parts[n][at : at + 32]
 
 
-def sum_units(z0, z1, z2, z3, o0, o1, o2, o3):
-    for i, out in enumerate((o0, o1, o2, o3)):
-        out[...] = (
-            z0[i].astype(F32) + z1[i].astype(F32) + z2[i].astype(F32) + z3[i].astype(F32)
-        ).astype(BF16)
-
-
-def finish_tokens(ids, o0, o1, o2, o3, sig, res, residual, skipped, grad_in):
-    j = ids[1] & 3
+def finish_tokens(o0, o1, o2, o3, sig, res, residual, skipped, grad_in):
+    j = lax.axis_index("chan") & 3
     for k, piece in enumerate((o0, o1, o2, o3)):
         cut = pl.ds(pl.multiple_of((j ^ k) * 256, 256), 256)
         residual[:, cut] = sig[:, cut].astype(F32) + piece[0:32, :].astype(F32)
@@ -288,41 +316,51 @@
         grad_in[:, cut] = res[:, cut].astype(F32) + piece[64:96, :].astype(F32)
 
 
-def update(ids, owners, grads, master, first, second, *refs):
-    outs, held, sems = refs[:3], refs[3:6], refs[6]
+def update(owners, grads, master, first, second, *refs):
+    outs, held, old, grad, sems = refs[:3], refs[3:6], refs[6:9], refs[9], refs[10]
     slots = grads.shape[1]
     rows = 8 * slots
-    owned = jnp.sum(jnp.where(owners[...] == ids[1], 1, 0))
-    keep = iota((rows, 1), 0) < 8 * owned
+    parts = [slice(n * rows // 4, (n + 1) * rows // 4) for n in range(4)]
+    fetches = []
+    for n, part in enumerate(parts):
+        for m, source in enumerate((first, second, master)):
+            fetch = pltpu.make_async_copy(
+                source.at[part, :], old[m].at[part, :], sems.at[12 + 3 * n + m]
+            )
+            fetch.start()
+            fetches.append(fetch)
+    owned = jnp.sum(jnp.where(owners[...] == lax.axis_index("chan"), 1, 0))
     to, of = iota((rows, rows), 0), iota((rows, rows), 1)
     spread = jnp.zeros((rows, rows), jnp.bool_)
     for r in range(8):
         inside = (of >= r * slots) & (of < (r + 1) * slots)
         spread = spread | (inside & (to == 8 * (of - r * slots) + r))
     spread = onehot(spread)
-    copies = []
     for z in range(4):
-        cut = slice(256 * z, 256 * z + 256)
-        grad = jnp.concatenate(
+        got = jnp.concatenate(
             [grads[16 * (r // 4) + 4 * z + r % 4].astype(F32) for r in range(8)], 0
         )
-        grad = dot(spread, grad.astype(BF16))
-        old_m = master[:, cut]
-        old_f = first[:, cut]
-        old_s = second[:, cut]
-        first_new = MOMENT_DECAY * old_f + (1.0 - MOMENT_DECAY) * grad
-        second_new = MOMENT_DECAY * old_s + (1.0 - MOMENT_DECAY) * grad * grad
+        grad[:, 256 * z : 256 * z + 256] = dot(spread, got.astype(BF16))
+    copies = []
+    for n, part in enumerate(parts):
+        for m in range(3):
+            fetches[3 * n + m].wait()
+        old_f, old_s, old_m = (ref[part, :] for ref in old)
+        new = grad[part, :]
+        keep = n * (rows // 4) + iota((rows // 4, 1), 0) < 8 * owned
+        first_new = MOMENT_DECAY * old_f + (1.0 - MOMENT_DECAY) * new
+        second_new = MOMENT_DECAY * old_s + (1.0 - MOMENT_DECAY) * new * new
         first_hat = first_new / (1.0 - MOMENT_DECAY**STEP)
         second_hat = second_new / (1.0 - MOMENT_DECAY**STEP)
         stepped = old_m - STEP_RATE * (
             first_hat / (jnp.sqrt(second_hat) + EPSILON) + WEIGHT_DECAY * old_m
         )
-        held[0][:, cut] = jnp.where(keep, first_new, old_f)
-        held[1][:, cut] = jnp.where(keep, second_new, old_s)
-        held[2][:, cut] = jnp.where(keep, stepped, old_m)
-        for n in range(3):
+        held[0][part, :] = jnp.where(keep, first_new, old_f)
+        held[1][part, :] = jnp.where(keep, second_new, old_s)
+        held[2][part, :] = jnp.where(keep, stepped, old_m)
+        for m in range(3):
             copy = pltpu.make_async_copy(
-                held[n].at[:, cut], outs[n].at[:, cut], sems.at[3 * z + n]
+                held[m].at[part, :], outs[m].at[part, :], sems.at[3 * n + m]
             )
             copy.start()
             copies.append(copy)
@@ -343,72 +381,68 @@
 ):
     slots_dev = master.shape[0]
     slots = 16 * slots_dev
-    half = lax.axis_index("tm")
-    ids = jnp.stack([half, lax.axis_index("chan")]).astype(jnp.int32)
     sig, res, skp, mel = signal.T, res_cot.T, skip_cot.T, mel_frames.T
     own_row = owners.reshape(1, NBLK)
     share = [[16 * y + 4 * z + j for y in range(2) for j in range(4)] for z in range(4)]
     sds = jax.ShapeDtypeStruct
-    turn = [(0, 1), (1, 0)]
-
-    edges = call(edge_tiles, sds((176, 128), BF16), 1, 4)(ids, sig, res, skp, mel)
-    other = lax.ppermute(edges, "tm", turn)
-    other_ids = lax.ppermute(speaker_ids, "tm", turn)
-    sids = jnp.where(
-        half == 0,
-        jnp.concatenate([speaker_ids, other_ids]),
-        jnp.concatenate([other_ids, speaker_ids]),
-    )
-    info = jnp.concatenate([ids, sids])
-
-    sent = call(pack_weights, sds((16, slots_dev, 256), BF16), 1, 1)(ids, master)
+    dma = pltpu.SemaphoreType.DMA
+
+    sent, edges = call(
+        begin,
+        (sds((16, slots_dev, 256), BF16), sds((192, 128), BF16)),
+        (SMEM,) + (HBM,) * 5,
+        scratch=(pltpu.VMEM((4, slots_dev, 8, 256), F32), dma((8,))),
+        room=MIB // 16,
+    )(speaker_ids, master, sig, res, skp, mel)
+    arrived = lax.all_to_all(sent, "chan", 0, 0, tiled=True)
+    other = lax.ppermute(edges, "tm", [(0, 1), (1, 0)])
     piece = sds((PIECE, 256), BF16)
-    o = call(pack_tokens, (piece,) * 4, 1, 4)(ids, sig, res, skp, other)
-    sent, _ = lax.optimization_barrier((sent, other))
-    arrived = lax.all_to_all(sent, "chan", 0, 0, tiled=True)
+    o = call(pack_tokens, (piece,) * 4, (VMEM,) * 4)(sig, res, skp, other)
     mine = jnp.stack([o[0], swap(o[1], 1), swap(o[2], 2), swap(o[3], 3)])
     p1, p2, p3 = (swap(mine, 4 * k) for k in (1, 2, 3))
 
-    pick, put = call(
+    at_col, at_row = call(
         functools.partial(place_blocks, slots_dev=slots_dev),
-        (sds((PACKED, slots), BF16), sds((slots, PACKED), BF16)),
-        1,
-        1,
-    )(info, own_row)
+        (sds((PACKED, 128), jnp.int32), sds((8, PACKED), jnp.int32)),
+        (SMEM, VMEM, VMEM),
+    )(speaker_ids, own_row, other)
     arrived, _ = lax.optimization_barrier((arrived, mine))
-    gathered = call(gather_blocks, sds((8, PACKED, 256), BF16), 0, 2)(
-        pick, arrived.reshape(slots, 256)
+    gathered = call(gather_blocks, sds((8, PACKED, 256), BF16), (VMEM, VMEM))(
+        at_col, arrived.reshape(slots, 256)
     )
     packed = lax.all_to_all(gathered, BOTH, 0, 0, axis_index_groups=share)
+    cots = sds((RESID, 384), BF16)
+    ready = call(
+        prepare,
+        (sds((8, OUT_AT, 384), BF16), cots, cots),
+        (SMEM,) + (VMEM,) * 6,
+        gflops=200,
+    )(speaker_ids, mine, p1, p2, p3, mel, other)
 
     quad = sds((4, 96, 256), BF16)
     grads, z0, z1, z2, z3 = call(
-        layer,
-        (sds((8, PACKED, 256), BF16), quad, quad, quad, quad),
-        1,
-        7,
-        scratch=(pltpu.VMEM((8, OUT_AT, 384), BF16),),
-    )(info, packed, mine, p1, p2, p3, mel, other)
+        layer, (sds((8, PACKED, 256), BF16), quad, quad, quad, quad), (VMEM,) * 4
+    )(packed, *ready)
 
     parts = lax.all_to_all(grads, BOTH, 0, 0, axis_index_groups=share)
     t1, t2, t3 = (swap(z, 4 * k) for k, z in ((1, z1), (2, z2), (3, z3)))
-    o = call(sum_units, (sds((96, 256), BF16),) * 4, 0, 4)(z0, t1, t2, t3)
-    parts, _ = lax.optimization_barrier((parts, o[0]))
-    spread = call(scatter_blocks, sds((2, slots, 256), BF16), 0, 2)(put, parts)
+    spread = call(scatter_blocks, sds((2, slots, 256), BF16), (VMEM, VMEM))(
+        at_row, parts
+    )
     returned = lax.all_to_all(spread.reshape(32, slots_dev, 256), BOTH, 0, 0)
+    o = call(sum_units, (sds((96, 256), BF16),) * 4, (VMEM,) * 4, gflops=20)(z0, t1, t2, t3)
     o = (o[0], swap(o[1], 1), swap(o[2], 2), swap(o[3], 3))
     narrow = sds(sig.shape, F32)
-    residual, skipped, grad_in = call(finish_tokens, (narrow,) * 3, 1, 6)(ids, *o, sig, res)
+    residual, skipped, grad_in = call(finish_tokens, (narrow,) * 3, (VMEM,) * 6)(*o, sig, res)
     flat = (8 * slots_dev, GATES)
     new = call(
         update,
         (sds(flat, F32),) * 3,
-        1,
-        5,
-        scratch=(pltpu.VMEM(flat, F32),) * 3 + (pltpu.SemaphoreType.DMA((12,)),),
-        out_space=pl.ANY,
+        (VMEM, VMEM, HBM, HBM, HBM),
+        scratch=(pltpu.VMEM(flat, F32),) * 7 + (dma((24,)),),
+        out_space=HBM,
+        room=6 * MIB // 5,
     )(
-        ids,
         own_row,
         returned,
         master.reshape(flat),

time: 117 us -> 102 us (0.87)
  waiting for transfers between devices: 52.7 us -> 44.6 us
  local copies, waits for them, and re-layouts: 10.3 us -> 3.99 us
  starting transfers between devices: 36.9 us -> 33.1 us
  Pallas kernels: 15.6 us -> 18.3 us
    ppermute x12, waiting for transfers between devices: 41.5 us -> 22.4 us  [swap(): return lax.ppermute(x, 'chan', [(i, i ^ k) for i in range(n)])]
    all_to_all x1, waiting for transfers between devices: 0.01 us -> 9.48 us  [local(): parts = lax.all_to_all(grads, BOTH, 0, 0, axis_index_groups=share)]
    unnamed x48 -> x20, local copies, waits for them, and re-layouts: 10.3 us -> 3.99 us
    pallas_call x9, Pallas kernels: 14.6 us -> 17.4 us  [the longest x1 4.87 us: local(): call(update, (sds(flat, F32),) * 3, (VMEM, VMEM, HBM, HBM, HBM), scratch=...]
    ppermute x2 -> x1, starting transfers between devices: 4.22 us -> 1.58 us  [local(): other = lax.ppermute(edges, 'tm', [(0, 1), (1, 0)])]
    ppermute x12, starting transfers between devices: 14.4 us -> 12.9 us  [swap(): return lax.ppermute(x, 'chan', [(i, i ^ k) for i in range(n)])]
    all_to_all x1, starting transfers between devices: 5.91 us -> 7.37 us  [local(): arrived = lax.all_to_all(sent, 'chan', 0, 0, tiled=True)]
    all_to_all x1, starting transfers between devices: 4.71 us -> 3.45 us  [local(): returned = lax.all_to_all(spread.reshape(32, slots_dev, 256), BOTH, 0, 0)]
  transfers between devices with their start and end apart: 18 -> 17, of which waited for: 12 -> 9; matrix products, arithmetic and copies ran while one was open for 0% -> 0% of each run, Pallas kernels for 4% -> 6%
where the time goes in v4:
time: 102 us; the launch traced here: 101 us
  waiting for transfers between devices  44.6 us (44%)
  starting transfers between devices  33.1 us (32%)
  Pallas kernels  18.3 us (18%)
  local copies, waits for them, and re-layouts  3.99 us (4%)
    ppermute x12, waiting for transfers between devices, swap(): return lax.ppermute(x, 'chan', [(i, i ^ k) for i in range(n)])  22.4 us
    ppermute x12, starting transfers between devices, swap(): return lax.ppermute(x, 'chan', [(i, i ^ k) for i in range(n)])  12.9 us
    all_to_all x1, waiting for transfers between devices, local(): parts = lax.all_to_all(grads, BOTH, 0, 0, axis_index_groups=share)  9.48 us
    all_to_all x1, waiting for transfers between devices, local(): returned = lax.all_to_all(spread.reshape(32, slots_dev, 256), BOTH, 0, 0)  9.06 us
    all_to_all x1, starting transfers between devices, local(): arrived = lax.all_to_all(sent, 'chan', 0, 0, tiled=True)  7.37 us
    pallas_call x1, Pallas kernels, local(): call(update, (sds(flat, F32),) * 3, (VMEM, VMEM, HBM, HBM, HBM), scratch=...  4.87 us
    all_to_all x1, starting transfers between devices, local(): packed = lax.all_to_all(gathered, BOTH, 0, 0, axis_index_groups=share)  4.23 us
    unnamed x20, local copies, waits for them, and re-layouts  3.99 us
  transfers between devices with their start and end apart: 17, of which 9 were waited for; matrix products, arithmetic and copies ran while one was open for 0% of the time, Pallas kernels for 6%

profile of v4, /device:TPU:0, one launch (start us, length us, event | category | flops | bytes accessed | tf_op | source)
XLA Modules:
  0.0 100.8 jit_solution(15649584337673099954)
XLA Ops:
  0.6 3.4 %shard_map.136 = (bf16[16,40,256]{2,1,0:T(8,128)(2,1)}, bf16[192,128]{1,0:T(8,128)(2,1)}) custom-call(s32[8]{0:T(128)} %spk.3, f32[40,8,1024]{2,1,0:T(8,128)} %master.1, bf16[32,1024]{1,0:T(8,128)(2,1)} %bitcast.20, bf16[32,1024]{1,0:T(8,128)(2,1)} %bitcast.23, bf16[32,1024]{1,0:T(8,128)(2,1)} %bitcast.26, bf16[80,1024]{1,0:T(8,128)(2,1)} %bitcast.28), custom_call_target="tpu_custom_call" | custom-call | bytes 1048576 | tf_op jit(solution)/shard_map/pallas_call | solution.py:390
  4.0 7.4 %all-to-all-start = ((bf16[16,40,256]{2,1,0:T(8,128)(2,1)}), bf16[16,40,256]{2,1,0:T(8,128)(2,1)S(1)}, u32[]{:S(2)}, u32[]{:S(2)}) async-start(bf16[16,40,256]{2,1,0:T(8,128)(2,1)} %get-tuple-element.35), calls=%async_computation | async-start | bytes 655360 | tf_op jit(solution)/shard_map/all_to_all | solution.py:397
  11.4 1.6 %collective-permute-start = (bf16[192,128]{1,0:T(8,128)(2,1)}, bf16[192,128]{1,0:T(8,128)(2,1)S(1)}, u32[]{:S(2)}, u32[]{:S(2)}) collective-permute-start(bf16[192,128]{1,0:T(8,128)(2,1)} %get-tuple-element.33), channel_id=1, source_target_pairs={{0,16},{16,0},{1,17},{17,1},{2,18},{18,2},{3,19},{19,3},{4,20},{20... | collective-permute-start | bytes 147464 | tf_op jit(solution)/shard_map/ppermute | solution.py:398
  13.0 2.8 %collective-permute-done.other = bf16[192,128]{1,0:T(8,128)(2,1)S(1)} collective-permute-done((bf16[192,128]{1,0:T(8,128)(2,1)}, bf16[192,128]{1,0:T(8,128)(2,1)S(1)}, u32[]{:S(2)}, u32[]{:S(2)}) %collective-permute-start) | collective-permute-done | bytes 49184 | tf_op jit(solution)/shard_map/ppermute | solution.py:398
  15.8 0.8 copy-done
  16.6 0.8 copy-done.2
  17.5 0.8 copy-done.4
  18.5 1.9 %collective-permute-start.2 = (bf16[112,256]{1,0:T(8,128)(2,1)S(1)}, bf16[112,256]{1,0:T(8,128)(2,1)S(1)}, u32[]{:S(2)}, u32[]{:S(2)}) collective-permute-start(bf16[112,256]{1,0:T(8,128)(2,1)S(1)} %get-tuple-element.38), channel_id=1, source_target_pairs={{0,2},{1,3},{2,0},{3,1},{4,6},{5,7},{6,4},{7,5},{8,10},{9,11},{10,... | collective-permute-start | bytes 172040 | tf_op jit(solution)/shard_map/ppermute | solution.py:376
  20.5 3.1 %collective-permute-done.2 = bf16[112,256]{1,0:T(8,128)(2,1)S(1)} collective-permute-done((bf16[112,256]{1,0:T(8,128)(2,1)S(1)}, bf16[112,256]{1,0:T(8,128)(2,1)S(1)}, u32[]{:S(2)}, u32[]{:S(2)}) %collective-permute-start.2) | collective-permute-done | bytes 57376 | tf_op jit(solution)/shard_map/ppermute | solution.py:376
  23.6 0.9 collective-permute-done.3
  24.6 3.1 %collective-permute-start.6 = (bf16[4,112,256]{2,1,0:T(8,128)(2,1)S(1)}, bf16[4,112,256]{2,1,0:T(8,128)(2,1)S(1)}, u32[]{:S(2)}, u32[]{:S(2)}) collective-permute-start(bf16[4,112,256]{2,1,0:T(8,128)(2,1)S(1)} %pad_maximum_fusion.p0), channel_id=1, source_target_pairs={{0,12},{1,13},{2,14},{3,15},{4,8},{5,9},{6,10},{7,11},{8,4},{9,5},... | collective-permute-start | bytes 688136 | tf_op jit(solution)/shard_map/ppermute | solution.py:376
  27.7 1.3 %collective-permute-start.4 = (bf16[4,112,256]{2,1,0:T(8,128)(2,1)S(1)}, bf16[4,112,256]{2,1,0:T(8,128)(2,1)S(1)}, u32[]{:S(2)}, u32[]{:S(2)}) collective-permute-start(bf16[4,112,256]{2,1,0:T(8,128)(2,1)S(1)} %pad_maximum_fusion.p0), channel_id=1, source_target_pairs={{0,4},{1,5},{2,6},{3,7},{4,0},{5,1},{6,2},{7,3},{8,12},{9,13},{10,... | collective-permute-start | bytes 688136 | tf_op jit(solution)/shard_map/ppermute | solution.py:376
  29.0 0.9 shard_map.137
  30.5 1.4 %shard_map.139 = bf16[8,224,256]{2,1,0:T(8,128)(2,1)} custom-call(s32[224,128]{1,0:T(8,128)S(1)} %get-tuple-element.34.at_col, bf16[640,256]{1,0:T(8,128)(2,1)S(1)} %bitcast.19), custom_call_target="tpu_custom_call" | custom-call | bytes 1048576 | tf_op jit(solution)/shard_map/pallas_call | solution.py:410
  31.9 4.2 %all-to-all-start.1 = ((bf16[8,224,256]{2,1,0:T(8,128)(2,1)}), bf16[8,224,256]{2,1,0:T(8,128)(2,1)}, u32[]{:S(2)}, u32[]{:S(2)}) async-start(bf16[8,224,256]{2,1,0:T(8,128)(2,1)} %shard_map.139), calls=%async_computation.1 | async-start | bytes 1835008 | tf_op jit(solution)/shard_map/all_to_all | solution.py:413
  36.1 11.7 %collective-permute-done.5.p2 = bf16[4,112,256]{2,1,0:T(8,128)(2,1)S(1)} collective-permute-done((bf16[4,112,256]{2,1,0:T(8,128)(2,1)S(1)}, bf16[4,112,256]{2,1,0:T(8,128)(2,1)S(1)}, u32[]{:S(2)}, u32[]{:S(2)}) %collective-permute-start.5) | collective-permute-done | bytes 229408 | tf_op jit(solution)/shard_map/ppermute | solution.py:376
  47.8 1.4 %shard_map.140 = (bf16[8,160,384]{2,1,0:T(8,128)(2,1)S(1)}, bf16[512,384]{1,0:T(8,128)(2,1)S(1)}, bf16[512,384]{1,0:T(8,128)(2,1)S(1)}) custom-call(s32[8]{0:T(128)S(1)} %copy-done.7, bf16[4,112,256]{2,1,0:T(8,128)(2,1)S(1)} %pad_maximum_fusion.p0, bf16[4,112,256]{2,1,0:T(8,128)(2,1)S(1)} %collective-permute-done.4.p1, ...), custom_call_target="tpu_custom_call" | custom-call | flops 199999995904 | bytes 1048576 | tf_op jit(solution)/shard_map/pallas_call | solution.py:415
  49.2 0.9 all-to-all-done.1.packed
  50.1 3.9 %shard_map.141 = (bf16[8,224,256]{2,1,0:T(8,128)(2,1)}, bf16[4,96,256]{2,1,0:T(8,128)(2,1)S(1)}, bf16[4,96,256]{2,1,0:T(8,128)(2,1)S(1)}, bf16[4,96,256]{2,1,0:T(8,128)(2,1)S(1)}, bf16[4,96,256]{2,1,0:T(8,128)(2,1)S(1)}) custom-call(bf16[8,224,256]{2,1,0:T(8,128)(2,1)} %all-to-all-done.1.packed, bf16[8,160,384]{2,1,0:T(8,128)(2,1)S(1)} %get-tuple-element.41.feat, ...), custom_call_target="tpu_custom_call" | custom-call | bytes 1048576 | tf_op jit(solution)/shard_map/pallas_call | solution.py:423
  54.1 3.6 %all-to-all-start.2 = ((bf16[8,224,256]{2,1,0:T(8,128)(2,1)}), bf16[8,224,256]{2,1,0:T(8,128)(2,1)S(1)}, u32[]{:S(2)}, u32[]{:S(2)}) async-start(bf16[8,224,256]{2,1,0:T(8,128)(2,1)} %get-tuple-element.56), calls=%async_computation.2 | async-start | bytes 1835008 | tf_op jit(solution)/shard_map/all_to_all | solution.py:427
  57.6 0.8 collective-permute-start.7
  58.4 2.9 %collective-permute-start.8 = (bf16[4,96,256]{2,1,0:T(8,128)(2,1)S(1)}, bf16[4,96,256]{2,1,0:T(8,128)(2,1)S(1)}, u32[]{:S(2)}, u32[]{:S(2)}) collective-permute-start(bf16[4,96,256]{2,1,0:T(8,128)(2,1)S(1)} %get-tuple-element.46), channel_id=1, source_target_pairs={{0,8},{1,9},{2,10},{3,11},{4,12},{5,13},{6,14},{7,15},{8,0},{9,1},... | collective-permute-start | bytes 589832 | tf_op jit(solution)/shard_map/ppermute | solution.py:376
  61.3 0.8 collective-permute-start.9
  62.1 9.5 %all-to-all-done.2.parts = bf16[8,224,256]{2,1,0:T(8,128)(2,1)S(1)} async-done(((bf16[8,224,256]{2,1,0:T(8,128)(2,1)}), bf16[8,224,256]{2,1,0:T(8,128)(2,1)S(1)}, u32[]{:S(2)}, u32[]{:S(2)}) %all-to-all-start.2) | async-done | bytes 917536 | tf_op jit(solution)/shard_map/all_to_all | solution.py:427
  71.6 1.4 %shard_map.144 = bf16[2,640,256]{2,1,0:T(8,128)(2,1)} custom-call(s32[8,224]{1,0:T(8,128)S(1)} %get-tuple-element.55.at_row, bf16[8,224,256]{2,1,0:T(8,128)(2,1)S(1)} %all-to-all-done.2.parts), custom_call_target="tpu_custom_call" | custom-call | bytes 1048576 | tf_op jit(solution)/shard_map/pallas_call | solution.py:429
  72.9 3.4 %all-to-all-start.3 = ((bf16[32,40,256]{2,1,0:T(8,128)(2,1)}), bf16[32,40,256]{2,1,0:T(8,128)(2,1)S(1)}, u32[]{:S(2)}, u32[]{:S(2)}) async-start(bf16[32,40,256]{2,1,0:T(8,128)(2,1)} %bitcast.12), calls=%async_computation.3 | async-start | bytes 1310720 | tf_op jit(solution)/shard_map/all_to_all | solution.py:432
  76.8 1.7 %collective-permute-start.11 = (bf16[96,256]{1,0:T(8,128)(2,1)S(1)}, bf16[96,256]{1,0:T(8,128)(2,1)S(1)}, u32[]{:S(2)}, u32[]{:S(2)}) collective-permute-start(bf16[96,256]{1,0:T(8,128)(2,1)S(1)} %get-tuple-element.50), channel_id=1, source_target_pairs={{0,2},{1,3},{2,0},{3,1},{4,6},{5,7},{6,4},{7,5},{8,10},{9,11},{10,... | collective-permute-start | bytes 147464 | tf_op jit(solution)/shard_map/ppermute | solution.py:376
  78.5 6.6 %collective-permute-done.11.o2 = bf16[96,256]{1,0:T(8,128)(2,1)S(1)} collective-permute-done((bf16[96,256]{1,0:T(8,128)(2,1)S(1)}, bf16[96,256]{1,0:T(8,128)(2,1)S(1)}, u32[]{:S(2)}, u32[]{:S(2)}) %collective-permute-start.11) | collective-permute-done | bytes 49184 | tf_op jit(solution)/shard_map/ppermute | solution.py:376
  85.2 0.8 shard_map.143
  86.0 9.1 %all-to-all-done.3.grads = bf16[32,40,256]{2,1,0:T(8,128)(2,1)S(1)} async-done(((bf16[32,40,256]{2,1,0:T(8,128)(2,1)}), bf16[32,40,256]{2,1,0:T(8,128)(2,1)S(1)}, u32[]{:S(2)}, u32[]{:S(2)}) %all-to-all-start.3) | async-done | bytes 655392 | tf_op jit(solution)/shard_map/all_to_all | solution.py:432
  95.1 0.9 copy-done.8
  95.9 4.9 %shard_map.145 = (f32[320,1024]{1,0:T(8,128)}, f32[320,1024]{1,0:T(8,128)}, f32[320,1024]{1,0:T(8,128)}) custom-call(s32[1,320]{1,0:T(1,128)} %copy-done.6, bf16[32,40,256]{2,1,0:T(8,128)(2,1)} %copy-done.8, f32[320,1024]{1,0:T(8,128)} %bitcast.31, f32[320,1024]{1,0:T(8,128)} %bitcast.32, f32[320,1024]{1,0:T(8,128)} %bitcast.33), custom_call_target="tpu_custom_call" | custom-call | bytes 1048576 | tf_op jit(solution)/shard_map/pallas_call | solution.py:438
  (34 shorter events, 1.5 us)
Async XLA Ops:
  4.0 25.0 %copy-start.9 = (s32[320]{0:T(512)S(1)}, s32[320]{0:T(512)}, u32[]{:S(2)}) copy-start(s32[320]{0:T(512)} %param.12) | copy-start | bytes 3844
  4.0 25.0 %copy-start.7 = (s32[8]{0:T(128)S(1)}, s32[8]{0:T(128)}, u32[]{:S(2)}) copy-start(s32[8]{0:T(128)} %spk.3) | copy-start | bytes 100
  4.0 26.5 %all-to-all-start = ((bf16[16,40,256]{2,1,0:T(8,128)(2,1)}), bf16[16,40,256]{2,1,0:T(8,128)(2,1)S(1)}, u32[]{:S(2)}, u32[]{:S(2)}) async-start(bf16[16,40,256]{2,1,0:T(8,128)(2,1)} %get-tuple-element.35), calls=%async_computation | async-start | bytes 655360 | tf_op jit(solution)/shard_map/all_to_all | solution.py:397
  11.4 4.4 %collective-permute-start = (bf16[192,128]{1,0:T(8,128)(2,1)}, bf16[192,128]{1,0:T(8,128)(2,1)S(1)}, u32[]{:S(2)}, u32[]{:S(2)}) collective-permute-start(bf16[192,128]{1,0:T(8,128)(2,1)} %get-tuple-element.33), channel_id=1, source_target_pairs={{0,16},{16,0},{1,17},{17,1},{2,18},{18,2},{3,19},{19,3},{4,20},{20... | collective-permute-start | bytes 147464 | tf_op jit(solution)/shard_map/ppermute | solution.py:398
  15.8 0.8 copy-start
  16.6 0.8 copy-start.2
  17.5 0.8 copy-start.4
  18.5 2.0 %collective-permute-start.1 = (bf16[112,256]{1,0:T(8,128)(2,1)S(1)}, bf16[112,256]{1,0:T(8,128)(2,1)S(1)}, u32[]{:S(2)}, u32[]{:S(2)}) collective-permute-start(bf16[112,256]{1,0:T(8,128)(2,1)S(1)} %get-tuple-element.37), channel_id=1, source_target_pairs={{0,1},{1,0},{2,3},{3,2},{4,5},{5,4},{6,7},{7,6},{8,9},{9,8},{10,11... | collective-permute-start | bytes 172040 | tf_op jit(solution)/shard_map/ppermute | solution.py:376
  18.5 5.1 %collective-permute-start.2 = (bf16[112,256]{1,0:T(8,128)(2,1)S(1)}, bf16[112,256]{1,0:T(8,128)(2,1)S(1)}, u32[]{:S(2)}, u32[]{:S(2)}) collective-permute-start(bf16[112,256]{1,0:T(8,128)(2,1)S(1)} %get-tuple-element.38), channel_id=1, source_target_pairs={{0,2},{1,3},{2,0},{3,1},{4,6},{5,7},{6,4},{7,5},{8,10},{9,11},{10,... | collective-permute-start | bytes 172040 | tf_op jit(solution)/shard_map/ppermute | solution.py:376
  20.5 4.1 %collective-permute-start.3 = (bf16[112,256]{1,0:T(8,128)(2,1)S(1)}, bf16[112,256]{1,0:T(8,128)(2,1)S(1)}, u32[]{:S(2)}, u32[]{:S(2)}) collective-permute-start(bf16[112,256]{1,0:T(8,128)(2,1)S(1)} %get-tuple-element.39), channel_id=1, source_target_pairs={{0,3},{1,2},{2,1},{3,0},{4,7},{5,6},{6,5},{7,4},{8,11},{9,10},{10,... | collective-permute-start | bytes 172040 | tf_op jit(solution)/shard_map/ppermute | solution.py:376
  24.6 11.5 %collective-permute-start.6 = (bf16[4,112,256]{2,1,0:T(8,128)(2,1)S(1)}, bf16[4,112,256]{2,1,0:T(8,128)(2,1)S(1)}, u32[]{:S(2)}, u32[]{:S(2)}) collective-permute-start(bf16[4,112,256]{2,1,0:T(8,128)(2,1)S(1)} %pad_maximum_fusion.p0), channel_id=1, source_target_pairs={{0,12},{1,13},{2,14},{3,15},{4,8},{5,9},{6,10},{7,11},{8,4},{9,5},... | collective-permute-start | bytes 688136 | tf_op jit(solution)/shard_map/ppermute | solution.py:376
  27.7 20.1 %collective-permute-start.5 = (bf16[4,112,256]{2,1,0:T(8,128)(2,1)S(1)}, bf16[4,112,256]{2,1,0:T(8,128)(2,1)S(1)}, u32[]{:S(2)}, u32[]{:S(2)}) collective-permute-start(bf16[4,112,256]{2,1,0:T(8,128)(2,1)S(1)} %pad_maximum_fusion.p0), channel_id=1, source_target_pairs={{0,8},{1,9},{2,10},{3,11},{4,12},{5,13},{6,14},{7,15},{8,0},{9,1},... | collective-permute-start | bytes 688136 | tf_op jit(solution)/shard_map/ppermute | solution.py:376
  27.7 20.1 %collective-permute-start.4 = (bf16[4,112,256]{2,1,0:T(8,128)(2,1)S(1)}, bf16[4,112,256]{2,1,0:T(8,128)(2,1)S(1)}, u32[]{:S(2)}, u32[]{:S(2)}) collective-permute-start(bf16[4,112,256]{2,1,0:T(8,128)(2,1)S(1)} %pad_maximum_fusion.p0), channel_id=1, source_target_pairs={{0,4},{1,5},{2,6},{3,7},{4,0},{5,1},{6,2},{7,3},{8,12},{9,13},{10,... | collective-permute-start | bytes 688136 | tf_op jit(solution)/shard_map/ppermute | solution.py:376
  29.9 0.6 copy-start.6
  30.5 17.3 %copy-start.5 = (bf16[1024,80]{0,1:T(8,128)(2,1)S(1)}, bf16[1024,80]{0,1:T(8,128)(2,1)}, u32[]{:S(2)}) copy-start(bf16[1024,80]{0,1:T(8,128)(2,1)} %param.10) | copy-start | bytes 491524
  31.9 18.2 %all-to-all-start.1 = ((bf16[8,224,256]{2,1,0:T(8,128)(2,1)}), bf16[8,224,256]{2,1,0:T(8,128)(2,1)}, u32[]{:S(2)}, u32[]{:S(2)}) async-start(bf16[8,224,256]{2,1,0:T(8,128)(2,1)} %shard_map.139), calls=%async_computation.1 | async-start | bytes 1835008 | tf_op jit(solution)/shard_map/all_to_all | solution.py:413
  54.1 17.5 %all-to-all-start.2 = ((bf16[8,224,256]{2,1,0:T(8,128)(2,1)}), bf16[8,224,256]{2,1,0:T(8,128)(2,1)S(1)}, u32[]{:S(2)}, u32[]{:S(2)}) async-start(bf16[8,224,256]{2,1,0:T(8,128)(2,1)} %get-tuple-element.56), calls=%async_computation.2 | async-start | bytes 1835008 | tf_op jit(solution)/shard_map/all_to_all | solution.py:427
  57.6 18.7 %collective-permute-start.7 = (bf16[4,96,256]{2,1,0:T(8,128)(2,1)S(1)}, bf16[4,96,256]{2,1,0:T(8,128)(2,1)S(1)}, u32[]{:S(2)}, u32[]{:S(2)}) collective-permute-start(bf16[4,96,256]{2,1,0:T(8,128)(2,1)S(1)} %get-tuple-element.45), channel_id=1, source_target_pairs={{0,4},{1,5},{2,6},{3,7},{4,0},{5,1},{6,2},{7,3},{8,12},{9,13},{10,... | collective-permute-start | bytes 589832 | tf_op jit(solution)/shard_map/ppermute | solution.py:376
  58.4 18.0 %collective-permute-start.8 = (bf16[4,96,256]{2,1,0:T(8,128)(2,1)S(1)}, bf16[4,96,256]{2,1,0:T(8,128)(2,1)S(1)}, u32[]{:S(2)}, u32[]{:S(2)}) collective-permute-start(bf16[4,96,256]{2,1,0:T(8,128)(2,1)S(1)} %get-tuple-element.46), channel_id=1, source_target_pairs={{0,8},{1,9},{2,10},{3,11},{4,12},{5,13},{6,14},{7,15},{8,0},{9,1},... | collective-permute-start | bytes 589832 | tf_op jit(solution)/shard_map/ppermute | solution.py:376
  61.3 15.1 %collective-permute-start.9 = (bf16[4,96,256]{2,1,0:T(8,128)(2,1)S(1)}, bf16[4,96,256]{2,1,0:T(8,128)(2,1)S(1)}, u32[]{:S(2)}, u32[]{:S(2)}) collective-permute-start(bf16[4,96,256]{2,1,0:T(8,128)(2,1)S(1)} %get-tuple-element.47), channel_id=1, source_target_pairs={{0,12},{1,13},{2,14},{3,15},{4,8},{5,9},{6,10},{7,11},{8,4},{9,5},... | collective-permute-start | bytes 589832 | tf_op jit(solution)/shard_map/ppermute | solution.py:376
  72.9 22.2 %all-to-all-start.3 = ((bf16[32,40,256]{2,1,0:T(8,128)(2,1)}), bf16[32,40,256]{2,1,0:T(8,128)(2,1)S(1)}, u32[]{:S(2)}, u32[]{:S(2)}) async-start(bf16[32,40,256]{2,1,0:T(8,128)(2,1)} %bitcast.12), calls=%async_computation.3 | async-start | bytes 1310720 | tf_op jit(solution)/shard_map/all_to_all | solution.py:432
  76.4 8.8 %copy-start.1 = (bf16[1024,32]{0,1:T(8,128)(2,1)S(1)}, bf16[1024,32]{0,1:T(8,128)(2,1)}, u32[]{:S(2)}) copy-start(bf16[1024,32]{0,1:T(8,128)(2,1)} %param.9) | copy-start | bytes 196612
  76.4 8.8 %copy-start.3 = (bf16[1024,32]{0,1:T(8,128)(2,1)S(1)}, bf16[1024,32]{0,1:T(8,128)(2,1)}, u32[]{:S(2)}) copy-start(bf16[1024,32]{0,1:T(8,128)(2,1)} %param.16) | copy-start | bytes 196612
  76.5 2.0 %collective-permute-start.10 = (bf16[96,256]{1,0:T(8,128)(2,1)S(1)}, bf16[96,256]{1,0:T(8,128)(2,1)S(1)}, u32[]{:S(2)}, u32[]{:S(2)}) collective-permute-start(bf16[96,256]{1,0:T(8,128)(2,1)S(1)} %get-tuple-element.49), channel_id=1, source_target_pairs={{0,1},{1,0},{2,3},{3,2},{4,5},{5,4},{6,7},{7,6},{8,9},{9,8},{10,11... | collective-permute-start | bytes 147464 | tf_op jit(solution)/shard_map/ppermute | solution.py:376
  76.8 8.3 %collective-permute-start.11 = (bf16[96,256]{1,0:T(8,128)(2,1)S(1)}, bf16[96,256]{1,0:T(8,128)(2,1)S(1)}, u32[]{:S(2)}, u32[]{:S(2)}) collective-permute-start(bf16[96,256]{1,0:T(8,128)(2,1)S(1)} %get-tuple-element.50), channel_id=1, source_target_pairs={{0,2},{1,3},{2,0},{3,1},{4,6},{5,7},{6,4},{7,5},{8,10},{9,11},{10,... | collective-permute-start | bytes 147464 | tf_op jit(solution)/shard_map/ppermute | solution.py:376
  78.5 6.7 %collective-permute-start.12 = (bf16[96,256]{1,0:T(8,128)(2,1)S(1)}, bf16[96,256]{1,0:T(8,128)(2,1)S(1)}, u32[]{:S(2)}, u32[]{:S(2)}) collective-permute-start(bf16[96,256]{1,0:T(8,128)(2,1)S(1)} %get-tuple-element.51), channel_id=1, source_target_pairs={{0,3},{1,2},{2,1},{3,0},{4,7},{5,6},{6,5},{7,4},{8,11},{9,10},{10,... | collective-permute-start | bytes 147464 | tf_op jit(solution)/shard_map/ppermute | solution.py:376
  95.1 0.9 copy-start.8

commit v5 on v4

--- a/solution.py
+++ b/solution.py
@@ -53,22 +53,24 @@
     return jnp.where(cond, 1.0, 0.0).astype(BF16)
 
 
-MIB = 2**20
+KIB, MIB = 2**10, 2**20
 VMEM, SMEM, HBM = pltpu.VMEM, pltpu.SMEM, pltpu.HBM
 
 
-def call(kernel, out, spaces, gflops=0, scratch=(), out_space=VMEM, room=40 * MIB):
-    return pl.pallas_call(
+def call(kernel, out, spaces, gflops=0, scratch=(), out_space=VMEM):
+    run = pl.pallas_call(
         kernel,
         out_shape=out,
         in_specs=[pl.BlockSpec(memory_space=space) for space in spaces],
         out_specs=jax.tree.map(lambda _: pl.BlockSpec(memory_space=out_space), out),
         scratch_shapes=list(scratch),
-        compiler_params=pltpu.CompilerParams(vmem_limit_bytes=64 * MIB - room),
+        compiler_params=pltpu.CompilerParams(vmem_limit_bytes=24 * MIB),
         cost_estimate=pl.CostEstimate(
             flops=gflops * 10**9, bytes_accessed=MIB, transcendentals=0
         ),
     )
+    pin = pltpu.with_memory_space_constraint
+    return lambda *args: run(*(pin(x, HBM) if space == HBM else x for x, space in zip(args, spaces, strict=True)))
 
 
 def gate_order(dim):
@@ -76,7 +78,7 @@
     return onehot(natural == 2 * (split & 127) + (split >> 7))
 
 
-def begin(spk, master, sig, res, skp, mel, sent, edges, strips, sems):
+def begin(speakers, master, sig, res, skp, mel, sent, edges, strips, spk, sems):
     half = lax.axis_index("tm")
     slots = master.shape[0]
     rows = 4 * slots
@@ -89,8 +91,10 @@
     for z in range(4):
         part = master.at[:, :, 256 * z : 256 * z + 256]
         copies.append(pltpu.make_async_copy(part, strips.at[z], sems.at[z]))
-    for copy in copies + tiles:
+    names = pltpu.make_async_copy(speakers, spk, sems.at[8])
+    for copy in (names, *copies, *tiles):
         copy.start()
+    names.wait()
     row, lane = iota((16, 128), 0), iota((16, 128), 1)
     table = jnp.zeros((16, 128), jnp.int32)
     for s in range(8):
@@ -114,7 +118,16 @@
         tile.wait()
 
 
-def pack_tokens(sig, res, skp, other, o0, o1, o2, o3):
+def pack_tokens(sig_hbm, res_hbm, skp_hbm, other, o0, o1, o2, o3, held, sems):
+    copies = [
+        pltpu.make_async_copy(part, held.at[n], sems.at[n])
+        for n, part in enumerate((sig_hbm, res_hbm, skp_hbm))
+    ]
+    for copy in copies:
+        copy.start()
+    for copy in copies:
+        copy.wait()
+    sig, res, skp = (held.at[n] for n in range(3))
     half, j = lax.axis_index("tm"), lax.axis_index("chan") & 3
     outs = (o0, o1, o2, o3)
     parts = (sig, res, skp)
@@ -148,9 +161,20 @@
             ).astype(BF16)
 
 
-def place_blocks(spk_ids, owners, other, at_col, at_row, *, slots_dev):
+def join(o0, o1, o2, o3, out):
+    ends = o0[96:112, :].astype(F32)
+    for piece in (o1, o2, o3):
+        ends = ends + piece[96:112, :].astype(F32)
+    for k, piece in enumerate((o0, o1, o2, o3)):
+        out[96 * k : 96 * k + 96, :] = piece[0:96, :]
+    out[384:400, :] = ends.astype(BF16)
+
+
+def place_blocks(spk_ids, owners, other, at_col, at_row, owned, *, slots_dev):
     half = lax.axis_index("tm")
     own_row = owners[...]
+    mine = jnp.where(own_row == lax.axis_index("chan"), 1, 0)
+    owned[...] = jnp.broadcast_to(jnp.sum(mine, axis=1, keepdims=True), owned.shape)
     down, across = iota((NBLK, NBLK), 0), iota((NBLK, NBLK), 1)
     row_all = jnp.broadcast_to(own_row, (NBLK, NBLK))
     own_col = jnp.sum(jnp.where(down == across, row_all, 0), axis=1, keepdims=True)
@@ -187,10 +211,16 @@
         out[n] = got
 
 
-def scatter_blocks(at_row, parts, out):
-    total = parts[0].astype(F32)
-    for n in range(1, 8):
-        total = total + parts[n].astype(F32)
+def sum_cores(kept, got, *outs):
+    i = 2 * lax.axis_index("tm") + ((lax.axis_index("chan") >> 1) & 1)
+    for k, out in enumerate(outs):
+        out[...] = (kept[i ^ k].astype(F32) + got[i ^ k].astype(F32)).astype(BF16)
+
+
+def scatter_blocks(at_row, p0, p1, p2, p3, out):
+    total = p0[...].astype(F32)
+    for part in (p1, p2, p3):
+        total = total + part[...].astype(F32)
     natural = dot(total.astype(BF16), gate_order(1)).astype(BF16)
     shape = (out.shape[1], PACKED)
     put = onehot(jnp.broadcast_to(at_row[0:1, :], shape) == iota(shape, 0))
@@ -225,15 +255,10 @@
 
     def stacked(n):
         return jnp.concatenate(
-            [got[k][i, 32 * n : 32 * n + 32, :] for k in range(4) for i in range(4)], 0
+            [got[k][96 * i + 32 * n : 96 * i + 32 * n + 32, :] for k in range(4) for i in range(4)], 0
         )
 
-    ends = []
-    for k in range(4):
-        end = got[k][0, 96:112, :].astype(F32)
-        for i in range(1, 4):
-            end = end + got[k][i, 96:112, :].astype(F32)
-        ends.append(end)
+    ends = [part[384:400, :].astype(F32) for part in got]
     ends = [jnp.concatenate([e[:, 128 * n : 128 * n + 128] for e in ends], 1) for n in range(2)]
     gap = jnp.zeros((120, RESID), F32)
     ends = jnp.concatenate(
@@ -267,7 +292,7 @@
         features[r, 144:160] = onehot((row == seg + (lane >> 7)) & (sub == r))
 
 
-def layer(packed, feat, res, skp, grads, z0, z1, z2, z3):
+def layer(packed, feat, res, skp, kept, given, z0, z1, z2, z3):
     tokens, wide = 256, 384
     to_place = to_major(lax.axis_index("chan"), 1)
     features = feat[...].reshape(8 * OUT_AT, wide)
@@ -296,9 +321,16 @@
     conv_grad = dot(features[:, :tokens], grad_pre, NT).astype(BF16)
     res_grad = dot(res[:, :tokens], hidden, NT).astype(BF16)
     skp_grad = dot(skp[:, :tokens], hidden, NT).astype(BF16)
-    grads[:, 0:OUT_AT, :] = conv_grad.reshape(8, OUT_AT, 256)
-    grads[:, OUT_AT:PACKED, 0:128] = res_grad.reshape(8, 64, 128)
-    grads[:, OUT_AT:PACKED, 128:256] = skp_grad.reshape(8, 64, 128)
+    core = lax.axis_index("chan") & 1
+    for part, rows, cols in (
+        (conv_grad.reshape(8, OUT_AT, 256), slice(0, OUT_AT), slice(0, 256)),
+        (res_grad.reshape(8, 64, 128), slice(OUT_AT, PACKED), slice(0, 128)),
+        (skp_grad.reshape(8, 64, 128), slice(OUT_AT, PACKED), slice(128, 256)),
+    ):
+        for i in range(4):
+            even, odd = part[2 * i], part[2 * i + 1]
+            kept[i, rows, cols] = jnp.where(core == 0, even, odd)
+            given[i, rows, cols] = jnp.where(core == 0, odd, even)
     parts = [dot(to_place, part).astype(BF16) for part in (res_part, skp_part, in_part)]
     for k, out in enumerate((z0, z1, z2, z3)):
         for i in range(4):
@@ -316,7 +348,7 @@
         grad_in[:, cut] = res[:, cut].astype(F32) + piece[64:96, :].astype(F32)
 
 
-def update(owners, grads, master, first, second, *refs):
+def update(owned, grads, master, first, second, *refs):
     outs, held, old, grad, sems = refs[:3], refs[3:6], refs[6:9], refs[9], refs[10]
     slots = grads.shape[1]
     rows = 8 * slots
@@ -329,7 +361,6 @@
             )
             fetch.start()
             fetches.append(fetch)
-    owned = jnp.sum(jnp.where(owners[...] == lax.axis_index("chan"), 1, 0))
     to, of = iota((rows, rows), 0), iota((rows, rows), 1)
     spread = jnp.zeros((rows, rows), jnp.bool_)
     for r in range(8):
@@ -347,7 +378,7 @@
             fetches[3 * n + m].wait()
         old_f, old_s, old_m = (ref[part, :] for ref in old)
         new = grad[part, :]
-        keep = n * (rows // 4) + iota((rows // 4, 1), 0) < 8 * owned
+        keep = n * (rows // 4) + iota((rows // 4, 1), 0) < 8 * owned[0:1, 0:1]
         first_new = MOMENT_DECAY * old_f + (1.0 - MOMENT_DECAY) * new
         second_new = MOMENT_DECAY * old_s + (1.0 - MOMENT_DECAY) * new * new
         first_hat = first_new / (1.0 - MOMENT_DECAY**STEP)
@@ -390,20 +421,35 @@
     sent, edges = call(
         begin,
         (sds((16, slots_dev, 256), BF16), sds((192, 128), BF16)),
-        (SMEM,) + (HBM,) * 5,
-        scratch=(pltpu.VMEM((4, slots_dev, 8, 256), F32), dma((8,))),
-        room=MIB // 16,
+        (HBM,) * 6,
+        scratch=(
+            pltpu.VMEM((4, slots_dev, 8, 256), F32),
+            pltpu.SMEM(speaker_ids.shape, jnp.int32),
+            dma((9,)),
+        ),
     )(speaker_ids, master, sig, res, skp, mel)
+    other = lax.ppermute(edges, "tm", [(0, 1), (1, 0)])
     arrived = lax.all_to_all(sent, "chan", 0, 0, tiled=True)
-    other = lax.ppermute(edges, "tm", [(0, 1), (1, 0)])
     piece = sds((PIECE, 256), BF16)
-    o = call(pack_tokens, (piece,) * 4, (VMEM,) * 4)(sig, res, skp, other)
-    mine = jnp.stack([o[0], swap(o[1], 1), swap(o[2], 2), swap(o[3], 3)])
+    o = call(
+        pack_tokens,
+        (piece,) * 4,
+        (HBM,) * 3 + (VMEM,),
+        gflops=200,
+        scratch=(pltpu.VMEM((3, *sig.shape), BF16), dma((3,))),
+    )(sig, res, skp, other)
+    mine = call(join, sds((400, 256), BF16), (VMEM,) * 4)(
+        o[0], swap(o[1], 1), swap(o[2], 2), swap(o[3], 3)
+    )
     p1, p2, p3 = (swap(mine, 4 * k) for k in (1, 2, 3))
 
-    at_col, at_row = call(
+    at_col, at_row, owned = call(
         functools.partial(place_blocks, slots_dev=slots_dev),
-        (sds((PACKED, 128), jnp.int32), sds((8, PACKED), jnp.int32)),
+        (
+            sds((PACKED, 128), jnp.int32),
+            sds((8, PACKED), jnp.int32),
+            sds((8, 128), jnp.int32),
+        ),
         (SMEM, VMEM, VMEM),
     )(speaker_ids, own_row, other)
     arrived, _ = lax.optimization_barrier((arrived, mine))
@@ -420,15 +466,17 @@
     )(speaker_ids, mine, p1, p2, p3, mel, other)
 
     quad = sds((4, 96, 256), BF16)
-    grads, z0, z1, z2, z3 = call(
-        layer, (sds((8, PACKED, 256), BF16), quad, quad, quad, quad), (VMEM,) * 4
-    )(packed, *ready)
-
-    parts = lax.all_to_all(grads, BOTH, 0, 0, axis_index_groups=share)
+    rows = sds((4, PACKED, 256), BF16)
+    kept, given, z0, z1, z2, z3 = call(layer, (rows, rows, quad, quad, quad, quad), (VMEM,) * 4)(
+        packed, *ready
+    )
+
+    n = lax.axis_size("chan")
+    g = call(sum_cores, (sds((PACKED, 256), BF16),) * 4, (VMEM,) * 2)(kept, swap(given, 1))
+    across = [(16 * y + i, 16 * (1 - y) + (i ^ 2)) for y in range(2) for i in range(n)]
+    g = (g[0], swap(g[1], 2), lax.ppermute(g[2], "tm", [(0, 1), (1, 0)]), lax.ppermute(g[3], BOTH, across))
     t1, t2, t3 = (swap(z, 4 * k) for k, z in ((1, z1), (2, z2), (3, z3)))
-    spread = call(scatter_blocks, sds((2, slots, 256), BF16), (VMEM, VMEM))(
-        at_row, parts
-    )
+    spread = call(scatter_blocks, sds((2, slots, 256), BF16), (VMEM,) * 5)(at_row, *g)
     returned = lax.all_to_all(spread.reshape(32, slots_dev, 256), BOTH, 0, 0)
     o = call(sum_units, (sds((96, 256), BF16),) * 4, (VMEM,) * 4, gflops=20)(z0, t1, t2, t3)
     o = (o[0], swap(o[1], 1), swap(o[2], 2), swap(o[3], 3))
@@ -441,9 +489,8 @@
         (VMEM, VMEM, HBM, HBM, HBM),
         scratch=(pltpu.VMEM(flat, F32),) * 7 + (dma((24,)),),
         out_space=HBM,
-        room=6 * MIB // 5,
     )(
-        own_row,
+        owned,
         returned,
         master.reshape(flat),
         first_moment.reshape(flat),

time: 102 us -> 94.2 us (0.924)
  waiting for transfers between devices: 44.6 us -> 39 us
  local copies, waits for them, and re-layouts: 3.99 us -> 0.03 us
  starting transfers between devices: 33.1 us -> 34.9 us
    all_to_all x1 -> x0, waiting for transfers between devices: 9.48 us -> none  [local(): parts = lax.all_to_all(grads, BOTH, 0, 0, axis_index_groups=share)]
    unnamed x20 -> x10, local copies, waits for them, and re-layouts: 3.99 us -> 0.03 us
    ppermute x0 -> x2, waiting for transfers between devices: none -> 3.8 us  [the longest x1 3.79 us: local(): lax.ppermute(g[2], 'tm', [(0, 1), (1, 0)])]
    all_to_all x1 -> x0, starting transfers between devices: 3.55 us -> none  [local(): parts = lax.all_to_all(grads, BOTH, 0, 0, axis_index_groups=share)]
    ppermute x0 -> x2, starting transfers between devices: none -> 2.98 us  [the longest x1 2.33 us: local(): lax.ppermute(g[3], BOTH, across)]
    ppermute x1, waiting for transfers between devices: 2.78 us -> 0.01 us  [local(): other = lax.ppermute(edges, 'tm', [(0, 1), (1, 0)])]
    all_to_all x1, starting transfers between devices: 3.45 us -> 5.23 us  [local(): returned = lax.all_to_all(spread.reshape(32, slots_dev, 256), BOTH, 0, 0)]
    ppermute x12 -> x14, waiting for transfers between devices: 22.4 us -> 23.9 us  [swap(): return lax.ppermute(x, 'chan', [(i, i ^ k) for i in range(n)])]
  transfers between devices with their start and end apart: 17 -> 20, of which waited for: 9 -> 10; matrix products, arithmetic and copies ran while one was open for 0% -> 0% of each run, Pallas kernels for 6% -> 9%
where the time goes in v5:
time: 94.2 us; the launch traced here: 93.7 us
  waiting for transfers between devices  39 us (41%)
  starting transfers between devices  34.9 us (37%)
  Pallas kernels  18.9 us (20%)
    ppermute x14, waiting for transfers between devices, swap(): return lax.ppermute(x, 'chan', [(i, i ^ k) for i in range(n)])  23.9 us
    pallas_call x12, Pallas kernels, call(): run(*(pin(x, HBM) if space == HBM else x for x, space in zip(args, spaces...  18.9 us
    ppermute x14, starting transfers between devices, swap(): return lax.ppermute(x, 'chan', [(i, i ^ k) for i in range(n)])  13.5 us
    all_to_all x1, waiting for transfers between devices, local(): returned = lax.all_to_all(spread.reshape(32, slots_dev, 256), BOTH, 0, 0)  9.06 us
    all_to_all x1, starting transfers between devices, local(): arrived = lax.all_to_all(sent, 'chan', 0, 0, tiled=True)  5.95 us
    all_to_all x1, starting transfers between devices, local(): returned = lax.all_to_all(spread.reshape(32, slots_dev, 256), BOTH, 0, 0)  5.23 us
    all_to_all x1, starting transfers between devices, local(): packed = lax.all_to_all(gathered, BOTH, 0, 0, axis_index_groups=share)  4.22 us
    ppermute x1, waiting for transfers between devices, local(): lax.ppermute(g[2], 'tm', [(0, 1), (1, 0)])  3.79 us
  transfers between devices with their start and end apart: 20, of which 10 were waited for; matrix products, arithmetic and copies ran while one was open for 0% of the time, Pallas kernels for 9%

profile of v5, /device:TPU:0, one launch (start us, length us, event | category | flops | bytes accessed | tf_op | source)
XLA Modules:
  0.0 93.7 jit_solution(7522785902595989440)
XLA Ops:
  0.6 2.7 %shard_map.136 = (bf16[16,40,256]{2,1,0:T(8,128)(2,1)}, bf16[192,128]{1,0:T(8,128)(2,1)S(1)}) custom-call(s32[8]{0:T(128)} %spk.1, f32[40,8,1024]{2,1,0:T(8,128)} %master.1, bf16[32,1024]{1,0:T(8,128)(2,1)} %bitcast.15, bf16[32,1024]{1,0:T(8,128)(2,1)} %bitcast.18, bf16[32,1024]{1,0:T(8,128)(2,1)} %bitcast.26, bf16[80,1024]{1,0:T(8,128)(2,1)} %bitcast.21), custom_call_target="tpu_custom_call" | custom-call | bytes 1048576 | tf_op jit(solution)/shard_map/pallas_call | solution.py:73
  3.4 3.0 %collective-permute-start = (bf16[192,128]{1,0:T(8,128)(2,1)S(1)}, bf16[192,128]{1,0:T(8,128)(2,1)S(1)}, u32[]{:S(2)}, u32[]{:S(2)}) collective-permute-start(bf16[192,128]{1,0:T(8,128)(2,1)S(1)} %get-tuple-element.39), channel_id=1, source_target_pairs={{0,16},{16,0},{1,17},{17,1},{2,18},{18,2},{3,19},{19,3},{4,20},{20... | collective-permute-start | bytes 147464 | tf_op jit(solution)/shard_map/ppermute | solution.py:431
  6.4 6.0 %all-to-all-start = ((bf16[16,40,256]{2,1,0:T(8,128)(2,1)}), bf16[16,40,256]{2,1,0:T(8,128)(2,1)}, u32[]{:S(2)}, u32[]{:S(2)}) async-start(bf16[16,40,256]{2,1,0:T(8,128)(2,1)} %get-tuple-element.41), calls=%async_computation | async-start | bytes 655360 | tf_op jit(solution)/shard_map/all_to_all | solution.py:432
  12.4 1.2 %shard_map.138 = (bf16[112,256]{1,0:T(8,128)(2,1)S(1)}, bf16[112,256]{1,0:T(8,128)(2,1)S(1)}, bf16[112,256]{1,0:T(8,128)(2,1)S(1)}, bf16[112,256]{1,0:T(8,128)(2,1)S(1)}) custom-call(bf16[32,1024]{1,0:T(8,128)(2,1)} %bitcast.16, bf16[32,1024]{1,0:T(8,128)(2,1)} %bitcast.19, bf16[32,1024]{1,0:T(8,128)(2,1)} %bitcast.27, ...), custom_call_target="tpu_custom_call" | custom-call | flops 199999995904 | bytes 1048576 | tf_op jit(solution)/shard_map/pallas_call | solution.py:73
  13.6 0.4 collective-permute-start.1
  14.0 1.7 %collective-permute-start.2 = (bf16[112,256]{1,0:T(8,128)(2,1)S(1)}, bf16[112,256]{1,0:T(8,128)(2,1)S(1)}, u32[]{:S(2)}, u32[]{:S(2)}) collective-permute-start(bf16[112,256]{1,0:T(8,128)(2,1)S(1)} %get-tuple-element.44), channel_id=1, source_target_pairs={{0,2},{1,3},{2,0},{3,1},{4,6},{5,7},{6,4},{7,5},{8,10},{9,11},{10,... | collective-permute-start | bytes 172040 | tf_op jit(solution)/shard_map/ppermute | solution.py:407
  15.7 3.6 %collective-permute-done.2.o2 = bf16[112,256]{1,0:T(8,128)(2,1)S(1)} collective-permute-done((bf16[112,256]{1,0:T(8,128)(2,1)S(1)}, bf16[112,256]{1,0:T(8,128)(2,1)S(1)}, u32[]{:S(2)}, u32[]{:S(2)}) %collective-permute-start.2) | collective-permute-done | bytes 57376 | tf_op jit(solution)/shard_map/ppermute | solution.py:407
  19.2 1.4 %collective-permute-done.3.o3 = bf16[112,256]{1,0:T(8,128)(2,1)S(1)} collective-permute-done((bf16[112,256]{1,0:T(8,128)(2,1)S(1)}, bf16[112,256]{1,0:T(8,128)(2,1)S(1)}, u32[]{:S(2)}, u32[]{:S(2)}) %collective-permute-start.3) | collective-permute-done | bytes 57376 | tf_op jit(solution)/shard_map/ppermute | solution.py:407
  20.6 3.5 %collective-permute-start.6 = (bf16[400,256]{1,0:T(8,128)(2,1)S(1)}, bf16[400,256]{1,0:T(8,128)(2,1)S(1)}, u32[]{:S(2)}, u32[]{:S(2)}) collective-permute-start(bf16[400,256]{1,0:T(8,128)(2,1)S(1)} %shard_map.139.p0), channel_id=1, source_target_pairs={{0,12},{1,13},{2,14},{3,15},{4,8},{5,9},{6,10},{7,11},{8,4},{9,5},... | collective-permute-start | bytes 614408 | tf_op jit(solution)/shard_map/ppermute | solution.py:407
  24.4 0.7 collective-permute-start.4
  25.1 0.9 shard_map.137
  26.0 2.4 %shard_map.140 = bf16[8,224,256]{2,1,0:T(8,128)(2,1)} custom-call(s32[224,128]{1,0:T(8,128)S(1)} %get-tuple-element.40.at_col, bf16[640,256]{1,0:T(8,128)(2,1)} %bitcast.4.slots), custom_call_target="tpu_custom_call" | custom-call | bytes 1048576 | tf_op jit(solution)/shard_map/pallas_call | solution.py:73
  28.4 4.2 %all-to-all-start.1 = ((bf16[8,224,256]{2,1,0:T(8,128)(2,1)}), bf16[8,224,256]{2,1,0:T(8,128)(2,1)}, u32[]{:S(2)}, u32[]{:S(2)}) async-start(bf16[8,224,256]{2,1,0:T(8,128)(2,1)} %shard_map.140), calls=%async_computation.1 | async-start | bytes 1835008 | tf_op jit(solution)/shard_map/all_to_all | solution.py:459
  32.6 10.4 %collective-permute-done.5.p2 = bf16[400,256]{1,0:T(8,128)(2,1)S(1)} collective-permute-done((bf16[400,256]{1,0:T(8,128)(2,1)S(1)}, bf16[400,256]{1,0:T(8,128)(2,1)S(1)}, u32[]{:S(2)}, u32[]{:S(2)}) %collective-permute-start.5) | collective-permute-done | bytes 204832 | tf_op jit(solution)/shard_map/ppermute | solution.py:407
  43.0 1.4 %shard_map.141 = (bf16[8,160,384]{2,1,0:T(8,128)(2,1)S(1)}, bf16[512,384]{1,0:T(8,128)(2,1)S(1)}, bf16[512,384]{1,0:T(8,128)(2,1)S(1)}) custom-call(s32[8]{0:T(128)S(1)} %copy-done.3, bf16[400,256]{1,0:T(8,128)(2,1)S(1)} %shard_map.139.p0, bf16[400,256]{1,0:T(8,128)(2,1)S(1)} %collective-permute-done.4.p1, bf16[400,256]{1,0:T(8,128)(2,1)S(1)} %collective-permute-done.5.p2, ...), custom_call_target="tpu_custom_call" | custom-call | flops 199999995904 | bytes 1048576 | tf_op jit(solution)/shard_map/pallas_call | solution.py:73
  44.4 2.2 %all-to-all-done.1.packed = bf16[8,224,256]{2,1,0:T(8,128)(2,1)} async-done(((bf16[8,224,256]{2,1,0:T(8,128)(2,1)}), bf16[8,224,256]{2,1,0:T(8,128)(2,1)}, u32[]{:S(2)}, u32[]{:S(2)}) %all-to-all-start.1) | async-done | bytes 917536 | tf_op jit(solution)/shard_map/all_to_all | solution.py:459
  46.6 3.3 %shard_map.142 = (bf16[4,224,256]{2,1,0:T(8,128)(2,1)S(1)}, bf16[4,224,256]{2,1,0:T(8,128)(2,1)S(1)}, bf16[4,96,256]{2,1,0:T(8,128)(2,1)S(1)}, bf16[4,96,256]{2,...) custom-call(bf16[8,224,256]{2,1,0:T(8,128)(2,1)} %all-to-all-done.1.packed, ...), custom_call_target="tpu_custom_call" | custom-call | bytes 1048576 | tf_op jit(solution)/shard_map/pallas_call | solution.py:73
  50.0 1.8 %collective-permute-done.13.got = bf16[4,224,256]{2,1,0:T(8,128)(2,1)S(1)} collective-permute-done((bf16[4,224,256]{2,1,0:T(8,128)(2,1)S(1)}, bf16[4,224,256]{2,1,0:T(8,128)(2,1)S(1)}, u32[]{:S(2)}, u32[]{:S(2)}) %collective-permute-start.13) | collective-permute-done | bytes 458784 | tf_op jit(solution)/shard_map/ppermute | solution.py:407
  51.9 0.6 collective-permute-start.14
  52.5 1.3 %collective-permute-start.7 = (bf16[4,96,256]{2,1,0:T(8,128)(2,1)S(1)}, bf16[4,96,256]{2,1,0:T(8,128)(2,1)S(1)}, u32[]{:S(2)}, u32[]{:S(2)}) collective-permute-start(bf16[4,96,256]{2,1,0:T(8,128)(2,1)S(1)} %get-tuple-element.51), channel_id=1, source_target_pairs={{0,4},{1,5},{2,6},{3,7},{4,0},{5,1},{6,2},{7,3},{8,12},{9,13},{10,... | collective-permute-start | bytes 589832 | tf_op jit(solution)/shard_map/ppermute | solution.py:407
  53.8 2.7 %collective-permute-start.8 = (bf16[4,96,256]{2,1,0:T(8,128)(2,1)S(1)}, bf16[4,96,256]{2,1,0:T(8,128)(2,1)S(1)}, u32[]{:S(2)}, u32[]{:S(2)}) collective-permute-start(bf16[4,96,256]{2,1,0:T(8,128)(2,1)S(1)} %get-tuple-element.52), channel_id=1, source_target_pairs={{0,8},{1,9},{2,10},{3,11},{4,12},{5,13},{6,14},{7,15},{8,0},{9,1},... | collective-permute-start | bytes 589832 | tf_op jit(solution)/shard_map/ppermute | solution.py:407
  56.9 0.7 collective-permute-start.15
  57.6 2.3 %collective-permute-start.16 = (bf16[224,256]{1,0:T(8,128)(2,1)S(1)}, bf16[224,256]{1,0:T(8,128)(2,1)S(1)}, u32[]{:S(2)}, u32[]{:S(2)}) collective-permute-start(bf16[224,256]{1,0:T(8,128)(2,1)S(1)} %get-tuple-element.68), channel_id=1, source_target_pairs={{0,18},{1,19},{2,16},{3,17},{4,22},{5,23},{6,20},{7,21},{8,26},{9,... | collective-permute-start | bytes 344072 | tf_op jit(solution)/shard_map/ppermute | solution.py:477
  59.9 3.8 %collective-permute-done.15.p2 = bf16[224,256]{1,0:T(8,128)(2,1)S(1)} collective-permute-done((bf16[224,256]{1,0:T(8,128)(2,1)S(1)}, bf16[224,256]{1,0:T(8,128)(2,1)S(1)}, u32[]{:S(2)}, u32[]{:S(2)}) %collective-permute-start.15) | collective-permute-done | bytes 114720 | tf_op jit(solution)/shard_map/ppermute | solution.py:477
  63.7 1.3 %shard_map.146 = bf16[2,640,256]{2,1,0:T(8,128)(2,1)} custom-call(s32[8,224]{1,0:T(8,128)S(1)} %get-tuple-element.62.at_row, bf16[224,256]{1,0:T(8,128)(2,1)S(1)} %get-tuple-element.65.p0, bf16[224,256]{1,0:T(8,128)(2,1)S(1)} %collective-permute-done.14.p1, bf16[224,256]{1,0:T(8,128)(2,1)S(1)} %collective-permute-done.15.p2, ...), custom_call_target="tpu_custom_call" | custom-call | bytes 1048576 | tf_op jit(solution)/shard_map/pallas_call | solution.py:73
  65.0 5.2 %all-to-all-start.2 = ((bf16[32,40,256]{2,1,0:T(8,128)(2,1)}), bf16[32,40,256]{2,1,0:T(8,128)(2,1)S(1)}, u32[]{:S(2)}, u32[]{:S(2)}) async-start(bf16[32,40,256]{2,1,0:T(8,128)(2,1)} %bitcast.8), calls=%async_computation.2 | async-start | bytes 1310720 | tf_op jit(solution)/shard_map/all_to_all | solution.py:480
  70.2 0.7 collective-permute-done.8.z2
  71.2 1.6 %collective-permute-start.11 = (bf16[96,256]{1,0:T(8,128)(2,1)S(1)}, bf16[96,256]{1,0:T(8,128)(2,1)S(1)}, u32[]{:S(2)}, u32[]{:S(2)}) collective-permute-start(bf16[96,256]{1,0:T(8,128)(2,1)S(1)} %get-tuple-element.56), channel_id=1, source_target_pairs={{0,2},{1,3},{2,0},{3,1},{4,6},{5,7},{6,4},{7,5},{8,10},{9,11},{10,... | collective-permute-start | bytes 147464 | tf_op jit(solution)/shard_map/ppermute | solution.py:407
  73.0 6.0 %collective-permute-done.11.o2 = bf16[96,256]{1,0:T(8,128)(2,1)S(1)} collective-permute-done((bf16[96,256]{1,0:T(8,128)(2,1)S(1)}, bf16[96,256]{1,0:T(8,128)(2,1)S(1)}, u32[]{:S(2)}, u32[]{:S(2)}) %collective-permute-start.11) | collective-permute-done | bytes 49184 | tf_op jit(solution)/shard_map/ppermute | solution.py:407
  79.1 0.8 shard_map.144
  79.9 9.1 %all-to-all-done.2.grads = bf16[32,40,256]{2,1,0:T(8,128)(2,1)S(1)} async-done(((bf16[32,40,256]{2,1,0:T(8,128)(2,1)}), bf16[32,40,256]{2,1,0:T(8,128)(2,1)S(1)}, u32[]{:S(2)}, u32[]{:S(2)}) %all-to-all-start.2) | async-done | bytes 655392 | tf_op jit(solution)/shard_map/all_to_all | solution.py:480
  89.0 4.8 %shard_map.147 = (f32[320,1024]{1,0:T(8,128)}, f32[320,1024]{1,0:T(8,128)}, f32[320,1024]{1,0:T(8,128)}) custom-call(s32[8,128]{1,0:T(8,128)S(1)} %get-tuple-element.61.owned, bf16[32,40,256]{2,1,0:T(8,128)(2,1)S(1)} %all-to-all-done.2.grads, f32[320,1024]{1,0:T(8,128)} %bitcast.23, f32[320,1024]{1,0:T(8,128)} %bitcast.24, f32[320,1024]{1,0:T(8,128)} %bitcast.25), custom_call_target="tpu_custom_call" | custom-call | bytes 1048576 | tf_op jit(solution)/shard_map/pallas_call | solution.py:73
  (31 shorter events, 1.4 us)
Async XLA Ops:
  3.4 9.0 %collective-permute-start = (bf16[192,128]{1,0:T(8,128)(2,1)S(1)}, bf16[192,128]{1,0:T(8,128)(2,1)S(1)}, u32[]{:S(2)}, u32[]{:S(2)}) collective-permute-start(bf16[192,128]{1,0:T(8,128)(2,1)S(1)} %get-tuple-element.39), channel_id=1, source_target_pairs={{0,16},{16,0},{1,17},{17,1},{2,18},{18,2},{3,19},{19,3},{4,20},{20... | collective-permute-start | bytes 147464 | tf_op jit(solution)/shard_map/ppermute | solution.py:431
  6.4 19.6 %all-to-all-start = ((bf16[16,40,256]{2,1,0:T(8,128)(2,1)}), bf16[16,40,256]{2,1,0:T(8,128)(2,1)}, u32[]{:S(2)}, u32[]{:S(2)}) async-start(bf16[16,40,256]{2,1,0:T(8,128)(2,1)} %get-tuple-element.41), calls=%async_computation | async-start | bytes 655360 | tf_op jit(solution)/shard_map/all_to_all | solution.py:432
  12.4 12.7 %copy-start.4 = (s32[320]{0:T(512)S(1)}, s32[320]{0:T(512)}, u32[]{:S(2)}) copy-start(s32[320]{0:T(512)} %param.12) | copy-start | bytes 3844
  12.4 12.7 %copy-start.3 = (s32[8]{0:T(128)S(1)}, s32[8]{0:T(128)}, u32[]{:S(2)}) copy-start(s32[8]{0:T(128)} %spk.1) | copy-start | bytes 100
  13.6 2.1 %collective-permute-start.1 = (bf16[112,256]{1,0:T(8,128)(2,1)S(1)}, bf16[112,256]{1,0:T(8,128)(2,1)S(1)}, u32[]{:S(2)}, u32[]{:S(2)}) collective-permute-start(bf16[112,256]{1,0:T(8,128)(2,1)S(1)} %get-tuple-element.43), channel_id=1, source_target_pairs={{0,1},{1,0},{2,3},{3,2},{4,5},{5,4},{6,7},{7,6},{8,9},{9,8},{10,11... | collective-permute-start | bytes 172040 | tf_op jit(solution)/shard_map/ppermute | solution.py:407
  14.0 5.3 %collective-permute-start.2 = (bf16[112,256]{1,0:T(8,128)(2,1)S(1)}, bf16[112,256]{1,0:T(8,128)(2,1)S(1)}, u32[]{:S(2)}, u32[]{:S(2)}) collective-permute-start(bf16[112,256]{1,0:T(8,128)(2,1)S(1)} %get-tuple-element.44), channel_id=1, source_target_pairs={{0,2},{1,3},{2,0},{3,1},{4,6},{5,7},{6,4},{7,5},{8,10},{9,11},{10,... | collective-permute-start | bytes 172040 | tf_op jit(solution)/shard_map/ppermute | solution.py:407
  15.7 4.9 %collective-permute-start.3 = (bf16[112,256]{1,0:T(8,128)(2,1)S(1)}, bf16[112,256]{1,0:T(8,128)(2,1)S(1)}, u32[]{:S(2)}, u32[]{:S(2)}) collective-permute-start(bf16[112,256]{1,0:T(8,128)(2,1)S(1)} %get-tuple-element.45), channel_id=1, source_target_pairs={{0,3},{1,2},{2,1},{3,0},{4,7},{5,6},{6,5},{7,4},{8,11},{9,10},{10,... | collective-permute-start | bytes 172040 | tf_op jit(solution)/shard_map/ppermute | solution.py:407
  20.6 12.0 %collective-permute-start.6 = (bf16[400,256]{1,0:T(8,128)(2,1)S(1)}, bf16[400,256]{1,0:T(8,128)(2,1)S(1)}, u32[]{:S(2)}, u32[]{:S(2)}) collective-permute-start(bf16[400,256]{1,0:T(8,128)(2,1)S(1)} %shard_map.139.p0), channel_id=1, source_target_pairs={{0,12},{1,13},{2,14},{3,15},{4,8},{5,9},{6,10},{7,11},{8,4},{9,5},... | collective-permute-start | bytes 614408 | tf_op jit(solution)/shard_map/ppermute | solution.py:407
  24.2 18.8 %collective-permute-start.5 = (bf16[400,256]{1,0:T(8,128)(2,1)S(1)}, bf16[400,256]{1,0:T(8,128)(2,1)S(1)}, u32[]{:S(2)}, u32[]{:S(2)}) collective-permute-start(bf16[400,256]{1,0:T(8,128)(2,1)S(1)} %shard_map.139.p0), channel_id=1, source_target_pairs={{0,8},{1,9},{2,10},{3,11},{4,12},{5,13},{6,14},{7,15},{8,0},{9,1},... | collective-permute-start | bytes 614408 | tf_op jit(solution)/shard_map/ppermute | solution.py:407
  24.4 18.6 %collective-permute-start.4 = (bf16[400,256]{1,0:T(8,128)(2,1)S(1)}, bf16[400,256]{1,0:T(8,128)(2,1)S(1)}, u32[]{:S(2)}, u32[]{:S(2)}) collective-permute-start(bf16[400,256]{1,0:T(8,128)(2,1)S(1)} %shard_map.139.p0), channel_id=1, source_target_pairs={{0,4},{1,5},{2,6},{3,7},{4,0},{5,1},{6,2},{7,3},{8,12},{9,13},{10,... | collective-permute-start | bytes 614408 | tf_op jit(solution)/shard_map/ppermute | solution.py:407
  26.0 17.0 %copy-start.2 = (bf16[1024,80]{0,1:T(8,128)(2,1)S(1)}, bf16[1024,80]{0,1:T(8,128)(2,1)}, u32[]{:S(2)}) copy-start(bf16[1024,80]{0,1:T(8,128)(2,1)} %param.10) | copy-start | bytes 491524
  28.4 18.2 %all-to-all-start.1 = ((bf16[8,224,256]{2,1,0:T(8,128)(2,1)}), bf16[8,224,256]{2,1,0:T(8,128)(2,1)}, u32[]{:S(2)}, u32[]{:S(2)}) async-start(bf16[8,224,256]{2,1,0:T(8,128)(2,1)} %shard_map.140), calls=%async_computation.1 | async-start | bytes 1835008 | tf_op jit(solution)/shard_map/all_to_all | solution.py:459
  49.9 1.9 %collective-permute-start.13 = (bf16[4,224,256]{2,1,0:T(8,128)(2,1)S(1)}, bf16[4,224,256]{2,1,0:T(8,128)(2,1)S(1)}, u32[]{:S(2)}, u32[]{:S(2)}) collective-permute-start(bf16[4,224,256]{2,1,0:T(8,128)(2,1)S(1)} %get-tuple-element.64), channel_id=1, source_target_pairs={{0,1},{1,0},{2,3},{3,2},{4,5},{5,4},{6,7},{7,6},{8,9},{9,8},{10,11... | collective-permute-start | bytes 1376264 | tf_op jit(solution)/shard_map/ppermute | solution.py:407
  51.9 5.6 %collective-permute-start.14 = (bf16[224,256]{1,0:T(8,128)(2,1)S(1)}, bf16[224,256]{1,0:T(8,128)(2,1)S(1)}, u32[]{:S(2)}, u32[]{:S(2)}) collective-permute-start(bf16[224,256]{1,0:T(8,128)(2,1)S(1)} %get-tuple-element.66), channel_id=1, source_target_pairs={{0,2},{1,3},{2,0},{3,1},{4,6},{5,7},{6,4},{7,5},{8,10},{9,11},{10,... | collective-permute-start | bytes 344072 | tf_op jit(solution)/shard_map/ppermute | solution.py:407
  52.5 17.7 %collective-permute-start.7 = (bf16[4,96,256]{2,1,0:T(8,128)(2,1)S(1)}, bf16[4,96,256]{2,1,0:T(8,128)(2,1)S(1)}, u32[]{:S(2)}, u32[]{:S(2)}) collective-permute-start(bf16[4,96,256]{2,1,0:T(8,128)(2,1)S(1)} %get-tuple-element.51), channel_id=1, source_target_pairs={{0,4},{1,5},{2,6},{3,7},{4,0},{5,1},{6,2},{7,3},{8,12},{9,13},{10,... | collective-permute-start | bytes 589832 | tf_op jit(solution)/shard_map/ppermute | solution.py:407
  53.8 17.1 %collective-permute-start.8 = (bf16[4,96,256]{2,1,0:T(8,128)(2,1)S(1)}, bf16[4,96,256]{2,1,0:T(8,128)(2,1)S(1)}, u32[]{:S(2)}, u32[]{:S(2)}) collective-permute-start(bf16[4,96,256]{2,1,0:T(8,128)(2,1)S(1)} %get-tuple-element.52), channel_id=1, source_target_pairs={{0,8},{1,9},{2,10},{3,11},{4,12},{5,13},{6,14},{7,15},{8,0},{9,1},... | collective-permute-start | bytes 589832 | tf_op jit(solution)/shard_map/ppermute | solution.py:407
  56.5 14.4 %collective-permute-start.9 = (bf16[4,96,256]{2,1,0:T(8,128)(2,1)S(1)}, bf16[4,96,256]{2,1,0:T(8,128)(2,1)S(1)}, u32[]{:S(2)}, u32[]{:S(2)}) collective-permute-start(bf16[4,96,256]{2,1,0:T(8,128)(2,1)S(1)} %get-tuple-element.53), channel_id=1, source_target_pairs={{0,12},{1,13},{2,14},{3,15},{4,8},{5,9},{6,10},{7,11},{8,4},{9,5},... | collective-permute-start | bytes 589832 | tf_op jit(solution)/shard_map/ppermute | solution.py:407
  56.9 6.8 %collective-permute-start.15 = (bf16[224,256]{1,0:T(8,128)(2,1)S(1)}, bf16[224,256]{1,0:T(8,128)(2,1)S(1)}, u32[]{:S(2)}, u32[]{:S(2)}) collective-permute-start(bf16[224,256]{1,0:T(8,128)(2,1)S(1)} %get-tuple-element.67), channel_id=1, source_target_pairs={{0,16},{16,0},{1,17},{17,1},{2,18},{18,2},{3,19},{19,3},{4,20},{20... | collective-permute-start | bytes 344072 | tf_op jit(solution)/shard_map/ppermute | solution.py:477
  57.6 6.1 %collective-permute-start.16 = (bf16[224,256]{1,0:T(8,128)(2,1)S(1)}, bf16[224,256]{1,0:T(8,128)(2,1)S(1)}, u32[]{:S(2)}, u32[]{:S(2)}) collective-permute-start(bf16[224,256]{1,0:T(8,128)(2,1)S(1)} %get-tuple-element.68), channel_id=1, source_target_pairs={{0,18},{1,19},{2,16},{3,17},{4,22},{5,23},{6,20},{7,21},{8,26},{9,... | collective-permute-start | bytes 344072 | tf_op jit(solution)/shard_map/ppermute | solution.py:477
  65.0 24.0 %all-to-all-start.2 = ((bf16[32,40,256]{2,1,0:T(8,128)(2,1)}), bf16[32,40,256]{2,1,0:T(8,128)(2,1)S(1)}, u32[]{:S(2)}, u32[]{:S(2)}) async-start(bf16[32,40,256]{2,1,0:T(8,128)(2,1)} %bitcast.8), calls=%async_computation.2 | async-start | bytes 1310720 | tf_op jit(solution)/shard_map/all_to_all | solution.py:480
  71.0 8.1 %copy-start = (bf16[1024,32]{0,1:T(8,128)(2,1)S(1)}, bf16[1024,32]{0,1:T(8,128)(2,1)}, u32[]{:S(2)}) copy-start(bf16[1024,32]{0,1:T(8,128)(2,1)} %param.9) | copy-start | bytes 196612
  71.0 8.1 %copy-start.1 = (bf16[1024,32]{0,1:T(8,128)(2,1)S(1)}, bf16[1024,32]{0,1:T(8,128)(2,1)}, u32[]{:S(2)}) copy-start(bf16[1024,32]{0,1:T(8,128)(2,1)} %param.16) | copy-start | bytes 196612
  71.1 1.9 %collective-permute-start.10 = (bf16[96,256]{1,0:T(8,128)(2,1)S(1)}, bf16[96,256]{1,0:T(8,128)(2,1)S(1)}, u32[]{:S(2)}, u32[]{:S(2)}) collective-permute-start(bf16[96,256]{1,0:T(8,128)(2,1)S(1)} %get-tuple-element.55), channel_id=1, source_target_pairs={{0,1},{1,0},{2,3},{3,2},{4,5},{5,4},{6,7},{7,6},{8,9},{9,8},{10,11... | collective-permute-start | bytes 147464 | tf_op jit(solution)/shard_map/ppermute | solution.py:407
  71.2 7.8 %collective-permute-start.11 = (bf16[96,256]{1,0:T(8,128)(2,1)S(1)}, bf16[96,256]{1,0:T(8,128)(2,1)S(1)}, u32[]{:S(2)}, u32[]{:S(2)}) collective-permute-start(bf16[96,256]{1,0:T(8,128)(2,1)S(1)} %get-tuple-element.56), channel_id=1, source_target_pairs={{0,2},{1,3},{2,0},{3,1},{4,6},{5,7},{6,4},{7,5},{8,10},{9,11},{10,... | collective-permute-start | bytes 147464 | tf_op jit(solution)/shard_map/ppermute | solution.py:407
  72.8 6.3 %collective-permute-start.12 = (bf16[96,256]{1,0:T(8,128)(2,1)S(1)}, bf16[96,256]{1,0:T(8,128)(2,1)S(1)}, u32[]{:S(2)}, u32[]{:S(2)}) collective-permute-start(bf16[96,256]{1,0:T(8,128)(2,1)S(1)} %get-tuple-element.57), channel_id=1, source_target_pairs={{0,3},{1,2},{2,1},{3,0},{4,7},{5,6},{6,5},{7,4},{8,11},{9,10},{10,... | collective-permute-start | bytes 147464 | tf_op jit(solution)/shard_map/ppermute | solution.py:407

commit v6 on v5

--- a/solution.py
+++ b/solution.py
@@ -206,9 +206,7 @@
     shape = (PACKED, slots.shape[0])
     pick = onehot(jnp.broadcast_to(at_col[:, 0:1], shape) == iota(shape, 1))
     got = dot(pick, slots[...]).astype(BF16)
-    got = dot(got, gate_order(0)).astype(BF16)
-    for n in range(8):
-        out[n] = got
+    out[...] = dot(got, gate_order(0)).astype(BF16)
 
 
 def sum_cores(kept, got, *outs):
@@ -453,10 +451,11 @@
         (SMEM, VMEM, VMEM),
     )(speaker_ids, own_row, other)
     arrived, _ = lax.optimization_barrier((arrived, mine))
-    gathered = call(gather_blocks, sds((8, PACKED, 256), BF16), (VMEM, VMEM))(
+    gathered = call(gather_blocks, sds((PACKED, 256), BF16), (VMEM, VMEM), gflops=200)(
         at_col, arrived.reshape(slots, 256)
     )
-    packed = lax.all_to_all(gathered, BOTH, 0, 0, axis_index_groups=share)
+    packed = lax.all_gather(gathered, BOTH, axis_index_groups=share)
+    mel, _ = lax.optimization_barrier((mel, packed))
     cots = sds((RESID, 384), BF16)
     ready = call(
         prepare,

time: 94.2 us -> 91 us (0.966)
  blocking collectives: 0 us -> 10.7 us
  waiting for transfers between devices: 39 us -> 31.8 us
  starting transfers between devices: 34.9 us -> 29 us
    all_gather x0 -> x1, blocking collectives: none -> 10.7 us  [local(): packed = lax.all_gather(gathered, BOTH, axis_index_groups=share)]
    ppermute x14, waiting for transfers between devices: 23.9 us -> 19.2 us  [swap(): return lax.ppermute(x, 'chan', [(i, i ^ k) for i in range(n)])]
    all_to_all x1 -> x0, starting transfers between devices: 4.22 us -> none  [local(): packed = lax.all_to_all(gathered, BOTH, 0, 0, axis_index_groups=share)]
    all_to_all x1 -> x0, waiting for transfers between devices: 2.22 us -> none  [local(): packed = lax.all_to_all(gathered, BOTH, 0, 0, axis_index_groups=share)]
    all_to_all x1, starting transfers between devices: 5.23 us -> 3.57 us  [local(): returned = lax.all_to_all(spread.reshape(32, slots_dev, 256), BOTH, 0, 0)]
  transfers between devices with their start and end apart: 20 -> 19, of which waited for: 10 -> 9; matrix products, arithmetic and copies ran while one was open for 0% -> 0% of each run, Pallas kernels for 9% -> 7%
where the time goes in v6:
time: 91 us; the launch traced here: 90.5 us
  waiting for transfers between devices  31.8 us (35%)
  starting transfers between devices  29 us (32%)
  Pallas kernels  18.2 us (20%)
  blocking collectives  10.7 us (12%)
    ppermute x14, waiting for transfers between devices, swap(): return lax.ppermute(x, 'chan', [(i, i ^ k) for i in range(n)])  19.2 us
    pallas_call x12, Pallas kernels, call(): run(*(pin(x, HBM) if space == HBM else x for x, space in zip(args, spaces...  18.2 us
    ppermute x14, starting transfers between devices, swap(): return lax.ppermute(x, 'chan', [(i, i ^ k) for i in range(n)])  13.9 us
    all_gather x1, blocking collectives, local(): packed = lax.all_gather(gathered, BOTH, axis_index_groups=share)  10.7 us
    all_to_all x1, waiting for transfers between devices, local(): returned = lax.all_to_all(spread.reshape(32, slots_dev, 256), BOTH, 0, 0)  8.58 us
    all_to_all x1, starting transfers between devices, local(): arrived = lax.all_to_all(sent, 'chan', 0, 0, tiled=True)  5.95 us
    ppermute x1, waiting for transfers between devices, local(): lax.ppermute(g[2], 'tm', [(0, 1), (1, 0)])  3.97 us
    all_to_all x1, starting transfers between devices, local(): returned = lax.all_to_all(spread.reshape(32, slots_dev, 256), BOTH, 0, 0)  3.57 us
  transfers between devices with their start and end apart: 19, of which 9 were waited for; matrix products, arithmetic and copies ran while one was open for 0% of the time, Pallas kernels for 7%

profile of v6, /device:TPU:0, one launch (start us, length us, event | category | flops | bytes accessed | tf_op | source)
XLA Modules:
  0.0 90.5 jit_solution(4782884018525995920)
XLA Ops:
  0.6 2.7 %shard_map.136 = (bf16[16,40,256]{2,1,0:T(8,128)(2,1)}, bf16[192,128]{1,0:T(8,128)(2,1)S(1)}) custom-call(s32[8]{0:T(128)} %spk.1, f32[40,8,1024]{2,1,0:T(8,128)} %master.1, bf16[32,1024]{1,0:T(8,128)(2,1)} %bitcast.17, bf16[32,1024]{1,0:T(8,128)(2,1)} %bitcast.20, bf16[32,1024]{1,0:T(8,128)(2,1)} %bitcast.28, bf16[80,1024]{1,0:T(8,128)(2,1)} %bitcast.23), custom_call_target="tpu_custom_call" | custom-call | bytes 1048576 | tf_op jit(solution)/shard_map/pallas_call | solution.py:73
  3.4 3.0 %collective-permute-start = (bf16[192,128]{1,0:T(8,128)(2,1)S(1)}, bf16[192,128]{1,0:T(8,128)(2,1)S(1)}, u32[]{:S(2)}, u32[]{:S(2)}) collective-permute-start(bf16[192,128]{1,0:T(8,128)(2,1)S(1)} %get-tuple-element.40), channel_id=1, source_target_pairs={{0,16},{16,0},{1,17},{17,1},{2,18},{18,2},{3,19},{19,3},{4,20},{20... | collective-permute-start | bytes 147464 | tf_op jit(solution)/shard_map/ppermute | solution.py:429
  6.4 6.0 %all-to-all-start = ((bf16[16,40,256]{2,1,0:T(8,128)(2,1)}), bf16[16,40,256]{2,1,0:T(8,128)(2,1)}, u32[]{:S(2)}, u32[]{:S(2)}) async-start(bf16[16,40,256]{2,1,0:T(8,128)(2,1)} %get-tuple-element.42), calls=%async_computation | async-start | bytes 655360 | tf_op jit(solution)/shard_map/all_to_all | solution.py:430
  12.4 1.2 %shard_map.138 = (bf16[112,256]{1,0:T(8,128)(2,1)S(1)}, bf16[112,256]{1,0:T(8,128)(2,1)S(1)}, bf16[112,256]{1,0:T(8,128)(2,1)S(1)}, bf16[112,256]{1,0:T(8,128)(2,1)S(1)}) custom-call(bf16[32,1024]{1,0:T(8,128)(2,1)} %bitcast.18, bf16[32,1024]{1,0:T(8,128)(2,1)} %bitcast.21, bf16[32,1024]{1,0:T(8,128)(2,1)} %bitcast.29, ...), custom_call_target="tpu_custom_call" | custom-call | flops 199999995904 | bytes 1048576 | tf_op jit(solution)/shard_map/pallas_call | solution.py:73
  14.0 1.7 %collective-permute-start.2 = (bf16[112,256]{1,0:T(8,128)(2,1)S(1)}, bf16[112,256]{1,0:T(8,128)(2,1)S(1)}, u32[]{:S(2)}, u32[]{:S(2)}) collective-permute-start(bf16[112,256]{1,0:T(8,128)(2,1)S(1)} %get-tuple-element.45), channel_id=1, source_target_pairs={{0,2},{1,3},{2,0},{3,1},{4,6},{5,7},{6,4},{7,5},{8,10},{9,11},{10,... | collective-permute-start | bytes 172040 | tf_op jit(solution)/shard_map/ppermute | solution.py:405
  15.7 0.9 shard_map.137
  16.6 2.7 %collective-permute-done.2.o2 = bf16[112,256]{1,0:T(8,128)(2,1)S(1)} collective-permute-done((bf16[112,256]{1,0:T(8,128)(2,1)S(1)}, bf16[112,256]{1,0:T(8,128)(2,1)S(1)}, u32[]{:S(2)}, u32[]{:S(2)}) %collective-permute-start.2) | collective-permute-done | bytes 57376 | tf_op jit(solution)/shard_map/ppermute | solution.py:405
  19.2 1.4 %collective-permute-done.3.o3 = bf16[112,256]{1,0:T(8,128)(2,1)S(1)} collective-permute-done((bf16[112,256]{1,0:T(8,128)(2,1)S(1)}, bf16[112,256]{1,0:T(8,128)(2,1)S(1)}, u32[]{:S(2)}, u32[]{:S(2)}) %collective-permute-start.3) | collective-permute-done | bytes 57376 | tf_op jit(solution)/shard_map/ppermute | solution.py:405
  20.6 0.7 shard_map.139.p0
  21.3 3.5 %collective-permute-start.6 = (bf16[400,256]{1,0:T(8,128)(2,1)}, bf16[400,256]{1,0:T(8,128)(2,1)}, u32[]{:S(2)}, u32[]{:S(2)}) collective-permute-start(bf16[400,256]{1,0:T(8,128)(2,1)} %shard_map.139.p0), channel_id=1, source_target_pairs={{0,12},{1,13},{2,14},{3,15},{4,8},{5,9},{6,10},{7,11},{8,4},{9,5},... | collective-permute-start | bytes 614408 | tf_op jit(solution)/shard_map/ppermute | solution.py:405
  25.0 0.7 collective-permute-start.4
  25.7 1.5 %shard_map.140 = bf16[224,256]{1,0:T(8,128)(2,1)S(1)} custom-call(s32[224,128]{1,0:T(8,128)S(1)} %get-tuple-element.41.at_col, bf16[640,256]{1,0:T(8,128)(2,1)} %bitcast.4.slots), custom_call_target="tpu_custom_call" | custom-call | flops 199999995904 | bytes 1048576 | tf_op jit(solution)/shard_map/pallas_call | solution.py:73
  27.2 10.7 %all-gather = bf16[1792,256]{1,0:T(8,128)(2,1)S(1)} all-gather(bf16[224,256]{1,0:T(8,128)(2,1)S(1)} %shard_map.140), channel_id=2, replica_groups={{0,1,2,3,16,17,18,19},{4,5,6,7,20,21,22,23},{8,9,10,11,24,25,26,27},{12..., dimensions={0}, use_global_device_ids=true | all-gather | bytes 1032192 | tf_op jit(solution)/shard_map/all_gather | solution.py:457
  37.9 6.0 %collective-permute-done.5.p2 = bf16[400,256]{1,0:T(8,128)(2,1)} collective-permute-done((bf16[400,256]{1,0:T(8,128)(2,1)}, bf16[400,256]{1,0:T(8,128)(2,1)}, u32[]{:S(2)}, u32[]{:S(2)}) %collective-permute-start.5) | collective-permute-done | bytes 204832 | tf_op jit(solution)/shard_map/ppermute | solution.py:405
  43.9 2.1 %shard_map.141 = (bf16[8,160,384]{2,1,0:T(8,128)(2,1)S(1)}, bf16[512,384]{1,0:T(8,128)(2,1)S(1)}, bf16[512,384]{1,0:T(8,128)(2,1)S(1)}) custom-call(s32[8]{0:T(128)S(1)} %copy-done.4, bf16[400,256]{1,0:T(8,128)(2,1)} %shard_map.139.p0, bf16[400,256]{1,0:T(8,128)(2,1)} %collective-permute-done.4.p1, bf16[400,256]{1,0:T(8,128)(2,1)} %collective-permute-done.5.p2, ...), custom_call_target="tpu_custom_call" | custom-call | flops 199999995904 | bytes 1048576 | tf_op jit(solution)/shard_map/pallas_call | solution.py:73
  46.0 2.1 %shard_map.142 = (bf16[4,224,256]{2,1,0:T(8,128)(2,1)S(1)}, bf16[4,224,256]{2,1,0:T(8,128)(2,1)S(1)}, bf16[4,96,256]{2,1,0:T(8,128)(2,1)S(1)}, bf16[4,96,256]{2,...) custom-call(bf16[8,224,256]{2,1,0:T(8,128)(2,1)S(1)} %bitcast.16, ...), custom_call_target="tpu_custom_call" | custom-call | bytes 1048576 | tf_op jit(solution)/shard_map/pallas_call | solution.py:73
  48.3 1.8 %collective-permute-done.13.got = bf16[4,224,256]{2,1,0:T(8,128)(2,1)S(1)} collective-permute-done((bf16[4,224,256]{2,1,0:T(8,128)(2,1)S(1)}, bf16[4,224,256]{2,1,0:T(8,128)(2,1)S(1)}, u32[]{:S(2)}, u32[]{:S(2)}) %collective-permute-start.13) | collective-permute-done | bytes 458784 | tf_op jit(solution)/shard_map/ppermute | solution.py:405
  50.2 1.0 %collective-permute-start.14 = (bf16[224,256]{1,0:T(8,128)(2,1)S(1)}, bf16[224,256]{1,0:T(8,128)(2,1)S(1)}, u32[]{:S(2)}, u32[]{:S(2)}) collective-permute-start(bf16[224,256]{1,0:T(8,128)(2,1)S(1)} %get-tuple-element.68), channel_id=1, source_target_pairs={{0,2},{1,3},{2,0},{3,1},{4,6},{5,7},{6,4},{7,5},{8,10},{9,11},{10,... | collective-permute-start | bytes 344072 | tf_op jit(solution)/shard_map/ppermute | solution.py:405
  51.2 3.1 %collective-permute-start.8 = (bf16[4,96,256]{2,1,0:T(8,128)(2,1)S(1)}, bf16[4,96,256]{2,1,0:T(8,128)(2,1)S(1)}, u32[]{:S(2)}, u32[]{:S(2)}) collective-permute-start(bf16[4,96,256]{2,1,0:T(8,128)(2,1)S(1)} %get-tuple-element.54), channel_id=1, source_target_pairs={{0,8},{1,9},{2,10},{3,11},{4,12},{5,13},{6,14},{7,15},{8,0},{9,1},... | collective-permute-start | bytes 589832 | tf_op jit(solution)/shard_map/ppermute | solution.py:405
  54.3 1.3 %collective-permute-start.9 = (bf16[4,96,256]{2,1,0:T(8,128)(2,1)S(1)}, bf16[4,96,256]{2,1,0:T(8,128)(2,1)S(1)}, u32[]{:S(2)}, u32[]{:S(2)}) collective-permute-start(bf16[4,96,256]{2,1,0:T(8,128)(2,1)S(1)} %get-tuple-element.55), channel_id=1, source_target_pairs={{0,12},{1,13},{2,14},{3,15},{4,8},{5,9},{6,10},{7,11},{8,4},{9,5},... | collective-permute-start | bytes 589832 | tf_op jit(solution)/shard_map/ppermute | solution.py:405
  56.1 2.0 %collective-permute-start.16 = (bf16[224,256]{1,0:T(8,128)(2,1)S(1)}, bf16[224,256]{1,0:T(8,128)(2,1)S(1)}, u32[]{:S(2)}, u32[]{:S(2)}) collective-permute-start(bf16[224,256]{1,0:T(8,128)(2,1)S(1)} %get-tuple-element.70), channel_id=1, source_target_pairs={{0,18},{1,19},{2,16},{3,17},{4,22},{5,23},{6,20},{7,21},{8,26},{9,... | collective-permute-start | bytes 344072 | tf_op jit(solution)/shard_map/ppermute | solution.py:476
  58.1 4.0 %collective-permute-done.15.p2 = bf16[224,256]{1,0:T(8,128)(2,1)S(1)} collective-permute-done((bf16[224,256]{1,0:T(8,128)(2,1)S(1)}, bf16[224,256]{1,0:T(8,128)(2,1)S(1)}, u32[]{:S(2)}, u32[]{:S(2)}) %collective-permute-start.15) | collective-permute-done | bytes 114720 | tf_op jit(solution)/shard_map/ppermute | solution.py:476
  62.1 1.3 %shard_map.146 = bf16[2,640,256]{2,1,0:T(8,128)(2,1)} custom-call(s32[8,224]{1,0:T(8,128)S(1)} %get-tuple-element.64.at_row, bf16[224,256]{1,0:T(8,128)(2,1)S(1)} %get-tuple-element.67.p0, bf16[224,256]{1,0:T(8,128)(2,1)S(1)} %collective-permute-done.14.p1, bf16[224,256]{1,0:T(8,128)(2,1)S(1)} %collective-permute-done.15.p2, ...), custom_call_target="tpu_custom_call" | custom-call | bytes 1048576 | tf_op jit(solution)/shard_map/pallas_call | solution.py:73
  63.4 3.6 %all-to-all-start.1 = ((bf16[32,40,256]{2,1,0:T(8,128)(2,1)}), bf16[32,40,256]{2,1,0:T(8,128)(2,1)S(1)}, u32[]{:S(2)}, u32[]{:S(2)}) async-start(bf16[32,40,256]{2,1,0:T(8,128)(2,1)} %bitcast.9), calls=%async_computation.1 | async-start | bytes 1310720 | tf_op jit(solution)/shard_map/all_to_all | solution.py:479
  67.0 1.5 %collective-permute-done.8.z2 = bf16[4,96,256]{2,1,0:T(8,128)(2,1)S(1)} collective-permute-done((bf16[4,96,256]{2,1,0:T(8,128)(2,1)S(1)}, bf16[4,96,256]{2,1,0:T(8,128)(2,1)S(1)}, u32[]{:S(2)}, u32[]{:S(2)}) %collective-permute-start.8) | collective-permute-done | bytes 196640 | tf_op jit(solution)/shard_map/ppermute | solution.py:405
  68.7 1.0 %collective-permute-start.11 = (bf16[96,256]{1,0:T(8,128)(2,1)S(1)}, bf16[96,256]{1,0:T(8,128)(2,1)S(1)}, u32[]{:S(2)}, u32[]{:S(2)}) collective-permute-start(bf16[96,256]{1,0:T(8,128)(2,1)S(1)} %get-tuple-element.58), channel_id=1, source_target_pairs={{0,2},{1,3},{2,0},{3,1},{4,6},{5,7},{6,4},{7,5},{8,10},{9,11},{10,... | collective-permute-start | bytes 147464 | tf_op jit(solution)/shard_map/ppermute | solution.py:405
  69.6 0.9 collective-permute-start.12
  70.5 3.6 %collective-permute-done.11.o2 = bf16[96,256]{1,0:T(8,128)(2,1)S(1)} collective-permute-done((bf16[96,256]{1,0:T(8,128)(2,1)S(1)}, bf16[96,256]{1,0:T(8,128)(2,1)S(1)}, u32[]{:S(2)}, u32[]{:S(2)}) %collective-permute-start.11) | collective-permute-done | bytes 49184 | tf_op jit(solution)/shard_map/ppermute | solution.py:405
  74.2 2.2 %collective-permute-done.12.o3 = bf16[96,256]{1,0:T(8,128)(2,1)S(1)} collective-permute-done((bf16[96,256]{1,0:T(8,128)(2,1)S(1)}, bf16[96,256]{1,0:T(8,128)(2,1)S(1)}, u32[]{:S(2)}, u32[]{:S(2)}) %collective-permute-start.12) | collective-permute-done | bytes 49184 | tf_op jit(solution)/shard_map/ppermute | solution.py:405
  76.4 0.8 shard_map.144
  77.2 8.6 %all-to-all-done.1.grads = bf16[32,40,256]{2,1,0:T(8,128)(2,1)S(1)} async-done(((bf16[32,40,256]{2,1,0:T(8,128)(2,1)}), bf16[32,40,256]{2,1,0:T(8,128)(2,1)S(1)}, u32[]{:S(2)}, u32[]{:S(2)}) %all-to-all-start.1) | async-done | bytes 655392 | tf_op jit(solution)/shard_map/all_to_all | solution.py:479
  85.8 4.8 %shard_map.147 = (f32[320,1024]{1,0:T(8,128)}, f32[320,1024]{1,0:T(8,128)}, f32[320,1024]{1,0:T(8,128)}) custom-call(s32[8,128]{1,0:T(8,128)S(1)} %get-tuple-element.63.owned, bf16[32,40,256]{2,1,0:T(8,128)(2,1)S(1)} %all-to-all-done.1.grads, f32[320,1024]{1,0:T(8,128)} %bitcast.25, f32[320,1024]{1,0:T(8,128)} %bitcast.26, f32[320,1024]{1,0:T(8,128)} %bitcast.27), custom_call_target="tpu_custom_call" | custom-call | bytes 1048576 | tf_op jit(solution)/shard_map/pallas_call | solution.py:73
  (32 shorter events, 1.6 us)
Async XLA Ops:
  3.4 9.0 %collective-permute-start = (bf16[192,128]{1,0:T(8,128)(2,1)S(1)}, bf16[192,128]{1,0:T(8,128)(2,1)S(1)}, u32[]{:S(2)}, u32[]{:S(2)}) collective-permute-start(bf16[192,128]{1,0:T(8,128)(2,1)S(1)} %get-tuple-element.40), channel_id=1, source_target_pairs={{0,16},{16,0},{1,17},{17,1},{2,18},{18,2},{3,19},{19,3},{4,20},{20... | collective-permute-start | bytes 147464 | tf_op jit(solution)/shard_map/ppermute | solution.py:429
  6.4 19.3 %all-to-all-start = ((bf16[16,40,256]{2,1,0:T(8,128)(2,1)}), bf16[16,40,256]{2,1,0:T(8,128)(2,1)}, u32[]{:S(2)}, u32[]{:S(2)}) async-start(bf16[16,40,256]{2,1,0:T(8,128)(2,1)} %get-tuple-element.42), calls=%async_computation | async-start | bytes 655360 | tf_op jit(solution)/shard_map/all_to_all | solution.py:430
  12.4 3.3 %copy-start.5 = (s32[320]{0:T(512)S(1)}, s32[320]{0:T(512)}, u32[]{:S(2)}) copy-start(s32[320]{0:T(512)} %param.12) | copy-start | bytes 3844
  12.4 3.3 %copy-start.3 = (s32[8]{0:T(128)S(1)}, s32[8]{0:T(128)}, u32[]{:S(2)}) copy-start(s32[8]{0:T(128)} %spk.1) | copy-start | bytes 100
  13.6 3.0 %collective-permute-start.1 = (bf16[112,256]{1,0:T(8,128)(2,1)S(1)}, bf16[112,256]{1,0:T(8,128)(2,1)S(1)}, u32[]{:S(2)}, u32[]{:S(2)}) collective-permute-start(bf16[112,256]{1,0:T(8,128)(2,1)S(1)} %get-tuple-element.44), channel_id=1, source_target_pairs={{0,1},{1,0},{2,3},{3,2},{4,5},{5,4},{6,7},{7,6},{8,9},{9,8},{10,11... | collective-permute-start | bytes 172040 | tf_op jit(solution)/shard_map/ppermute | solution.py:405
  14.0 5.3 %collective-permute-start.2 = (bf16[112,256]{1,0:T(8,128)(2,1)S(1)}, bf16[112,256]{1,0:T(8,128)(2,1)S(1)}, u32[]{:S(2)}, u32[]{:S(2)}) collective-permute-start(bf16[112,256]{1,0:T(8,128)(2,1)S(1)} %get-tuple-element.45), channel_id=1, source_target_pairs={{0,2},{1,3},{2,0},{3,1},{4,6},{5,7},{6,4},{7,5},{8,10},{9,11},{10,... | collective-permute-start | bytes 172040 | tf_op jit(solution)/shard_map/ppermute | solution.py:405
  15.7 4.9 %collective-permute-start.3 = (bf16[112,256]{1,0:T(8,128)(2,1)S(1)}, bf16[112,256]{1,0:T(8,128)(2,1)S(1)}, u32[]{:S(2)}, u32[]{:S(2)}) collective-permute-start(bf16[112,256]{1,0:T(8,128)(2,1)S(1)} %get-tuple-element.46), channel_id=1, source_target_pairs={{0,3},{1,2},{2,1},{3,0},{4,7},{5,6},{6,5},{7,4},{8,11},{9,10},{10,... | collective-permute-start | bytes 172040 | tf_op jit(solution)/shard_map/ppermute | solution.py:405
  21.3 16.6 %collective-permute-start.6 = (bf16[400,256]{1,0:T(8,128)(2,1)}, bf16[400,256]{1,0:T(8,128)(2,1)}, u32[]{:S(2)}, u32[]{:S(2)}) collective-permute-start(bf16[400,256]{1,0:T(8,128)(2,1)} %shard_map.139.p0), channel_id=1, source_target_pairs={{0,12},{1,13},{2,14},{3,15},{4,8},{5,9},{6,10},{7,11},{8,4},{9,5},... | collective-permute-start | bytes 614408 | tf_op jit(solution)/shard_map/ppermute | solution.py:405
  24.8 19.1 %collective-permute-start.5 = (bf16[400,256]{1,0:T(8,128)(2,1)}, bf16[400,256]{1,0:T(8,128)(2,1)}, u32[]{:S(2)}, u32[]{:S(2)}) collective-permute-start(bf16[400,256]{1,0:T(8,128)(2,1)} %shard_map.139.p0), channel_id=1, source_target_pairs={{0,8},{1,9},{2,10},{3,11},{4,12},{5,13},{6,14},{7,15},{8,0},{9,1},... | collective-permute-start | bytes 614408 | tf_op jit(solution)/shard_map/ppermute | solution.py:405
  25.0 18.9 %collective-permute-start.4 = (bf16[400,256]{1,0:T(8,128)(2,1)}, bf16[400,256]{1,0:T(8,128)(2,1)}, u32[]{:S(2)}, u32[]{:S(2)}) collective-permute-start(bf16[400,256]{1,0:T(8,128)(2,1)} %shard_map.139.p0), channel_id=1, source_target_pairs={{0,4},{1,5},{2,6},{3,7},{4,0},{5,1},{6,2},{7,3},{8,12},{9,13},{10,... | collective-permute-start | bytes 614408 | tf_op jit(solution)/shard_map/ppermute | solution.py:405
  25.7 18.2 %copy-start.2 = (bf16[1024,80]{0,1:T(8,128)(2,1)S(1)}, bf16[1024,80]{0,1:T(8,128)(2,1)}, u32[]{:S(2)}) copy-start(bf16[1024,80]{0,1:T(8,128)(2,1)} %param.10) | copy-start | bytes 491524
  25.7 18.2 %copy-start.4 = (s32[8]{0:T(128)S(1)}, s32[8]{0:T(128)}, u32[]{:S(2)}) copy-start(s32[8]{0:T(128)} %spk.1) | copy-start | bytes 100
  48.2 1.9 %collective-permute-start.13 = (bf16[4,224,256]{2,1,0:T(8,128)(2,1)S(1)}, bf16[4,224,256]{2,1,0:T(8,128)(2,1)S(1)}, u32[]{:S(2)}, u32[]{:S(2)}) collective-permute-start(bf16[4,224,256]{2,1,0:T(8,128)(2,1)S(1)} %get-tuple-element.66), channel_id=1, source_target_pairs={{0,1},{1,0},{2,3},{3,2},{4,5},{5,4},{6,7},{7,6},{8,9},{9,8},{10,11... | collective-permute-start | bytes 1376264 | tf_op jit(solution)/shard_map/ppermute | solution.py:405
  50.2 5.9 %collective-permute-start.14 = (bf16[224,256]{1,0:T(8,128)(2,1)S(1)}, bf16[224,256]{1,0:T(8,128)(2,1)S(1)}, u32[]{:S(2)}, u32[]{:S(2)}) collective-permute-start(bf16[224,256]{1,0:T(8,128)(2,1)S(1)} %get-tuple-element.68), channel_id=1, source_target_pairs={{0,2},{1,3},{2,0},{3,1},{4,6},{5,7},{6,4},{7,5},{8,10},{9,11},{10,... | collective-permute-start | bytes 344072 | tf_op jit(solution)/shard_map/ppermute | solution.py:405
  51.2 15.8 %collective-permute-start.7 = (bf16[4,96,256]{2,1,0:T(8,128)(2,1)S(1)}, bf16[4,96,256]{2,1,0:T(8,128)(2,1)S(1)}, u32[]{:S(2)}, u32[]{:S(2)}) collective-permute-start(bf16[4,96,256]{2,1,0:T(8,128)(2,1)S(1)} %get-tuple-element.53), channel_id=1, source_target_pairs={{0,4},{1,5},{2,6},{3,7},{4,0},{5,1},{6,2},{7,3},{8,12},{9,13},{10,... | collective-permute-start | bytes 589832 | tf_op jit(solution)/shard_map/ppermute | solution.py:405
  51.2 17.3 %collective-permute-start.8 = (bf16[4,96,256]{2,1,0:T(8,128)(2,1)S(1)}, bf16[4,96,256]{2,1,0:T(8,128)(2,1)S(1)}, u32[]{:S(2)}, u32[]{:S(2)}) collective-permute-start(bf16[4,96,256]{2,1,0:T(8,128)(2,1)S(1)} %get-tuple-element.54), channel_id=1, source_target_pairs={{0,8},{1,9},{2,10},{3,11},{4,12},{5,13},{6,14},{7,15},{8,0},{9,1},... | collective-permute-start | bytes 589832 | tf_op jit(solution)/shard_map/ppermute | solution.py:405
  54.3 14.2 %collective-permute-start.9 = (bf16[4,96,256]{2,1,0:T(8,128)(2,1)S(1)}, bf16[4,96,256]{2,1,0:T(8,128)(2,1)S(1)}, u32[]{:S(2)}, u32[]{:S(2)}) collective-permute-start(bf16[4,96,256]{2,1,0:T(8,128)(2,1)S(1)} %get-tuple-element.55), channel_id=1, source_target_pairs={{0,12},{1,13},{2,14},{3,15},{4,8},{5,9},{6,10},{7,11},{8,4},{9,5},... | collective-permute-start | bytes 589832 | tf_op jit(solution)/shard_map/ppermute | solution.py:405
  55.6 6.5 %collective-permute-start.15 = (bf16[224,256]{1,0:T(8,128)(2,1)S(1)}, bf16[224,256]{1,0:T(8,128)(2,1)S(1)}, u32[]{:S(2)}, u32[]{:S(2)}) collective-permute-start(bf16[224,256]{1,0:T(8,128)(2,1)S(1)} %get-tuple-element.69), channel_id=1, source_target_pairs={{0,16},{16,0},{1,17},{17,1},{2,18},{18,2},{3,19},{19,3},{4,20},{20... | collective-permute-start | bytes 344072 | tf_op jit(solution)/shard_map/ppermute | solution.py:476
  56.1 6.0 %collective-permute-start.16 = (bf16[224,256]{1,0:T(8,128)(2,1)S(1)}, bf16[224,256]{1,0:T(8,128)(2,1)S(1)}, u32[]{:S(2)}, u32[]{:S(2)}) collective-permute-start(bf16[224,256]{1,0:T(8,128)(2,1)S(1)} %get-tuple-element.70), channel_id=1, source_target_pairs={{0,18},{1,19},{2,16},{3,17},{4,22},{5,23},{6,20},{7,21},{8,26},{9,... | collective-permute-start | bytes 344072 | tf_op jit(solution)/shard_map/ppermute | solution.py:476
  63.4 22.4 %all-to-all-start.1 = ((bf16[32,40,256]{2,1,0:T(8,128)(2,1)}), bf16[32,40,256]{2,1,0:T(8,128)(2,1)S(1)}, u32[]{:S(2)}, u32[]{:S(2)}) async-start(bf16[32,40,256]{2,1,0:T(8,128)(2,1)} %bitcast.9), calls=%async_computation.1 | async-start | bytes 1310720 | tf_op jit(solution)/shard_map/all_to_all | solution.py:479
  68.5 7.9 %copy-start = (bf16[1024,32]{0,1:T(8,128)(2,1)S(1)}, bf16[1024,32]{0,1:T(8,128)(2,1)}, u32[]{:S(2)}) copy-start(bf16[1024,32]{0,1:T(8,128)(2,1)} %param.9) | copy-start | bytes 196612
  68.5 7.9 %copy-start.1 = (bf16[1024,32]{0,1:T(8,128)(2,1)S(1)}, bf16[1024,32]{0,1:T(8,128)(2,1)}, u32[]{:S(2)}) copy-start(bf16[1024,32]{0,1:T(8,128)(2,1)} %param.16) | copy-start | bytes 196612
  68.6 1.9 %collective-permute-start.10 = (bf16[96,256]{1,0:T(8,128)(2,1)S(1)}, bf16[96,256]{1,0:T(8,128)(2,1)S(1)}, u32[]{:S(2)}, u32[]{:S(2)}) collective-permute-start(bf16[96,256]{1,0:T(8,128)(2,1)S(1)} %get-tuple-element.57), channel_id=1, source_target_pairs={{0,1},{1,0},{2,3},{3,2},{4,5},{5,4},{6,7},{7,6},{8,9},{9,8},{10,11... | collective-permute-start | bytes 147464 | tf_op jit(solution)/shard_map/ppermute | solution.py:405
  68.7 5.5 %collective-permute-start.11 = (bf16[96,256]{1,0:T(8,128)(2,1)S(1)}, bf16[96,256]{1,0:T(8,128)(2,1)S(1)}, u32[]{:S(2)}, u32[]{:S(2)}) collective-permute-start(bf16[96,256]{1,0:T(8,128)(2,1)S(1)} %get-tuple-element.58), channel_id=1, source_target_pairs={{0,2},{1,3},{2,0},{3,1},{4,6},{5,7},{6,4},{7,5},{8,10},{9,11},{10,... | collective-permute-start | bytes 147464 | tf_op jit(solution)/shard_map/ppermute | solution.py:405
  69.6 6.8 %collective-permute-start.12 = (bf16[96,256]{1,0:T(8,128)(2,1)S(1)}, bf16[96,256]{1,0:T(8,128)(2,1)S(1)}, u32[]{:S(2)}, u32[]{:S(2)}) collective-permute-start(bf16[96,256]{1,0:T(8,128)(2,1)S(1)} %get-tuple-element.59), channel_id=1, source_target_pairs={{0,3},{1,2},{2,1},{3,0},{4,7},{5,6},{6,5},{7,4},{8,11},{9,10},{10,... | collective-permute-start | bytes 147464 | tf_op jit(solution)/shard_map/ppermute | solution.py:405

commit v7 on v6

--- a/solution.py
+++ b/solution.py
@@ -57,7 +57,7 @@
 VMEM, SMEM, HBM = pltpu.VMEM, pltpu.SMEM, pltpu.HBM
 
 
-def call(kernel, out, spaces, gflops=0, scratch=(), out_space=VMEM):
+def call(kernel, out, spaces, gflops=0, scratch=(), out_space=VMEM, pinned=()):
     run = pl.pallas_call(
         kernel,
         out_shape=out,
@@ -70,7 +70,8 @@
         ),
     )
     pin = pltpu.with_memory_space_constraint
-    return lambda *args: run(*(pin(x, HBM) if space == HBM else x for x, space in zip(args, spaces, strict=True)))
+    fixed = [space if space == HBM or n in pinned else None for n, space in enumerate(spaces)]
+    return lambda *args: run(*(pin(x, f) if f else x for x, f in zip(args, fixed, strict=True)))
 
 
 def gate_order(dim):
@@ -80,18 +81,17 @@
 
 def begin(speakers, master, sig, res, skp, mel, sent, edges, strips, spk, sems):
     half = lax.axis_index("tm")
-    slots = master.shape[0]
-    rows = 4 * slots
+    slots = sent.shape[1]
     cut = pl.ds(pl.multiple_of((1 - half) * 896, 128), 128)
     tiles = []
     for n, part in enumerate((sig, res, skp, mel)):
         to = edges.at[32 * n : 32 * n + part.shape[0], :]
-        tiles.append(pltpu.make_async_copy(part.at[:, cut], to, sems.at[4 + n]))
+        tiles.append(pltpu.make_async_copy(part.at[:, cut], to, sems.at[8 + n]))
     copies = []
-    for z in range(4):
-        part = master.at[:, :, 256 * z : 256 * z + 256]
-        copies.append(pltpu.make_async_copy(part, strips.at[z], sems.at[z]))
-    names = pltpu.make_async_copy(speakers, spk, sems.at[8])
+    for t in range(8):
+        part = master.at[:, 128 * t : 128 * t + 128]
+        copies.append(pltpu.make_async_copy(part, strips.at[t], sems.at[t]))
+    names = pltpu.make_async_copy(speakers, spk, sems.at[12])
     for copy in (names, *copies, *tiles):
         copy.start()
     names.wait()
@@ -101,19 +101,13 @@
         code = jnp.where(row == 0, spk[s] >> 3, spk[s] & 7)
         table = jnp.where((lane == s) & (row < 2), code, table)
     edges[176:192, :] = table.astype(F32).astype(BF16)
-    here = iota((rows, 8 * slots), 0)
-    there = iota((rows, 8 * slots), 1)
-    row, slot = jnp.zeros_like(here), here
-    for step in range(1, 4):
-        past = here >= step * slots
-        row = jnp.where(past, step, row)
-        slot = jnp.where(past, here - step * slots, slot)
-    pick = onehot(there == 8 * slot + 4 * half + row)
-    for z in range(4):
-        copies[z].wait()
-        got = dot(pick, strips[z].reshape(8 * slots, 256).astype(BF16))
+    for t in range(8):
+        copies[t].wait()
+        lanes = slice(128 * (t % 2), 128 * (t % 2) + 128)
         for j in range(4):
-            sent[4 * z + j] = got[j * slots : (j + 1) * slots].astype(BF16)
+            low = strips[t, pl.ds(j, slots, stride=8), :]
+            high = strips[t, pl.ds(4 + j, slots, stride=8), :]
+            sent[4 * (t // 2) + j, :, lanes] = jnp.where(half == 0, low, high).astype(BF16)
     for tile in tiles:
         tile.wait()
 
@@ -170,7 +164,7 @@
     out[384:400, :] = ends.astype(BF16)
 
 
-def place_blocks(spk_ids, owners, other, at_col, at_row, owned, *, slots_dev):
+def place_blocks(spk_ids, owners, other, at_col, put, owned, *, slots_dev):
     half = lax.axis_index("tm")
     own_row = owners[...]
     mine = jnp.where(own_row == lax.axis_index("chan"), 1, 0)
@@ -199,7 +193,7 @@
     at_col[...] = jnp.broadcast_to(at, (PACKED, 128))
     same = iota((PACKED, PACKED), 0) == iota((PACKED, PACKED), 1)
     row = jnp.sum(jnp.where(same, jnp.broadcast_to(at, (PACKED, PACKED)), 0), axis=0, keepdims=True)
-    at_row[...] = jnp.broadcast_to(row, (8, PACKED))
+    put[...] = onehot(jnp.broadcast_to(row, put.shape) == iota(put.shape, 0))
 
 
 def gather_blocks(at_col, slots, out):
@@ -215,14 +209,12 @@
         out[...] = (kept[i ^ k].astype(F32) + got[i ^ k].astype(F32)).astype(BF16)
 
 
-def scatter_blocks(at_row, p0, p1, p2, p3, out):
+def scatter_blocks(put, p0, p1, p2, p3, out):
     total = p0[...].astype(F32)
     for part in (p1, p2, p3):
         total = total + part[...].astype(F32)
     natural = dot(total.astype(BF16), gate_order(1)).astype(BF16)
-    shape = (out.shape[1], PACKED)
-    put = onehot(jnp.broadcast_to(at_row[0:1, :], shape) == iota(shape, 0))
-    spread = dot(put, natural).astype(BF16)
+    spread = dot(put[...], natural).astype(BF16)
     out[0] = spread
     out[1] = spread
 
@@ -234,38 +226,37 @@
         ).astype(BF16)
 
 
-def channel_of(pos, ch):
-    return ((pos >> 5) ^ ch) * 32 + (pos & 31)
-
-
-def to_major(ch, dim):
-    shape = (RESID, RESID)
-    major = iota(shape, dim)
-    return onehot(channel_of(iota(shape, 1 - dim), ch) == 8 * (major & 63) + (major >> 6))
-
-
-def prepare(spk, p0, p1, p2, p3, mel, other, features, res, skp):
+def prepare(spk, p0, p1, p2, p3, mel, other, features, res, skp, natural):
     half, ch = lax.axis_index("tm"), lax.axis_index("chan")
     j = ch & 3
     got = (p0, p1, p2, p3)
     tokens, wide = 256, 384
-    order = to_major(ch, 0)
-
-    def stacked(n):
-        return jnp.concatenate(
-            [got[k][96 * i + 32 * n : 96 * i + 32 * n + 32, :] for k in range(4) for i in range(4)], 0
-        )
+    for k in range(4):
+        for i in range(4):
+            rows = pl.ds(pl.multiple_of(32 * (ch ^ (4 * k + i)), 32), 32)
+            for n in range(3):
+                at = 96 * i + 32 * n
+                for h in range(2):
+                    natural[2 * n + h, rows, :] = got[k][at : at + 32, 128 * h : 128 * h + 128].astype(F32)
 
     ends = [part[384:400, :].astype(F32) for part in got]
-    ends = [jnp.concatenate([e[:, 128 * n : 128 * n + 128] for e in ends], 1) for n in range(2)]
-    gap = jnp.zeros((120, RESID), F32)
-    ends = jnp.concatenate(
-        [ends[0][8:16], gap[:112], ends[0][0:8], ends[1][0:8], gap, ends[1][8:16], gap], 0
-    ).astype(BF16)
-    ends = dot(order, ends, NT)
-    sig = jnp.concatenate([dot(order, stacked(0)), ends[:, 0:128]], 1)
-    res[...] = jnp.concatenate([dot(order, stacked(1)), ends[:, 128:256]], 1).astype(BF16)
-    skp[...] = jnp.concatenate([dot(order, stacked(2)), ends[:, 256:384]], 1).astype(BF16)
+    gap = jnp.zeros((96, 128), F32)
+    for k, end in enumerate(ends):
+        left, right = end[:, 0:128], end[:, 128:256]
+        tile = jnp.concatenate([left[8:16], right, gap, left[0:8]], 0).T
+        for i in range(4):
+            rows = pl.ds(pl.multiple_of(32 * (ch ^ (4 * k + i)), 32), 32)
+            natural[6, rows, :] = tile[32 * i : 32 * i + 32]
+
+    def majors(n):
+        return jnp.concatenate([natural[n, pl.ds(r, 64, stride=8), :] for r in range(8)], 0)
+
+    tile = majors(6)
+    sig = jnp.concatenate([majors(0), majors(1), tile], 1)
+    for n, out in ((1, res), (2, skp)):
+        out[:, 0:128] = majors(2 * n).astype(BF16)
+        out[:, 128:256] = majors(2 * n + 1).astype(BF16)
+        out[:, 256:384] = pltpu.roll(tile, 128 - 8 * n, 1).astype(BF16)
     shifted = pltpu.roll(sig, DILATION, 1).astype(BF16)
     sig = sig.astype(BF16)
     m = iota((128, MELS), 0)
@@ -290,9 +281,8 @@
         features[r, 144:160] = onehot((row == seg + (lane >> 7)) & (sub == r))
 
 
-def layer(packed, feat, res, skp, kept, given, z0, z1, z2, z3):
+def layer(packed, feat, res, skp, kept, given, z0, z1, z2, z3, natural):
     tokens, wide = 256, 384
-    to_place = to_major(lax.axis_index("chan"), 1)
     features = feat[...].reshape(8 * OUT_AT, wide)
     conv = packed[:, 0:OUT_AT, :].reshape(8 * OUT_AT, 256)
     pre = dot(conv, features, TN)
@@ -301,8 +291,8 @@
     hidden = (filt[:, :tokens] * gate[:, :tokens]).astype(BF16)
     out_res = packed[:, OUT_AT:PACKED, 0:128].reshape(RESID, 128)
     out_skp = packed[:, OUT_AT:PACKED, 128:256].reshape(RESID, 128)
-    res_part = dot(out_res, hidden).astype(BF16)
-    skp_part = dot(out_skp, hidden).astype(BF16)
+    res_part = dot(out_res, hidden)
+    skp_part = dot(out_skp, hidden)
     grad_hidden = dot(out_res, res[...], TN) + dot(out_skp, skp[...], TN)
     grad_pre = jnp.concatenate(
         [
@@ -315,7 +305,7 @@
     now = packed[:, 64:128, :].reshape(RESID, 256)
     later = pltpu.roll(dot(prev, grad_pre), wide - DILATION, 1)[:, :tokens]
     grad_pre = grad_pre[:, :tokens]
-    in_part = (dot(now, grad_pre) + later).astype(BF16)
+    in_part = dot(now, grad_pre) + later
     conv_grad = dot(features[:, :tokens], grad_pre, NT).astype(BF16)
     res_grad = dot(res[:, :tokens], hidden, NT).astype(BF16)
     skp_grad = dot(skp[:, :tokens], hidden, NT).astype(BF16)
@@ -329,12 +319,21 @@
             even, odd = part[2 * i], part[2 * i + 1]
             kept[i, rows, cols] = jnp.where(core == 0, even, odd)
             given[i, rows, cols] = jnp.where(core == 0, odd, even)
-    parts = [dot(to_place, part).astype(BF16) for part in (res_part, skp_part, in_part)]
+    for n, part in enumerate((res_part, skp_part, in_part)):
+        for h in range(2):
+            for r in range(8):
+                natural[2 * n + h, pl.ds(r, 64, stride=8), :] = part[
+                    64 * r : 64 * r + 64, 128 * h : 128 * h + 128
+                ]
+    ch = lax.axis_index("chan")
     for k, out in enumerate((z0, z1, z2, z3)):
         for i in range(4):
-            at = 128 * k + 32 * i
+            rows = pl.ds(pl.multiple_of(32 * (ch ^ (4 * k + i)), 32), 32)
             for n in range(3):
-                out[i, 32 * n : 32 * n + 32] = parts[n][at : at + 32]
+                for h in range(2):
+                    out[i, 32 * n : 32 * n + 32, 128 * h : 128 * h + 128] = natural[
+                        2 * n + h, rows, :
+                    ].astype(BF16)
 
 
 def finish_tokens(o0, o1, o2, o3, sig, res, residual, skipped, grad_in):
@@ -347,42 +346,39 @@
 
 
 def update(owned, grads, master, first, second, *refs):
-    outs, held, old, grad, sems = refs[:3], refs[3:6], refs[6:9], refs[9], refs[10]
+    outs, held, old, grad, sems = refs[:3], refs[3:6], (*refs[6:8], first), refs[8], refs[9]
     slots = grads.shape[1]
     rows = 8 * slots
-    parts = [slice(n * rows // 4, (n + 1) * rows // 4) for n in range(4)]
+    steps = 8
+    parts = [slice(n * rows // steps, (n + 1) * rows // steps) for n in range(steps)]
     fetches = []
     for n, part in enumerate(parts):
-        for m, source in enumerate((first, second, master)):
+        for m, source in enumerate((second, master)):
             fetch = pltpu.make_async_copy(
-                source.at[part, :], old[m].at[part, :], sems.at[12 + 3 * n + m]
+                source.at[part, :], old[m].at[part, :], sems.at[3 * steps + 2 * n + m]
             )
             fetch.start()
             fetches.append(fetch)
-    to, of = iota((rows, rows), 0), iota((rows, rows), 1)
-    spread = jnp.zeros((rows, rows), jnp.bool_)
     for r in range(8):
-        inside = (of >= r * slots) & (of < (r + 1) * slots)
-        spread = spread | (inside & (to == 8 * (of - r * slots) + r))
-    spread = onehot(spread)
-    for z in range(4):
-        got = jnp.concatenate(
-            [grads[16 * (r // 4) + 4 * z + r % 4].astype(F32) for r in range(8)], 0
-        )
-        grad[:, 256 * z : 256 * z + 256] = dot(spread, got.astype(BF16))
+        for z in range(4):
+            got = grads[16 * (r // 4) + 4 * z + r % 4].astype(F32)
+            for h in range(2):
+                grad[2 * z + h, pl.ds(r, slots, stride=8), :] = got[:, 128 * h : 128 * h + 128]
+    unbias = 1.0 / (1.0 - MOMENT_DECAY**STEP)
     copies = []
     for n, part in enumerate(parts):
-        for m in range(3):
-            fetches[3 * n + m].wait()
-        old_f, old_s, old_m = (ref[part, :] for ref in old)
-        new = grad[part, :]
-        keep = n * (rows // 4) + iota((rows // 4, 1), 0) < 8 * owned[0:1, 0:1]
+        for m in range(2):
+            fetches[2 * n + m].wait()
+        old_s, old_m, old_f = (ref[part, :] for ref in old)
+        new = jnp.concatenate([grad[t, part, :] for t in range(8)], 1)
+        keep = n * (rows // steps) + iota((rows // steps, 1), 0) < 8 * owned[0:1, 0:1]
         first_new = MOMENT_DECAY * old_f + (1.0 - MOMENT_DECAY) * new
         second_new = MOMENT_DECAY * old_s + (1.0 - MOMENT_DECAY) * new * new
-        first_hat = first_new / (1.0 - MOMENT_DECAY**STEP)
-        second_hat = second_new / (1.0 - MOMENT_DECAY**STEP)
+        first_hat = first_new * unbias
+        second_hat = second_new * unbias
+        root = second_hat * lax.rsqrt(second_hat)
         stepped = old_m - STEP_RATE * (
-            first_hat / (jnp.sqrt(second_hat) + EPSILON) + WEIGHT_DECAY * old_m
+            first_hat * pl.reciprocal(root + EPSILON) + WEIGHT_DECAY * old_m
         )
         held[0][part, :] = jnp.where(keep, first_new, old_f)
         held[1][part, :] = jnp.where(keep, second_new, old_s)
@@ -410,6 +406,7 @@
 ):
     slots_dev = master.shape[0]
     slots = 16 * slots_dev
+    flat = (8 * slots_dev, GATES)
     sig, res, skp, mel = signal.T, res_cot.T, skip_cot.T, mel_frames.T
     own_row = owners.reshape(1, NBLK)
     share = [[16 * y + 4 * z + j for y in range(2) for j in range(4)] for z in range(4)]
@@ -421,11 +418,11 @@
         (sds((16, slots_dev, 256), BF16), sds((192, 128), BF16)),
         (HBM,) * 6,
         scratch=(
-            pltpu.VMEM((4, slots_dev, 8, 256), F32),
+            pltpu.VMEM((8, 8 * slots_dev, 128), F32),
             pltpu.SMEM(speaker_ids.shape, jnp.int32),
-            dma((9,)),
+            dma((13,)),
         ),
-    )(speaker_ids, master, sig, res, skp, mel)
+    )(speaker_ids, master.reshape(flat), sig, res, skp, mel)
     other = lax.ppermute(edges, "tm", [(0, 1), (1, 0)])
     arrived = lax.all_to_all(sent, "chan", 0, 0, tiled=True)
     piece = sds((PIECE, 256), BF16)
@@ -441,11 +438,11 @@
     )
     p1, p2, p3 = (swap(mine, 4 * k) for k in (1, 2, 3))
 
-    at_col, at_row, owned = call(
+    at_col, put, owned = call(
         functools.partial(place_blocks, slots_dev=slots_dev),
         (
             sds((PACKED, 128), jnp.int32),
-            sds((8, PACKED), jnp.int32),
+            sds((slots, PACKED), BF16),
             sds((8, 128), jnp.int32),
         ),
         (SMEM, VMEM, VMEM),
@@ -462,31 +459,36 @@
         (sds((8, OUT_AT, 384), BF16), cots, cots),
         (SMEM,) + (VMEM,) * 6,
         gflops=200,
+        pinned=(1,),
+        scratch=(pltpu.VMEM((7, RESID, 128), F32),),
     )(speaker_ids, mine, p1, p2, p3, mel, other)
 
     quad = sds((4, 96, 256), BF16)
     rows = sds((4, PACKED, 256), BF16)
-    kept, given, z0, z1, z2, z3 = call(layer, (rows, rows, quad, quad, quad, quad), (VMEM,) * 4)(
-        packed, *ready
-    )
+    kept, given, z0, z1, z2, z3 = call(
+        layer,
+        (rows, rows, quad, quad, quad, quad),
+        (VMEM,) * 4,
+        scratch=(pltpu.VMEM((6, RESID, 128), F32),),
+    )(packed, *ready)
 
     n = lax.axis_size("chan")
     g = call(sum_cores, (sds((PACKED, 256), BF16),) * 4, (VMEM,) * 2)(kept, swap(given, 1))
     across = [(16 * y + i, 16 * (1 - y) + (i ^ 2)) for y in range(2) for i in range(n)]
     g = (g[0], swap(g[1], 2), lax.ppermute(g[2], "tm", [(0, 1), (1, 0)]), lax.ppermute(g[3], BOTH, across))
     t1, t2, t3 = (swap(z, 4 * k) for k, z in ((1, z1), (2, z2), (3, z3)))
-    spread = call(scatter_blocks, sds((2, slots, 256), BF16), (VMEM,) * 5)(at_row, *g)
+    spread = call(scatter_blocks, sds((2, slots, 256), BF16), (VMEM,) * 5)(put, *g)
     returned = lax.all_to_all(spread.reshape(32, slots_dev, 256), BOTH, 0, 0)
     o = call(sum_units, (sds((96, 256), BF16),) * 4, (VMEM,) * 4, gflops=20)(z0, t1, t2, t3)
     o = (o[0], swap(o[1], 1), swap(o[2], 2), swap(o[3], 3))
     narrow = sds(sig.shape, F32)
     residual, skipped, grad_in = call(finish_tokens, (narrow,) * 3, (VMEM,) * 6)(*o, sig, res)
-    flat = (8 * slots_dev, GATES)
     new = call(
         update,
         (sds(flat, F32),) * 3,
-        (VMEM, VMEM, HBM, HBM, HBM),
-        scratch=(pltpu.VMEM(flat, F32),) * 7 + (dma((24,)),),
+        (VMEM, VMEM, HBM, VMEM, HBM),
+        scratch=(pltpu.VMEM(flat, F32),) * 5
+        + (pltpu.VMEM((8, flat[0], 128), F32), dma((40,))),
         out_space=HBM,
     )(
         owned,

time: 91 us -> 88.9 us (0.977)
  Pallas kernels: 18.2 us -> 16.3 us
    pallas_call x12, Pallas kernels: 18.2 us -> 16.3 us  [call(): run(*(pin(x, f) if f else x for x, f in zip(args, fixed, strict=True)))]
where the time goes in v7:
time: 88.9 us; the launch traced here: 88.5 us
  waiting for transfers between devices  31.7 us (36%)
  starting transfers between devices  29 us (33%)
  Pallas kernels  16.3 us (18%)
  blocking collectives  10.7 us (12%)
    ppermute x14, waiting for transfers between devices, swap(): return lax.ppermute(x, 'chan', [(i, i ^ k) for i in range(n)])  19.1 us
    pallas_call x12, Pallas kernels, call(): run(*(pin(x, f) if f else x for x, f in zip(args, fixed, strict=True)))  16.3 us
    ppermute x14, starting transfers between devices, swap(): return lax.ppermute(x, 'chan', [(i, i ^ k) for i in range(n)])  13.9 us
    all_gather x1, blocking collectives, local(): packed = lax.all_gather(gathered, BOTH, axis_index_groups=share)  10.7 us
    all_to_all x1, waiting for transfers between devices, local(): returned = lax.all_to_all(spread.reshape(32, slots_dev, 256), BOTH, 0, 0)  8.62 us
    all_to_all x1, starting transfers between devices, local(): arrived = lax.all_to_all(sent, 'chan', 0, 0, tiled=True)  5.95 us
    ppermute x1, waiting for transfers between devices, local(): lax.ppermute(g[2], 'tm', [(0, 1), (1, 0)])  3.97 us
    all_to_all x1, starting transfers between devices, local(): returned = lax.all_to_all(spread.reshape(32, slots_dev, 256), BOTH, 0, 0)  3.57 us
  transfers between devices with their start and end apart: 19, of which 9 were waited for; matrix products, arithmetic and copies ran while one was open for 0% of the time, Pallas kernels for 7%

profile of v7, /device:TPU:0, one launch (start us, length us, event | category | flops | bytes accessed | tf_op | source)
XLA Modules:
  0.0 88.5 jit_solution(264768905159188011)
XLA Ops:
  0.6 2.3 %shard_map.136 = (bf16[16,40,256]{2,1,0:T(8,128)(2,1)}, bf16[192,128]{1,0:T(8,128)(2,1)S(1)}) custom-call(s32[8]{0:T(128)} %spk.1, f32[320,1024]{1,0:T(8,128)} %bitcast.26, bf16[32,1024]{1,0:T(8,128)(2,1)} %bitcast.18, bf16[32,1024]{1,0:T(8,128)(2,1)} %bitcast.21, bf16[32,1024]{1,0:T(8,128)(2,1)} %bitcast.29, bf16[80,1024]{1,0:T(8,128)(2,1)} %bitcast.24), custom_call_target="tpu_custom_call" | custom-call | bytes 1048576 | tf_op jit(solution)/shard_map/pallas_call | solution.py:74
  2.9 3.0 %collective-permute-start = (bf16[192,128]{1,0:T(8,128)(2,1)S(1)}, bf16[192,128]{1,0:T(8,128)(2,1)S(1)}, u32[]{:S(2)}, u32[]{:S(2)}) collective-permute-start(bf16[192,128]{1,0:T(8,128)(2,1)S(1)} %get-tuple-element.40), channel_id=1, source_target_pairs={{0,16},{16,0},{1,17},{17,1},{2,18},{18,2},{3,19},{19,3},{4,20},{20... | collective-permute-start | bytes 147464 | tf_op jit(solution)/shard_map/ppermute | solution.py:426
  6.0 6.0 %all-to-all-start = ((bf16[16,40,256]{2,1,0:T(8,128)(2,1)}), bf16[16,40,256]{2,1,0:T(8,128)(2,1)}, u32[]{:S(2)}, u32[]{:S(2)}) async-start(bf16[16,40,256]{2,1,0:T(8,128)(2,1)} %get-tuple-element.42), calls=%async_computation | async-start | bytes 655360 | tf_op jit(solution)/shard_map/all_to_all | solution.py:427
  12.0 1.2 %shard_map.138 = (bf16[112,256]{1,0:T(8,128)(2,1)S(1)}, bf16[112,256]{1,0:T(8,128)(2,1)S(1)}, bf16[112,256]{1,0:T(8,128)(2,1)S(1)}, bf16[112,256]{1,0:T(8,128)(2,1)S(1)}) custom-call(bf16[32,1024]{1,0:T(8,128)(2,1)} %bitcast.19, bf16[32,1024]{1,0:T(8,128)(2,1)} %bitcast.22, bf16[32,1024]{1,0:T(8,128)(2,1)} %bitcast.30, ...), custom_call_target="tpu_custom_call" | custom-call | flops 199999995904 | bytes 1048576 | tf_op jit(solution)/shard_map/pallas_call | solution.py:74
  13.5 1.7 %collective-permute-start.2 = (bf16[112,256]{1,0:T(8,128)(2,1)S(1)}, bf16[112,256]{1,0:T(8,128)(2,1)S(1)}, u32[]{:S(2)}, u32[]{:S(2)}) collective-permute-start(bf16[112,256]{1,0:T(8,128)(2,1)S(1)} %get-tuple-element.45), channel_id=1, source_target_pairs={{0,2},{1,3},{2,0},{3,1},{4,6},{5,7},{6,4},{7,5},{8,10},{9,11},{10,... | collective-permute-start | bytes 172040 | tf_op jit(solution)/shard_map/ppermute | solution.py:401
  15.2 1.0 %shard_map.137 = (s32[224,128]{1,0:T(8,128)S(1)}, bf16[640,224]{1,0:T(8,128)(2,1)S(1)}, s32[8,128]{1,0:T(8,128)S(1)}) custom-call(s32[8]{0:T(128)S(1)} %copy-done.4, s32[1,320]{1,0:T(1,128)S(1)} %reshape.40.owners, bf16[192,128]{1,0:T(8,128)(2,1)S(1)} %collective-permute-done.other), custom_call_target="tpu_custom_call" | custom-call | bytes 1048576 | tf_op jit(solution)/shard_map/pallas_call | solution.py:74
  16.3 2.5 %collective-permute-done.2.o2 = bf16[112,256]{1,0:T(8,128)(2,1)S(1)} collective-permute-done((bf16[112,256]{1,0:T(8,128)(2,1)S(1)}, bf16[112,256]{1,0:T(8,128)(2,1)S(1)}, u32[]{:S(2)}, u32[]{:S(2)}) %collective-permute-start.2) | collective-permute-done | bytes 57376 | tf_op jit(solution)/shard_map/ppermute | solution.py:401
  18.8 1.4 %collective-permute-done.3.o3 = bf16[112,256]{1,0:T(8,128)(2,1)S(1)} collective-permute-done((bf16[112,256]{1,0:T(8,128)(2,1)S(1)}, bf16[112,256]{1,0:T(8,128)(2,1)S(1)}, u32[]{:S(2)}, u32[]{:S(2)}) %collective-permute-start.3) | collective-permute-done | bytes 57376 | tf_op jit(solution)/shard_map/ppermute | solution.py:401
  20.2 0.7 shard_map.139.p0
  20.9 3.5 %collective-permute-start.6 = (bf16[400,256]{1,0:T(8,128)(2,1)}, bf16[400,256]{1,0:T(8,128)(2,1)}, u32[]{:S(2)}, u32[]{:S(2)}) collective-permute-start(bf16[400,256]{1,0:T(8,128)(2,1)} %shard_map.139.p0), channel_id=1, source_target_pairs={{0,12},{1,13},{2,14},{3,15},{4,8},{5,9},{6,10},{7,11},{8,4},{9,5},... | collective-permute-start | bytes 614408 | tf_op jit(solution)/shard_map/ppermute | solution.py:401
  24.6 0.7 collective-permute-start.4
  25.3 1.5 %shard_map.140 = bf16[224,256]{1,0:T(8,128)(2,1)S(1)} custom-call(s32[224,128]{1,0:T(8,128)S(1)} %get-tuple-element.41.at_col, bf16[640,256]{1,0:T(8,128)(2,1)} %bitcast.5.slots), custom_call_target="tpu_custom_call" | custom-call | flops 199999995904 | bytes 1048576 | tf_op jit(solution)/shard_map/pallas_call | solution.py:74
  26.7 10.7 %all-gather = bf16[1792,256]{1,0:T(8,128)(2,1)S(1)} all-gather(bf16[224,256]{1,0:T(8,128)(2,1)S(1)} %shard_map.140), channel_id=2, replica_groups={{0,1,2,3,16,17,18,19},{4,5,6,7,20,21,22,23},{8,9,10,11,24,25,26,27},{12..., dimensions={0}, use_global_device_ids=true | all-gather | bytes 1032192 | tf_op jit(solution)/shard_map/all_gather | solution.py:454
  37.4 6.0 %collective-permute-done.5.p2 = bf16[400,256]{1,0:T(8,128)(2,1)} collective-permute-done((bf16[400,256]{1,0:T(8,128)(2,1)}, bf16[400,256]{1,0:T(8,128)(2,1)}, u32[]{:S(2)}, u32[]{:S(2)}) %collective-permute-start.5) | collective-permute-done | bytes 204832 | tf_op jit(solution)/shard_map/ppermute | solution.py:401
  43.5 1.9 %shard_map.141 = (bf16[8,160,384]{2,1,0:T(8,128)(2,1)S(1)}, bf16[512,384]{1,0:T(8,128)(2,1)S(1)}, bf16[512,384]{1,0:T(8,128)(2,1)S(1)}) custom-call(s32[8]{0:T(128)S(1)} %copy-done.5, bf16[400,256]{1,0:T(8,128)(2,1)} %shard_map.139.p0, bf16[400,256]{1,0:T(8,128)(2,1)} %collective-permute-done.4.p1, bf16[400,256]{1,0:T(8,128)(2,1)} %collective-permute-done.5.p2, ...), custom_call_target="tpu_custom_call" | custom-call | flops 199999995904 | bytes 1048576 | tf_op jit(solution)/shard_map/pallas_call | solution.py:74
  45.4 2.0 %shard_map.142 = (bf16[4,224,256]{2,1,0:T(8,128)(2,1)S(1)}, bf16[4,224,256]{2,1,0:T(8,128)(2,1)S(1)}, bf16[4,96,256]{2,1,0:T(8,128)(2,1)S(1)}, bf16[4,96,256]{2,...) custom-call(bf16[8,224,256]{2,1,0:T(8,128)(2,1)S(1)} %bitcast.16, ...), custom_call_target="tpu_custom_call" | custom-call | bytes 1048576 | tf_op jit(solution)/shard_map/pallas_call | solution.py:74
  47.5 1.8 %collective-permute-done.13.got = bf16[4,224,256]{2,1,0:T(8,128)(2,1)S(1)} collective-permute-done((bf16[4,224,256]{2,1,0:T(8,128)(2,1)S(1)}, bf16[4,224,256]{2,1,0:T(8,128)(2,1)S(1)}, u32[]{:S(2)}, u32[]{:S(2)}) %collective-permute-start.13) | collective-permute-done | bytes 458784 | tf_op jit(solution)/shard_map/ppermute | solution.py:401
  49.4 1.0 %collective-permute-start.14 = (bf16[224,256]{1,0:T(8,128)(2,1)S(1)}, bf16[224,256]{1,0:T(8,128)(2,1)S(1)}, u32[]{:S(2)}, u32[]{:S(2)}) collective-permute-start(bf16[224,256]{1,0:T(8,128)(2,1)S(1)} %get-tuple-element.68), channel_id=1, source_target_pairs={{0,2},{1,3},{2,0},{3,1},{4,6},{5,7},{6,4},{7,5},{8,10},{9,11},{10,... | collective-permute-start | bytes 344072 | tf_op jit(solution)/shard_map/ppermute | solution.py:401
  50.4 3.1 %collective-permute-start.8 = (bf16[4,96,256]{2,1,0:T(8,128)(2,1)S(1)}, bf16[4,96,256]{2,1,0:T(8,128)(2,1)S(1)}, u32[]{:S(2)}, u32[]{:S(2)}) collective-permute-start(bf16[4,96,256]{2,1,0:T(8,128)(2,1)S(1)} %get-tuple-element.54), channel_id=1, source_target_pairs={{0,8},{1,9},{2,10},{3,11},{4,12},{5,13},{6,14},{7,15},{8,0},{9,1},... | collective-permute-start | bytes 589832 | tf_op jit(solution)/shard_map/ppermute | solution.py:401
  53.5 1.3 %collective-permute-start.9 = (bf16[4,96,256]{2,1,0:T(8,128)(2,1)S(1)}, bf16[4,96,256]{2,1,0:T(8,128)(2,1)S(1)}, u32[]{:S(2)}, u32[]{:S(2)}) collective-permute-start(bf16[4,96,256]{2,1,0:T(8,128)(2,1)S(1)} %get-tuple-element.55), channel_id=1, source_target_pairs={{0,12},{1,13},{2,14},{3,15},{4,8},{5,9},{6,10},{7,11},{8,4},{9,5},... | collective-permute-start | bytes 589832 | tf_op jit(solution)/shard_map/ppermute | solution.py:401
  55.3 2.0 %collective-permute-start.16 = (bf16[224,256]{1,0:T(8,128)(2,1)S(1)}, bf16[224,256]{1,0:T(8,128)(2,1)S(1)}, u32[]{:S(2)}, u32[]{:S(2)}) collective-permute-start(bf16[224,256]{1,0:T(8,128)(2,1)S(1)} %get-tuple-element.70), channel_id=1, source_target_pairs={{0,18},{1,19},{2,16},{3,17},{4,22},{5,23},{6,20},{7,21},{8,26},{9,... | collective-permute-start | bytes 344072 | tf_op jit(solution)/shard_map/ppermute | solution.py:478
  57.4 4.0 %collective-permute-done.15.p2 = bf16[224,256]{1,0:T(8,128)(2,1)S(1)} collective-permute-done((bf16[224,256]{1,0:T(8,128)(2,1)S(1)}, bf16[224,256]{1,0:T(8,128)(2,1)S(1)}, u32[]{:S(2)}, u32[]{:S(2)}) %collective-permute-start.15) | collective-permute-done | bytes 114720 | tf_op jit(solution)/shard_map/ppermute | solution.py:478
  61.3 1.3 %shard_map.146 = bf16[2,640,256]{2,1,0:T(8,128)(2,1)} custom-call(bf16[640,224]{1,0:T(8,128)(2,1)S(1)} %get-tuple-element.64.put, bf16[224,256]{1,0:T(8,128)(2,1)S(1)} %get-tuple-element.67.p0, bf16[224,256]{1,0:T(8,128)(2,1)S(1)} %collective-permute-done.14.p1, bf16[224,256]{1,0:T(8,128)(2,1)S(1)} %collective-permute-done.15.p2, ...), custom_call_target="tpu_custom_call" | custom-call | bytes 1048576 | tf_op jit(solution)/shard_map/pallas_call | solution.py:74
  62.6 3.6 %all-to-all-start.1 = ((bf16[32,40,256]{2,1,0:T(8,128)(2,1)}), bf16[32,40,256]{2,1,0:T(8,128)(2,1)S(1)}, u32[]{:S(2)}, u32[]{:S(2)}) async-start(bf16[32,40,256]{2,1,0:T(8,128)(2,1)} %bitcast.10), calls=%async_computation.1 | async-start | bytes 1310720 | tf_op jit(solution)/shard_map/all_to_all | solution.py:481
  66.2 1.5 %collective-permute-done.8.z2 = bf16[4,96,256]{2,1,0:T(8,128)(2,1)S(1)} collective-permute-done((bf16[4,96,256]{2,1,0:T(8,128)(2,1)S(1)}, bf16[4,96,256]{2,1,0:T(8,128)(2,1)S(1)}, u32[]{:S(2)}, u32[]{:S(2)}) %collective-permute-start.8) | collective-permute-done | bytes 196640 | tf_op jit(solution)/shard_map/ppermute | solution.py:401
  67.9 1.0 %collective-permute-start.11 = (bf16[96,256]{1,0:T(8,128)(2,1)S(1)}, bf16[96,256]{1,0:T(8,128)(2,1)S(1)}, u32[]{:S(2)}, u32[]{:S(2)}) collective-permute-start(bf16[96,256]{1,0:T(8,128)(2,1)S(1)} %get-tuple-element.58), channel_id=1, source_target_pairs={{0,2},{1,3},{2,0},{3,1},{4,6},{5,7},{6,4},{7,5},{8,10},{9,11},{10,... | collective-permute-start | bytes 147464 | tf_op jit(solution)/shard_map/ppermute | solution.py:401
  68.9 0.9 %collective-permute-start.12 = (bf16[96,256]{1,0:T(8,128)(2,1)S(1)}, bf16[96,256]{1,0:T(8,128)(2,1)S(1)}, u32[]{:S(2)}, u32[]{:S(2)}) collective-permute-start(bf16[96,256]{1,0:T(8,128)(2,1)S(1)} %get-tuple-element.59), channel_id=1, source_target_pairs={{0,3},{1,2},{2,1},{3,0},{4,7},{5,6},{6,5},{7,4},{8,11},{9,10},{10,... | collective-permute-start | bytes 147464 | tf_op jit(solution)/shard_map/ppermute | solution.py:401
  69.8 3.6 %collective-permute-done.11.o2 = bf16[96,256]{1,0:T(8,128)(2,1)S(1)} collective-permute-done((bf16[96,256]{1,0:T(8,128)(2,1)S(1)}, bf16[96,256]{1,0:T(8,128)(2,1)S(1)}, u32[]{:S(2)}, u32[]{:S(2)}) %collective-permute-start.11) | collective-permute-done | bytes 49184 | tf_op jit(solution)/shard_map/ppermute | solution.py:401
  73.4 2.2 %collective-permute-done.12.o3 = bf16[96,256]{1,0:T(8,128)(2,1)S(1)} collective-permute-done((bf16[96,256]{1,0:T(8,128)(2,1)S(1)}, bf16[96,256]{1,0:T(8,128)(2,1)S(1)}, u32[]{:S(2)}, u32[]{:S(2)}) %collective-permute-start.12) | collective-permute-done | bytes 49184 | tf_op jit(solution)/shard_map/ppermute | solution.py:401
  75.6 0.8 shard_map.144
  76.4 8.6 %all-to-all-done.1.grads = bf16[32,40,256]{2,1,0:T(8,128)(2,1)S(1)} async-done(((bf16[32,40,256]{2,1,0:T(8,128)(2,1)}), bf16[32,40,256]{2,1,0:T(8,128)(2,1)S(1)}, u32[]{:S(2)}, u32[]{:S(2)}) %all-to-all-start.1) | async-done | bytes 655392 | tf_op jit(solution)/shard_map/all_to_all | solution.py:481
  85.0 3.5 %shard_map.147 = (f32[320,1024]{1,0:T(8,128)}, f32[320,1024]{1,0:T(8,128)}, f32[320,1024]{1,0:T(8,128)}) custom-call(s32[8,128]{1,0:T(8,128)S(1)} %get-tuple-element.63.owned, bf16[32,40,256]{2,1,0:T(8,128)(2,1)S(1)} %all-to-all-done.1.grads, f32[320,1024]{1,0:T(8,128)} %bitcast.27, f32[320,1024]{1,0:T(8,128)S(1)} %bitcast.17, f32[320,1024]{1,0:T(8,128)} %bitcast.28), custom_call_target="tpu_custom_call" | custom-call | bytes 1048576 | tf_op jit(solution)/shard_map/pallas_call | solution.py:74
  (34 shorter events, 1.6 us)
Async XLA Ops:
  2.9 9.0 %collective-permute-start = (bf16[192,128]{1,0:T(8,128)(2,1)S(1)}, bf16[192,128]{1,0:T(8,128)(2,1)S(1)}, u32[]{:S(2)}, u32[]{:S(2)}) collective-permute-start(bf16[192,128]{1,0:T(8,128)(2,1)S(1)} %get-tuple-element.40), channel_id=1, source_target_pairs={{0,16},{16,0},{1,17},{17,1},{2,18},{18,2},{3,19},{19,3},{4,20},{20... | collective-permute-start | bytes 147464 | tf_op jit(solution)/shard_map/ppermute | solution.py:426
  6.0 19.3 %all-to-all-start = ((bf16[16,40,256]{2,1,0:T(8,128)(2,1)}), bf16[16,40,256]{2,1,0:T(8,128)(2,1)}, u32[]{:S(2)}, u32[]{:S(2)}) async-start(bf16[16,40,256]{2,1,0:T(8,128)(2,1)} %get-tuple-element.42), calls=%async_computation | async-start | bytes 655360 | tf_op jit(solution)/shard_map/all_to_all | solution.py:427
  11.9 3.3 %copy-start.6 = (s32[320]{0:T(512)S(1)}, s32[320]{0:T(512)}, u32[]{:S(2)}) copy-start(s32[320]{0:T(512)} %param.12) | copy-start | bytes 3844
  11.9 3.3 %copy-start.4 = (s32[8]{0:T(128)S(1)}, s32[8]{0:T(128)}, u32[]{:S(2)}) copy-start(s32[8]{0:T(128)} %spk.1) | copy-start | bytes 100
  13.1 3.1 %collective-permute-start.1 = (bf16[112,256]{1,0:T(8,128)(2,1)S(1)}, bf16[112,256]{1,0:T(8,128)(2,1)S(1)}, u32[]{:S(2)}, u32[]{:S(2)}) collective-permute-start(bf16[112,256]{1,0:T(8,128)(2,1)S(1)} %get-tuple-element.44), channel_id=1, source_target_pairs={{0,1},{1,0},{2,3},{3,2},{4,5},{5,4},{6,7},{7,6},{8,9},{9,8},{10,11... | collective-permute-start | bytes 172040 | tf_op jit(solution)/shard_map/ppermute | solution.py:401
  13.5 5.3 %collective-permute-start.2 = (bf16[112,256]{1,0:T(8,128)(2,1)S(1)}, bf16[112,256]{1,0:T(8,128)(2,1)S(1)}, u32[]{:S(2)}, u32[]{:S(2)}) collective-permute-start(bf16[112,256]{1,0:T(8,128)(2,1)S(1)} %get-tuple-element.45), channel_id=1, source_target_pairs={{0,2},{1,3},{2,0},{3,1},{4,6},{5,7},{6,4},{7,5},{8,10},{9,11},{10,... | collective-permute-start | bytes 172040 | tf_op jit(solution)/shard_map/ppermute | solution.py:401
  15.2 4.9 %collective-permute-start.3 = (bf16[112,256]{1,0:T(8,128)(2,1)S(1)}, bf16[112,256]{1,0:T(8,128)(2,1)S(1)}, u32[]{:S(2)}, u32[]{:S(2)}) collective-permute-start(bf16[112,256]{1,0:T(8,128)(2,1)S(1)} %get-tuple-element.46), channel_id=1, source_target_pairs={{0,3},{1,2},{2,1},{3,0},{4,7},{5,6},{6,5},{7,4},{8,11},{9,10},{10,... | collective-permute-start | bytes 172040 | tf_op jit(solution)/shard_map/ppermute | solution.py:401
  20.9 16.6 %collective-permute-start.6 = (bf16[400,256]{1,0:T(8,128)(2,1)}, bf16[400,256]{1,0:T(8,128)(2,1)}, u32[]{:S(2)}, u32[]{:S(2)}) collective-permute-start(bf16[400,256]{1,0:T(8,128)(2,1)} %shard_map.139.p0), channel_id=1, source_target_pairs={{0,12},{1,13},{2,14},{3,15},{4,8},{5,9},{6,10},{7,11},{8,4},{9,5},... | collective-permute-start | bytes 614408 | tf_op jit(solution)/shard_map/ppermute | solution.py:401
  24.3 19.1 %collective-permute-start.5 = (bf16[400,256]{1,0:T(8,128)(2,1)}, bf16[400,256]{1,0:T(8,128)(2,1)}, u32[]{:S(2)}, u32[]{:S(2)}) collective-permute-start(bf16[400,256]{1,0:T(8,128)(2,1)} %shard_map.139.p0), channel_id=1, source_target_pairs={{0,8},{1,9},{2,10},{3,11},{4,12},{5,13},{6,14},{7,15},{8,0},{9,1},... | collective-permute-start | bytes 614408 | tf_op jit(solution)/shard_map/ppermute | solution.py:401
  24.6 18.9 %collective-permute-start.4 = (bf16[400,256]{1,0:T(8,128)(2,1)}, bf16[400,256]{1,0:T(8,128)(2,1)}, u32[]{:S(2)}, u32[]{:S(2)}) collective-permute-start(bf16[400,256]{1,0:T(8,128)(2,1)} %shard_map.139.p0), channel_id=1, source_target_pairs={{0,4},{1,5},{2,6},{3,7},{4,0},{5,1},{6,2},{7,3},{8,12},{9,13},{10,... | collective-permute-start | bytes 614408 | tf_op jit(solution)/shard_map/ppermute | solution.py:401
  25.3 18.2 %copy-start.3 = (bf16[1024,80]{0,1:T(8,128)(2,1)S(1)}, bf16[1024,80]{0,1:T(8,128)(2,1)}, u32[]{:S(2)}) copy-start(bf16[1024,80]{0,1:T(8,128)(2,1)} %param.10) | copy-start | bytes 491524
  25.3 18.2 %copy-start.5 = (s32[8]{0:T(128)S(1)}, s32[8]{0:T(128)}, u32[]{:S(2)}) copy-start(s32[8]{0:T(128)} %spk.1) | copy-start | bytes 100
  47.4 1.9 %collective-permute-start.13 = (bf16[4,224,256]{2,1,0:T(8,128)(2,1)S(1)}, bf16[4,224,256]{2,1,0:T(8,128)(2,1)S(1)}, u32[]{:S(2)}, u32[]{:S(2)}) collective-permute-start(bf16[4,224,256]{2,1,0:T(8,128)(2,1)S(1)} %get-tuple-element.66), channel_id=1, source_target_pairs={{0,1},{1,0},{2,3},{3,2},{4,5},{5,4},{6,7},{7,6},{8,9},{9,8},{10,11... | collective-permute-start | bytes 1376264 | tf_op jit(solution)/shard_map/ppermute | solution.py:401
  49.4 5.9 %collective-permute-start.14 = (bf16[224,256]{1,0:T(8,128)(2,1)S(1)}, bf16[224,256]{1,0:T(8,128)(2,1)S(1)}, u32[]{:S(2)}, u32[]{:S(2)}) collective-permute-start(bf16[224,256]{1,0:T(8,128)(2,1)S(1)} %get-tuple-element.68), channel_id=1, source_target_pairs={{0,2},{1,3},{2,0},{3,1},{4,6},{5,7},{6,4},{7,5},{8,10},{9,11},{10,... | collective-permute-start | bytes 344072 | tf_op jit(solution)/shard_map/ppermute | solution.py:401
  50.4 15.8 %collective-permute-start.7 = (bf16[4,96,256]{2,1,0:T(8,128)(2,1)S(1)}, bf16[4,96,256]{2,1,0:T(8,128)(2,1)S(1)}, u32[]{:S(2)}, u32[]{:S(2)}) collective-permute-start(bf16[4,96,256]{2,1,0:T(8,128)(2,1)S(1)} %get-tuple-element.53), channel_id=1, source_target_pairs={{0,4},{1,5},{2,6},{3,7},{4,0},{5,1},{6,2},{7,3},{8,12},{9,13},{10,... | collective-permute-start | bytes 589832 | tf_op jit(solution)/shard_map/ppermute | solution.py:401
  50.4 17.3 %collective-permute-start.8 = (bf16[4,96,256]{2,1,0:T(8,128)(2,1)S(1)}, bf16[4,96,256]{2,1,0:T(8,128)(2,1)S(1)}, u32[]{:S(2)}, u32[]{:S(2)}) collective-permute-start(bf16[4,96,256]{2,1,0:T(8,128)(2,1)S(1)} %get-tuple-element.54), channel_id=1, source_target_pairs={{0,8},{1,9},{2,10},{3,11},{4,12},{5,13},{6,14},{7,15},{8,0},{9,1},... | collective-permute-start | bytes 589832 | tf_op jit(solution)/shard_map/ppermute | solution.py:401
  53.5 14.2 %collective-permute-start.9 = (bf16[4,96,256]{2,1,0:T(8,128)(2,1)S(1)}, bf16[4,96,256]{2,1,0:T(8,128)(2,1)S(1)}, u32[]{:S(2)}, u32[]{:S(2)}) collective-permute-start(bf16[4,96,256]{2,1,0:T(8,128)(2,1)S(1)} %get-tuple-element.55), channel_id=1, source_target_pairs={{0,12},{1,13},{2,14},{3,15},{4,8},{5,9},{6,10},{7,11},{8,4},{9,5},... | collective-permute-start | bytes 589832 | tf_op jit(solution)/shard_map/ppermute | solution.py:401
  54.8 6.5 %collective-permute-start.15 = (bf16[224,256]{1,0:T(8,128)(2,1)S(1)}, bf16[224,256]{1,0:T(8,128)(2,1)S(1)}, u32[]{:S(2)}, u32[]{:S(2)}) collective-permute-start(bf16[224,256]{1,0:T(8,128)(2,1)S(1)} %get-tuple-element.69), channel_id=1, source_target_pairs={{0,16},{16,0},{1,17},{17,1},{2,18},{18,2},{3,19},{19,3},{4,20},{20... | collective-permute-start | bytes 344072 | tf_op jit(solution)/shard_map/ppermute | solution.py:478
  55.3 6.0 %collective-permute-start.16 = (bf16[224,256]{1,0:T(8,128)(2,1)S(1)}, bf16[224,256]{1,0:T(8,128)(2,1)S(1)}, u32[]{:S(2)}, u32[]{:S(2)}) collective-permute-start(bf16[224,256]{1,0:T(8,128)(2,1)S(1)} %get-tuple-element.70), channel_id=1, source_target_pairs={{0,18},{1,19},{2,16},{3,17},{4,22},{5,23},{6,20},{7,21},{8,26},{9,... | collective-permute-start | bytes 344072 | tf_op jit(solution)/shard_map/ppermute | solution.py:478
  62.6 22.4 %all-to-all-start.1 = ((bf16[32,40,256]{2,1,0:T(8,128)(2,1)}), bf16[32,40,256]{2,1,0:T(8,128)(2,1)S(1)}, u32[]{:S(2)}, u32[]{:S(2)}) async-start(bf16[32,40,256]{2,1,0:T(8,128)(2,1)} %bitcast.10), calls=%async_computation.1 | async-start | bytes 1310720 | tf_op jit(solution)/shard_map/all_to_all | solution.py:481
  67.7 7.9 %copy-start.1 = (bf16[1024,32]{0,1:T(8,128)(2,1)S(1)}, bf16[1024,32]{0,1:T(8,128)(2,1)}, u32[]{:S(2)}) copy-start(bf16[1024,32]{0,1:T(8,128)(2,1)} %param.9) | copy-start | bytes 196612
  67.7 7.9 %copy-start.2 = (bf16[1024,32]{0,1:T(8,128)(2,1)S(1)}, bf16[1024,32]{0,1:T(8,128)(2,1)}, u32[]{:S(2)}) copy-start(bf16[1024,32]{0,1:T(8,128)(2,1)} %param.16) | copy-start | bytes 196612
  67.7 17.3 %copy-start = (f32[40,8,1024]{2,1,0:T(8,128)S(1)}, f32[40,8,1024]{2,1,0:T(8,128)}, u32[]{:S(2)}) copy-start(f32[40,8,1024]{2,1,0:T(8,128)} %param.14) | copy-start | bytes 3932164
  67.8 1.9 %collective-permute-start.10 = (bf16[96,256]{1,0:T(8,128)(2,1)S(1)}, bf16[96,256]{1,0:T(8,128)(2,1)S(1)}, u32[]{:S(2)}, u32[]{:S(2)}) collective-permute-start(bf16[96,256]{1,0:T(8,128)(2,1)S(1)} %get-tuple-element.57), channel_id=1, source_target_pairs={{0,1},{1,0},{2,3},{3,2},{4,5},{5,4},{6,7},{7,6},{8,9},{9,8},{10,11... | collective-permute-start | bytes 147464 | tf_op jit(solution)/shard_map/ppermute | solution.py:401
  67.9 5.5 %collective-permute-start.11 = (bf16[96,256]{1,0:T(8,128)(2,1)S(1)}, bf16[96,256]{1,0:T(8,128)(2,1)S(1)}, u32[]{:S(2)}, u32[]{:S(2)}) collective-permute-start(bf16[96,256]{1,0:T(8,128)(2,1)S(1)} %get-tuple-element.58), channel_id=1, source_target_pairs={{0,2},{1,3},{2,0},{3,1},{4,6},{5,7},{6,4},{7,5},{8,10},{9,11},{10,... | collective-permute-start | bytes 147464 | tf_op jit(solution)/shard_map/ppermute | solution.py:401
  68.9 6.7 %collective-permute-start.12 = (bf16[96,256]{1,0:T(8,128)(2,1)S(1)}, bf16[96,256]{1,0:T(8,128)(2,1)S(1)}, u32[]{:S(2)}, u32[]{:S(2)}) collective-permute-start(bf16[96,256]{1,0:T(8,128)(2,1)S(1)} %get-tuple-element.59), channel_id=1, source_target_pairs={{0,3},{1,2},{2,1},{3,0},{4,7},{5,6},{6,5},{7,4},{8,11},{9,10},{10,... | collective-permute-start | bytes 147464 | tf_op jit(solution)/shard_map/ppermute | solution.py:401

commit v8 on v7

--- a/solution.py
+++ b/solution.py
@@ -79,28 +79,15 @@
     return onehot(natural == 2 * (split & 127) + (split >> 7))
 
 
-def begin(speakers, master, sig, res, skp, mel, sent, edges, strips, spk, sems):
+def pack_weights(master, sent, strips, sems):
     half = lax.axis_index("tm")
     slots = sent.shape[1]
-    cut = pl.ds(pl.multiple_of((1 - half) * 896, 128), 128)
-    tiles = []
-    for n, part in enumerate((sig, res, skp, mel)):
-        to = edges.at[32 * n : 32 * n + part.shape[0], :]
-        tiles.append(pltpu.make_async_copy(part.at[:, cut], to, sems.at[8 + n]))
     copies = []
     for t in range(8):
         part = master.at[:, 128 * t : 128 * t + 128]
         copies.append(pltpu.make_async_copy(part, strips.at[t], sems.at[t]))
-    names = pltpu.make_async_copy(speakers, spk, sems.at[12])
-    for copy in (names, *copies, *tiles):
+    for copy in copies:
         copy.start()
-    names.wait()
-    row, lane = iota((16, 128), 0), iota((16, 128), 1)
-    table = jnp.zeros((16, 128), jnp.int32)
-    for s in range(8):
-        code = jnp.where(row == 0, spk[s] >> 3, spk[s] & 7)
-        table = jnp.where((lane == s) & (row < 2), code, table)
-    edges[176:192, :] = table.astype(F32).astype(BF16)
     for t in range(8):
         copies[t].wait()
         lanes = slice(128 * (t % 2), 128 * (t % 2) + 128)
@@ -108,20 +95,33 @@
             low = strips[t, pl.ds(j, slots, stride=8), :]
             high = strips[t, pl.ds(4 + j, slots, stride=8), :]
             sent[4 * (t // 2) + j, :, lanes] = jnp.where(half == 0, low, high).astype(BF16)
-    for tile in tiles:
-        tile.wait()
-
-
-def pack_tokens(sig_hbm, res_hbm, skp_hbm, other, o0, o1, o2, o3, held, sems):
+
+
+def begin(speakers, sig, res, skp, mel, acts, edges, spk, sems):
+    cut = pl.ds(pl.multiple_of((1 - lax.axis_index("tm")) * 896, 128), 128)
     copies = [
-        pltpu.make_async_copy(part, held.at[n], sems.at[n])
-        for n, part in enumerate((sig_hbm, res_hbm, skp_hbm))
+        pltpu.make_async_copy(speakers, spk, sems.at[0]),
+        pltpu.make_async_copy(mel.at[:, cut], edges.at[96:176, :], sems.at[1]),
     ]
+    for n, part in enumerate((sig, res, skp)):
+        copies.append(pltpu.make_async_copy(part, acts.at[n], sems.at[2 + n]))
     for copy in copies:
         copy.start()
-    for copy in copies:
+    copies[0].wait()
+    row, lane = iota((16, 128), 0), iota((16, 128), 1)
+    table = jnp.zeros((16, 128), jnp.int32)
+    for s in range(8):
+        code = jnp.where(row == 0, spk[s] >> 3, spk[s] & 7)
+        table = jnp.where((lane == s) & (row < 2), code, table)
+    edges[176:192, :] = table.astype(F32).astype(BF16)
+    for copy in copies[1:]:
         copy.wait()
-    sig, res, skp = (held.at[n] for n in range(3))
+    for n in range(3):
+        edges[32 * n : 32 * n + 32, :] = acts[n, :, cut]
+
+
+def pack_tokens(acts, other, o0, o1, o2, o3):
+    sig, res, skp = (acts.at[n] for n in range(3))
     half, j = lax.axis_index("tm"), lax.axis_index("chan") & 3
     outs = (o0, o1, o2, o3)
     parts = (sig, res, skp)
@@ -226,7 +226,7 @@
         ).astype(BF16)
 
 
-def prepare(spk, p0, p1, p2, p3, mel, other, features, res, skp, natural):
+def layer(spk, packed, p0, p1, p2, p3, mel, other, kept, given, hidden_out, grad_out, feat, res, skp, natural):
     half, ch = lax.axis_index("tm"), lax.axis_index("chan")
     j = ch & 3
     got = (p0, p1, p2, p3)
@@ -275,14 +275,10 @@
         jnp.where(lane < 2 * SEG, spk[2 * j + 1] & 7, jnp.broadcast_to(beyond, (16, wide))),
     )
     for r in range(8):
-        features[r, 0:64] = shifted[64 * r : 64 * r + 64]
-        features[r, 64:128] = sig[64 * r : 64 * r + 64]
-        features[r, 128:144] = mels[16 * r : 16 * r + 16]
-        features[r, 144:160] = onehot((row == seg + (lane >> 7)) & (sub == r))
-
-
-def layer(packed, feat, res, skp, kept, given, z0, z1, z2, z3, natural):
-    tokens, wide = 256, 384
+        feat[r, 0:64] = shifted[64 * r : 64 * r + 64]
+        feat[r, 64:128] = sig[64 * r : 64 * r + 64]
+        feat[r, 128:144] = mels[16 * r : 16 * r + 16]
+        feat[r, 144:160] = onehot((row == seg + (lane >> 7)) & (sub == r))
     features = feat[...].reshape(8 * OUT_AT, wide)
     conv = packed[:, 0:OUT_AT, :].reshape(8 * OUT_AT, 256)
     pre = dot(conv, features, TN)
@@ -291,8 +287,7 @@
     hidden = (filt[:, :tokens] * gate[:, :tokens]).astype(BF16)
     out_res = packed[:, OUT_AT:PACKED, 0:128].reshape(RESID, 128)
     out_skp = packed[:, OUT_AT:PACKED, 128:256].reshape(RESID, 128)
-    res_part = dot(out_res, hidden)
-    skp_part = dot(out_skp, hidden)
+    hidden_out[...] = hidden
     grad_hidden = dot(out_res, res[...], TN) + dot(out_skp, skp[...], TN)
     grad_pre = jnp.concatenate(
         [
@@ -301,15 +296,12 @@
         ],
         0,
     ).astype(BF16)
-    prev = packed[:, 0:64, :].reshape(RESID, 256)
-    now = packed[:, 64:128, :].reshape(RESID, 256)
-    later = pltpu.roll(dot(prev, grad_pre), wide - DILATION, 1)[:, :tokens]
+    grad_out[...] = grad_pre
     grad_pre = grad_pre[:, :tokens]
-    in_part = dot(now, grad_pre) + later
     conv_grad = dot(features[:, :tokens], grad_pre, NT).astype(BF16)
     res_grad = dot(res[:, :tokens], hidden, NT).astype(BF16)
     skp_grad = dot(skp[:, :tokens], hidden, NT).astype(BF16)
-    core = lax.axis_index("chan") & 1
+    core = ch & 1
     for part, rows, cols in (
         (conv_grad.reshape(8, OUT_AT, 256), slice(0, OUT_AT), slice(0, 256)),
         (res_grad.reshape(8, 64, 128), slice(OUT_AT, PACKED), slice(0, 128)),
@@ -319,13 +311,24 @@
             even, odd = part[2 * i], part[2 * i + 1]
             kept[i, rows, cols] = jnp.where(core == 0, even, odd)
             given[i, rows, cols] = jnp.where(core == 0, odd, even)
+
+
+def outputs(packed, hidden, grad_pre, z0, z1, z2, z3, natural):
+    ch = lax.axis_index("chan")
+    tokens, wide = 256, 384
+    hidden = hidden[...]
+    res_part = dot(packed[:, OUT_AT:PACKED, 0:128].reshape(RESID, 128), hidden)
+    skp_part = dot(packed[:, OUT_AT:PACKED, 128:256].reshape(RESID, 128), hidden)
+    prev = packed[:, 0:64, :].reshape(RESID, 256)
+    now = packed[:, 64:128, :].reshape(RESID, 256)
+    later = pltpu.roll(dot(prev, grad_pre[...]), wide - DILATION, 1)[:, :tokens]
+    in_part = dot(now, grad_pre[:, :tokens]) + later
     for n, part in enumerate((res_part, skp_part, in_part)):
         for h in range(2):
             for r in range(8):
                 natural[2 * n + h, pl.ds(r, 64, stride=8), :] = part[
                     64 * r : 64 * r + 64, 128 * h : 128 * h + 128
                 ]
-    ch = lax.axis_index("chan")
     for k, out in enumerate((z0, z1, z2, z3)):
         for i in range(4):
             rows = pl.ds(pl.multiple_of(32 * (ch ^ (4 * k + i)), 32), 32)
@@ -413,27 +416,23 @@
     sds = jax.ShapeDtypeStruct
     dma = pltpu.SemaphoreType.DMA
 
-    sent, edges = call(
+    acts, edges = call(
         begin,
-        (sds((16, slots_dev, 256), BF16), sds((192, 128), BF16)),
-        (HBM,) * 6,
-        scratch=(
-            pltpu.VMEM((8, 8 * slots_dev, 128), F32),
-            pltpu.SMEM(speaker_ids.shape, jnp.int32),
-            dma((13,)),
-        ),
-    )(speaker_ids, master.reshape(flat), sig, res, skp, mel)
+        (sds((3, *sig.shape), BF16), sds((192, 128), BF16)),
+        (HBM,) * 5,
+        scratch=(pltpu.SMEM(speaker_ids.shape, jnp.int32), dma((5,))),
+    )(speaker_ids, sig, res, skp, mel)
     other = lax.ppermute(edges, "tm", [(0, 1), (1, 0)])
+    sent = call(
+        pack_weights,
+        sds((16, slots_dev, 256), BF16),
+        (HBM,),
+        scratch=(pltpu.VMEM((8, 8 * slots_dev, 128), F32), dma((8,))),
+    )(master.reshape(flat))
+    piece = sds((PIECE, 256), BF16)
+    o = call(pack_tokens, (piece,) * 4, (VMEM,) * 2, gflops=200)(acts, other)
     arrived = lax.all_to_all(sent, "chan", 0, 0, tiled=True)
-    piece = sds((PIECE, 256), BF16)
-    o = call(
-        pack_tokens,
-        (piece,) * 4,
-        (HBM,) * 3 + (VMEM,),
-        gflops=200,
-        scratch=(pltpu.VMEM((3, *sig.shape), BF16), dma((3,))),
-    )(sig, res, skp, other)
-    mine = call(join, sds((400, 256), BF16), (VMEM,) * 4)(
+    mine = call(join, sds((400, 256), BF16), (VMEM,) * 4, gflops=0)(
         o[0], swap(o[1], 1), swap(o[2], 2), swap(o[3], 3)
     )
     p1, p2, p3 = (swap(mine, 4 * k) for k in (1, 2, 3))
@@ -452,26 +451,29 @@
         at_col, arrived.reshape(slots, 256)
     )
     packed = lax.all_gather(gathered, BOTH, axis_index_groups=share)
-    mel, _ = lax.optimization_barrier((mel, packed))
-    cots = sds((RESID, 384), BF16)
-    ready = call(
-        prepare,
-        (sds((8, OUT_AT, 384), BF16), cots, cots),
-        (SMEM,) + (VMEM,) * 6,
+    rows = sds((4, PACKED, 256), BF16)
+    kept, given, hidden, grad_pre = call(
+        layer,
+        (rows, rows, sds((128, 256), BF16), sds((256, 384), BF16)),
+        (SMEM,) + (VMEM,) * 7,
         gflops=200,
-        pinned=(1,),
-        scratch=(pltpu.VMEM((7, RESID, 128), F32),),
-    )(speaker_ids, mine, p1, p2, p3, mel, other)
-
-    quad = sds((4, 96, 256), BF16)
-    rows = sds((4, PACKED, 256), BF16)
-    kept, given, z0, z1, z2, z3 = call(
-        layer,
-        (rows, rows, quad, quad, quad, quad),
-        (VMEM,) * 4,
+        pinned=(2,),
+        scratch=(
+            pltpu.VMEM((8, OUT_AT, 384), BF16),
+            pltpu.VMEM((RESID, 384), BF16),
+            pltpu.VMEM((RESID, 384), BF16),
+            pltpu.VMEM((7, RESID, 128), F32),
+        ),
+    )(speaker_ids, packed, mine, p1, p2, p3, mel, other)
+    z0, z1, z2, z3 = call(
+        outputs,
+        (sds((4, 96, 256), BF16),) * 4,
+        (VMEM,) * 3,
+        gflops=0,
         scratch=(pltpu.VMEM((6, RESID, 128), F32),),
-    )(packed, *ready)
-
+    )(packed, hidden, grad_pre)
+
+    kept, _ = lax.optimization_barrier((kept, z0))
     n = lax.axis_size("chan")
     g = call(sum_cores, (sds((PACKED, 256), BF16),) * 4, (VMEM,) * 2)(kept, swap(given, 1))
     across = [(16 * y + i, 16 * (1 - y) + (i ^ 2)) for y in range(2) for i in range(n)]

time: 88.9 us -> 87.7 us (0.987)
  waiting for transfers between devices: 31.7 us -> 30.5 us
    ppermute x14, waiting for transfers between devices: 19.1 us -> 17.8 us  [swap(): return lax.ppermute(x, 'chan', [(i, i ^ k) for i in range(n)])]
    pallas_call x12 -> x13, Pallas kernels: 16.3 us -> 15.8 us  [call(): run(*(pin(x, f) if f else x for x, f in zip(args, fixed, strict=True)))]
  transfers between devices with their start and end apart: 19 -> 19, of which waited for: 9 -> 9; matrix products, arithmetic and copies ran while one was open for 0% -> 0% of each run, Pallas kernels for 7% -> 10%
where the time goes in v8:
time: 87.7 us; the launch traced here: 87.2 us
  waiting for transfers between devices  30.5 us (35%)
  starting transfers between devices  29.7 us (34%)
  Pallas kernels  15.8 us (18%)
  blocking collectives  10.3 us (12%)
    ppermute x14, waiting for transfers between devices, swap(): return lax.ppermute(x, 'chan', [(i, i ^ k) for i in range(n)])  17.8 us
    pallas_call x13, Pallas kernels, call(): run(*(pin(x, f) if f else x for x, f in zip(args, fixed, strict=True)))  15.8 us
    ppermute x14, starting transfers between devices, swap(): return lax.ppermute(x, 'chan', [(i, i ^ k) for i in range(n)])  14.1 us
    all_gather x1, blocking collectives, local(): packed = lax.all_gather(gathered, BOTH, axis_index_groups=share)  10.3 us
    all_to_all x1, waiting for transfers between devices, local(): returned = lax.all_to_all(spread.reshape(32, slots_dev, 256), BOTH, 0, 0)  8.92 us
    all_to_all x1, starting transfers between devices, local(): arrived = lax.all_to_all(sent, 'chan', 0, 0, tiled=True)  5.97 us
    ppermute x1, waiting for transfers between devices, local(): lax.ppermute(g[2], 'tm', [(0, 1), (1, 0)])  3.79 us
    all_to_all x1, starting transfers between devices, local(): returned = lax.all_to_all(spread.reshape(32, slots_dev, 256), BOTH, 0, 0)  3.76 us
  transfers between devices with their start and end apart: 19, of which 9 were waited for; matrix products, arithmetic and copies ran while one was open for 0% of the time, Pallas kernels for 10%

profile of v8, /device:TPU:0, one launch (start us, length us, event | category | flops | bytes accessed | tf_op | source)
XLA Modules:
  0.0 87.2 jit_solution(6197664566464894255)
XLA Ops:
  0.6 1.0 %shard_map.136 = (bf16[3,32,1024]{2,1,0:T(8,128)(2,1)S(1)}, bf16[192,128]{1,0:T(8,128)(2,1)S(1)}) custom-call(s32[8]{0:T(128)} %spk.1, bf16[32,1024]{1,0:T(8,128)(2,1)} %bitcast.19, bf16[32,1024]{1,0:T(8,128)(2,1)} %bitcast.21, bf16[32,1024]{1,0:T(8,128)(2,1)} %bitcast.28, bf16[80,1024]{1,0:T(8,128)(2,1)} %bitcast.23), custom_call_target="tpu_custom_call" | custom-call | bytes 1048576 | tf_op jit(solution)/shard_map/pallas_call | solution.py:74
  1.6 3.0 %collective-permute-start = (bf16[192,128]{1,0:T(8,128)(2,1)S(1)}, bf16[192,128]{1,0:T(8,128)(2,1)S(1)}, u32[]{:S(2)}, u32[]{:S(2)}) collective-permute-start(bf16[192,128]{1,0:T(8,128)(2,1)S(1)} %get-tuple-element.39), channel_id=1, source_target_pairs={{0,16},{16,0},{1,17},{17,1},{2,18},{18,2},{3,19},{19,3},{4,20},{20... | collective-permute-start | bytes 147464 | tf_op jit(solution)/shard_map/ppermute | solution.py:425
  4.7 2.2 %shard_map.138 = bf16[16,40,256]{2,1,0:T(8,128)(2,1)} custom-call(f32[320,1024]{1,0:T(8,128)} %bitcast.25), custom_call_target="tpu_custom_call" | custom-call | bytes 1048576 | tf_op jit(solution)/shard_map/pallas_call | solution.py:74
  6.9 6.0 %all-to-all-start = ((bf16[16,40,256]{2,1,0:T(8,128)(2,1)}), bf16[16,40,256]{2,1,0:T(8,128)(2,1)}, u32[]{:S(2)}, u32[]{:S(2)}) async-start(bf16[16,40,256]{2,1,0:T(8,128)(2,1)} %shard_map.138), calls=%async_computation | async-start | bytes 655360 | tf_op jit(solution)/shard_map/all_to_all | solution.py:434
  13.5 1.7 %collective-permute-start.2 = (bf16[112,256]{1,0:T(8,128)(2,1)S(1)}, bf16[112,256]{1,0:T(8,128)(2,1)S(1)}, u32[]{:S(2)}, u32[]{:S(2)}) collective-permute-start(bf16[112,256]{1,0:T(8,128)(2,1)S(1)} %get-tuple-element.44), channel_id=1, source_target_pairs={{0,2},{1,3},{2,0},{3,1},{4,6},{5,7},{6,4},{7,5},{8,10},{9,11},{10,... | collective-permute-start | bytes 172040 | tf_op jit(solution)/shard_map/ppermute | solution.py:404
  15.2 1.0 %shard_map.137 = (s32[224,128]{1,0:T(8,128)S(1)}, bf16[640,224]{1,0:T(8,128)(2,1)S(1)}, s32[8,128]{1,0:T(8,128)S(1)}) custom-call(s32[8]{0:T(128)S(1)} %copy-done.4, s32[1,320]{1,0:T(1,128)S(1)} %reshape.40.owners, bf16[192,128]{1,0:T(8,128)(2,1)S(1)} %collective-permute-done.other), custom_call_target="tpu_custom_call" | custom-call | bytes 1048576 | tf_op jit(solution)/shard_map/pallas_call | solution.py:74
  16.2 3.6 %collective-permute-done.2.o2 = bf16[112,256]{1,0:T(8,128)(2,1)S(1)} collective-permute-done((bf16[112,256]{1,0:T(8,128)(2,1)S(1)}, bf16[112,256]{1,0:T(8,128)(2,1)S(1)}, u32[]{:S(2)}, u32[]{:S(2)}) %collective-permute-start.2) | collective-permute-done | bytes 57376 | tf_op jit(solution)/shard_map/ppermute | solution.py:404
  20.1 0.7 shard_map.140.p0
  20.8 4.3 %collective-permute-start.6 = (bf16[400,256]{1,0:T(8,128)(2,1)}, bf16[400,256]{1,0:T(8,128)(2,1)}, u32[]{:S(2)}, u32[]{:S(2)}) collective-permute-start(bf16[400,256]{1,0:T(8,128)(2,1)} %shard_map.140.p0), channel_id=1, source_target_pairs={{0,12},{1,13},{2,14},{3,15},{4,8},{5,9},{6,10},{7,11},{8,4},{9,5},... | collective-permute-start | bytes 614408 | tf_op jit(solution)/shard_map/ppermute | solution.py:404
  25.1 0.6 collective-permute-start.4
  25.7 1.5 %shard_map.141 = bf16[224,256]{1,0:T(8,128)(2,1)S(1)} custom-call(s32[224,128]{1,0:T(8,128)S(1)} %get-tuple-element.40.at_col, bf16[640,256]{1,0:T(8,128)(2,1)} %bitcast.5.slots), custom_call_target="tpu_custom_call" | custom-call | flops 199999995904 | bytes 1048576 | tf_op jit(solution)/shard_map/pallas_call | solution.py:74
  27.2 10.3 %all-gather = bf16[1792,256]{1,0:T(8,128)(2,1)S(1)} all-gather(bf16[224,256]{1,0:T(8,128)(2,1)S(1)} %shard_map.141), channel_id=2, replica_groups={{0,1,2,3,16,17,18,19},{4,5,6,7,20,21,22,23},{8,9,10,11,24,25,26,27},{12..., dimensions={0}, use_global_device_ids=true | all-gather | bytes 1032192 | tf_op jit(solution)/shard_map/all_gather | solution.py:453
  37.5 5.9 %collective-permute-done.5.p2 = bf16[400,256]{1,0:T(8,128)(2,1)} collective-permute-done((bf16[400,256]{1,0:T(8,128)(2,1)}, bf16[400,256]{1,0:T(8,128)(2,1)}, u32[]{:S(2)}, u32[]{:S(2)}) %collective-permute-start.5) | collective-permute-done | bytes 204832 | tf_op jit(solution)/shard_map/ppermute | solution.py:404
  43.4 2.8 %shard_map.142 = (bf16[4,224,256]{2,1,0:T(8,128)(2,1)S(1)}, bf16[4,224,256]{2,1,0:T(8,128)(2,1)S(1)}, bf16[128,256]{1,0:T(8,128)(2,1)S(1)}, bf16[256,384]{1,0:T(8,128)(2,1)S(1)}) custom-call(s32[8]{0:T(128)S(1)} %copy-done.5, bf16[8,224,256]{2,1,0:T(8,128)(2,1)S(1)} %bitcast.16, bf16[400,256]{1,0:T(8,128)(2,1)} %shard_map.140.p0, ...), custom_call_target="tpu_custom_call" | custom-call | flops 199999995904 | bytes 1048576 | tf_op jit(solution)/shard_map/pallas_call | solution.py:74
  46.4 0.7 shard_map.143
  47.1 1.0 %collective-permute-done.13.got = bf16[4,224,256]{2,1,0:T(8,128)(2,1)S(1)} collective-permute-done((bf16[4,224,256]{2,1,0:T(8,128)(2,1)S(1)}, bf16[4,224,256]{2,1,0:T(8,128)(2,1)S(1)}, u32[]{:S(2)}, u32[]{:S(2)}) %collective-permute-start.13) | collective-permute-done | bytes 458784 | tf_op jit(solution)/shard_map/ppermute | solution.py:404
  48.2 0.7 collective-permute-start.14
  48.8 3.0 %collective-permute-start.8 = (bf16[4,96,256]{2,1,0:T(8,128)(2,1)S(1)}, bf16[4,96,256]{2,1,0:T(8,128)(2,1)S(1)}, u32[]{:S(2)}, u32[]{:S(2)}) collective-permute-start(bf16[4,96,256]{2,1,0:T(8,128)(2,1)S(1)} %get-tuple-element.51), channel_id=1, source_target_pairs={{0,8},{1,9},{2,10},{3,11},{4,12},{5,13},{6,14},{7,15},{8,0},{9,1},... | collective-permute-start | bytes 589832 | tf_op jit(solution)/shard_map/ppermute | solution.py:404
  51.9 1.3 %collective-permute-start.9 = (bf16[4,96,256]{2,1,0:T(8,128)(2,1)S(1)}, bf16[4,96,256]{2,1,0:T(8,128)(2,1)S(1)}, u32[]{:S(2)}, u32[]{:S(2)}) collective-permute-start(bf16[4,96,256]{2,1,0:T(8,128)(2,1)S(1)} %get-tuple-element.52), channel_id=1, source_target_pairs={{0,12},{1,13},{2,14},{3,15},{4,8},{5,9},{6,10},{7,11},{8,4},{9,5},... | collective-permute-start | bytes 589832 | tf_op jit(solution)/shard_map/ppermute | solution.py:404
  53.2 0.5 collective-permute-start.15
  53.7 2.4 %collective-permute-start.16 = (bf16[224,256]{1,0:T(8,128)(2,1)S(1)}, bf16[224,256]{1,0:T(8,128)(2,1)S(1)}, u32[]{:S(2)}, u32[]{:S(2)}) collective-permute-start(bf16[224,256]{1,0:T(8,128)(2,1)S(1)} %get-tuple-element.68), channel_id=1, source_target_pairs={{0,18},{1,19},{2,16},{3,17},{4,22},{5,23},{6,20},{7,21},{8,26},{9,... | collective-permute-start | bytes 344072 | tf_op jit(solution)/shard_map/ppermute | solution.py:480
  56.1 3.8 %collective-permute-done.15.p2 = bf16[224,256]{1,0:T(8,128)(2,1)S(1)} collective-permute-done((bf16[224,256]{1,0:T(8,128)(2,1)S(1)}, bf16[224,256]{1,0:T(8,128)(2,1)S(1)}, u32[]{:S(2)}, u32[]{:S(2)}) %collective-permute-start.15) | collective-permute-done | bytes 114720 | tf_op jit(solution)/shard_map/ppermute | solution.py:480
  59.9 1.3 %shard_map.147 = bf16[2,640,256]{2,1,0:T(8,128)(2,1)} custom-call(bf16[640,224]{1,0:T(8,128)(2,1)S(1)} %get-tuple-element.61.put, bf16[224,256]{1,0:T(8,128)(2,1)S(1)} %get-tuple-element.65.p0, bf16[224,256]{1,0:T(8,128)(2,1)S(1)} %collective-permute-done.14.p1, bf16[224,256]{1,0:T(8,128)(2,1)S(1)} %collective-permute-done.15.p2, ...), custom_call_target="tpu_custom_call" | custom-call | bytes 1048576 | tf_op jit(solution)/shard_map/pallas_call | solution.py:74
  61.2 3.8 %all-to-all-start.1 = ((bf16[32,40,256]{2,1,0:T(8,128)(2,1)}), bf16[32,40,256]{2,1,0:T(8,128)(2,1)S(1)}, u32[]{:S(2)}, u32[]{:S(2)}) async-start(bf16[32,40,256]{2,1,0:T(8,128)(2,1)} %bitcast.10), calls=%async_computation.1 | async-start | bytes 1310720 | tf_op jit(solution)/shard_map/all_to_all | solution.py:483
  65.0 1.0 %collective-permute-done.8.z2 = bf16[4,96,256]{2,1,0:T(8,128)(2,1)S(1)} collective-permute-done((bf16[4,96,256]{2,1,0:T(8,128)(2,1)S(1)}, bf16[4,96,256]{2,1,0:T(8,128)(2,1)S(1)}, u32[]{:S(2)}, u32[]{:S(2)}) %collective-permute-start.8) | collective-permute-done | bytes 196640 | tf_op jit(solution)/shard_map/ppermute | solution.py:404
  66.2 1.4 %collective-permute-start.11 = (bf16[96,256]{1,0:T(8,128)(2,1)S(1)}, bf16[96,256]{1,0:T(8,128)(2,1)S(1)}, u32[]{:S(2)}, u32[]{:S(2)}) collective-permute-start(bf16[96,256]{1,0:T(8,128)(2,1)S(1)} %get-tuple-element.55), channel_id=1, source_target_pairs={{0,2},{1,3},{2,0},{3,1},{4,6},{5,7},{6,4},{7,5},{8,10},{9,11},{10,... | collective-permute-start | bytes 147464 | tf_op jit(solution)/shard_map/ppermute | solution.py:404
  67.6 0.5 collective-permute-start.12
  68.1 5.0 %collective-permute-done.11.o2 = bf16[96,256]{1,0:T(8,128)(2,1)S(1)} collective-permute-done((bf16[96,256]{1,0:T(8,128)(2,1)S(1)}, bf16[96,256]{1,0:T(8,128)(2,1)S(1)}, u32[]{:S(2)}, u32[]{:S(2)}) %collective-permute-start.11) | collective-permute-done | bytes 49184 | tf_op jit(solution)/shard_map/ppermute | solution.py:404
  73.1 1.0 %collective-permute-done.12.o3 = bf16[96,256]{1,0:T(8,128)(2,1)S(1)} collective-permute-done((bf16[96,256]{1,0:T(8,128)(2,1)S(1)}, bf16[96,256]{1,0:T(8,128)(2,1)S(1)}, u32[]{:S(2)}, u32[]{:S(2)}) %collective-permute-start.12) | collective-permute-done | bytes 49184 | tf_op jit(solution)/shard_map/ppermute | solution.py:404
  74.0 0.8 shard_map.145
  74.8 8.9 %all-to-all-done.1.grads = bf16[32,40,256]{2,1,0:T(8,128)(2,1)S(1)} async-done(((bf16[32,40,256]{2,1,0:T(8,128)(2,1)}), bf16[32,40,256]{2,1,0:T(8,128)(2,1)S(1)}, u32[]{:S(2)}, u32[]{:S(2)}) %all-to-all-start.1) | async-done | bytes 655392 | tf_op jit(solution)/shard_map/all_to_all | solution.py:483
  83.7 3.5 %shard_map.148 = (f32[320,1024]{1,0:T(8,128)}, f32[320,1024]{1,0:T(8,128)}, f32[320,1024]{1,0:T(8,128)}) custom-call(s32[8,128]{1,0:T(8,128)S(1)} %get-tuple-element.60.owned, bf16[32,40,256]{2,1,0:T(8,128)(2,1)S(1)} %all-to-all-done.1.grads, f32[320,1024]{1,0:T(8,128)} %bitcast.26, f32[320,1024]{1,0:T(8,128)S(1)} %bitcast.18, f32[320,1024]{1,0:T(8,128)} %bitcast.27), custom_call_target="tpu_custom_call" | custom-call | bytes 1048576 | tf_op jit(solution)/shard_map/pallas_call | solution.py:74
  (35 shorter events, 1.4 us)
Async XLA Ops:
  1.6 11.2 %collective-permute-start = (bf16[192,128]{1,0:T(8,128)(2,1)S(1)}, bf16[192,128]{1,0:T(8,128)(2,1)S(1)}, u32[]{:S(2)}, u32[]{:S(2)}) collective-permute-start(bf16[192,128]{1,0:T(8,128)(2,1)S(1)} %get-tuple-element.39), channel_id=1, source_target_pairs={{0,16},{16,0},{1,17},{17,1},{2,18},{18,2},{3,19},{19,3},{4,20},{20... | collective-permute-start | bytes 147464 | tf_op jit(solution)/shard_map/ppermute | solution.py:425
  6.9 18.8 %all-to-all-start = ((bf16[16,40,256]{2,1,0:T(8,128)(2,1)}), bf16[16,40,256]{2,1,0:T(8,128)(2,1)}, u32[]{:S(2)}, u32[]{:S(2)}) async-start(bf16[16,40,256]{2,1,0:T(8,128)(2,1)} %shard_map.138), calls=%async_computation | async-start | bytes 655360 | tf_op jit(solution)/shard_map/all_to_all | solution.py:434
  12.9 2.3 %copy-start.6 = (s32[320]{0:T(512)S(1)}, s32[320]{0:T(512)}, u32[]{:S(2)}) copy-start(s32[320]{0:T(512)} %param.12) | copy-start | bytes 3844
  12.9 2.3 %copy-start.4 = (s32[8]{0:T(128)S(1)}, s32[8]{0:T(128)}, u32[]{:S(2)}) copy-start(s32[8]{0:T(128)} %spk.1) | copy-start | bytes 100
  13.1 3.1 %collective-permute-start.1 = (bf16[112,256]{1,0:T(8,128)(2,1)S(1)}, bf16[112,256]{1,0:T(8,128)(2,1)S(1)}, u32[]{:S(2)}, u32[]{:S(2)}) collective-permute-start(bf16[112,256]{1,0:T(8,128)(2,1)S(1)} %get-tuple-element.43), channel_id=1, source_target_pairs={{0,1},{1,0},{2,3},{3,2},{4,5},{5,4},{6,7},{7,6},{8,9},{9,8},{10,11... | collective-permute-start | bytes 172040 | tf_op jit(solution)/shard_map/ppermute | solution.py:404
  13.5 6.4 %collective-permute-start.2 = (bf16[112,256]{1,0:T(8,128)(2,1)S(1)}, bf16[112,256]{1,0:T(8,128)(2,1)S(1)}, u32[]{:S(2)}, u32[]{:S(2)}) collective-permute-start(bf16[112,256]{1,0:T(8,128)(2,1)S(1)} %get-tuple-element.44), channel_id=1, source_target_pairs={{0,2},{1,3},{2,0},{3,1},{4,6},{5,7},{6,4},{7,5},{8,10},{9,11},{10,... | collective-permute-start | bytes 172040 | tf_op jit(solution)/shard_map/ppermute | solution.py:404
  15.2 4.9 %collective-permute-start.3 = (bf16[112,256]{1,0:T(8,128)(2,1)S(1)}, bf16[112,256]{1,0:T(8,128)(2,1)S(1)}, u32[]{:S(2)}, u32[]{:S(2)}) collective-permute-start(bf16[112,256]{1,0:T(8,128)(2,1)S(1)} %get-tuple-element.45), channel_id=1, source_target_pairs={{0,3},{1,2},{2,1},{3,0},{4,7},{5,6},{6,5},{7,4},{8,11},{9,10},{10,... | collective-permute-start | bytes 172040 | tf_op jit(solution)/shard_map/ppermute | solution.py:404
  20.8 16.7 %collective-permute-start.6 = (bf16[400,256]{1,0:T(8,128)(2,1)}, bf16[400,256]{1,0:T(8,128)(2,1)}, u32[]{:S(2)}, u32[]{:S(2)}) collective-permute-start(bf16[400,256]{1,0:T(8,128)(2,1)} %shard_map.140.p0), channel_id=1, source_target_pairs={{0,12},{1,13},{2,14},{3,15},{4,8},{5,9},{6,10},{7,11},{8,4},{9,5},... | collective-permute-start | bytes 614408 | tf_op jit(solution)/shard_map/ppermute | solution.py:404
  25.1 18.2 %collective-permute-start.5 = (bf16[400,256]{1,0:T(8,128)(2,1)}, bf16[400,256]{1,0:T(8,128)(2,1)}, u32[]{:S(2)}, u32[]{:S(2)}) collective-permute-start(bf16[400,256]{1,0:T(8,128)(2,1)} %shard_map.140.p0), channel_id=1, source_target_pairs={{0,8},{1,9},{2,10},{3,11},{4,12},{5,13},{6,14},{7,15},{8,0},{9,1},... | collective-permute-start | bytes 614408 | tf_op jit(solution)/shard_map/ppermute | solution.py:404
  25.1 18.2 %collective-permute-start.4 = (bf16[400,256]{1,0:T(8,128)(2,1)}, bf16[400,256]{1,0:T(8,128)(2,1)}, u32[]{:S(2)}, u32[]{:S(2)}) collective-permute-start(bf16[400,256]{1,0:T(8,128)(2,1)} %shard_map.140.p0), channel_id=1, source_target_pairs={{0,4},{1,5},{2,6},{3,7},{4,0},{5,1},{6,2},{7,3},{8,12},{9,13},{10,... | collective-permute-start | bytes 614408 | tf_op jit(solution)/shard_map/ppermute | solution.py:404
  25.7 17.7 %copy-start.3 = (bf16[1024,80]{0,1:T(8,128)(2,1)S(1)}, bf16[1024,80]{0,1:T(8,128)(2,1)}, u32[]{:S(2)}) copy-start(bf16[1024,80]{0,1:T(8,128)(2,1)} %param.10) | copy-start | bytes 491524
  25.7 17.7 %copy-start.5 = (s32[8]{0:T(128)S(1)}, s32[8]{0:T(128)}, u32[]{:S(2)}) copy-start(s32[8]{0:T(128)} %spk.1) | copy-start | bytes 100
  46.2 1.9 %collective-permute-start.13 = (bf16[4,224,256]{2,1,0:T(8,128)(2,1)S(1)}, bf16[4,224,256]{2,1,0:T(8,128)(2,1)S(1)}, u32[]{:S(2)}, u32[]{:S(2)}) collective-permute-start(bf16[4,224,256]{2,1,0:T(8,128)(2,1)S(1)} %get-tuple-element.64), channel_id=1, source_target_pairs={{0,1},{1,0},{2,3},{3,2},{4,5},{5,4},{6,7},{7,6},{8,9},{9,8},{10,11... | collective-permute-start | bytes 1376264 | tf_op jit(solution)/shard_map/ppermute | solution.py:404
  48.2 5.6 %collective-permute-start.14 = (bf16[224,256]{1,0:T(8,128)(2,1)S(1)}, bf16[224,256]{1,0:T(8,128)(2,1)S(1)}, u32[]{:S(2)}, u32[]{:S(2)}) collective-permute-start(bf16[224,256]{1,0:T(8,128)(2,1)S(1)} %get-tuple-element.66), channel_id=1, source_target_pairs={{0,2},{1,3},{2,0},{3,1},{4,6},{5,7},{6,4},{7,5},{8,10},{9,11},{10,... | collective-permute-start | bytes 344072 | tf_op jit(solution)/shard_map/ppermute | solution.py:404
  48.8 16.2 %collective-permute-start.7 = (bf16[4,96,256]{2,1,0:T(8,128)(2,1)S(1)}, bf16[4,96,256]{2,1,0:T(8,128)(2,1)S(1)}, u32[]{:S(2)}, u32[]{:S(2)}) collective-permute-start(bf16[4,96,256]{2,1,0:T(8,128)(2,1)S(1)} %get-tuple-element.50), channel_id=1, source_target_pairs={{0,4},{1,5},{2,6},{3,7},{4,0},{5,1},{6,2},{7,3},{8,12},{9,13},{10,... | collective-permute-start | bytes 589832 | tf_op jit(solution)/shard_map/ppermute | solution.py:404
  48.8 17.2 %collective-permute-start.8 = (bf16[4,96,256]{2,1,0:T(8,128)(2,1)S(1)}, bf16[4,96,256]{2,1,0:T(8,128)(2,1)S(1)}, u32[]{:S(2)}, u32[]{:S(2)}) collective-permute-start(bf16[4,96,256]{2,1,0:T(8,128)(2,1)S(1)} %get-tuple-element.51), channel_id=1, source_target_pairs={{0,8},{1,9},{2,10},{3,11},{4,12},{5,13},{6,14},{7,15},{8,0},{9,1},... | collective-permute-start | bytes 589832 | tf_op jit(solution)/shard_map/ppermute | solution.py:404
  51.9 14.2 %collective-permute-start.9 = (bf16[4,96,256]{2,1,0:T(8,128)(2,1)S(1)}, bf16[4,96,256]{2,1,0:T(8,128)(2,1)S(1)}, u32[]{:S(2)}, u32[]{:S(2)}) collective-permute-start(bf16[4,96,256]{2,1,0:T(8,128)(2,1)S(1)} %get-tuple-element.52), channel_id=1, source_target_pairs={{0,12},{1,13},{2,14},{3,15},{4,8},{5,9},{6,10},{7,11},{8,4},{9,5},... | collective-permute-start | bytes 589832 | tf_op jit(solution)/shard_map/ppermute | solution.py:404
  53.2 6.7 %collective-permute-start.15 = (bf16[224,256]{1,0:T(8,128)(2,1)S(1)}, bf16[224,256]{1,0:T(8,128)(2,1)S(1)}, u32[]{:S(2)}, u32[]{:S(2)}) collective-permute-start(bf16[224,256]{1,0:T(8,128)(2,1)S(1)} %get-tuple-element.67), channel_id=1, source_target_pairs={{0,16},{16,0},{1,17},{17,1},{2,18},{18,2},{3,19},{19,3},{4,20},{20... | collective-permute-start | bytes 344072 | tf_op jit(solution)/shard_map/ppermute | solution.py:480
  53.7 6.2 %collective-permute-start.16 = (bf16[224,256]{1,0:T(8,128)(2,1)S(1)}, bf16[224,256]{1,0:T(8,128)(2,1)S(1)}, u32[]{:S(2)}, u32[]{:S(2)}) collective-permute-start(bf16[224,256]{1,0:T(8,128)(2,1)S(1)} %get-tuple-element.68), channel_id=1, source_target_pairs={{0,18},{1,19},{2,16},{3,17},{4,22},{5,23},{6,20},{7,21},{8,26},{9,... | collective-permute-start | bytes 344072 | tf_op jit(solution)/shard_map/ppermute | solution.py:480
  61.2 22.5 %all-to-all-start.1 = ((bf16[32,40,256]{2,1,0:T(8,128)(2,1)}), bf16[32,40,256]{2,1,0:T(8,128)(2,1)S(1)}, u32[]{:S(2)}, u32[]{:S(2)}) async-start(bf16[32,40,256]{2,1,0:T(8,128)(2,1)} %bitcast.10), calls=%async_computation.1 | async-start | bytes 1310720 | tf_op jit(solution)/shard_map/all_to_all | solution.py:483
  65.0 9.0 %copy-start.1 = (bf16[1024,32]{0,1:T(8,128)(2,1)S(1)}, bf16[1024,32]{0,1:T(8,128)(2,1)}, u32[]{:S(2)}) copy-start(bf16[1024,32]{0,1:T(8,128)(2,1)} %param.9) | copy-start | bytes 196612
  65.0 9.0 %copy-start.2 = (bf16[1024,32]{0,1:T(8,128)(2,1)S(1)}, bf16[1024,32]{0,1:T(8,128)(2,1)}, u32[]{:S(2)}) copy-start(bf16[1024,32]{0,1:T(8,128)(2,1)} %param.16) | copy-start | bytes 196612
  65.0 18.7 %copy-start = (f32[40,8,1024]{2,1,0:T(8,128)S(1)}, f32[40,8,1024]{2,1,0:T(8,128)}, u32[]{:S(2)}) copy-start(f32[40,8,1024]{2,1,0:T(8,128)} %param.14) | copy-start | bytes 3932164
  66.2 1.9 %collective-permute-start.10 = (bf16[96,256]{1,0:T(8,128)(2,1)S(1)}, bf16[96,256]{1,0:T(8,128)(2,1)S(1)}, u32[]{:S(2)}, u32[]{:S(2)}) collective-permute-start(bf16[96,256]{1,0:T(8,128)(2,1)S(1)} %get-tuple-element.54), channel_id=1, source_target_pairs={{0,1},{1,0},{2,3},{3,2},{4,5},{5,4},{6,7},{7,6},{8,9},{9,8},{10,11... | collective-permute-start | bytes 147464 | tf_op jit(solution)/shard_map/ppermute | solution.py:404
  66.2 6.8 %collective-permute-start.11 = (bf16[96,256]{1,0:T(8,128)(2,1)S(1)}, bf16[96,256]{1,0:T(8,128)(2,1)S(1)}, u32[]{:S(2)}, u32[]{:S(2)}) collective-permute-start(bf16[96,256]{1,0:T(8,128)(2,1)S(1)} %get-tuple-element.55), channel_id=1, source_target_pairs={{0,2},{1,3},{2,0},{3,1},{4,6},{5,7},{6,4},{7,5},{8,10},{9,11},{10,... | collective-permute-start | bytes 147464 | tf_op jit(solution)/shard_map/ppermute | solution.py:404
  67.6 6.4 %collective-permute-start.12 = (bf16[96,256]{1,0:T(8,128)(2,1)S(1)}, bf16[96,256]{1,0:T(8,128)(2,1)S(1)}, u32[]{:S(2)}, u32[]{:S(2)}) collective-permute-start(bf16[96,256]{1,0:T(8,128)(2,1)S(1)} %get-tuple-element.56), channel_id=1, source_target_pairs={{0,3},{1,2},{2,1},{3,0},{4,7},{5,6},{6,5},{7,4},{8,11},{9,10},{10,... | collective-permute-start | bytes 147464 | tf_op jit(solution)/shard_map/ppermute | solution.py:404

commit v9 on v8

--- a/solution.py
+++ b/solution.py
@@ -79,32 +79,15 @@
     return onehot(natural == 2 * (split & 127) + (split >> 7))
 
 
-def pack_weights(master, sent, strips, sems):
+def begin(speakers, master, sig, res, skp, mel, sent, acts, edges, strips, spk, sems):
     half = lax.axis_index("tm")
     slots = sent.shape[1]
-    copies = []
-    for t in range(8):
-        part = master.at[:, 128 * t : 128 * t + 128]
-        copies.append(pltpu.make_async_copy(part, strips.at[t], sems.at[t]))
-    for copy in copies:
-        copy.start()
-    for t in range(8):
-        copies[t].wait()
-        lanes = slice(128 * (t % 2), 128 * (t % 2) + 128)
-        for j in range(4):
-            low = strips[t, pl.ds(j, slots, stride=8), :]
-            high = strips[t, pl.ds(4 + j, slots, stride=8), :]
-            sent[4 * (t // 2) + j, :, lanes] = jnp.where(half == 0, low, high).astype(BF16)
-
-
-def begin(speakers, sig, res, skp, mel, acts, edges, spk, sems):
-    cut = pl.ds(pl.multiple_of((1 - lax.axis_index("tm")) * 896, 128), 128)
-    copies = [
-        pltpu.make_async_copy(speakers, spk, sems.at[0]),
-        pltpu.make_async_copy(mel.at[:, cut], edges.at[96:176, :], sems.at[1]),
-    ]
-    for n, part in enumerate((sig, res, skp)):
-        copies.append(pltpu.make_async_copy(part, acts.at[n], sems.at[2 + n]))
+    cut = pl.ds(pl.multiple_of((1 - half) * 896, 128), 128)
+    moves = [(speakers, spk)]
+    moves += [(part, acts.at[n]) for n, part in enumerate((sig, res, skp))]
+    moves += [(mel.at[:, cut], edges.at[96:176, :])]
+    moves += [(master.at[:, 128 * t : 128 * t + 128], strips.at[t]) for t in range(8)]
+    copies = [pltpu.make_async_copy(a, b, sems.at[n]) for n, (a, b) in enumerate(moves)]
     for copy in copies:
         copy.start()
     copies[0].wait()
@@ -114,10 +97,17 @@
         code = jnp.where(row == 0, spk[s] >> 3, spk[s] & 7)
         table = jnp.where((lane == s) & (row < 2), code, table)
     edges[176:192, :] = table.astype(F32).astype(BF16)
-    for copy in copies[1:]:
+    for copy in copies[1:5]:
         copy.wait()
     for n in range(3):
         edges[32 * n : 32 * n + 32, :] = acts[n, :, cut]
+    for t in range(8):
+        copies[5 + t].wait()
+        lanes = slice(128 * (t % 2), 128 * (t % 2) + 128)
+        for j in range(4):
+            low = strips[t, pl.ds(j, slots, stride=8), :]
+            high = strips[t, pl.ds(4 + j, slots, stride=8), :]
+            sent[4 * (t // 2) + j, :, lanes] = jnp.where(half == 0, low, high).astype(BF16)
 
 
 def pack_tokens(acts, other, o0, o1, o2, o3):
@@ -206,7 +196,7 @@
 def sum_cores(kept, got, *outs):
     i = 2 * lax.axis_index("tm") + ((lax.axis_index("chan") >> 1) & 1)
     for k, out in enumerate(outs):
-        out[...] = (kept[i ^ k].astype(F32) + got[i ^ k].astype(F32)).astype(BF16)
+        out[...] = (kept[i ^ k] + got[i ^ k].astype(F32)).astype(out.dtype)
 
 
 def scatter_blocks(put, p0, p1, p2, p3, out):
@@ -226,7 +216,8 @@
         ).astype(BF16)
 
 
-def layer(spk, packed, p0, p1, p2, p3, mel, other, kept, given, hidden_out, grad_out, feat, res, skp, natural):
+def layer(spk, packed, o0, o1, o2, o3, p1, p2, p3, mel, other, kept, given, hidden_out, grad_out, feat, res, skp, natural, p0):
+    join(o0, o1, o2, o3, p0)
     half, ch = lax.axis_index("tm"), lax.axis_index("chan")
     j = ch & 3
     got = (p0, p1, p2, p3)
@@ -298,9 +289,9 @@
     ).astype(BF16)
     grad_out[...] = grad_pre
     grad_pre = grad_pre[:, :tokens]
-    conv_grad = dot(features[:, :tokens], grad_pre, NT).astype(BF16)
-    res_grad = dot(res[:, :tokens], hidden, NT).astype(BF16)
-    skp_grad = dot(skp[:, :tokens], hidden, NT).astype(BF16)
+    conv_grad = dot(features[:, :tokens], grad_pre, NT)
+    res_grad = dot(res[:, :tokens], hidden, NT)
+    skp_grad = dot(skp[:, :tokens], hidden, NT)
     core = ch & 1
     for part, rows, cols in (
         (conv_grad.reshape(8, OUT_AT, 256), slice(0, OUT_AT), slice(0, 256)),
@@ -310,7 +301,7 @@
         for i in range(4):
             even, odd = part[2 * i], part[2 * i + 1]
             kept[i, rows, cols] = jnp.where(core == 0, even, odd)
-            given[i, rows, cols] = jnp.where(core == 0, odd, even)
+            given[i, rows, cols] = jnp.where(core == 0, odd, even).astype(BF16)
 
 
 def outputs(packed, hidden, grad_pre, z0, z1, z2, z3, natural):
@@ -416,25 +407,22 @@
     sds = jax.ShapeDtypeStruct
     dma = pltpu.SemaphoreType.DMA
 
-    acts, edges = call(
+    sent, acts, edges = call(
         begin,
-        (sds((3, *sig.shape), BF16), sds((192, 128), BF16)),
-        (HBM,) * 5,
-        scratch=(pltpu.SMEM(speaker_ids.shape, jnp.int32), dma((5,))),
-    )(speaker_ids, sig, res, skp, mel)
+        (sds((16, slots_dev, 256), BF16), sds((3, *sig.shape), BF16), sds((192, 128), BF16)),
+        (HBM,) * 6,
+        scratch=(
+            pltpu.VMEM((8, 8 * slots_dev, 128), F32),
+            pltpu.SMEM(speaker_ids.shape, jnp.int32),
+            dma((13,)),
+        ),
+    )(speaker_ids, master.reshape(flat), sig, res, skp, mel)
     other = lax.ppermute(edges, "tm", [(0, 1), (1, 0)])
-    sent = call(
-        pack_weights,
-        sds((16, slots_dev, 256), BF16),
-        (HBM,),
-        scratch=(pltpu.VMEM((8, 8 * slots_dev, 128), F32), dma((8,))),
-    )(master.reshape(flat))
     piece = sds((PIECE, 256), BF16)
     o = call(pack_tokens, (piece,) * 4, (VMEM,) * 2, gflops=200)(acts, other)
     arrived = lax.all_to_all(sent, "chan", 0, 0, tiled=True)
-    mine = call(join, sds((400, 256), BF16), (VMEM,) * 4, gflops=0)(
-        o[0], swap(o[1], 1), swap(o[2], 2), swap(o[3], 3)
-    )
+    o = (o[0], swap(o[1], 1), swap(o[2], 2), swap(o[3], 3))
+    mine = call(join, sds((400, 256), BF16), (VMEM,) * 4)(*o)
     p1, p2, p3 = (swap(mine, 4 * k) for k in (1, 2, 3))
 
     at_col, put, owned = call(
@@ -451,20 +439,20 @@
         at_col, arrived.reshape(slots, 256)
     )
     packed = lax.all_gather(gathered, BOTH, axis_index_groups=share)
-    rows = sds((4, PACKED, 256), BF16)
+    rows = (4, PACKED, 256)
     kept, given, hidden, grad_pre = call(
         layer,
-        (rows, rows, sds((128, 256), BF16), sds((256, 384), BF16)),
-        (SMEM,) + (VMEM,) * 7,
+        (sds(rows, F32), sds(rows, BF16), sds((128, 256), BF16), sds((256, 384), BF16)),
+        (SMEM,) + (VMEM,) * 10,
         gflops=200,
-        pinned=(2,),
         scratch=(
             pltpu.VMEM((8, OUT_AT, 384), BF16),
             pltpu.VMEM((RESID, 384), BF16),
             pltpu.VMEM((RESID, 384), BF16),
             pltpu.VMEM((7, RESID, 128), F32),
+            pltpu.VMEM((400, 256), BF16),
         ),
-    )(speaker_ids, packed, mine, p1, p2, p3, mel, other)
+    )(speaker_ids, packed, *o, p1, p2, p3, mel, other)
     z0, z1, z2, z3 = call(
         outputs,
         (sds((4, 96, 256), BF16),) * 4,
@@ -475,7 +463,7 @@
 
     kept, _ = lax.optimization_barrier((kept, z0))
     n = lax.axis_size("chan")
-    g = call(sum_cores, (sds((PACKED, 256), BF16),) * 4, (VMEM,) * 2)(kept, swap(given, 1))
+    g = call(sum_cores, tuple(sds((PACKED, 256), t) for t in (F32, BF16, BF16, BF16)), (VMEM,) * 2)(kept, swap(given, 1))
     across = [(16 * y + i, 16 * (1 - y) + (i ^ 2)) for y in range(2) for i in range(n)]
     g = (g[0], swap(g[1], 2), lax.ppermute(g[2], "tm", [(0, 1), (1, 0)]), lax.ppermute(g[3], BOTH, across))
     t1, t2, t3 = (swap(z, 4 * k) for k, z in ((1, z1), (2, z2), (3, z3)))

time: 87.7 us -> 86.6 us (0.987)
  Pallas kernels: 15.8 us -> 14.8 us
    pallas_call x13 -> x12, Pallas kernels: 15.8 us -> 14.8 us  [call(): run(*(pin(x, f) if f else x for x, f in zip(args, fixed, strict=True)))]
  transfers between devices with their start and end apart: 19 -> 19, of which waited for: 9 -> 9; matrix products, arithmetic and copies ran while one was open for 0% -> 0% of each run, Pallas kernels for 10% -> 7%
where the time goes in v9:
time: 86.6 us; the launch traced here: 86.2 us
  waiting for transfers between devices  30.2 us (35%)
  starting transfers between devices  29.9 us (35%)
  Pallas kernels  14.8 us (17%)
  blocking collectives  10.3 us (12%)
  between operations  0.88 us (1%)
    ppermute x14, waiting for transfers between devices, swap(): return lax.ppermute(x, 'chan', [(i, i ^ k) for i in range(n)])  17.6 us
    pallas_call x12, Pallas kernels, call(): run(*(pin(x, f) if f else x for x, f in zip(args, fixed, strict=True)))  14.8 us
    ppermute x14, starting transfers between devices, swap(): return lax.ppermute(x, 'chan', [(i, i ^ k) for i in range(n)])  14.4 us
    all_gather x1, blocking collectives, local(): packed = lax.all_gather(gathered, BOTH, axis_index_groups=share)  10.3 us
    all_to_all x1, waiting for transfers between devices, local(): returned = lax.all_to_all(spread.reshape(32, slots_dev, 256), BOTH, 0, 0)  8.79 us
    all_to_all x1, starting transfers between devices, local(): arrived = lax.all_to_all(sent, 'chan', 0, 0, tiled=True)  5.95 us
    all_to_all x1, starting transfers between devices, local(): returned = lax.all_to_all(spread.reshape(32, slots_dev, 256), BOTH, 0, 0)  3.85 us
    ppermute x1, waiting for transfers between devices, local(): lax.ppermute(g[2], 'tm', [(0, 1), (1, 0)])  3.81 us
  transfers between devices with their start and end apart: 19, of which 9 were waited for; matrix products, arithmetic and copies ran while one was open for 0% of the time, Pallas kernels for 7%

profile of v9, /device:TPU:0, one launch (start us, length us, event | category | flops | bytes accessed | tf_op | source)
XLA Modules:
  0.0 86.2 jit_solution(7333521712990005273)
XLA Ops:
  0.6 2.3 %shard_map.136 = (bf16[16,40,256]{2,1,0:T(8,128)(2,1)}, bf16[3,32,1024]{2,1,0:T(8,128)(2,1)S(1)}, bf16[192,128]{1,0:T(8,128)(2,1)S(1)}) custom-call(s32[8]{0:T(128)} %spk.1, f32[320,1024]{1,0:T(8,128)} %bitcast.25, bf16[32,1024]{1,0:T(8,128)(2,1)} %bitcast.19, bf16[32,1024]{1,0:T(8,128)(2,1)} %bitcast.21, bf16[32,1024]{1,0:T(8,128)(2,1)} %bitcast.28, ...), custom_call_target="tpu_custom_call" | custom-call | bytes 1048576 | tf_op jit(solution)/shard_map/pallas_call | solution.py:74
  3.0 3.0 %collective-permute-start = (bf16[192,128]{1,0:T(8,128)(2,1)S(1)}, bf16[192,128]{1,0:T(8,128)(2,1)S(1)}, u32[]{:S(2)}, u32[]{:S(2)}) collective-permute-start(bf16[192,128]{1,0:T(8,128)(2,1)S(1)} %get-tuple-element.40), channel_id=1, source_target_pairs={{0,16},{16,0},{1,17},{17,1},{2,18},{18,2},{3,19},{19,3},{4,20},{20... | collective-permute-start | bytes 147464 | tf_op jit(solution)/shard_map/ppermute | solution.py:420
  6.0 6.0 %all-to-all-start = ((bf16[16,40,256]{2,1,0:T(8,128)(2,1)}), bf16[16,40,256]{2,1,0:T(8,128)(2,1)}, u32[]{:S(2)}, u32[]{:S(2)}) async-start(bf16[16,40,256]{2,1,0:T(8,128)(2,1)} %get-tuple-element.42), calls=%async_computation | async-start | bytes 655360 | tf_op jit(solution)/shard_map/all_to_all | solution.py:423
  12.2 0.4 collective-permute-start.1
  12.7 1.7 %collective-permute-start.2 = (bf16[112,256]{1,0:T(8,128)(2,1)S(1)}, bf16[112,256]{1,0:T(8,128)(2,1)S(1)}, u32[]{:S(2)}, u32[]{:S(2)}) collective-permute-start(bf16[112,256]{1,0:T(8,128)(2,1)S(1)} %get-tuple-element.46), channel_id=1, source_target_pairs={{0,2},{1,3},{2,0},{3,1},{4,6},{5,7},{6,4},{7,5},{8,10},{9,11},{10,... | collective-permute-start | bytes 172040 | tf_op jit(solution)/shard_map/ppermute | solution.py:395
  14.4 1.0 %shard_map.137 = (s32[224,128]{1,0:T(8,128)S(1)}, bf16[640,224]{1,0:T(8,128)(2,1)S(1)}, s32[8,128]{1,0:T(8,128)S(1)}) custom-call(s32[8]{0:T(128)S(1)} %copy-done.12, s32[1,320]{1,0:T(1,128)S(1)} %reshape.40.owners, bf16[192,128]{1,0:T(8,128)(2,1)S(1)} %collective-permute-done.other), custom_call_target="tpu_custom_call" | custom-call | bytes 1048576 | tf_op jit(solution)/shard_map/pallas_call | solution.py:74
  15.4 3.6 %collective-permute-done.2.o2 = bf16[112,256]{1,0:T(8,128)(2,1)S(1)} collective-permute-done((bf16[112,256]{1,0:T(8,128)(2,1)S(1)}, bf16[112,256]{1,0:T(8,128)(2,1)S(1)}, u32[]{:S(2)}, u32[]{:S(2)}) %collective-permute-start.2) | collective-permute-done | bytes 57376 | tf_op jit(solution)/shard_map/ppermute | solution.py:395
  19.3 0.7 shard_map.139
  20.0 4.3 %collective-permute-start.6 = (bf16[400,256]{1,0:T(8,128)(2,1)}, bf16[400,256]{1,0:T(8,128)(2,1)}, u32[]{:S(2)}, u32[]{:S(2)}) collective-permute-start(bf16[400,256]{1,0:T(8,128)(2,1)} %shard_map.139), channel_id=1, source_target_pairs={{0,12},{1,13},{2,14},{3,15},{4,8},{5,9},{6,10},{7,11},{8,4},{9,5},... | collective-permute-start | bytes 614408 | tf_op jit(solution)/shard_map/ppermute | solution.py:395
  24.3 0.6 collective-permute-start.4
  24.9 1.5 %shard_map.140 = bf16[224,256]{1,0:T(8,128)(2,1)S(1)} custom-call(s32[224,128]{1,0:T(8,128)S(1)} %get-tuple-element.41.at_col, bf16[640,256]{1,0:T(8,128)(2,1)} %bitcast.5.slots), custom_call_target="tpu_custom_call" | custom-call | flops 199999995904 | bytes 1048576 | tf_op jit(solution)/shard_map/pallas_call | solution.py:74
  26.4 10.3 %all-gather = bf16[1792,256]{1,0:T(8,128)(2,1)S(1)} all-gather(bf16[224,256]{1,0:T(8,128)(2,1)S(1)} %shard_map.140), channel_id=2, replica_groups={{0,1,2,3,16,17,18,19},{4,5,6,7,20,21,22,23},{8,9,10,11,24,25,26,27},{12..., dimensions={0}, use_global_device_ids=true | all-gather | bytes 1032192 | tf_op jit(solution)/shard_map/all_gather | solution.py:441
  36.8 5.6 %collective-permute-done.5.p2 = bf16[400,256]{1,0:T(8,128)(2,1)} collective-permute-done((bf16[400,256]{1,0:T(8,128)(2,1)}, bf16[400,256]{1,0:T(8,128)(2,1)}, u32[]{:S(2)}, u32[]{:S(2)}) %collective-permute-start.5) | collective-permute-done | bytes 204832 | tf_op jit(solution)/shard_map/ppermute | solution.py:395
  42.4 2.7 %shard_map.141 = (f32[4,224,256]{2,1,0:T(8,128)S(1)}, bf16[4,224,256]{2,1,0:T(8,128)(2,1)S(1)}, bf16[128,256]{1,0:T(8,128)(2,1)S(1)}, bf16[256,384]{1,0:T(8,128)(2,1)S(1)}) custom-call(s32[8]{0:T(128)S(1)} %copy-done.13, bf16[8,224,256]{2,1,0:T(8,128)(2,1)S(1)} %bitcast.16, bf16[112,256]{1,0:T(8,128)(2,1)S(1)} %copy-done.5, bf16[112,256]{1,0:T(8,128)(2,1)S(1)} %copy-done.7, ...), custom_call_target="tpu_custom_call" | custom-call | flops 199999995904 | bytes 1048576 | tf_op jit(solution)/shard_map/pallas_call | solution.py:74
  45.3 0.7 shard_map.142
  46.0 1.0 %collective-permute-done.13.got = bf16[4,224,256]{2,1,0:T(8,128)(2,1)S(1)} collective-permute-done((bf16[4,224,256]{2,1,0:T(8,128)(2,1)S(1)}, bf16[4,224,256]{2,1,0:T(8,128)(2,1)S(1)}, u32[]{:S(2)}, u32[]{:S(2)}) %collective-permute-start.13) | collective-permute-done | bytes 458784 | tf_op jit(solution)/shard_map/ppermute | solution.py:395
  47.1 0.8 collective-permute-start.14
  47.9 3.0 %collective-permute-start.8 = (bf16[4,96,256]{2,1,0:T(8,128)(2,1)S(1)}, bf16[4,96,256]{2,1,0:T(8,128)(2,1)S(1)}, u32[]{:S(2)}, u32[]{:S(2)}) collective-permute-start(bf16[4,96,256]{2,1,0:T(8,128)(2,1)S(1)} %get-tuple-element.53), channel_id=1, source_target_pairs={{0,8},{1,9},{2,10},{3,11},{4,12},{5,13},{6,14},{7,15},{8,0},{9,1},... | collective-permute-start | bytes 589832 | tf_op jit(solution)/shard_map/ppermute | solution.py:395
  51.0 1.4 %collective-permute-start.9 = (bf16[4,96,256]{2,1,0:T(8,128)(2,1)S(1)}, bf16[4,96,256]{2,1,0:T(8,128)(2,1)S(1)}, u32[]{:S(2)}, u32[]{:S(2)}) collective-permute-start(bf16[4,96,256]{2,1,0:T(8,128)(2,1)S(1)} %get-tuple-element.54), channel_id=1, source_target_pairs={{0,12},{1,13},{2,14},{3,15},{4,8},{5,9},{6,10},{7,11},{8,4},{9,5},... | collective-permute-start | bytes 589832 | tf_op jit(solution)/shard_map/ppermute | solution.py:395
  52.3 0.5 collective-permute-start.15
  52.8 2.2 %collective-permute-start.16 = (bf16[224,256]{1,0:T(8,128)(2,1)S(1)}, bf16[224,256]{1,0:T(8,128)(2,1)S(1)}, u32[]{:S(2)}, u32[]{:S(2)}) collective-permute-start(bf16[224,256]{1,0:T(8,128)(2,1)S(1)} %get-tuple-element.70), channel_id=1, source_target_pairs={{0,18},{1,19},{2,16},{3,17},{4,22},{5,23},{6,20},{7,21},{8,26},{9,... | collective-permute-start | bytes 344072 | tf_op jit(solution)/shard_map/ppermute | solution.py:468
  55.0 3.8 %collective-permute-done.15.p2 = bf16[224,256]{1,0:T(8,128)(2,1)S(1)} collective-permute-done((bf16[224,256]{1,0:T(8,128)(2,1)S(1)}, bf16[224,256]{1,0:T(8,128)(2,1)S(1)}, u32[]{:S(2)}, u32[]{:S(2)}) %collective-permute-start.15) | collective-permute-done | bytes 114720 | tf_op jit(solution)/shard_map/ppermute | solution.py:468
  58.8 1.3 %shard_map.146 = bf16[2,640,256]{2,1,0:T(8,128)(2,1)} custom-call(bf16[640,224]{1,0:T(8,128)(2,1)S(1)} %get-tuple-element.63.put, f32[224,256]{1,0:T(8,128)S(1)} %get-tuple-element.67.p0, bf16[224,256]{1,0:T(8,128)(2,1)S(1)} %collective-permute-done.14.p1, bf16[224,256]{1,0:T(8,128)(2,1)S(1)} %collective-permute-done.15.p2, ...), custom_call_target="tpu_custom_call" | custom-call | bytes 1048576 | tf_op jit(solution)/shard_map/pallas_call | solution.py:74
  60.1 3.9 %all-to-all-start.1 = ((bf16[32,40,256]{2,1,0:T(8,128)(2,1)}), bf16[32,40,256]{2,1,0:T(8,128)(2,1)S(1)}, u32[]{:S(2)}, u32[]{:S(2)}) async-start(bf16[32,40,256]{2,1,0:T(8,128)(2,1)} %bitcast.10), calls=%async_computation.1 | async-start | bytes 1310720 | tf_op jit(solution)/shard_map/all_to_all | solution.py:471
  64.1 1.1 %collective-permute-done.8.z2 = bf16[4,96,256]{2,1,0:T(8,128)(2,1)S(1)} collective-permute-done((bf16[4,96,256]{2,1,0:T(8,128)(2,1)S(1)}, bf16[4,96,256]{2,1,0:T(8,128)(2,1)S(1)}, u32[]{:S(2)}, u32[]{:S(2)}) %collective-permute-start.8) | collective-permute-done | bytes 196640 | tf_op jit(solution)/shard_map/ppermute | solution.py:395
  65.3 1.2 %collective-permute-start.11 = (bf16[96,256]{1,0:T(8,128)(2,1)S(1)}, bf16[96,256]{1,0:T(8,128)(2,1)S(1)}, u32[]{:S(2)}, u32[]{:S(2)}) collective-permute-start(bf16[96,256]{1,0:T(8,128)(2,1)S(1)} %get-tuple-element.57), channel_id=1, source_target_pairs={{0,2},{1,3},{2,0},{3,1},{4,6},{5,7},{6,4},{7,5},{8,10},{9,11},{10,... | collective-permute-start | bytes 147464 | tf_op jit(solution)/shard_map/ppermute | solution.py:395
  66.5 0.7 collective-permute-start.12
  67.2 4.7 %collective-permute-done.11.o2 = bf16[96,256]{1,0:T(8,128)(2,1)S(1)} collective-permute-done((bf16[96,256]{1,0:T(8,128)(2,1)S(1)}, bf16[96,256]{1,0:T(8,128)(2,1)S(1)}, u32[]{:S(2)}, u32[]{:S(2)}) %collective-permute-start.11) | collective-permute-done | bytes 49184 | tf_op jit(solution)/shard_map/ppermute | solution.py:395
  71.9 1.2 %collective-permute-done.12.o3 = bf16[96,256]{1,0:T(8,128)(2,1)S(1)} collective-permute-done((bf16[96,256]{1,0:T(8,128)(2,1)S(1)}, bf16[96,256]{1,0:T(8,128)(2,1)S(1)}, u32[]{:S(2)}, u32[]{:S(2)}) %collective-permute-start.12) | collective-permute-done | bytes 49184 | tf_op jit(solution)/shard_map/ppermute | solution.py:395
  73.2 0.8 shard_map.144
  73.9 8.8 %all-to-all-done.1.grads = bf16[32,40,256]{2,1,0:T(8,128)(2,1)S(1)} async-done(((bf16[32,40,256]{2,1,0:T(8,128)(2,1)}), bf16[32,40,256]{2,1,0:T(8,128)(2,1)S(1)}, u32[]{:S(2)}, u32[]{:S(2)}) %all-to-all-start.1) | async-done | bytes 655392 | tf_op jit(solution)/shard_map/all_to_all | solution.py:471
  82.7 3.5 %shard_map.147 = (f32[320,1024]{1,0:T(8,128)}, f32[320,1024]{1,0:T(8,128)}, f32[320,1024]{1,0:T(8,128)}) custom-call(s32[8,128]{1,0:T(8,128)S(1)} %get-tuple-element.62.owned, bf16[32,40,256]{2,1,0:T(8,128)(2,1)S(1)} %all-to-all-done.1.grads, f32[320,1024]{1,0:T(8,128)} %bitcast.26, f32[320,1024]{1,0:T(8,128)S(1)} %bitcast.18, f32[320,1024]{1,0:T(8,128)} %bitcast.27), custom_call_target="tpu_custom_call" | custom-call | bytes 1048576 | tf_op jit(solution)/shard_map/pallas_call | solution.py:74
  (50 shorter events, 1.0 us)
Async XLA Ops:
  3.0 9.0 %collective-permute-start = (bf16[192,128]{1,0:T(8,128)(2,1)S(1)}, bf16[192,128]{1,0:T(8,128)(2,1)S(1)}, u32[]{:S(2)}, u32[]{:S(2)}) collective-permute-start(bf16[192,128]{1,0:T(8,128)(2,1)S(1)} %get-tuple-element.40), channel_id=1, source_target_pairs={{0,16},{16,0},{1,17},{17,1},{2,18},{18,2},{3,19},{19,3},{4,20},{20... | collective-permute-start | bytes 147464 | tf_op jit(solution)/shard_map/ppermute | solution.py:420
  6.0 18.9 %all-to-all-start = ((bf16[16,40,256]{2,1,0:T(8,128)(2,1)}), bf16[16,40,256]{2,1,0:T(8,128)(2,1)}, u32[]{:S(2)}, u32[]{:S(2)}) async-start(bf16[16,40,256]{2,1,0:T(8,128)(2,1)} %get-tuple-element.42), calls=%async_computation | async-start | bytes 655360 | tf_op jit(solution)/shard_map/all_to_all | solution.py:423
  12.2 7.0 %copy-start.4 = (bf16[112,256]{1,0:T(8,128)(2,1)}, bf16[112,256]{1,0:T(8,128)(2,1)S(1)}, u32[]{:S(2)}) copy-start(bf16[112,256]{1,0:T(8,128)(2,1)S(1)} %get-tuple-element.44.o0) | copy-start | bytes 172036
  12.2 3.1 %collective-permute-start.1 = (bf16[112,256]{1,0:T(8,128)(2,1)S(1)}, bf16[112,256]{1,0:T(8,128)(2,1)S(1)}, u32[]{:S(2)}, u32[]{:S(2)}) collective-permute-start(bf16[112,256]{1,0:T(8,128)(2,1)S(1)} %get-tuple-element.45), channel_id=1, source_target_pairs={{0,1},{1,0},{2,3},{3,2},{4,5},{5,4},{6,7},{7,6},{8,9},{9,8},{10,11... | collective-permute-start | bytes 172040 | tf_op jit(solution)/shard_map/ppermute | solution.py:395
  12.7 6.3 %collective-permute-start.2 = (bf16[112,256]{1,0:T(8,128)(2,1)S(1)}, bf16[112,256]{1,0:T(8,128)(2,1)S(1)}, u32[]{:S(2)}, u32[]{:S(2)}) collective-permute-start(bf16[112,256]{1,0:T(8,128)(2,1)S(1)} %get-tuple-element.46), channel_id=1, source_target_pairs={{0,2},{1,3},{2,0},{3,1},{4,6},{5,7},{6,4},{7,5},{8,10},{9,11},{10,... | collective-permute-start | bytes 172040 | tf_op jit(solution)/shard_map/ppermute | solution.py:395
  14.4 4.9 %collective-permute-start.3 = (bf16[112,256]{1,0:T(8,128)(2,1)S(1)}, bf16[112,256]{1,0:T(8,128)(2,1)S(1)}, u32[]{:S(2)}, u32[]{:S(2)}) collective-permute-start(bf16[112,256]{1,0:T(8,128)(2,1)S(1)} %get-tuple-element.47), channel_id=1, source_target_pairs={{0,3},{1,2},{2,1},{3,0},{4,7},{5,6},{6,5},{7,4},{8,11},{9,10},{10,... | collective-permute-start | bytes 172040 | tf_op jit(solution)/shard_map/ppermute | solution.py:395
  15.4 4.6 %copy-start.6 = (bf16[112,256]{1,0:T(8,128)(2,1)}, bf16[112,256]{1,0:T(8,128)(2,1)S(1)}, u32[]{:S(2)}) copy-start(bf16[112,256]{1,0:T(8,128)(2,1)S(1)} %collective-permute-done.1.o1) | copy-start | bytes 172036
  19.0 5.2 %copy-start.8 = (bf16[112,256]{1,0:T(8,128)(2,1)}, bf16[112,256]{1,0:T(8,128)(2,1)S(1)}, u32[]{:S(2)}) copy-start(bf16[112,256]{1,0:T(8,128)(2,1)S(1)} %collective-permute-done.2.o2) | copy-start | bytes 172036
  19.3 5.0 %copy-start.10 = (bf16[112,256]{1,0:T(8,128)(2,1)}, bf16[112,256]{1,0:T(8,128)(2,1)S(1)}, u32[]{:S(2)}) copy-start(bf16[112,256]{1,0:T(8,128)(2,1)S(1)} %collective-permute-done.3.o3) | copy-start | bytes 172036
  20.0 16.8 %collective-permute-start.6 = (bf16[400,256]{1,0:T(8,128)(2,1)}, bf16[400,256]{1,0:T(8,128)(2,1)}, u32[]{:S(2)}, u32[]{:S(2)}) collective-permute-start(bf16[400,256]{1,0:T(8,128)(2,1)} %shard_map.139), channel_id=1, source_target_pairs={{0,12},{1,13},{2,14},{3,15},{4,8},{5,9},{6,10},{7,11},{8,4},{9,5},... | collective-permute-start | bytes 614408 | tf_op jit(solution)/shard_map/ppermute | solution.py:395
  24.3 18.1 %collective-permute-start.5 = (bf16[400,256]{1,0:T(8,128)(2,1)}, bf16[400,256]{1,0:T(8,128)(2,1)}, u32[]{:S(2)}, u32[]{:S(2)}) collective-permute-start(bf16[400,256]{1,0:T(8,128)(2,1)} %shard_map.139), channel_id=1, source_target_pairs={{0,8},{1,9},{2,10},{3,11},{4,12},{5,13},{6,14},{7,15},{8,0},{9,1},... | collective-permute-start | bytes 614408 | tf_op jit(solution)/shard_map/ppermute | solution.py:395
  24.3 18.1 %collective-permute-start.4 = (bf16[400,256]{1,0:T(8,128)(2,1)}, bf16[400,256]{1,0:T(8,128)(2,1)}, u32[]{:S(2)}, u32[]{:S(2)}) collective-permute-start(bf16[400,256]{1,0:T(8,128)(2,1)} %shard_map.139), channel_id=1, source_target_pairs={{0,4},{1,5},{2,6},{3,7},{4,0},{5,1},{6,2},{7,3},{8,12},{9,13},{10,... | collective-permute-start | bytes 614408 | tf_op jit(solution)/shard_map/ppermute | solution.py:395
  24.9 17.5 %copy-start.3 = (bf16[1024,80]{0,1:T(8,128)(2,1)S(1)}, bf16[1024,80]{0,1:T(8,128)(2,1)}, u32[]{:S(2)}) copy-start(bf16[1024,80]{0,1:T(8,128)(2,1)} %param.10) | copy-start | bytes 491524
  24.9 17.5 %copy-start.5 = (bf16[112,256]{1,0:T(8,128)(2,1)S(1)}, bf16[112,256]{1,0:T(8,128)(2,1)}, u32[]{:S(2)}) copy-start(bf16[112,256]{1,0:T(8,128)(2,1)} %copy-done.4) | copy-start | bytes 172036
  24.9 17.5 %copy-start.7 = (bf16[112,256]{1,0:T(8,128)(2,1)S(1)}, bf16[112,256]{1,0:T(8,128)(2,1)}, u32[]{:S(2)}) copy-start(bf16[112,256]{1,0:T(8,128)(2,1)} %copy-done.6) | copy-start | bytes 172036
  24.9 17.5 %copy-start.9 = (bf16[112,256]{1,0:T(8,128)(2,1)S(1)}, bf16[112,256]{1,0:T(8,128)(2,1)}, u32[]{:S(2)}) copy-start(bf16[112,256]{1,0:T(8,128)(2,1)} %copy-done.8) | copy-start | bytes 172036
  24.9 17.5 %copy-start.11 = (bf16[112,256]{1,0:T(8,128)(2,1)S(1)}, bf16[112,256]{1,0:T(8,128)(2,1)}, u32[]{:S(2)}) copy-start(bf16[112,256]{1,0:T(8,128)(2,1)} %copy-done.10) | copy-start | bytes 172036
  24.9 17.5 %copy-start.13 = (s32[8]{0:T(128)S(1)}, s32[8]{0:T(128)}, u32[]{:S(2)}) copy-start(s32[8]{0:T(128)} %spk.1) | copy-start | bytes 100
  45.1 1.9 %collective-permute-start.13 = (bf16[4,224,256]{2,1,0:T(8,128)(2,1)S(1)}, bf16[4,224,256]{2,1,0:T(8,128)(2,1)S(1)}, u32[]{:S(2)}, u32[]{:S(2)}) collective-permute-start(bf16[4,224,256]{2,1,0:T(8,128)(2,1)S(1)} %get-tuple-element.66), channel_id=1, source_target_pairs={{0,1},{1,0},{2,3},{3,2},{4,5},{5,4},{6,7},{7,6},{8,9},{9,8},{10,11... | collective-permute-start | bytes 1376264 | tf_op jit(solution)/shard_map/ppermute | solution.py:395
  47.1 5.7 %collective-permute-start.14 = (bf16[224,256]{1,0:T(8,128)(2,1)S(1)}, bf16[224,256]{1,0:T(8,128)(2,1)S(1)}, u32[]{:S(2)}, u32[]{:S(2)}) collective-permute-start(bf16[224,256]{1,0:T(8,128)(2,1)S(1)} %get-tuple-element.68), channel_id=1, source_target_pairs={{0,2},{1,3},{2,0},{3,1},{4,6},{5,7},{6,4},{7,5},{8,10},{9,11},{10,... | collective-permute-start | bytes 344072 | tf_op jit(solution)/shard_map/ppermute | solution.py:395
  47.9 16.1 %collective-permute-start.7 = (bf16[4,96,256]{2,1,0:T(8,128)(2,1)S(1)}, bf16[4,96,256]{2,1,0:T(8,128)(2,1)S(1)}, u32[]{:S(2)}, u32[]{:S(2)}) collective-permute-start(bf16[4,96,256]{2,1,0:T(8,128)(2,1)S(1)} %get-tuple-element.52), channel_id=1, source_target_pairs={{0,4},{1,5},{2,6},{3,7},{4,0},{5,1},{6,2},{7,3},{8,12},{9,13},{10,... | collective-permute-start | bytes 589832 | tf_op jit(solution)/shard_map/ppermute | solution.py:395
  47.9 17.2 %collective-permute-start.8 = (bf16[4,96,256]{2,1,0:T(8,128)(2,1)S(1)}, bf16[4,96,256]{2,1,0:T(8,128)(2,1)S(1)}, u32[]{:S(2)}, u32[]{:S(2)}) collective-permute-start(bf16[4,96,256]{2,1,0:T(8,128)(2,1)S(1)} %get-tuple-element.53), channel_id=1, source_target_pairs={{0,8},{1,9},{2,10},{3,11},{4,12},{5,13},{6,14},{7,15},{8,0},{9,1},... | collective-permute-start | bytes 589832 | tf_op jit(solution)/shard_map/ppermute | solution.py:395
  51.0 14.2 %collective-permute-start.9 = (bf16[4,96,256]{2,1,0:T(8,128)(2,1)S(1)}, bf16[4,96,256]{2,1,0:T(8,128)(2,1)S(1)}, u32[]{:S(2)}, u32[]{:S(2)}) collective-permute-start(bf16[4,96,256]{2,1,0:T(8,128)(2,1)S(1)} %get-tuple-element.54), channel_id=1, source_target_pairs={{0,12},{1,13},{2,14},{3,15},{4,8},{5,9},{6,10},{7,11},{8,4},{9,5},... | collective-permute-start | bytes 589832 | tf_op jit(solution)/shard_map/ppermute | solution.py:395
  52.3 6.5 %collective-permute-start.15 = (bf16[224,256]{1,0:T(8,128)(2,1)S(1)}, bf16[224,256]{1,0:T(8,128)(2,1)S(1)}, u32[]{:S(2)}, u32[]{:S(2)}) collective-permute-start(bf16[224,256]{1,0:T(8,128)(2,1)S(1)} %get-tuple-element.69), channel_id=1, source_target_pairs={{0,16},{16,0},{1,17},{17,1},{2,18},{18,2},{3,19},{19,3},{4,20},{20... | collective-permute-start | bytes 344072 | tf_op jit(solution)/shard_map/ppermute | solution.py:468
  52.8 6.0 %collective-permute-start.16 = (bf16[224,256]{1,0:T(8,128)(2,1)S(1)}, bf16[224,256]{1,0:T(8,128)(2,1)S(1)}, u32[]{:S(2)}, u32[]{:S(2)}) collective-permute-start(bf16[224,256]{1,0:T(8,128)(2,1)S(1)} %get-tuple-element.70), channel_id=1, source_target_pairs={{0,18},{1,19},{2,16},{3,17},{4,22},{5,23},{6,20},{7,21},{8,26},{9,... | collective-permute-start | bytes 344072 | tf_op jit(solution)/shard_map/ppermute | solution.py:468
  60.1 22.6 %all-to-all-start.1 = ((bf16[32,40,256]{2,1,0:T(8,128)(2,1)}), bf16[32,40,256]{2,1,0:T(8,128)(2,1)S(1)}, u32[]{:S(2)}, u32[]{:S(2)}) async-start(bf16[32,40,256]{2,1,0:T(8,128)(2,1)} %bitcast.10), calls=%async_computation.1 | async-start | bytes 1310720 | tf_op jit(solution)/shard_map/all_to_all | solution.py:471
  64.0 9.1 %copy-start.1 = (bf16[1024,32]{0,1:T(8,128)(2,1)S(1)}, bf16[1024,32]{0,1:T(8,128)(2,1)}, u32[]{:S(2)}) copy-start(bf16[1024,32]{0,1:T(8,128)(2,1)} %param.9) | copy-start | bytes 196612
  64.0 9.1 %copy-start.2 = (bf16[1024,32]{0,1:T(8,128)(2,1)S(1)}, bf16[1024,32]{0,1:T(8,128)(2,1)}, u32[]{:S(2)}) copy-start(bf16[1024,32]{0,1:T(8,128)(2,1)} %param.16) | copy-start | bytes 196612
  64.0 18.7 %copy-start = (f32[40,8,1024]{2,1,0:T(8,128)S(1)}, f32[40,8,1024]{2,1,0:T(8,128)}, u32[]{:S(2)}) copy-start(f32[40,8,1024]{2,1,0:T(8,128)} %param.14) | copy-start | bytes 3932164
  65.2 1.9 %collective-permute-start.10 = (bf16[96,256]{1,0:T(8,128)(2,1)S(1)}, bf16[96,256]{1,0:T(8,128)(2,1)S(1)}, u32[]{:S(2)}, u32[]{:S(2)}) collective-permute-start(bf16[96,256]{1,0:T(8,128)(2,1)S(1)} %get-tuple-element.56), channel_id=1, source_target_pairs={{0,1},{1,0},{2,3},{3,2},{4,5},{5,4},{6,7},{7,6},{8,9},{9,8},{10,11... | collective-permute-start | bytes 147464 | tf_op jit(solution)/shard_map/ppermute | solution.py:395
  65.3 6.6 %collective-permute-start.11 = (bf16[96,256]{1,0:T(8,128)(2,1)S(1)}, bf16[96,256]{1,0:T(8,128)(2,1)S(1)}, u32[]{:S(2)}, u32[]{:S(2)}) collective-permute-start(bf16[96,256]{1,0:T(8,128)(2,1)S(1)} %get-tuple-element.57), channel_id=1, source_target_pairs={{0,2},{1,3},{2,0},{3,1},{4,6},{5,7},{6,4},{7,5},{8,10},{9,11},{10,... | collective-permute-start | bytes 147464 | tf_op jit(solution)/shard_map/ppermute | solution.py:395
  66.5 6.6 %collective-permute-start.12 = (bf16[96,256]{1,0:T(8,128)(2,1)S(1)}, bf16[96,256]{1,0:T(8,128)(2,1)S(1)}, u32[]{:S(2)}, u32[]{:S(2)}) collective-permute-start(bf16[96,256]{1,0:T(8,128)(2,1)S(1)} %get-tuple-element.58), channel_id=1, source_target_pairs={{0,3},{1,2},{2,1},{3,0},{4,7},{5,6},{6,5},{7,4},{8,11},{9,10},{10,... | collective-permute-start | bytes 147464 | tf_op jit(solution)/shard_map/ppermute | solution.py:395
  (2 other events, 4.7 us)

commit v10 on v9

--- a/solution.py
+++ b/solution.py
@@ -58,11 +58,12 @@
 
 
 def call(kernel, out, spaces, gflops=0, scratch=(), out_space=VMEM, pinned=()):
+    out_spaces = out_space if isinstance(out_space, tuple) else jax.tree.map(lambda _: out_space, out)
     run = pl.pallas_call(
         kernel,
         out_shape=out,
         in_specs=[pl.BlockSpec(memory_space=space) for space in spaces],
-        out_specs=jax.tree.map(lambda _: pl.BlockSpec(memory_space=out_space), out),
+        out_specs=jax.tree.map(lambda _, space: pl.BlockSpec(memory_space=space), out, out_spaces),
         scratch_shapes=list(scratch),
         compiler_params=pltpu.CompilerParams(vmem_limit_bytes=24 * MIB),
         cost_estimate=pl.CostEstimate(
@@ -79,7 +80,7 @@
     return onehot(natural == 2 * (split & 127) + (split >> 7))
 
 
-def begin(speakers, master, sig, res, skp, mel, sent, acts, edges, strips, spk, sems):
+def begin(speakers, master, sig, res, skp, mel, sent, acts, edges, strips, packed, spk, sems):
     half = lax.axis_index("tm")
     slots = sent.shape[1]
     cut = pl.ds(pl.multiple_of((1 - half) * 896, 128), 128)
@@ -107,7 +108,13 @@
         for j in range(4):
             low = strips[t, pl.ds(j, slots, stride=8), :]
             high = strips[t, pl.ds(4 + j, slots, stride=8), :]
-            sent[4 * (t // 2) + j, :, lanes] = jnp.where(half == 0, low, high).astype(BF16)
+            packed[4 * (t // 2) + j, :, lanes] = jnp.where(half == 0, low, high).astype(BF16)
+        if t % 2:
+            part = slice(2 * t - 2, 2 * t + 2)
+            copies.append(pltpu.make_async_copy(packed.at[part], sent.at[part], sems.at[13 + t // 2]))
+            copies[-1].start()
+    for copy in copies[13:]:
+        copy.wait()
 
 
 def pack_tokens(acts, other, o0, o1, o2, o3):
@@ -199,14 +206,22 @@
         out[...] = (kept[i ^ k] + got[i ^ k].astype(F32)).astype(out.dtype)
 
 
-def scatter_blocks(put, p0, p1, p2, p3, out):
+def scatter_blocks(put, p0, p1, p2, p3, out, held, sems):
     total = p0[...].astype(F32)
     for part in (p1, p2, p3):
         total = total + part[...].astype(F32)
     natural = dot(total.astype(BF16), gate_order(1)).astype(BF16)
-    spread = dot(put[...], natural).astype(BF16)
-    out[0] = spread
-    out[1] = spread
+    copies = []
+    rows = held.shape[0] // 2
+    for n in range(2):
+        part = slice(n * rows, (n + 1) * rows)
+        held[part, :] = dot(put[part, :], natural).astype(BF16)
+        for m in range(2):
+            copy = pltpu.make_async_copy(held.at[part], out.at[m, part], sems.at[2 * n + m])
+            copy.start()
+            copies.append(copy)
+    for copy in copies:
+        copy.wait()
 
 
 def sum_units(z0, z1, z2, z3, o0, o1, o2, o3):
@@ -216,40 +231,12 @@
         ).astype(BF16)
 
 
-def layer(spk, packed, o0, o1, o2, o3, p1, p2, p3, mel, other, kept, given, hidden_out, grad_out, feat, res, skp, natural, p0):
-    join(o0, o1, o2, o3, p0)
-    half, ch = lax.axis_index("tm"), lax.axis_index("chan")
-    j = ch & 3
-    got = (p0, p1, p2, p3)
+def turn(spk, packed, mel, other, conv, out, extra):
+    half, j = lax.axis_index("tm"), lax.axis_index("chan") & 3
     tokens, wide = 256, 384
-    for k in range(4):
-        for i in range(4):
-            rows = pl.ds(pl.multiple_of(32 * (ch ^ (4 * k + i)), 32), 32)
-            for n in range(3):
-                at = 96 * i + 32 * n
-                for h in range(2):
-                    natural[2 * n + h, rows, :] = got[k][at : at + 32, 128 * h : 128 * h + 128].astype(F32)
-
-    ends = [part[384:400, :].astype(F32) for part in got]
-    gap = jnp.zeros((96, 128), F32)
-    for k, end in enumerate(ends):
-        left, right = end[:, 0:128], end[:, 128:256]
-        tile = jnp.concatenate([left[8:16], right, gap, left[0:8]], 0).T
-        for i in range(4):
-            rows = pl.ds(pl.multiple_of(32 * (ch ^ (4 * k + i)), 32), 32)
-            natural[6, rows, :] = tile[32 * i : 32 * i + 32]
-
-    def majors(n):
-        return jnp.concatenate([natural[n, pl.ds(r, 64, stride=8), :] for r in range(8)], 0)
-
-    tile = majors(6)
-    sig = jnp.concatenate([majors(0), majors(1), tile], 1)
-    for n, out in ((1, res), (2, skp)):
-        out[:, 0:128] = majors(2 * n).astype(BF16)
-        out[:, 128:256] = majors(2 * n + 1).astype(BF16)
-        out[:, 256:384] = pltpu.roll(tile, 128 - 8 * n, 1).astype(BF16)
-    shifted = pltpu.roll(sig, DILATION, 1).astype(BF16)
-    sig = sig.astype(BF16)
+    same = onehot(iota((256, 256), 0) == iota((256, 256), 1))
+    conv[...] = dot(same, packed[:, 0:OUT_AT, :].reshape(8 * OUT_AT, 256), NT).astype(BF16)
+    out[...] = dot(same, packed[:, OUT_AT:PACKED, :].reshape(RESID, 256), NT).astype(BF16)
     m = iota((128, MELS), 0)
     mel_pick = onehot(((m & 15) < MEL_BLOCKS) & (iota((128, MELS), 1) == 8 * (m & 15) + (m >> 4)))
     cut = pl.ds(pl.multiple_of(j * tokens, tokens), tokens)
@@ -266,20 +253,54 @@
         jnp.where(lane < 2 * SEG, spk[2 * j + 1] & 7, jnp.broadcast_to(beyond, (16, wide))),
     )
     for r in range(8):
+        extra[r, 0:16] = mels[16 * r : 16 * r + 16]
+        extra[r, 16:32] = onehot((row == seg + (lane >> 7)) & (sub == r))
+
+
+def layer(conv, out, extra, o0, o1, o2, o3, p1, p2, p3, kept, given, hidden_out, grad_out, feat, res, skp, natural, p0):
+    join(o0, o1, o2, o3, p0)
+    ch = lax.axis_index("chan")
+    got = (p0, p1, p2, p3)
+    tokens, wide = 256, 384
+    for k in range(4):
+        for i in range(4):
+            rows = pl.ds(pl.multiple_of(32 * (ch ^ (4 * k + i)), 32), 32)
+            for n in range(3):
+                at = 96 * i + 32 * n
+                for h in range(2):
+                    natural[2 * n + h, rows, :] = got[k][at : at + 32, 128 * h : 128 * h + 128].astype(F32)
+
+    ends = [part[384:400, :].astype(F32) for part in got]
+    gap = jnp.zeros((96, 128), F32)
+    for k, end in enumerate(ends):
+        left, right = end[:, 0:128], end[:, 128:256]
+        tile = jnp.concatenate([left[8:16], right, gap, left[0:8]], 0).T
+        for i in range(4):
+            rows = pl.ds(pl.multiple_of(32 * (ch ^ (4 * k + i)), 32), 32)
+            natural[6, rows, :] = tile[32 * i : 32 * i + 32]
+
+    def majors(n):
+        return jnp.concatenate([natural[n, pl.ds(r, 64, stride=8), :] for r in range(8)], 0)
+
+    tile = majors(6)
+    sig = jnp.concatenate([majors(0), majors(1), tile], 1)
+    for n, cot in ((1, res), (2, skp)):
+        cot[:, 0:128] = majors(2 * n).astype(BF16)
+        cot[:, 128:256] = majors(2 * n + 1).astype(BF16)
+        cot[:, 256:384] = pltpu.roll(tile, 128 - 8 * n, 1).astype(BF16)
+    shifted = pltpu.roll(sig, DILATION, 1).astype(BF16)
+    sig = sig.astype(BF16)
+    for r in range(8):
         feat[r, 0:64] = shifted[64 * r : 64 * r + 64]
         feat[r, 64:128] = sig[64 * r : 64 * r + 64]
-        feat[r, 128:144] = mels[16 * r : 16 * r + 16]
-        feat[r, 144:160] = onehot((row == seg + (lane >> 7)) & (sub == r))
+        feat[r, 128:160] = extra[r]
     features = feat[...].reshape(8 * OUT_AT, wide)
-    conv = packed[:, 0:OUT_AT, :].reshape(8 * OUT_AT, 256)
-    pre = dot(conv, features, TN)
+    pre = dot(conv[...], features)
     filt = jnp.tanh(pre[:128])
     gate = jax.nn.sigmoid(pre[128:])
     hidden = (filt[:, :tokens] * gate[:, :tokens]).astype(BF16)
-    out_res = packed[:, OUT_AT:PACKED, 0:128].reshape(RESID, 128)
-    out_skp = packed[:, OUT_AT:PACKED, 128:256].reshape(RESID, 128)
     hidden_out[...] = hidden
-    grad_hidden = dot(out_res, res[...], TN) + dot(out_skp, skp[...], TN)
+    grad_hidden = dot(out[0:128, :], res[...]) + dot(out[128:256, :], skp[...])
     grad_pre = jnp.concatenate(
         [
             grad_hidden * gate * (1.0 - filt * filt),
@@ -413,13 +434,15 @@
         (HBM,) * 6,
         scratch=(
             pltpu.VMEM((8, 8 * slots_dev, 128), F32),
+            pltpu.VMEM((16, slots_dev, 256), BF16),
             pltpu.SMEM(speaker_ids.shape, jnp.int32),
-            dma((13,)),
+            dma((17,)),
         ),
+        out_space=(HBM, VMEM, VMEM),
     )(speaker_ids, master.reshape(flat), sig, res, skp, mel)
     other = lax.ppermute(edges, "tm", [(0, 1), (1, 0)])
     piece = sds((PIECE, 256), BF16)
-    o = call(pack_tokens, (piece,) * 4, (VMEM,) * 2, gflops=200)(acts, other)
+    o = call(pack_tokens, (piece,) * 4, (VMEM,) * 2, gflops=8)(acts, other)
     arrived = lax.all_to_all(sent, "chan", 0, 0, tiled=True)
     o = (o[0], swap(o[1], 1), swap(o[2], 2), swap(o[3], 3))
     mine = call(join, sds((400, 256), BF16), (VMEM,) * 4)(*o)
@@ -435,16 +458,26 @@
         (SMEM, VMEM, VMEM),
     )(speaker_ids, own_row, other)
     arrived, _ = lax.optimization_barrier((arrived, mine))
-    gathered = call(gather_blocks, sds((PACKED, 256), BF16), (VMEM, VMEM), gflops=200)(
+    gathered = call(gather_blocks, sds((PACKED, 256), BF16), (VMEM, VMEM), gflops=8)(
         at_col, arrived.reshape(slots, 256)
     )
     packed = lax.all_gather(gathered, BOTH, axis_index_groups=share)
     rows = (4, PACKED, 256)
+    turned = call(
+        turn,
+        (
+            sds((256, 8 * OUT_AT), BF16),
+            sds((256, RESID), BF16),
+            sds((8, OUT_AT - TAPS, 384), BF16),
+        ),
+        (SMEM,) + (VMEM,) * 3,
+        gflops=8,
+    )(speaker_ids, packed, mel, other)
     kept, given, hidden, grad_pre = call(
         layer,
         (sds(rows, F32), sds(rows, BF16), sds((128, 256), BF16), sds((256, 384), BF16)),
-        (SMEM,) + (VMEM,) * 10,
-        gflops=200,
+        (VMEM,) * 10,
+        gflops=0,
         scratch=(
             pltpu.VMEM((8, OUT_AT, 384), BF16),
             pltpu.VMEM((RESID, 384), BF16),
@@ -452,7 +485,7 @@
             pltpu.VMEM((7, RESID, 128), F32),
             pltpu.VMEM((400, 256), BF16),
         ),
-    )(speaker_ids, packed, *o, p1, p2, p3, mel, other)
+    )(*turned, *o, p1, p2, p3)
     z0, z1, z2, z3 = call(
         outputs,
         (sds((4, 96, 256), BF16),) * 4,
@@ -467,7 +500,13 @@
     across = [(16 * y + i, 16 * (1 - y) + (i ^ 2)) for y in range(2) for i in range(n)]
     g = (g[0], swap(g[1], 2), lax.ppermute(g[2], "tm", [(0, 1), (1, 0)]), lax.ppermute(g[3], BOTH, across))
     t1, t2, t3 = (swap(z, 4 * k) for k, z in ((1, z1), (2, z2), (3, z3)))
-    spread = call(scatter_blocks, sds((2, slots, 256), BF16), (VMEM,) * 5)(put, *g)
+    spread = call(
+        scatter_blocks,
+        sds((2, slots, 256), BF16),
+        (VMEM,) * 5,
+        scratch=(pltpu.VMEM((slots, 256), BF16), dma((4,))),
+        out_space=HBM,
+    )(put, *g)
     returned = lax.all_to_all(spread.reshape(32, slots_dev, 256), BOTH, 0, 0)
     o = call(sum_units, (sds((96, 256), BF16),) * 4, (VMEM,) * 4, gflops=20)(z0, t1, t2, t3)
     o = (o[0], swap(o[1], 1), swap(o[2], 2), swap(o[3], 3))

time: 86.6 us -> 84.4 us (0.975)
  Pallas kernels: 14.8 us -> 12.9 us
    pallas_call x12 -> x13, Pallas kernels: 14.8 us -> 12.9 us  [call(): run(*(pin(x, f) if f else x for x, f in zip(args, fixed, strict=True)))]
where the time goes in v10:
time: 84.4 us; the launch traced here: 84 us
  waiting for transfers between devices  30.3 us (36%)
  starting transfers between devices  29.7 us (35%)
  Pallas kernels  12.9 us (15%)
  blocking collectives  10.2 us (12%)
    ppermute x14, waiting for transfers between devices, swap(): return lax.ppermute(x, 'chan', [(i, i ^ k) for i in range(n)])  17.4 us
    ppermute x14, starting transfers between devices, swap(): return lax.ppermute(x, 'chan', [(i, i ^ k) for i in range(n)])  14.1 us
    pallas_call x13, Pallas kernels, call(): run(*(pin(x, f) if f else x for x, f in zip(args, fixed, strict=True)))  12.9 us
    all_gather x1, blocking collectives, local(): packed = lax.all_gather(gathered, BOTH, axis_index_groups=share)  10.2 us
    all_to_all x1, waiting for transfers between devices, local(): returned = lax.all_to_all(spread.reshape(32, slots_dev, 256), BOTH, 0, 0)  9.1 us
    all_to_all x1, starting transfers between devices, local(): arrived = lax.all_to_all(sent, 'chan', 0, 0, tiled=True)  5.91 us
    ppermute x1, waiting for transfers between devices, local(): lax.ppermute(g[2], 'tm', [(0, 1), (1, 0)])  3.79 us
    all_to_all x1, starting transfers between devices, local(): returned = lax.all_to_all(spread.reshape(32, slots_dev, 256), BOTH, 0, 0)  3.62 us
  transfers between devices with their start and end apart: 19, of which 9 were waited for; matrix products, arithmetic and copies ran while one was open for 0% of the time, Pallas kernels for 7%

profile of v10, /device:TPU:0, one launch (start us, length us, event | category | flops | bytes accessed | tf_op | source)
XLA Modules:
  0.0 84.0 jit_solution(6801103624778841159)
XLA Ops:
  0.6 2.3 %shard_map.136 = (bf16[16,40,256]{2,1,0:T(8,128)(2,1)}, bf16[3,32,1024]{2,1,0:T(8,128)(2,1)S(1)}, bf16[192,128]{1,0:T(8,128)(2,1)S(1)}) custom-call(s32[8]{0:T(128)} %spk.1, f32[320,1024]{1,0:T(8,128)} %bitcast.26, bf16[32,1024]{1,0:T(8,128)(2,1)} %bitcast.20, bf16[32,1024]{1,0:T(8,128)(2,1)} %bitcast.22, bf16[32,1024]{1,0:T(8,128)(2,1)} %bitcast.29, ...), custom_call_target="tpu_custom_call" | custom-call | bytes 1048576 | tf_op jit(solution)/shard_map/pallas_call | solution.py:75
  2.9 3.0 %collective-permute-start = (bf16[192,128]{1,0:T(8,128)(2,1)S(1)}, bf16[192,128]{1,0:T(8,128)(2,1)S(1)}, u32[]{:S(2)}, u32[]{:S(2)}) collective-permute-start(bf16[192,128]{1,0:T(8,128)(2,1)S(1)} %get-tuple-element.43), channel_id=1, source_target_pairs={{0,16},{16,0},{1,17},{17,1},{2,18},{18,2},{3,19},{19,3},{4,20},{20... | collective-permute-start | bytes 147464 | tf_op jit(solution)/shard_map/ppermute | solution.py:443
  6.0 5.9 %all-to-all-start = ((bf16[16,40,256]{2,1,0:T(8,128)(2,1)}), bf16[16,40,256]{2,1,0:T(8,128)(2,1)S(1)}, u32[]{:S(2)}, u32[]{:S(2)}) async-start(bf16[16,40,256]{2,1,0:T(8,128)(2,1)} %get-tuple-element.45), calls=%async_computation | async-start | bytes 655360 | tf_op jit(solution)/shard_map/all_to_all | solution.py:446
  12.1 0.4 collective-permute-start.1
  12.5 1.7 %collective-permute-start.2 = (bf16[112,256]{1,0:T(8,128)(2,1)S(1)}, bf16[112,256]{1,0:T(8,128)(2,1)S(1)}, u32[]{:S(2)}, u32[]{:S(2)}) collective-permute-start(bf16[112,256]{1,0:T(8,128)(2,1)S(1)} %get-tuple-element.49), channel_id=1, source_target_pairs={{0,2},{1,3},{2,0},{3,1},{4,6},{5,7},{6,4},{7,5},{8,10},{9,11},{10,... | collective-permute-start | bytes 172040 | tf_op jit(solution)/shard_map/ppermute | solution.py:416
  14.2 1.0 %shard_map.137 = (s32[224,128]{1,0:T(8,128)S(1)}, bf16[640,224]{1,0:T(8,128)(2,1)S(1)}, s32[8,128]{1,0:T(8,128)S(1)}) custom-call(s32[8]{0:T(128)S(1)} %copy-done.4, s32[1,320]{1,0:T(1,128)S(1)} %reshape.40.owners, bf16[192,128]{1,0:T(8,128)(2,1)S(1)} %collective-permute-done.other), custom_call_target="tpu_custom_call" | custom-call | bytes 1048576 | tf_op jit(solution)/shard_map/pallas_call | solution.py:75
  15.3 3.6 %collective-permute-done.2.o2 = bf16[112,256]{1,0:T(8,128)(2,1)S(1)} collective-permute-done((bf16[112,256]{1,0:T(8,128)(2,1)S(1)}, bf16[112,256]{1,0:T(8,128)(2,1)S(1)}, u32[]{:S(2)}, u32[]{:S(2)}) %collective-permute-start.2) | collective-permute-done | bytes 57376 | tf_op jit(solution)/shard_map/ppermute | solution.py:416
  19.2 4.4 %collective-permute-start.6 = (bf16[400,256]{1,0:T(8,128)(2,1)S(1)}, bf16[400,256]{1,0:T(8,128)(2,1)S(1)}, u32[]{:S(2)}, u32[]{:S(2)}) collective-permute-start(bf16[400,256]{1,0:T(8,128)(2,1)S(1)} %shard_map.139), channel_id=1, source_target_pairs={{0,12},{1,13},{2,14},{3,15},{4,8},{5,9},{6,10},{7,11},{8,4},{9,5},... | collective-permute-start | bytes 614408 | tf_op jit(solution)/shard_map/ppermute | solution.py:416
  23.6 0.6 collective-permute-start.4
  24.2 0.4 shard_map.140
  24.7 10.2 %all-gather = bf16[1792,256]{1,0:T(8,128)(2,1)S(1)} all-gather(bf16[224,256]{1,0:T(8,128)(2,1)S(1)} %shard_map.140), channel_id=2, replica_groups={{0,1,2,3,16,17,18,19},{4,5,6,7,20,21,22,23},{8,9,10,11,24,25,26,27},{12..., dimensions={0}, use_global_device_ids=true | all-gather | bytes 1032192 | tf_op jit(solution)/shard_map/all_gather | solution.py:464
  34.9 1.0 %shard_map.141 = (bf16[256,1280]{1,0:T(8,128)(2,1)S(1)}, bf16[256,512]{1,0:T(8,128)(2,1)S(1)}, bf16[8,32,384]{2,1,0:T(8,128)(2,1)S(1)}) custom-call(s32[8]{0:T(128)S(1)} %copy-done.4, bf16[8,224,256]{2,1,0:T(8,128)(2,1)S(1)} %bitcast.16, bf16[80,1024]{1,0:T(8,128)(2,1)S(1)} %bitcast.25, bf16[192,128]{1,0:T(8,128)(2,1)S(1)} %collective-permute-done.other), custom_call_target="tpu_custom_call" | custom-call | flops 8000000000 | bytes 1048576 | tf_op jit(solution)/shard_map/pallas_call | solution.py:75
  35.9 5.6 %collective-permute-done.5.p2 = bf16[400,256]{1,0:T(8,128)(2,1)S(1)} collective-permute-done((bf16[400,256]{1,0:T(8,128)(2,1)S(1)}, bf16[400,256]{1,0:T(8,128)(2,1)S(1)}, u32[]{:S(2)}, u32[]{:S(2)}) %collective-permute-start.5) | collective-permute-done | bytes 204832 | tf_op jit(solution)/shard_map/ppermute | solution.py:416
  41.5 1.5 %shard_map.142 = (f32[4,224,256]{2,1,0:T(8,128)S(1)}, bf16[4,224,256]{2,1,0:T(8,128)(2,1)S(1)}, bf16[128,256]{1,0:T(8,128)(2,1)S(1)}, bf16[256,384]{1,0:T(8,128)(2,1)S(1)}) custom-call(bf16[256,1280]{1,0:T(8,128)(2,1)S(1)} %get-tuple-element.52.conv, bf16[256,512]{1,0:T(8,128)(2,1)S(1)} %get-tuple-element.53.out, ...), custom_call_target="tpu_custom_call" | custom-call | bytes 1048576 | tf_op jit(solution)/shard_map/pallas_call | solution.py:75
  43.2 0.7 shard_map.143
  43.9 1.0 %collective-permute-done.13.got = bf16[4,224,256]{2,1,0:T(8,128)(2,1)S(1)} collective-permute-done((bf16[4,224,256]{2,1,0:T(8,128)(2,1)S(1)}, bf16[4,224,256]{2,1,0:T(8,128)(2,1)S(1)}, u32[]{:S(2)}, u32[]{:S(2)}) %collective-permute-start.13) | collective-permute-done | bytes 458784 | tf_op jit(solution)/shard_map/ppermute | solution.py:416
  45.1 0.5 collective-permute-start.14
  45.6 3.0 %collective-permute-start.8 = (bf16[4,96,256]{2,1,0:T(8,128)(2,1)S(1)}, bf16[4,96,256]{2,1,0:T(8,128)(2,1)S(1)}, u32[]{:S(2)}, u32[]{:S(2)}) collective-permute-start(bf16[4,96,256]{2,1,0:T(8,128)(2,1)S(1)} %get-tuple-element.59), channel_id=1, source_target_pairs={{0,8},{1,9},{2,10},{3,11},{4,12},{5,13},{6,14},{7,15},{8,0},{9,1},... | collective-permute-start | bytes 589832 | tf_op jit(solution)/shard_map/ppermute | solution.py:416
  48.6 1.3 %collective-permute-start.9 = (bf16[4,96,256]{2,1,0:T(8,128)(2,1)S(1)}, bf16[4,96,256]{2,1,0:T(8,128)(2,1)S(1)}, u32[]{:S(2)}, u32[]{:S(2)}) collective-permute-start(bf16[4,96,256]{2,1,0:T(8,128)(2,1)S(1)} %get-tuple-element.60), channel_id=1, source_target_pairs={{0,12},{1,13},{2,14},{3,15},{4,8},{5,9},{6,10},{7,11},{8,4},{9,5},... | collective-permute-start | bytes 589832 | tf_op jit(solution)/shard_map/ppermute | solution.py:416
  50.0 0.5 collective-permute-start.15
  50.5 2.5 %collective-permute-start.16 = (bf16[224,256]{1,0:T(8,128)(2,1)S(1)}, bf16[224,256]{1,0:T(8,128)(2,1)S(1)}, u32[]{:S(2)}, u32[]{:S(2)}) collective-permute-start(bf16[224,256]{1,0:T(8,128)(2,1)S(1)} %get-tuple-element.76), channel_id=1, source_target_pairs={{0,18},{1,19},{2,16},{3,17},{4,22},{5,23},{6,20},{7,21},{8,26},{9,... | collective-permute-start | bytes 344072 | tf_op jit(solution)/shard_map/ppermute | solution.py:501
  53.0 3.8 %collective-permute-done.15.p2 = bf16[224,256]{1,0:T(8,128)(2,1)S(1)} collective-permute-done((bf16[224,256]{1,0:T(8,128)(2,1)S(1)}, bf16[224,256]{1,0:T(8,128)(2,1)S(1)}, u32[]{:S(2)}, u32[]{:S(2)}) %collective-permute-start.15) | collective-permute-done | bytes 114720 | tf_op jit(solution)/shard_map/ppermute | solution.py:501
  56.8 1.3 %shard_map.147 = bf16[2,640,256]{2,1,0:T(8,128)(2,1)} custom-call(bf16[640,224]{1,0:T(8,128)(2,1)S(1)} %get-tuple-element.69.put, f32[224,256]{1,0:T(8,128)S(1)} %get-tuple-element.73.p0, bf16[224,256]{1,0:T(8,128)(2,1)S(1)} %collective-permute-done.14.p1, bf16[224,256]{1,0:T(8,128)(2,1)S(1)} %collective-permute-done.15.p2, ...), custom_call_target="tpu_custom_call" | custom-call | bytes 1048576 | tf_op jit(solution)/shard_map/pallas_call | solution.py:75
  58.1 3.6 %all-to-all-start.1 = ((bf16[32,40,256]{2,1,0:T(8,128)(2,1)}), bf16[32,40,256]{2,1,0:T(8,128)(2,1)S(1)}, u32[]{:S(2)}, u32[]{:S(2)}) async-start(bf16[32,40,256]{2,1,0:T(8,128)(2,1)} %bitcast.10), calls=%async_computation.1 | async-start | bytes 1310720 | tf_op jit(solution)/shard_map/all_to_all | solution.py:510
  61.8 1.0 %collective-permute-done.8.z2 = bf16[4,96,256]{2,1,0:T(8,128)(2,1)S(1)} collective-permute-done((bf16[4,96,256]{2,1,0:T(8,128)(2,1)S(1)}, bf16[4,96,256]{2,1,0:T(8,128)(2,1)S(1)}, u32[]{:S(2)}, u32[]{:S(2)}) %collective-permute-start.8) | collective-permute-done | bytes 196640 | tf_op jit(solution)/shard_map/ppermute | solution.py:416
  63.0 1.5 %collective-permute-start.11 = (bf16[96,256]{1,0:T(8,128)(2,1)S(1)}, bf16[96,256]{1,0:T(8,128)(2,1)S(1)}, u32[]{:S(2)}, u32[]{:S(2)}) collective-permute-start(bf16[96,256]{1,0:T(8,128)(2,1)S(1)} %get-tuple-element.63), channel_id=1, source_target_pairs={{0,2},{1,3},{2,0},{3,1},{4,6},{5,7},{6,4},{7,5},{8,10},{9,11},{10,... | collective-permute-start | bytes 147464 | tf_op jit(solution)/shard_map/ppermute | solution.py:416
  64.5 0.3 collective-permute-start.12
  64.9 4.9 %collective-permute-done.11.o2 = bf16[96,256]{1,0:T(8,128)(2,1)S(1)} collective-permute-done((bf16[96,256]{1,0:T(8,128)(2,1)S(1)}, bf16[96,256]{1,0:T(8,128)(2,1)S(1)}, u32[]{:S(2)}, u32[]{:S(2)}) %collective-permute-start.11) | collective-permute-done | bytes 49184 | tf_op jit(solution)/shard_map/ppermute | solution.py:416
  69.8 0.8 collective-permute-done.12.o3
  70.6 0.8 shard_map.145
  71.4 9.1 %all-to-all-done.1.grads = bf16[32,40,256]{2,1,0:T(8,128)(2,1)S(1)} async-done(((bf16[32,40,256]{2,1,0:T(8,128)(2,1)}), bf16[32,40,256]{2,1,0:T(8,128)(2,1)S(1)}, u32[]{:S(2)}, u32[]{:S(2)}) %all-to-all-start.1) | async-done | bytes 655392 | tf_op jit(solution)/shard_map/all_to_all | solution.py:510
  80.5 3.5 %shard_map.148 = (f32[320,1024]{1,0:T(8,128)}, f32[320,1024]{1,0:T(8,128)}, f32[320,1024]{1,0:T(8,128)}) custom-call(s32[8,128]{1,0:T(8,128)S(1)} %get-tuple-element.68.owned, bf16[32,40,256]{2,1,0:T(8,128)(2,1)S(1)} %all-to-all-done.1.grads, f32[320,1024]{1,0:T(8,128)} %bitcast.27, f32[320,1024]{1,0:T(8,128)S(1)} %bitcast.18, f32[320,1024]{1,0:T(8,128)} %bitcast.28), custom_call_target="tpu_custom_call" | custom-call | bytes 1048576 | tf_op jit(solution)/shard_map/pallas_call | solution.py:75
  (33 shorter events, 1.0 us)
Async XLA Ops:
  2.9 9.0 %collective-permute-start = (bf16[192,128]{1,0:T(8,128)(2,1)S(1)}, bf16[192,128]{1,0:T(8,128)(2,1)S(1)}, u32[]{:S(2)}, u32[]{:S(2)}) collective-permute-start(bf16[192,128]{1,0:T(8,128)(2,1)S(1)} %get-tuple-element.43), channel_id=1, source_target_pairs={{0,16},{16,0},{1,17},{17,1},{2,18},{18,2},{3,19},{19,3},{4,20},{20... | collective-permute-start | bytes 147464 | tf_op jit(solution)/shard_map/ppermute | solution.py:443
  6.0 18.3 %all-to-all-start = ((bf16[16,40,256]{2,1,0:T(8,128)(2,1)}), bf16[16,40,256]{2,1,0:T(8,128)(2,1)S(1)}, u32[]{:S(2)}, u32[]{:S(2)}) async-start(bf16[16,40,256]{2,1,0:T(8,128)(2,1)} %get-tuple-element.45), calls=%async_computation | async-start | bytes 655360 | tf_op jit(solution)/shard_map/all_to_all | solution.py:446
  11.9 2.4 %copy-start.5 = (s32[320]{0:T(512)S(1)}, s32[320]{0:T(512)}, u32[]{:S(2)}) copy-start(s32[320]{0:T(512)} %param.12) | copy-start | bytes 3844
  11.9 2.3 %copy-start.4 = (s32[8]{0:T(128)S(1)}, s32[8]{0:T(128)}, u32[]{:S(2)}) copy-start(s32[8]{0:T(128)} %spk.1) | copy-start | bytes 100
  12.1 3.1 %collective-permute-start.1 = (bf16[112,256]{1,0:T(8,128)(2,1)S(1)}, bf16[112,256]{1,0:T(8,128)(2,1)S(1)}, u32[]{:S(2)}, u32[]{:S(2)}) collective-permute-start(bf16[112,256]{1,0:T(8,128)(2,1)S(1)} %get-tuple-element.48), channel_id=1, source_target_pairs={{0,1},{1,0},{2,3},{3,2},{4,5},{5,4},{6,7},{7,6},{8,9},{9,8},{10,11... | collective-permute-start | bytes 172040 | tf_op jit(solution)/shard_map/ppermute | solution.py:416
  12.5 6.4 %collective-permute-start.2 = (bf16[112,256]{1,0:T(8,128)(2,1)S(1)}, bf16[112,256]{1,0:T(8,128)(2,1)S(1)}, u32[]{:S(2)}, u32[]{:S(2)}) collective-permute-start(bf16[112,256]{1,0:T(8,128)(2,1)S(1)} %get-tuple-element.49), channel_id=1, source_target_pairs={{0,2},{1,3},{2,0},{3,1},{4,6},{5,7},{6,4},{7,5},{8,10},{9,11},{10,... | collective-permute-start | bytes 172040 | tf_op jit(solution)/shard_map/ppermute | solution.py:416
  14.2 4.9 %collective-permute-start.3 = (bf16[112,256]{1,0:T(8,128)(2,1)S(1)}, bf16[112,256]{1,0:T(8,128)(2,1)S(1)}, u32[]{:S(2)}, u32[]{:S(2)}) collective-permute-start(bf16[112,256]{1,0:T(8,128)(2,1)S(1)} %get-tuple-element.50), channel_id=1, source_target_pairs={{0,3},{1,2},{2,1},{3,0},{4,7},{5,6},{6,5},{7,4},{8,11},{9,10},{10,... | collective-permute-start | bytes 172040 | tf_op jit(solution)/shard_map/ppermute | solution.py:416
  19.2 16.7 %collective-permute-start.6 = (bf16[400,256]{1,0:T(8,128)(2,1)S(1)}, bf16[400,256]{1,0:T(8,128)(2,1)S(1)}, u32[]{:S(2)}, u32[]{:S(2)}) collective-permute-start(bf16[400,256]{1,0:T(8,128)(2,1)S(1)} %shard_map.139), channel_id=1, source_target_pairs={{0,12},{1,13},{2,14},{3,15},{4,8},{5,9},{6,10},{7,11},{8,4},{9,5},... | collective-permute-start | bytes 614408 | tf_op jit(solution)/shard_map/ppermute | solution.py:416
  23.6 18.0 %collective-permute-start.5 = (bf16[400,256]{1,0:T(8,128)(2,1)S(1)}, bf16[400,256]{1,0:T(8,128)(2,1)S(1)}, u32[]{:S(2)}, u32[]{:S(2)}) collective-permute-start(bf16[400,256]{1,0:T(8,128)(2,1)S(1)} %shard_map.139), channel_id=1, source_target_pairs={{0,8},{1,9},{2,10},{3,11},{4,12},{5,13},{6,14},{7,15},{8,0},{9,1},... | collective-permute-start | bytes 614408 | tf_op jit(solution)/shard_map/ppermute | solution.py:416
  23.6 18.0 %collective-permute-start.4 = (bf16[400,256]{1,0:T(8,128)(2,1)S(1)}, bf16[400,256]{1,0:T(8,128)(2,1)S(1)}, u32[]{:S(2)}, u32[]{:S(2)}) collective-permute-start(bf16[400,256]{1,0:T(8,128)(2,1)S(1)} %shard_map.139), channel_id=1, source_target_pairs={{0,4},{1,5},{2,6},{3,7},{4,0},{5,1},{6,2},{7,3},{8,12},{9,13},{10,... | collective-permute-start | bytes 614408 | tf_op jit(solution)/shard_map/ppermute | solution.py:416
  24.2 10.7 %copy-start.3 = (bf16[1024,80]{0,1:T(8,128)(2,1)S(1)}, bf16[1024,80]{0,1:T(8,128)(2,1)}, u32[]{:S(2)}) copy-start(bf16[1024,80]{0,1:T(8,128)(2,1)} %param.10) | copy-start | bytes 491524
  43.1 1.9 %collective-permute-start.13 = (bf16[4,224,256]{2,1,0:T(8,128)(2,1)S(1)}, bf16[4,224,256]{2,1,0:T(8,128)(2,1)S(1)}, u32[]{:S(2)}, u32[]{:S(2)}) collective-permute-start(bf16[4,224,256]{2,1,0:T(8,128)(2,1)S(1)} %get-tuple-element.72), channel_id=1, source_target_pairs={{0,1},{1,0},{2,3},{3,2},{4,5},{5,4},{6,7},{7,6},{8,9},{9,8},{10,11... | collective-permute-start | bytes 1376264 | tf_op jit(solution)/shard_map/ppermute | solution.py:416
  45.1 5.4 %collective-permute-start.14 = (bf16[224,256]{1,0:T(8,128)(2,1)S(1)}, bf16[224,256]{1,0:T(8,128)(2,1)S(1)}, u32[]{:S(2)}, u32[]{:S(2)}) collective-permute-start(bf16[224,256]{1,0:T(8,128)(2,1)S(1)} %get-tuple-element.74), channel_id=1, source_target_pairs={{0,2},{1,3},{2,0},{3,1},{4,6},{5,7},{6,4},{7,5},{8,10},{9,11},{10,... | collective-permute-start | bytes 344072 | tf_op jit(solution)/shard_map/ppermute | solution.py:416
  45.6 16.2 %collective-permute-start.7 = (bf16[4,96,256]{2,1,0:T(8,128)(2,1)S(1)}, bf16[4,96,256]{2,1,0:T(8,128)(2,1)S(1)}, u32[]{:S(2)}, u32[]{:S(2)}) collective-permute-start(bf16[4,96,256]{2,1,0:T(8,128)(2,1)S(1)} %get-tuple-element.58), channel_id=1, source_target_pairs={{0,4},{1,5},{2,6},{3,7},{4,0},{5,1},{6,2},{7,3},{8,12},{9,13},{10,... | collective-permute-start | bytes 589832 | tf_op jit(solution)/shard_map/ppermute | solution.py:416
  45.6 17.2 %collective-permute-start.8 = (bf16[4,96,256]{2,1,0:T(8,128)(2,1)S(1)}, bf16[4,96,256]{2,1,0:T(8,128)(2,1)S(1)}, u32[]{:S(2)}, u32[]{:S(2)}) collective-permute-start(bf16[4,96,256]{2,1,0:T(8,128)(2,1)S(1)} %get-tuple-element.59), channel_id=1, source_target_pairs={{0,8},{1,9},{2,10},{3,11},{4,12},{5,13},{6,14},{7,15},{8,0},{9,1},... | collective-permute-start | bytes 589832 | tf_op jit(solution)/shard_map/ppermute | solution.py:416
  48.6 14.2 %collective-permute-start.9 = (bf16[4,96,256]{2,1,0:T(8,128)(2,1)S(1)}, bf16[4,96,256]{2,1,0:T(8,128)(2,1)S(1)}, u32[]{:S(2)}, u32[]{:S(2)}) collective-permute-start(bf16[4,96,256]{2,1,0:T(8,128)(2,1)S(1)} %get-tuple-element.60), channel_id=1, source_target_pairs={{0,12},{1,13},{2,14},{3,15},{4,8},{5,9},{6,10},{7,11},{8,4},{9,5},... | collective-permute-start | bytes 589832 | tf_op jit(solution)/shard_map/ppermute | solution.py:416
  50.0 6.8 %collective-permute-start.15 = (bf16[224,256]{1,0:T(8,128)(2,1)S(1)}, bf16[224,256]{1,0:T(8,128)(2,1)S(1)}, u32[]{:S(2)}, u32[]{:S(2)}) collective-permute-start(bf16[224,256]{1,0:T(8,128)(2,1)S(1)} %get-tuple-element.75), channel_id=1, source_target_pairs={{0,16},{16,0},{1,17},{17,1},{2,18},{18,2},{3,19},{19,3},{4,20},{20... | collective-permute-start | bytes 344072 | tf_op jit(solution)/shard_map/ppermute | solution.py:501
  50.5 6.3 %collective-permute-start.16 = (bf16[224,256]{1,0:T(8,128)(2,1)S(1)}, bf16[224,256]{1,0:T(8,128)(2,1)S(1)}, u32[]{:S(2)}, u32[]{:S(2)}) collective-permute-start(bf16[224,256]{1,0:T(8,128)(2,1)S(1)} %get-tuple-element.76), channel_id=1, source_target_pairs={{0,18},{1,19},{2,16},{3,17},{4,22},{5,23},{6,20},{7,21},{8,26},{9,... | collective-permute-start | bytes 344072 | tf_op jit(solution)/shard_map/ppermute | solution.py:501
  58.1 22.4 %all-to-all-start.1 = ((bf16[32,40,256]{2,1,0:T(8,128)(2,1)}), bf16[32,40,256]{2,1,0:T(8,128)(2,1)S(1)}, u32[]{:S(2)}, u32[]{:S(2)}) async-start(bf16[32,40,256]{2,1,0:T(8,128)(2,1)} %bitcast.10), calls=%async_computation.1 | async-start | bytes 1310720 | tf_op jit(solution)/shard_map/all_to_all | solution.py:510
  61.8 8.9 %copy-start.1 = (bf16[1024,32]{0,1:T(8,128)(2,1)S(1)}, bf16[1024,32]{0,1:T(8,128)(2,1)}, u32[]{:S(2)}) copy-start(bf16[1024,32]{0,1:T(8,128)(2,1)} %param.9) | copy-start | bytes 196612
  61.8 8.9 %copy-start.2 = (bf16[1024,32]{0,1:T(8,128)(2,1)S(1)}, bf16[1024,32]{0,1:T(8,128)(2,1)}, u32[]{:S(2)}) copy-start(bf16[1024,32]{0,1:T(8,128)(2,1)} %param.16) | copy-start | bytes 196612
  61.8 18.8 %copy-start = (f32[40,8,1024]{2,1,0:T(8,128)S(1)}, f32[40,8,1024]{2,1,0:T(8,128)}, u32[]{:S(2)}) copy-start(f32[40,8,1024]{2,1,0:T(8,128)} %param.14) | copy-start | bytes 3932164
  62.9 1.9 %collective-permute-start.10 = (bf16[96,256]{1,0:T(8,128)(2,1)S(1)}, bf16[96,256]{1,0:T(8,128)(2,1)S(1)}, u32[]{:S(2)}, u32[]{:S(2)}) collective-permute-start(bf16[96,256]{1,0:T(8,128)(2,1)S(1)} %get-tuple-element.62), channel_id=1, source_target_pairs={{0,1},{1,0},{2,3},{3,2},{4,5},{5,4},{6,7},{7,6},{8,9},{9,8},{10,11... | collective-permute-start | bytes 147464 | tf_op jit(solution)/shard_map/ppermute | solution.py:416
  63.0 6.8 %collective-permute-start.11 = (bf16[96,256]{1,0:T(8,128)(2,1)S(1)}, bf16[96,256]{1,0:T(8,128)(2,1)S(1)}, u32[]{:S(2)}, u32[]{:S(2)}) collective-permute-start(bf16[96,256]{1,0:T(8,128)(2,1)S(1)} %get-tuple-element.63), channel_id=1, source_target_pairs={{0,2},{1,3},{2,0},{3,1},{4,6},{5,7},{6,4},{7,5},{8,10},{9,11},{10,... | collective-permute-start | bytes 147464 | tf_op jit(solution)/shard_map/ppermute | solution.py:416
  64.5 6.1 %collective-permute-start.12 = (bf16[96,256]{1,0:T(8,128)(2,1)S(1)}, bf16[96,256]{1,0:T(8,128)(2,1)S(1)}, u32[]{:S(2)}, u32[]{:S(2)}) collective-permute-start(bf16[96,256]{1,0:T(8,128)(2,1)S(1)} %get-tuple-element.64), channel_id=1, source_target_pairs={{0,3},{1,2},{2,1},{3,0},{4,7},{5,6},{6,5},{7,4},{8,11},{9,10},{10,... | collective-permute-start | bytes 147464 | tf_op jit(solution)/shard_map/ppermute | solution.py:416

commit v11 on v10

--- a/solution.py
+++ b/solution.py
@@ -231,11 +231,11 @@
         ).astype(BF16)
 
 
-def turn(spk, packed, mel, other, conv, out, extra):
+def turn(spk, packed, mel, other, conv, out, extra, start):
     half, j = lax.axis_index("tm"), lax.axis_index("chan") & 3
     tokens, wide = 256, 384
     same = onehot(iota((256, 256), 0) == iota((256, 256), 1))
-    conv[...] = dot(same, packed[:, 0:OUT_AT, :].reshape(8 * OUT_AT, 256), NT).astype(BF16)
+    conv[...] = dot(same, packed[:, 0:TAPS, :].reshape(8 * TAPS, 256), NT).astype(BF16)
     out[...] = dot(same, packed[:, OUT_AT:PACKED, :].reshape(RESID, 256), NT).astype(BF16)
     m = iota((128, MELS), 0)
     mel_pick = onehot(((m & 15) < MEL_BLOCKS) & (iota((128, MELS), 1) == 8 * (m & 15) + (m >> 4)))
@@ -255,9 +255,11 @@
     for r in range(8):
         extra[r, 0:16] = mels[16 * r : 16 * r + 16]
         extra[r, 16:32] = onehot((row == seg + (lane >> 7)) & (sub == r))
-
-
-def layer(conv, out, extra, o0, o1, o2, o3, p1, p2, p3, kept, given, hidden_out, grad_out, feat, res, skp, natural, p0):
+    side = 8 * (OUT_AT - TAPS)
+    start[...] = dot(packed[:, TAPS:OUT_AT, :].reshape(side, 256), extra[...].reshape(side, wide), TN)
+
+
+def layer(conv, out, extra, start, o0, o1, o2, o3, p1, p2, p3, kept, given, hidden_out, grad_out, feat, res, skp, natural, p0):
     join(o0, o1, o2, o3, p0)
     ch = lax.axis_index("chan")
     got = (p0, p1, p2, p3)
@@ -293,9 +295,8 @@
     for r in range(8):
         feat[r, 0:64] = shifted[64 * r : 64 * r + 64]
         feat[r, 64:128] = sig[64 * r : 64 * r + 64]
-        feat[r, 128:160] = extra[r]
-    features = feat[...].reshape(8 * OUT_AT, wide)
-    pre = dot(conv[...], features)
+    features = feat[...].reshape(8 * TAPS, wide)
+    pre = start[...] + dot(conv[...], features)
     filt = jnp.tanh(pre[:128])
     gate = jax.nn.sigmoid(pre[128:])
     hidden = (filt[:, :tokens] * gate[:, :tokens]).astype(BF16)
@@ -311,11 +312,13 @@
     grad_out[...] = grad_pre
     grad_pre = grad_pre[:, :tokens]
     conv_grad = dot(features[:, :tokens], grad_pre, NT)
+    side_grad = dot(extra[:, :, :tokens].reshape(8 * (OUT_AT - TAPS), tokens), grad_pre, NT)
     res_grad = dot(res[:, :tokens], hidden, NT)
     skp_grad = dot(skp[:, :tokens], hidden, NT)
     core = ch & 1
     for part, rows, cols in (
-        (conv_grad.reshape(8, OUT_AT, 256), slice(0, OUT_AT), slice(0, 256)),
+        (conv_grad.reshape(8, TAPS, 256), slice(0, TAPS), slice(0, 256)),
+        (side_grad.reshape(8, OUT_AT - TAPS, 256), slice(TAPS, OUT_AT), slice(0, 256)),
         (res_grad.reshape(8, 64, 128), slice(OUT_AT, PACKED), slice(0, 128)),
         (skp_grad.reshape(8, 64, 128), slice(OUT_AT, PACKED), slice(128, 256)),
     ):
@@ -364,7 +367,7 @@
     outs, held, old, grad, sems = refs[:3], refs[3:6], (*refs[6:8], first), refs[8], refs[9]
     slots = grads.shape[1]
     rows = 8 * slots
-    steps = 8
+    steps = 10
     parts = [slice(n * rows // steps, (n + 1) * rows // steps) for n in range(steps)]
     fetches = []
     for n, part in enumerate(parts):
@@ -466,9 +469,10 @@
     turned = call(
         turn,
         (
-            sds((256, 8 * OUT_AT), BF16),
+            sds((256, 8 * TAPS), BF16),
             sds((256, RESID), BF16),
             sds((8, OUT_AT - TAPS, 384), BF16),
+            sds((256, 384), F32),
         ),
         (SMEM,) + (VMEM,) * 3,
         gflops=8,
@@ -476,10 +480,10 @@
     kept, given, hidden, grad_pre = call(
         layer,
         (sds(rows, F32), sds(rows, BF16), sds((128, 256), BF16), sds((256, 384), BF16)),
-        (VMEM,) * 10,
+        (VMEM,) * 11,
         gflops=0,
         scratch=(
-            pltpu.VMEM((8, OUT_AT, 384), BF16),
+            pltpu.VMEM((8, TAPS, 384), BF16),
             pltpu.VMEM((RESID, 384), BF16),
             pltpu.VMEM((RESID, 384), BF16),
             pltpu.VMEM((7, RESID, 128), F32),
@@ -517,7 +521,7 @@
         (sds(flat, F32),) * 3,
         (VMEM, VMEM, HBM, VMEM, HBM),
         scratch=(pltpu.VMEM(flat, F32),) * 5
-        + (pltpu.VMEM((8, flat[0], 128), F32), dma((40,))),
+        + (pltpu.VMEM((8, flat[0], 128), F32), dma((50,))),
         out_space=HBM,
     )(
         owned,

time: 84.4 us -> 84.3 us (level)
  no operation moved by 1% of the time
where the time goes in v11:
time: 84.3 us; the launch traced here: 83.9 us
  waiting for transfers between devices  30.1 us (36%)
  starting transfers between devices  29.7 us (35%)
  Pallas kernels  13 us (15%)
  blocking collectives  10.2 us (12%)
    ppermute x14, waiting for transfers between devices, swap(): return lax.ppermute(x, 'chan', [(i, i ^ k) for i in range(n)])  17.2 us
    ppermute x14, starting transfers between devices, swap(): return lax.ppermute(x, 'chan', [(i, i ^ k) for i in range(n)])  14.1 us
    pallas_call x13, Pallas kernels, call(): run(*(pin(x, f) if f else x for x, f in zip(args, fixed, strict=True)))  13 us
    all_gather x1, blocking collectives, local(): packed = lax.all_gather(gathered, BOTH, axis_index_groups=share)  10.2 us
    all_to_all x1, waiting for transfers between devices, local(): returned = lax.all_to_all(spread.reshape(32, slots_dev, 256), BOTH, 0, 0)  9.09 us
    all_to_all x1, starting transfers between devices, local(): arrived = lax.all_to_all(sent, 'chan', 0, 0, tiled=True)  5.91 us
    ppermute x1, waiting for transfers between devices, local(): lax.ppermute(g[2], 'tm', [(0, 1), (1, 0)])  3.79 us
    all_to_all x1, starting transfers between devices, local(): returned = lax.all_to_all(spread.reshape(32, slots_dev, 256), BOTH, 0, 0)  3.62 us
  transfers between devices with their start and end apart: 19, of which 9 were waited for; matrix products, arithmetic and copies ran while one was open for 0% of the time, Pallas kernels for 7%

profile of v11, /device:TPU:0, one launch (start us, length us, event | category | flops | bytes accessed | tf_op | source)
XLA Modules:
  0.0 83.9 jit_solution(11418814946916169485)
XLA Ops:
  0.6 2.3 %shard_map.136 = (bf16[16,40,256]{2,1,0:T(8,128)(2,1)}, bf16[3,32,1024]{2,1,0:T(8,128)(2,1)S(1)}, bf16[192,128]{1,0:T(8,128)(2,1)S(1)}) custom-call(s32[8]{0:T(128)} %spk.1, f32[320,1024]{1,0:T(8,128)} %bitcast.26, bf16[32,1024]{1,0:T(8,128)(2,1)} %bitcast.20, bf16[32,1024]{1,0:T(8,128)(2,1)} %bitcast.22, bf16[32,1024]{1,0:T(8,128)(2,1)} %bitcast.29, ...), custom_call_target="tpu_custom_call" | custom-call | bytes 1048576 | tf_op jit(solution)/shard_map/pallas_call | solution.py:75
  2.9 3.0 %collective-permute-start = (bf16[192,128]{1,0:T(8,128)(2,1)S(1)}, bf16[192,128]{1,0:T(8,128)(2,1)S(1)}, u32[]{:S(2)}, u32[]{:S(2)}) collective-permute-start(bf16[192,128]{1,0:T(8,128)(2,1)S(1)} %get-tuple-element.44), channel_id=1, source_target_pairs={{0,16},{16,0},{1,17},{17,1},{2,18},{18,2},{3,19},{19,3},{4,20},{20... | collective-permute-start | bytes 147464 | tf_op jit(solution)/shard_map/ppermute | solution.py:446
  6.0 5.9 %all-to-all-start = ((bf16[16,40,256]{2,1,0:T(8,128)(2,1)}), bf16[16,40,256]{2,1,0:T(8,128)(2,1)S(1)}, u32[]{:S(2)}, u32[]{:S(2)}) async-start(bf16[16,40,256]{2,1,0:T(8,128)(2,1)} %get-tuple-element.46), calls=%async_computation | async-start | bytes 655360 | tf_op jit(solution)/shard_map/all_to_all | solution.py:449
  12.1 0.4 collective-permute-start.1
  12.5 1.7 %collective-permute-start.2 = (bf16[112,256]{1,0:T(8,128)(2,1)S(1)}, bf16[112,256]{1,0:T(8,128)(2,1)S(1)}, u32[]{:S(2)}, u32[]{:S(2)}) collective-permute-start(bf16[112,256]{1,0:T(8,128)(2,1)S(1)} %get-tuple-element.50), channel_id=1, source_target_pairs={{0,2},{1,3},{2,0},{3,1},{4,6},{5,7},{6,4},{7,5},{8,10},{9,11},{10,... | collective-permute-start | bytes 172040 | tf_op jit(solution)/shard_map/ppermute | solution.py:419
  14.2 1.0 %shard_map.137 = (s32[224,128]{1,0:T(8,128)S(1)}, bf16[640,224]{1,0:T(8,128)(2,1)S(1)}, s32[8,128]{1,0:T(8,128)S(1)}) custom-call(s32[8]{0:T(128)S(1)} %copy-done.4, s32[1,320]{1,0:T(1,128)S(1)} %reshape.40.owners, bf16[192,128]{1,0:T(8,128)(2,1)S(1)} %collective-permute-done.other), custom_call_target="tpu_custom_call" | custom-call | bytes 1048576 | tf_op jit(solution)/shard_map/pallas_call | solution.py:75
  15.3 3.6 %collective-permute-done.2.o2 = bf16[112,256]{1,0:T(8,128)(2,1)S(1)} collective-permute-done((bf16[112,256]{1,0:T(8,128)(2,1)S(1)}, bf16[112,256]{1,0:T(8,128)(2,1)S(1)}, u32[]{:S(2)}, u32[]{:S(2)}) %collective-permute-start.2) | collective-permute-done | bytes 57376 | tf_op jit(solution)/shard_map/ppermute | solution.py:419
  19.2 4.4 %collective-permute-start.6 = (bf16[400,256]{1,0:T(8,128)(2,1)S(1)}, bf16[400,256]{1,0:T(8,128)(2,1)S(1)}, u32[]{:S(2)}, u32[]{:S(2)}) collective-permute-start(bf16[400,256]{1,0:T(8,128)(2,1)S(1)} %shard_map.139), channel_id=1, source_target_pairs={{0,12},{1,13},{2,14},{3,15},{4,8},{5,9},{6,10},{7,11},{8,4},{9,5},... | collective-permute-start | bytes 614408 | tf_op jit(solution)/shard_map/ppermute | solution.py:419
  23.6 0.6 collective-permute-start.4
  24.2 0.4 shard_map.140
  24.7 10.2 %all-gather = bf16[1792,256]{1,0:T(8,128)(2,1)S(1)} all-gather(bf16[224,256]{1,0:T(8,128)(2,1)S(1)} %shard_map.140), channel_id=2, replica_groups={{0,1,2,3,16,17,18,19},{4,5,6,7,20,21,22,23},{8,9,10,11,24,25,26,27},{12..., dimensions={0}, use_global_device_ids=true | all-gather | bytes 1032192 | tf_op jit(solution)/shard_map/all_gather | solution.py:467
  34.9 1.2 %shard_map.141 = (bf16[256,1024]{1,0:T(8,128)(2,1)S(1)}, bf16[256,512]{1,0:T(8,128)(2,1)S(1)}, bf16[8,32,384]{2,1,0:T(8,128)(2,1)S(1)}, f32[256,384]{1,0:T(8,128)S(1)}) custom-call(s32[8]{0:T(128)S(1)} %copy-done.4, bf16[8,224,256]{2,1,0:T(8,128)(2,1)S(1)} %bitcast.16, bf16[80,1024]{1,0:T(8,128)(2,1)S(1)} %bitcast.25, ...), custom_call_target="tpu_custom_call" | custom-call | flops 8000000000 | bytes 1048576 | tf_op jit(solution)/shard_map/pallas_call | solution.py:75
  36.1 5.4 %collective-permute-done.5.p2 = bf16[400,256]{1,0:T(8,128)(2,1)S(1)} collective-permute-done((bf16[400,256]{1,0:T(8,128)(2,1)S(1)}, bf16[400,256]{1,0:T(8,128)(2,1)S(1)}, u32[]{:S(2)}, u32[]{:S(2)}) %collective-permute-start.5) | collective-permute-done | bytes 204832 | tf_op jit(solution)/shard_map/ppermute | solution.py:419
  41.5 1.5 %shard_map.142 = (f32[4,224,256]{2,1,0:T(8,128)S(1)}, bf16[4,224,256]{2,1,0:T(8,128)(2,1)S(1)}, bf16[128,256]{1,0:T(8,128)(2,1)S(1)}, bf16[256,384]{1,0:T(8,128)(2,1)S(1)}) custom-call(bf16[256,1024]{1,0:T(8,128)(2,1)S(1)} %get-tuple-element.53.conv, bf16[256,512]{1,0:T(8,128)(2,1)S(1)} %get-tuple-element.54.out, ...), custom_call_target="tpu_custom_call" | custom-call | bytes 1048576 | tf_op jit(solution)/shard_map/pallas_call | solution.py:75
  43.2 0.7 shard_map.143
  43.9 1.0 %collective-permute-done.13.got = bf16[4,224,256]{2,1,0:T(8,128)(2,1)S(1)} collective-permute-done((bf16[4,224,256]{2,1,0:T(8,128)(2,1)S(1)}, bf16[4,224,256]{2,1,0:T(8,128)(2,1)S(1)}, u32[]{:S(2)}, u32[]{:S(2)}) %collective-permute-start.13) | collective-permute-done | bytes 458784 | tf_op jit(solution)/shard_map/ppermute | solution.py:419
  45.0 0.5 collective-permute-start.14
  45.5 3.0 %collective-permute-start.8 = (bf16[4,96,256]{2,1,0:T(8,128)(2,1)S(1)}, bf16[4,96,256]{2,1,0:T(8,128)(2,1)S(1)}, u32[]{:S(2)}, u32[]{:S(2)}) collective-permute-start(bf16[4,96,256]{2,1,0:T(8,128)(2,1)S(1)} %get-tuple-element.61), channel_id=1, source_target_pairs={{0,8},{1,9},{2,10},{3,11},{4,12},{5,13},{6,14},{7,15},{8,0},{9,1},... | collective-permute-start | bytes 589832 | tf_op jit(solution)/shard_map/ppermute | solution.py:419
  48.5 1.3 %collective-permute-start.9 = (bf16[4,96,256]{2,1,0:T(8,128)(2,1)S(1)}, bf16[4,96,256]{2,1,0:T(8,128)(2,1)S(1)}, u32[]{:S(2)}, u32[]{:S(2)}) collective-permute-start(bf16[4,96,256]{2,1,0:T(8,128)(2,1)S(1)} %get-tuple-element.62), channel_id=1, source_target_pairs={{0,12},{1,13},{2,14},{3,15},{4,8},{5,9},{6,10},{7,11},{8,4},{9,5},... | collective-permute-start | bytes 589832 | tf_op jit(solution)/shard_map/ppermute | solution.py:419
  49.9 0.5 collective-permute-start.15
  50.4 2.5 %collective-permute-start.16 = (bf16[224,256]{1,0:T(8,128)(2,1)S(1)}, bf16[224,256]{1,0:T(8,128)(2,1)S(1)}, u32[]{:S(2)}, u32[]{:S(2)}) collective-permute-start(bf16[224,256]{1,0:T(8,128)(2,1)S(1)} %get-tuple-element.78), channel_id=1, source_target_pairs={{0,18},{1,19},{2,16},{3,17},{4,22},{5,23},{6,20},{7,21},{8,26},{9,... | collective-permute-start | bytes 344072 | tf_op jit(solution)/shard_map/ppermute | solution.py:505
  52.9 3.8 %collective-permute-done.15.p2 = bf16[224,256]{1,0:T(8,128)(2,1)S(1)} collective-permute-done((bf16[224,256]{1,0:T(8,128)(2,1)S(1)}, bf16[224,256]{1,0:T(8,128)(2,1)S(1)}, u32[]{:S(2)}, u32[]{:S(2)}) %collective-permute-start.15) | collective-permute-done | bytes 114720 | tf_op jit(solution)/shard_map/ppermute | solution.py:505
  56.7 1.3 %shard_map.147 = bf16[2,640,256]{2,1,0:T(8,128)(2,1)} custom-call(bf16[640,224]{1,0:T(8,128)(2,1)S(1)} %get-tuple-element.71.put, f32[224,256]{1,0:T(8,128)S(1)} %get-tuple-element.75.p0, bf16[224,256]{1,0:T(8,128)(2,1)S(1)} %collective-permute-done.14.p1, bf16[224,256]{1,0:T(8,128)(2,1)S(1)} %collective-permute-done.15.p2, ...), custom_call_target="tpu_custom_call" | custom-call | bytes 1048576 | tf_op jit(solution)/shard_map/pallas_call | solution.py:75
  58.0 3.6 %all-to-all-start.1 = ((bf16[32,40,256]{2,1,0:T(8,128)(2,1)}), bf16[32,40,256]{2,1,0:T(8,128)(2,1)S(1)}, u32[]{:S(2)}, u32[]{:S(2)}) async-start(bf16[32,40,256]{2,1,0:T(8,128)(2,1)} %bitcast.10), calls=%async_computation.1 | async-start | bytes 1310720 | tf_op jit(solution)/shard_map/all_to_all | solution.py:514
  61.7 1.0 %collective-permute-done.8.z2 = bf16[4,96,256]{2,1,0:T(8,128)(2,1)S(1)} collective-permute-done((bf16[4,96,256]{2,1,0:T(8,128)(2,1)S(1)}, bf16[4,96,256]{2,1,0:T(8,128)(2,1)S(1)}, u32[]{:S(2)}, u32[]{:S(2)}) %collective-permute-start.8) | collective-permute-done | bytes 196640 | tf_op jit(solution)/shard_map/ppermute | solution.py:419
  62.9 1.5 %collective-permute-start.11 = (bf16[96,256]{1,0:T(8,128)(2,1)S(1)}, bf16[96,256]{1,0:T(8,128)(2,1)S(1)}, u32[]{:S(2)}, u32[]{:S(2)}) collective-permute-start(bf16[96,256]{1,0:T(8,128)(2,1)S(1)} %get-tuple-element.65), channel_id=1, source_target_pairs={{0,2},{1,3},{2,0},{3,1},{4,6},{5,7},{6,4},{7,5},{8,10},{9,11},{10,... | collective-permute-start | bytes 147464 | tf_op jit(solution)/shard_map/ppermute | solution.py:419
  64.4 0.3 collective-permute-start.12
  64.8 4.9 %collective-permute-done.11.o2 = bf16[96,256]{1,0:T(8,128)(2,1)S(1)} collective-permute-done((bf16[96,256]{1,0:T(8,128)(2,1)S(1)}, bf16[96,256]{1,0:T(8,128)(2,1)S(1)}, u32[]{:S(2)}, u32[]{:S(2)}) %collective-permute-start.11) | collective-permute-done | bytes 49184 | tf_op jit(solution)/shard_map/ppermute | solution.py:419
  69.7 0.8 collective-permute-done.12.o3
  70.5 0.8 shard_map.145
  71.3 9.1 %all-to-all-done.1.grads = bf16[32,40,256]{2,1,0:T(8,128)(2,1)S(1)} async-done(((bf16[32,40,256]{2,1,0:T(8,128)(2,1)}), bf16[32,40,256]{2,1,0:T(8,128)(2,1)S(1)}, u32[]{:S(2)}, u32[]{:S(2)}) %all-to-all-start.1) | async-done | bytes 655392 | tf_op jit(solution)/shard_map/all_to_all | solution.py:514
  80.4 3.5 %shard_map.148 = (f32[320,1024]{1,0:T(8,128)}, f32[320,1024]{1,0:T(8,128)}, f32[320,1024]{1,0:T(8,128)}) custom-call(s32[8,128]{1,0:T(8,128)S(1)} %get-tuple-element.70.owned, bf16[32,40,256]{2,1,0:T(8,128)(2,1)S(1)} %all-to-all-done.1.grads, f32[320,1024]{1,0:T(8,128)} %bitcast.27, f32[320,1024]{1,0:T(8,128)S(1)} %bitcast.18, f32[320,1024]{1,0:T(8,128)} %bitcast.28), custom_call_target="tpu_custom_call" | custom-call | bytes 1048576 | tf_op jit(solution)/shard_map/pallas_call | solution.py:75
  (33 shorter events, 1.0 us)
Async XLA Ops:
  2.9 9.0 %collective-permute-start = (bf16[192,128]{1,0:T(8,128)(2,1)S(1)}, bf16[192,128]{1,0:T(8,128)(2,1)S(1)}, u32[]{:S(2)}, u32[]{:S(2)}) collective-permute-start(bf16[192,128]{1,0:T(8,128)(2,1)S(1)} %get-tuple-element.44), channel_id=1, source_target_pairs={{0,16},{16,0},{1,17},{17,1},{2,18},{18,2},{3,19},{19,3},{4,20},{20... | collective-permute-start | bytes 147464 | tf_op jit(solution)/shard_map/ppermute | solution.py:446
  6.0 18.3 %all-to-all-start = ((bf16[16,40,256]{2,1,0:T(8,128)(2,1)}), bf16[16,40,256]{2,1,0:T(8,128)(2,1)S(1)}, u32[]{:S(2)}, u32[]{:S(2)}) async-start(bf16[16,40,256]{2,1,0:T(8,128)(2,1)} %get-tuple-element.46), calls=%async_computation | async-start | bytes 655360 | tf_op jit(solution)/shard_map/all_to_all | solution.py:449
  11.9 2.4 %copy-start.5 = (s32[320]{0:T(512)S(1)}, s32[320]{0:T(512)}, u32[]{:S(2)}) copy-start(s32[320]{0:T(512)} %param.12) | copy-start | bytes 3844
  11.9 2.3 %copy-start.4 = (s32[8]{0:T(128)S(1)}, s32[8]{0:T(128)}, u32[]{:S(2)}) copy-start(s32[8]{0:T(128)} %spk.1) | copy-start | bytes 100
  12.1 3.1 %collective-permute-start.1 = (bf16[112,256]{1,0:T(8,128)(2,1)S(1)}, bf16[112,256]{1,0:T(8,128)(2,1)S(1)}, u32[]{:S(2)}, u32[]{:S(2)}) collective-permute-start(bf16[112,256]{1,0:T(8,128)(2,1)S(1)} %get-tuple-element.49), channel_id=1, source_target_pairs={{0,1},{1,0},{2,3},{3,2},{4,5},{5,4},{6,7},{7,6},{8,9},{9,8},{10,11... | collective-permute-start | bytes 172040 | tf_op jit(solution)/shard_map/ppermute | solution.py:419
  12.5 6.4 %collective-permute-start.2 = (bf16[112,256]{1,0:T(8,128)(2,1)S(1)}, bf16[112,256]{1,0:T(8,128)(2,1)S(1)}, u32[]{:S(2)}, u32[]{:S(2)}) collective-permute-start(bf16[112,256]{1,0:T(8,128)(2,1)S(1)} %get-tuple-element.50), channel_id=1, source_target_pairs={{0,2},{1,3},{2,0},{3,1},{4,6},{5,7},{6,4},{7,5},{8,10},{9,11},{10,... | collective-permute-start | bytes 172040 | tf_op jit(solution)/shard_map/ppermute | solution.py:419
  14.2 4.9 %collective-permute-start.3 = (bf16[112,256]{1,0:T(8,128)(2,1)S(1)}, bf16[112,256]{1,0:T(8,128)(2,1)S(1)}, u32[]{:S(2)}, u32[]{:S(2)}) collective-permute-start(bf16[112,256]{1,0:T(8,128)(2,1)S(1)} %get-tuple-element.51), channel_id=1, source_target_pairs={{0,3},{1,2},{2,1},{3,0},{4,7},{5,6},{6,5},{7,4},{8,11},{9,10},{10,... | collective-permute-start | bytes 172040 | tf_op jit(solution)/shard_map/ppermute | solution.py:419
  19.2 16.9 %collective-permute-start.6 = (bf16[400,256]{1,0:T(8,128)(2,1)S(1)}, bf16[400,256]{1,0:T(8,128)(2,1)S(1)}, u32[]{:S(2)}, u32[]{:S(2)}) collective-permute-start(bf16[400,256]{1,0:T(8,128)(2,1)S(1)} %shard_map.139), channel_id=1, source_target_pairs={{0,12},{1,13},{2,14},{3,15},{4,8},{5,9},{6,10},{7,11},{8,4},{9,5},... | collective-permute-start | bytes 614408 | tf_op jit(solution)/shard_map/ppermute | solution.py:419
  23.6 18.0 %collective-permute-start.5 = (bf16[400,256]{1,0:T(8,128)(2,1)S(1)}, bf16[400,256]{1,0:T(8,128)(2,1)S(1)}, u32[]{:S(2)}, u32[]{:S(2)}) collective-permute-start(bf16[400,256]{1,0:T(8,128)(2,1)S(1)} %shard_map.139), channel_id=1, source_target_pairs={{0,8},{1,9},{2,10},{3,11},{4,12},{5,13},{6,14},{7,15},{8,0},{9,1},... | collective-permute-start | bytes 614408 | tf_op jit(solution)/shard_map/ppermute | solution.py:419
  23.6 18.0 %collective-permute-start.4 = (bf16[400,256]{1,0:T(8,128)(2,1)S(1)}, bf16[400,256]{1,0:T(8,128)(2,1)S(1)}, u32[]{:S(2)}, u32[]{:S(2)}) collective-permute-start(bf16[400,256]{1,0:T(8,128)(2,1)S(1)} %shard_map.139), channel_id=1, source_target_pairs={{0,4},{1,5},{2,6},{3,7},{4,0},{5,1},{6,2},{7,3},{8,12},{9,13},{10,... | collective-permute-start | bytes 614408 | tf_op jit(solution)/shard_map/ppermute | solution.py:419
  24.2 10.7 %copy-start.3 = (bf16[1024,80]{0,1:T(8,128)(2,1)S(1)}, bf16[1024,80]{0,1:T(8,128)(2,1)}, u32[]{:S(2)}) copy-start(bf16[1024,80]{0,1:T(8,128)(2,1)} %param.10) | copy-start | bytes 491524
  43.0 1.9 %collective-permute-start.13 = (bf16[4,224,256]{2,1,0:T(8,128)(2,1)S(1)}, bf16[4,224,256]{2,1,0:T(8,128)(2,1)S(1)}, u32[]{:S(2)}, u32[]{:S(2)}) collective-permute-start(bf16[4,224,256]{2,1,0:T(8,128)(2,1)S(1)} %get-tuple-element.74), channel_id=1, source_target_pairs={{0,1},{1,0},{2,3},{3,2},{4,5},{5,4},{6,7},{7,6},{8,9},{9,8},{10,11... | collective-permute-start | bytes 1376264 | tf_op jit(solution)/shard_map/ppermute | solution.py:419
  45.0 5.4 %collective-permute-start.14 = (bf16[224,256]{1,0:T(8,128)(2,1)S(1)}, bf16[224,256]{1,0:T(8,128)(2,1)S(1)}, u32[]{:S(2)}, u32[]{:S(2)}) collective-permute-start(bf16[224,256]{1,0:T(8,128)(2,1)S(1)} %get-tuple-element.76), channel_id=1, source_target_pairs={{0,2},{1,3},{2,0},{3,1},{4,6},{5,7},{6,4},{7,5},{8,10},{9,11},{10,... | collective-permute-start | bytes 344072 | tf_op jit(solution)/shard_map/ppermute | solution.py:419
  45.5 16.2 %collective-permute-start.7 = (bf16[4,96,256]{2,1,0:T(8,128)(2,1)S(1)}, bf16[4,96,256]{2,1,0:T(8,128)(2,1)S(1)}, u32[]{:S(2)}, u32[]{:S(2)}) collective-permute-start(bf16[4,96,256]{2,1,0:T(8,128)(2,1)S(1)} %get-tuple-element.60), channel_id=1, source_target_pairs={{0,4},{1,5},{2,6},{3,7},{4,0},{5,1},{6,2},{7,3},{8,12},{9,13},{10,... | collective-permute-start | bytes 589832 | tf_op jit(solution)/shard_map/ppermute | solution.py:419
  45.5 17.2 %collective-permute-start.8 = (bf16[4,96,256]{2,1,0:T(8,128)(2,1)S(1)}, bf16[4,96,256]{2,1,0:T(8,128)(2,1)S(1)}, u32[]{:S(2)}, u32[]{:S(2)}) collective-permute-start(bf16[4,96,256]{2,1,0:T(8,128)(2,1)S(1)} %get-tuple-element.61), channel_id=1, source_target_pairs={{0,8},{1,9},{2,10},{3,11},{4,12},{5,13},{6,14},{7,15},{8,0},{9,1},... | collective-permute-start | bytes 589832 | tf_op jit(solution)/shard_map/ppermute | solution.py:419
  48.5 14.2 %collective-permute-start.9 = (bf16[4,96,256]{2,1,0:T(8,128)(2,1)S(1)}, bf16[4,96,256]{2,1,0:T(8,128)(2,1)S(1)}, u32[]{:S(2)}, u32[]{:S(2)}) collective-permute-start(bf16[4,96,256]{2,1,0:T(8,128)(2,1)S(1)} %get-tuple-element.62), channel_id=1, source_target_pairs={{0,12},{1,13},{2,14},{3,15},{4,8},{5,9},{6,10},{7,11},{8,4},{9,5},... | collective-permute-start | bytes 589832 | tf_op jit(solution)/shard_map/ppermute | solution.py:419
  49.9 6.8 %collective-permute-start.15 = (bf16[224,256]{1,0:T(8,128)(2,1)S(1)}, bf16[224,256]{1,0:T(8,128)(2,1)S(1)}, u32[]{:S(2)}, u32[]{:S(2)}) collective-permute-start(bf16[224,256]{1,0:T(8,128)(2,1)S(1)} %get-tuple-element.77), channel_id=1, source_target_pairs={{0,16},{16,0},{1,17},{17,1},{2,18},{18,2},{3,19},{19,3},{4,20},{20... | collective-permute-start | bytes 344072 | tf_op jit(solution)/shard_map/ppermute | solution.py:505
  50.4 6.3 %collective-permute-start.16 = (bf16[224,256]{1,0:T(8,128)(2,1)S(1)}, bf16[224,256]{1,0:T(8,128)(2,1)S(1)}, u32[]{:S(2)}, u32[]{:S(2)}) collective-permute-start(bf16[224,256]{1,0:T(8,128)(2,1)S(1)} %get-tuple-element.78), channel_id=1, source_target_pairs={{0,18},{1,19},{2,16},{3,17},{4,22},{5,23},{6,20},{7,21},{8,26},{9,... | collective-permute-start | bytes 344072 | tf_op jit(solution)/shard_map/ppermute | solution.py:505
  58.0 22.4 %all-to-all-start.1 = ((bf16[32,40,256]{2,1,0:T(8,128)(2,1)}), bf16[32,40,256]{2,1,0:T(8,128)(2,1)S(1)}, u32[]{:S(2)}, u32[]{:S(2)}) async-start(bf16[32,40,256]{2,1,0:T(8,128)(2,1)} %bitcast.10), calls=%async_computation.1 | async-start | bytes 1310720 | tf_op jit(solution)/shard_map/all_to_all | solution.py:514
  61.7 8.9 %copy-start.1 = (bf16[1024,32]{0,1:T(8,128)(2,1)S(1)}, bf16[1024,32]{0,1:T(8,128)(2,1)}, u32[]{:S(2)}) copy-start(bf16[1024,32]{0,1:T(8,128)(2,1)} %param.9) | copy-start | bytes 196612
  61.7 8.9 %copy-start.2 = (bf16[1024,32]{0,1:T(8,128)(2,1)S(1)}, bf16[1024,32]{0,1:T(8,128)(2,1)}, u32[]{:S(2)}) copy-start(bf16[1024,32]{0,1:T(8,128)(2,1)} %param.16) | copy-start | bytes 196612
  61.7 18.8 %copy-start = (f32[40,8,1024]{2,1,0:T(8,128)S(1)}, f32[40,8,1024]{2,1,0:T(8,128)}, u32[]{:S(2)}) copy-start(f32[40,8,1024]{2,1,0:T(8,128)} %param.14) | copy-start | bytes 3932164
  62.8 1.9 %collective-permute-start.10 = (bf16[96,256]{1,0:T(8,128)(2,1)S(1)}, bf16[96,256]{1,0:T(8,128)(2,1)S(1)}, u32[]{:S(2)}, u32[]{:S(2)}) collective-permute-start(bf16[96,256]{1,0:T(8,128)(2,1)S(1)} %get-tuple-element.64), channel_id=1, source_target_pairs={{0,1},{1,0},{2,3},{3,2},{4,5},{5,4},{6,7},{7,6},{8,9},{9,8},{10,11... | collective-permute-start | bytes 147464 | tf_op jit(solution)/shard_map/ppermute | solution.py:419
  62.9 6.8 %collective-permute-start.11 = (bf16[96,256]{1,0:T(8,128)(2,1)S(1)}, bf16[96,256]{1,0:T(8,128)(2,1)S(1)}, u32[]{:S(2)}, u32[]{:S(2)}) collective-permute-start(bf16[96,256]{1,0:T(8,128)(2,1)S(1)} %get-tuple-element.65), channel_id=1, source_target_pairs={{0,2},{1,3},{2,0},{3,1},{4,6},{5,7},{6,4},{7,5},{8,10},{9,11},{10,... | collective-permute-start | bytes 147464 | tf_op jit(solution)/shard_map/ppermute | solution.py:419
  64.4 6.1 %collective-permute-start.12 = (bf16[96,256]{1,0:T(8,128)(2,1)S(1)}, bf16[96,256]{1,0:T(8,128)(2,1)S(1)}, u32[]{:S(2)}, u32[]{:S(2)}) collective-permute-start(bf16[96,256]{1,0:T(8,128)(2,1)S(1)} %get-tuple-element.66), channel_id=1, source_target_pairs={{0,3},{1,2},{2,1},{3,0},{4,7},{5,6},{6,5},{7,4},{8,11},{9,10},{10,... | collective-permute-start | bytes 147464 | tf_op jit(solution)/shard_map/ppermute | solution.py:419
